TPU v7x, 256 devices: a whole 4x4x8 slice. The times are simulated.
256 devices in a mesh: user: 64 (over z, y, x_hi), feat: 4 (over x_lo, core).
Axes of the slice: x: 4 (x_hi: 2, x_lo: 2; x = x_hi * 2 + x_lo), y: 4, z: 8, core: 2. Of those that a mesh axis runs over, the one named last changes fastest.
Arguments:
- view_one: bfloat16 [8192, 2048], P('user', 'feat'), may hold values from -8 to 8
- view_two: bfloat16 [8192, 2048], P('user', 'feat'), may hold values from -8 to 8
- partner: int32 [8192], P('user'), may hold values from 0 to 8191, each once
Outputs:
- grad_one: float32 [8192, 2048], P('user', 'feat')
- grad_two: float32 [8192, 2048], P('user', 'feat')
Inputs may be any that keep to these rules, and one draw needn't show every extreme that they name: `partner`: each index of view_two appears exactly once.
All inputs are finite; a program needn't handle non-finite values.
Results may differ from a plain program's by a relative error of at most 0.0028.
Values may be sent and summed in bfloat16 or wider, within the bound.
No kernel may reach another device: no remote copies, remote signals or barrier semaphores. Data moves between devices by JAX's collectives and lax.ppermute only.
A program may use at most 128 MiB of HBM per device.

v0:
```python
import math

import jax
import jax.numpy as jnp
from jax import lax
from jax.sharding import PartitionSpec as P

D = 2048


def combined_all(value, axis, join):
    pieces = jax.tree.map(lambda part: lax.all_gather(part, axis), value)
    head = jax.tree.map(lambda part: part[0], pieces)
    tail = jax.tree.map(lambda part: part[1:], pieces)
    total, _ = lax.scan(lambda total, piece: (join(total, piece), None), head, tail)
    return total


def merge_stats(first, second):
    highest = jnp.maximum(first[0], second[0])
    return (
        highest,
        first[1] * jnp.exp(first[0] - highest) + second[1] * jnp.exp(second[0] - highest),
    )


def couple(scores_cols, row_lse, col_lse, partner, column_index):
    positive_mask = (column_index[:, None] == partner[None, :]).astype(jnp.float32)
    both = jnp.exp(scores_cols - row_lse[None, :]) + jnp.exp(scores_cols - col_lse[:, None])
    return (0.5 * both - positive_mask).astype(jnp.bfloat16)


def column_local(scores_cols):
    col_highest = jnp.max(scores_cols, axis=1)
    col_total = jnp.sum(jnp.exp(scores_cols - col_highest[:, None]), axis=1)
    return (col_highest, col_total)


def row_local(scores_cols):
    row_highest = jnp.max(scores_cols, axis=0)
    row_total = jnp.sum(jnp.exp(scores_cols - row_highest[None, :]), axis=0)
    return (row_highest, row_total)


def on_device(view_one, view_two, partner):
    logit_scale = 2.0 / math.sqrt(D)
    contract_width = (((1,), (1,)), ((), ()))
    contract_rows = (((0,), (0,)), ((), ()))
    every_two = lax.all_gather(view_two, "user", axis=0, tiled=True)
    block_rows = every_two
    scores_cols = lax.psum_scatter(
        logit_scale
        * lax.dot_general(block_rows, view_one, contract_width, preferred_element_type=jnp.float32),
        "feat",
        scatter_dimension=0,
        tiled=True,
    )
    row_highest, row_total = row_local(scores_cols)
    row_highest, row_total = combined_all((row_highest, row_total), "feat", merge_stats)
    col_highest, col_total = column_local(scores_cols)
    col_highest, col_total = combined_all((col_highest, col_total), "user", merge_stats)
    row_lse = row_highest + jnp.log(row_total)
    col_lse = col_highest + jnp.log(col_total)
    column_index = lax.axis_index("feat") * scores_cols.shape[0] + jnp.arange(
        scores_cols.shape[0], dtype=jnp.int32
    )
    coupling_local = couple(scores_cols, row_lse, col_lse, partner, column_index)
    coupling_all = lax.all_gather(coupling_local, "feat", axis=0, tiled=True)
    grad_one = lax.dot_general(
        coupling_all, every_two, contract_rows, preferred_element_type=jnp.float32
    )
    block_rows = coupling_all
    grad_two = lax.psum_scatter(
        jnp.dot(block_rows, view_one, preferred_element_type=jnp.float32),
        "user",
        scatter_dimension=0,
        tiled=True,
    )
    return (grad_one, grad_two)


def solution(mesh):
    return jax.shard_map(
        on_device,
        mesh=mesh,
        in_specs=(P("user", "feat"), P("user", "feat"), P("user")),
        out_specs=(P("user", "feat"), P("user", "feat")),
        check_vma=False,
    )
```

profile of v0, /device:TPU:4, one launch (start us, length us, event | category | flops | bytes accessed | tf_op | source)
XLA Modules:
  0.0 1041.4 jit_solution(6270216447361381772)
XLA Ops:
  7.2 0.0 copy-start
  7.2 0.0 all-gather.9.cloned.1.call-start
  7.2 0.7 all-gather.9.cloned.1.call-update
  7.9 0.0 reduce-scatter.3.cloned.1.call-start
  8.0 154.7 %all-gather.9.cloned.1.call-done = bf16[8192,512]{1,0:T(8,128)(2,1)} async-done(((bf16[128,512]{1,0:T(8,128)(2,1)}), bf16[8192,512]{1,0:T(8,128)(2,1)}) %all-gather.9.cloned.1.call-update) | async-done | bytes 8388624 | tf_op jit(solution)/shard_map/all_gather | solution.py:49
  162.7 0.0 copy-done
  162.7 7.7 convolution_multiply_fusion
  170.3 0.0 reduce-scatter.3.cloned.1.call-update
  170.4 0.0 copy-start.3
  170.4 0.0 all-gather.11.cloned.1.call-start
  170.4 47.0 %reduce-scatter.3.cloned.1.call-done = f32[2048,128]{1,0:T(8,128)} async-done(((f32[8192,128]{1,0:T(8,128)}), f32[2048,128]{1,0:T(8,128)}) %reduce-scatter.3.cloned.1.call-update) | async-done | bytes 1048592 | tf_op jit(solution)/shard_map/reduce_scatter | solution.py:51
  217.5 0.0 copy-start.2
  217.5 1.7 fusion.5
  219.1 5.0 all-gather.4
  224.2 1.9 exponential_reduce_fusion.1
  226.0 5.0 all-gather.5
  231.1 178.4 %all-gather.2 = f32[131072]{0:T(1024)S(1)} all-gather(f32[2048]{0:T(1024)S(1)} %get-tuple-element.65), channel_id=4, replica_groups=mesh['user'=64,'feat'=4] {'user'}, dimensions={0}, use_global_device_ids=true | all-gather | bytes 532480 | tf_op jit(solution)/shard_map/all_gather | solution.py:12
  409.5 183.5 %all-gather.3 = f32[131072]{0:T(1024)S(1)} all-gather(f32[2048]{0:T(1024)S(1)} %get-tuple-element.63), channel_id=5, replica_groups=mesh['user'=64,'feat'=4] {'user'}, dimensions={0}, use_global_device_ids=true | all-gather | bytes 532480 | tf_op jit(solution)/shard_map/all_gather | solution.py:12
  593.1 0.1 while.24
  593.2 0.1 reshape.27
  593.3 0.1 reshape.28
  593.4 3.9 while.25
  597.4 0.0 copy-done.3
  597.4 0.0 copy-done.2
  597.4 1.4 subtract_convert_fusion
  598.8 0.0 all-gather.11.cloned.1.call-update
  598.8 0.0 reduce-scatter.5.cloned.1.call-start
  598.9 27.3 %all-gather.11.cloned.1.call-done = bf16[8192,128]{1,0:T(8,128)(2,1)} async-done(((bf16[2048,128]{1,0:T(8,128)(2,1)}), bf16[8192,128]{1,0:T(8,128)(2,1)}) %all-gather.11.cloned.1.call-update) | async-done | bytes 2097168 | tf_op jit(solution)/shard_map/all_gather | solution.py:68
  626.1 9.6 fusion.8
  635.8 0.0 copy-start.1
  635.8 0.0 reduce-scatter.5.cloned.1.call-update
  635.8 1.6 copy-done.1
  637.4 5.4 fusion.7
  642.7 392.1 %reduce-scatter.5.cloned.1.call-done = f32[128,512]{1,0:T(8,128)} async-done(((f32[8192,512]{1,0:T(8,128)}), f32[128,512]{1,0:T(8,128)}) %reduce-scatter.5.cloned.1.call-update) | async-done | bytes 262160 | tf_op jit(solution)/shard_map/reduce_scatter | solution.py:73
  (142 shorter events, 2.3 us)
Async XLA Ops:
  7.2 155.5 %copy-start = (bf16[128,512]{1,0:T(8,128)(2,1)S(1)}, bf16[128,512]{1,0:T(8,128)(2,1)}, u32[]{:S(2)}) copy-start(bf16[128,512]{1,0:T(8,128)(2,1)} %param.7) | copy-start | bytes 393220
  7.2 155.5 %all-gather.9.cloned.1.call-start = ((), (), s32[]{:S(2)}) async-start(), calls=%async_computation.2 | async-start | bytes 8519680 | tf_op jit(solution)/shard_map/all_gather | solution.py:49
  7.9 209.6 %reduce-scatter.3.cloned.1.call-start = ((), (), s32[]{:S(2)}) async-start(), calls=%async_computation.3 | async-start | bytes 5242880 | tf_op jit(solution)/shard_map/reduce_scatter | solution.py:51
  170.4 427.0 %copy-start.3 = (s32[128]{0:T(128)S(1)}, s32[128]{0:T(128)}, u32[]{:S(2)}) copy-start(s32[128]{0:T(128)} %param.9) | copy-start | bytes 1540
  170.4 455.8 %all-gather.11.cloned.1.call-start = ((), (), s32[]{:S(2)}) async-start(), calls=%async_computation.4 | async-start | bytes 2621440 | tf_op jit(solution)/shard_map/all_gather | solution.py:68
  217.5 379.9 %copy-start.2 = (f32[2048,128]{1,0:T(8,128)S(1)}, f32[2048,128]{1,0:T(8,128)}, u32[]{:S(2)}) copy-start(f32[2048,128]{1,0:T(8,128)} %reduce-scatter.3.cloned.1.call-done) | copy-start | bytes 3145732
  598.8 436.1 %reduce-scatter.5.cloned.1.call-start = ((), (), s32[]{:S(2)}) async-start(), calls=%async_computation.5 | async-start | bytes 17039360 | tf_op jit(solution)/shard_map/reduce_scatter | solution.py:73
  635.8 1.6 copy-start.1
Sparse Core Ops, SparseCore 0:
  11.5 151.1 all-gather.8
  170.5 46.9 reduce-scatter.2
  598.9 27.1 all-gather.10
  635.9 398.9 reduce-scatter.4
where the time goes:
time: 1050 us; the launch traced here: 1040 us
  waiting for transfers between devices  622 us (59%)
  blocking collectives  372 us (35%)
  matrix products  22.7 us (2%)
  between operations  13.9 us (1%)
    reduce_scatter x1, waiting for transfers between devices, on_device(): lax.psum_scatter(jnp.dot(block_rows, view_one, preferred_element_type=jnp...  392 us
    all_gather x4, blocking collectives, combined_all(): pieces = jax.tree.map(lambda part: lax.all_gather(part, axis), value)  372 us
    all_gather x1, waiting for transfers between devices, on_device(): every_two = lax.all_gather(view_two, 'user', axis=0, tiled=True)  155 us
    reduce_scatter x1, waiting for transfers between devices, on_device(): lax.psum_scatter(logit_scale * lax.dot_general(block_rows, view_one, cont...  47 us
    all_gather x1, waiting for transfers between devices, on_device(): coupling_all = lax.all_gather(coupling_local, 'feat', axis=0, tiled=True)  27.3 us
  transfers between devices with their start and end apart: 4, of which 4 were waited for; matrix products, arithmetic and copies ran while one was open for 1% of the time, Pallas kernels for 0%

commit v1 on v0

v1 whole, which is shorter than its diff:
```python
import math

import jax
import jax.numpy as jnp
from jax import lax
from jax.experimental import pallas as pl
from jax.experimental.pallas import tpu as pltpu
from jax.sharding import Mesh
from jax.sharding import PartitionSpec as P

D = 2048
NZ, NY, NXH, NXL, NC = 8, 4, 2, 2, 2
PLANE = ("y", "xh", "xl")
EVERY = ("z", "y", "xh", "xl", "core")
ROWS = 128
HALF = 64
WIDTH = 512
NI = NY * NXH * ROWS
NJ = NZ * HALF


def score_kernel(v1_ref, *refs):
    v2_refs, s_ref, cat_ref = refs[:NZ], refs[NZ], refs[NZ + 1]
    for k in range(NZ):
        cat_ref[:, k * HALF : (k + 1) * HALF, :] = v2_refs[k][...]
    contract = (((1,), (1,)), ((), ()))
    for u in range(NI // ROWS):
        s_ref[u * ROWS : (u + 1) * ROWS, :] = lax.dot_general(
            v1_ref[u, 0], cat_ref[0], contract, preferred_element_type=jnp.float32
        ) + lax.dot_general(
            v1_ref[u, 1], cat_ref[1], contract, preferred_element_type=jnp.float32
        )
    most_two = jnp.max(jnp.abs(cat_ref[...]).astype(jnp.float32))
    most_one = jnp.max(jnp.abs(v1_ref[...]).astype(jnp.float32))
    row = lax.broadcasted_iota(jnp.int32, (8, NJ), 0)
    s_ref[NI : NI + 8, :] = jnp.where(row < 4, most_two, most_one)


def partial_scores(v1_all, v2_parts):
    vmem = pl.BlockSpec(memory_space=pltpu.VMEM)
    return pl.pallas_call(
        score_kernel,
        out_shape=(
            jax.ShapeDtypeStruct((NI + 8, NJ), jnp.float32),
            jax.ShapeDtypeStruct((NXL, NJ, WIDTH), jnp.bfloat16),
        ),
        in_specs=[vmem] * (1 + NZ),
        out_specs=(vmem, vmem),
        compiler_params=pltpu.CompilerParams(vmem_limit_bytes=48 * 1024 * 1024),
        cost_estimate=pl.CostEstimate(
            flops=2 * NI * NJ * NXL * WIDTH, bytes_accessed=6 * 2**20, transcendentals=0
        ),
    )(v1_all, *v2_parts)


def swap(x, axis):
    return lax.ppermute(x, axis, [(0, 1), (1, 0)])


def merged_lse(highest, total):
    top = jnp.max(highest, axis=0)
    return top + jnp.log(jnp.sum(total * jnp.exp(highest - top[None]), axis=0))


def stat_groups():
    def number(z, y, xh, xl, c):
        return (((z * NY + y) * NXH + xh) * NXL + xl) * NC + c

    planes = [
        [number(z, y, xh, xl, 0) for y in range(NY) for xh in range(NXH) for xl in range(NXL)]
        for z in range(NZ)
    ]
    columns = [
        [number(z, y, xh, xl, 1) for z in range(NZ) for xl in range(NXL)]
        for y in range(NY)
        for xh in range(NXH)
    ]
    return planes + columns


def on_device(view_one, view_two, partner):
    logit_scale = 2.0 / math.sqrt(D)
    z = lax.axis_index("z")
    uhigh = lax.axis_index("y") * NXH + lax.axis_index("xh")
    xl = lax.axis_index("xl")
    core = lax.axis_index("core")

    keep = lax.dynamic_slice(view_two, (xl * HALF, 0), (HALF, WIDTH))
    give = lax.dynamic_slice(view_two, ((1 - xl) * HALF, 0), (HALF, WIDTH))
    got = swap(give, "xl")
    mine = jnp.where(xl == 0, jnp.stack([keep, got]), jnp.stack([got, keep]))
    v2_parts = [mine] + [
        lax.ppermute(mine, "z", [(i, (i + k) % NZ) for i in range(NZ)]) for k in range(1, NZ)
    ]
    v1_all = lax.all_to_all(
        jnp.broadcast_to(view_one[None], (16, ROWS, WIDTH)), PLANE, 0, 0, tiled=True
    ).reshape(NY * NXH, NXL, ROWS, WIDTH)

    part, v2_all = partial_scores(v1_all, v2_parts)
    other = swap(part, "core")
    scores = logit_scale * (part[:NI] + other[:NI])
    most = jnp.maximum(part[NI:, 0], other[NI:, 0])
    most_two = jnp.maximum(most[0], 1e-30)
    most_one = jnp.maximum(most[4], 1e-30)

    row_highest = jnp.max(scores, axis=1)
    row_total = jnp.sum(jnp.exp(scores - row_highest[:, None]), axis=1)
    col_highest = jnp.max(scores, axis=0)
    col_total = jnp.sum(jnp.exp(scores - col_highest[None, :]), axis=0)

    turn = (z - jnp.arange(NZ)) % NZ
    pick = turn[:, None] == jnp.arange(NZ)[None, :]

    def reorder(x):
        return jnp.sum(jnp.where(pick[:, :, None], x.reshape(1, NZ, HALF), 0.0), axis=1).reshape(-1)

    row_tail = jnp.concatenate(
        [partner.astype(jnp.float32), jnp.full((128,), most_two), jnp.zeros((256,), jnp.float32)]
    )
    row_pack = jnp.concatenate(
        [row_highest, row_total, row_tail, jnp.zeros((3 * 512,), jnp.float32)]
    )
    col_pack = jnp.concatenate(
        [
            reorder(col_highest),
            reorder(col_total),
            jnp.zeros((2 * 512,), jnp.float32),
            jnp.full((512,), most_one),
            jnp.zeros((3 * 512,), jnp.float32),
        ]
    )
    pack = jnp.where(core == 0, row_pack, col_pack).reshape(8, 512)
    seen = lax.all_to_all(
        jnp.broadcast_to(pack[None], (16, 8, 512)),
        EVERY,
        0,
        0,
        axis_index_groups=stat_groups(),
        tiled=True,
    )
    row_lse = merged_lse(seen[:, 0:2].reshape(16, NI), seen[:, 2:4].reshape(16, NI))
    row_partner = seen.reshape(8, 2, 8, 512)[:, 0, 4, :ROWS].reshape(NI)
    two_most = seen[:, 4, 128]
    by_z = seen.reshape(NZ, NXL, 8, 512)
    by_z = jnp.where(xl == 0, by_z[:, 0], by_z[:, 1])
    col_lse = reorder(merged_lse(by_z[:, 0], by_z[:, 1]))
    one_most = by_z[:, 4, 128]
    tail0 = jnp.concatenate([two_most, jnp.zeros((512 - 16,), jnp.float32)])
    tail1 = jnp.concatenate([one_most, jnp.zeros((512 - 8,), jnp.float32)])
    zeros = jnp.zeros((512,), jnp.float32)
    known0 = jnp.concatenate([row_lse, row_partner, tail0, zeros, zeros, zeros])
    known1 = jnp.concatenate([col_lse, zeros, zeros, zeros, tail1, zeros, zeros, zeros])
    known = jnp.where(core == 0, known0, known1).reshape(8, 512)
    told = swap(known, "core")
    rows = jnp.where(core == 0, known, told)
    cols = jnp.where(core == 0, told, known)
    row_lse = rows[0:2].reshape(NI)
    row_partner = rows[2:4].reshape(NI).astype(jnp.int32)
    two_most = rows[4, :16]
    col_lse = cols[0]
    one_most = cols[4, :NZ]

    block = (z - jnp.arange(NZ)) % NZ
    index = ((block * (NY * NXH) + uhigh) * ROWS + xl * HALF)[:, None] + jnp.arange(HALF)[None, :]
    positive = (index.reshape(1, NJ) == row_partner[:, None]).astype(jnp.float32)
    both = jnp.exp(scores - row_lse[:, None]) + jnp.exp(scores - col_lse[None, :])
    coupling = (0.5 * both - positive).astype(jnp.bfloat16)

    part_two = jnp.einsum(
        "uij,uxik->jxk",
        coupling.reshape(8, ROWS, NJ),
        v1_all,
        preferred_element_type=jnp.float32,
    )
    part_two = (part_two * (64.0 / most_one)).astype(jnp.float16).reshape(NZ, HALF, NXL, WIDTH)
    two_parts = [part_two[0]] + [
        lax.ppermute(part_two[k], "z", [(i, (i - k) % NZ) for i in range(NZ)])
        for k in range(1, NZ)
    ]
    part_one = jnp.einsum(
        "uij,xjk->uxik",
        coupling.reshape(8, ROWS, NJ),
        v2_all,
        preferred_element_type=jnp.float32,
    )
    part_one = (part_one * (128.0 / most_two)).astype(jnp.float16)
    one_parts = lax.all_to_all(
        part_one.reshape(16, ROWS, WIDTH), PLANE, 0, 0, tiled=True
    )
    grad_one = jnp.sum(one_parts.astype(jnp.float32) * (two_most / 128.0)[:, None, None], axis=0)

    grad_half = jnp.zeros((HALF, NXL, WIDTH), jnp.float32)
    for k in range(NZ):
        source = jnp.sum(jnp.where(jnp.arange(NZ) == (z + k) % NZ, one_most, 0.0))
        grad_half = grad_half + two_parts[k].astype(jnp.float32) * (source / 64.0)
    stay = jnp.where(xl == 0, grad_half[:, 0], grad_half[:, 1])
    leave = jnp.where(xl == 0, grad_half[:, 1], grad_half[:, 0])
    come = swap(leave, "xl")
    grad_two = jnp.where(
        xl == 0, jnp.concatenate([stay, come]), jnp.concatenate([come, stay])
    )
    return (grad_one, grad_two)


def solution(mesh):
    fine = Mesh(mesh.devices.reshape(NZ, NY, NXH, NXL, NC), EVERY)
    users = P(("z", "y", "xh"))
    both = P(("z", "y", "xh"), ("xl", "core"))
    return jax.shard_map(
        on_device,
        mesh=fine,
        in_specs=(both, both, users),
        out_specs=(both, both),
        check_vma=False,
    )
```

time: 1050 us -> 171 us (0.16)
  waiting for transfers between devices: 622 us -> 72.9 us
  blocking collectives: 372 us -> 0 us
  starting transfers between devices: 0.16 us -> 55.4 us
  matrix products: 22.7 us -> 5.1 us
    reduce_scatter x2 -> x0, waiting for transfers between devices: 439 us -> none  [the longest x1 392 us: on_device(): lax.psum_scatter(jnp.dot(block_rows, view_one, preferred_element_type=jnp...]
    all_gather x4 -> x0, blocking collectives: 372 us -> none  [combined_all(): pieces = jax.tree.map(lambda part: lax.all_gather(part, axis), value)]
    all_gather x2 -> x0, waiting for transfers between devices: 182 us -> none  [the longest x1 155 us: on_device(): every_two = lax.all_gather(view_two, 'user', axis=0, tiled=True)]
    ppermute x0 -> x18, waiting for transfers between devices: none -> 66 us  [the longest x4 35.9 us: swap(): return lax.ppermute(x, axis, [(0, 1), (1, 0)])]
    ppermute x0 -> x18, starting transfers between devices: none -> 33.5 us  [the longest x7 17.5 us: on_device(): lax.ppermute(mine, 'z', [(i, (i + k) % NZ) for i in range(NZ)])]
    all_to_all x0 -> x3, starting transfers between devices: none -> 22 us  [the longest x1 7.7 us: on_device(): lax.all_to_all(jnp.broadcast_to(pack[None], (16, 8, 512)), EVERY, 0, 0, a...]
    dot_general x3 -> x2, matrix products: 22.7 us -> 5.1 us  [the longest x1 2.6 us: on_device(): jnp.einsum('uij,xjk->uxik', coupling.reshape(8, ROWS, NJ), v2_all, prefer...]
  transfers between devices with their start and end apart: 4 -> 21, of which waited for: 4 -> 14; matrix products, arithmetic and copies ran while one was open for 1% -> 3% of each run, Pallas kernels for 0% -> 0%
where the time goes in v1:
time: 171 us
  waiting for transfers between devices  72.9 us (43%)
  starting transfers between devices  55.4 us (32%)
  other arithmetic  14.3 us (8%)
  local copies, waits for them, and re-layouts  11.3 us (7%)
  between operations  7.3 us (4%)
  matrix products  5.1 us (3%)
  Pallas kernels  4.24 us (2%)
    ppermute x4, waiting for transfers between devices, swap(): return lax.ppermute(x, axis, [(0, 1), (1, 0)])  35.9 us
    ppermute x7, starting transfers between devices, on_device(): lax.ppermute(mine, 'z', [(i, (i + k) % NZ) for i in range(NZ)])  17.5 us
    ppermute x7, waiting for transfers between devices, on_device(): lax.ppermute(mine, 'z', [(i, (i + k) % NZ) for i in range(NZ)])  16.8 us
    ppermute x7, waiting for transfers between devices, on_device(): lax.ppermute(part_two[k], 'z', [(i, (i - k) % NZ) for i in range(NZ)])  13.3 us
    ppermute x7, starting transfers between devices, on_device(): lax.ppermute(part_two[k], 'z', [(i, (i - k) % NZ) for i in range(NZ)])  12.4 us
    all_to_all x1, starting transfers between devices, on_device(): lax.all_to_all(jnp.broadcast_to(pack[None], (16, 8, 512)), EVERY, 0, 0, a...  7.7 us
    all_to_all x1, starting transfers between devices, on_device(): lax.all_to_all(jnp.broadcast_to(view_one[None], (16, ROWS, WIDTH)), PLANE...  7.58 us
    all_to_all x1, waiting for transfers between devices, on_device(): lax.all_to_all(jnp.broadcast_to(pack[None], (16, 8, 512)), EVERY, 0, 0, a...  6.9 us
  transfers between devices with their start and end apart: 21, of which 14 were waited for; matrix products, arithmetic and copies ran while one was open for 3% of the time, Pallas kernels for 0%

profile of v1, /device:TPU:4, one launch (start us, length us, event | category | flops | bytes accessed | tf_op | source)
XLA Modules:
  0.0 170.6 jit_solution(12649473834699901191)
XLA Ops:
  0.6 2.5 %broadcast_in_dim.95 = bf16[16,128,512]{2,1,0:T(8,128)(2,1)} broadcast(bf16[128,512]{1,0:T(8,128)(2,1)} %param.3), dimensions={1,2} | broadcast | bytes 2228224 | tf_op jit(solution)/shard_map/broadcast_in_dim | solution.py:96
  3.1 7.6 %all-to-all-start = ((bf16[16,128,512]{2,1,0:T(8,128)(2,1)}), bf16[16,128,512]{2,1,0:T(8,128)(2,1)S(1)}, u32[]{:S(2)}, u32[]{:S(2)}) async-start(bf16[16,128,512]{2,1,0:T(8,128)(2,1)} %broadcast_in_dim.95), calls=%async_computation | async-start | bytes 4194304 | tf_op jit(solution)/shard_map/all_to_all | solution.py:95
  10.7 1.3 collective-permute-start
  12.0 27.1 %collective-permute-done = bf16[64,512]{1,0:T(8,128)(2,1)S(1)} collective-permute-done((bf16[64,512]{1,0:T(8,128)(2,1)S(1)}, bf16[64,512]{1,0:T(8,128)(2,1)S(1)}, u32[]{:S(2)}, u32[]{:S(2)}) %collective-permute-start) | collective-permute-done | bytes 65568 | tf_op jit(solution)/shard_map/ppermute | solution.py:57
  39.0 2.0 %collective-permute-start.1 = (bf16[2,64,512]{2,1,0:T(8,128)(2,1)S(1)}, bf16[2,64,512]{2,1,0:T(8,128)(2,1)S(1)}, u32[]{:S(2)}, u32[]{:S(2)}) collective-permute-start(bf16[2,64,512]{2,1,0:T(8,128)(2,1)S(1)} %maximum_select_fusion.1.refs_0_), channel_id=1, source_target_pairs={{0,32},{32,64},{64,96},{96,128},{128,160},{160,192},{192,224},{224... | collective-permute-start | bytes 393224 | tf_op jit(solution)/shard_map/ppermute | solution.py:93
  41.0 3.3 %collective-permute-start.2 = (bf16[2,64,512]{2,1,0:T(8,128)(2,1)S(1)}, bf16[2,64,512]{2,1,0:T(8,128)(2,1)S(1)}, u32[]{:S(2)}, u32[]{:S(2)}) collective-permute-start(bf16[2,64,512]{2,1,0:T(8,128)(2,1)S(1)} %maximum_select_fusion.1.refs_0_), channel_id=1, source_target_pairs={{0,64},{32,96},{64,128},{96,160},{128,192},{160,224},{192,0},{224,... | collective-permute-start | bytes 393224 | tf_op jit(solution)/shard_map/ppermute | solution.py:93
  44.3 4.0 %collective-permute-start.3 = (bf16[2,64,512]{2,1,0:T(8,128)(2,1)S(1)}, bf16[2,64,512]{2,1,0:T(8,128)(2,1)S(1)}, u32[]{:S(2)}, u32[]{:S(2)}) collective-permute-start(bf16[2,64,512]{2,1,0:T(8,128)(2,1)S(1)} %maximum_select_fusion.1.refs_0_), channel_id=1, source_target_pairs={{0,96},{32,128},{64,160},{96,192},{128,224},{160,0},{192,32},{224,... | collective-permute-start | bytes 393224 | tf_op jit(solution)/shard_map/ppermute | solution.py:93
  48.4 0.5 collective-permute-start.4
  48.9 4.9 %collective-permute-start.5 = (bf16[2,64,512]{2,1,0:T(8,128)(2,1)S(1)}, bf16[2,64,512]{2,1,0:T(8,128)(2,1)S(1)}, u32[]{:S(2)}, u32[]{:S(2)}) collective-permute-start(bf16[2,64,512]{2,1,0:T(8,128)(2,1)S(1)} %maximum_select_fusion.1.refs_0_), channel_id=1, source_target_pairs={{0,160},{32,192},{64,224},{96,0},{128,32},{160,64},{192,96},{224,1... | collective-permute-start | bytes 393224 | tf_op jit(solution)/shard_map/ppermute | solution.py:93
  53.8 2.7 %collective-permute-start.6 = (bf16[2,64,512]{2,1,0:T(8,128)(2,1)S(1)}, bf16[2,64,512]{2,1,0:T(8,128)(2,1)S(1)}, u32[]{:S(2)}, u32[]{:S(2)}) collective-permute-start(bf16[2,64,512]{2,1,0:T(8,128)(2,1)S(1)} %maximum_select_fusion.1.refs_0_), channel_id=1, source_target_pairs={{0,192},{32,224},{64,0},{96,32},{128,64},{160,96},{192,128},{224,1... | collective-permute-start | bytes 393224 | tf_op jit(solution)/shard_map/ppermute | solution.py:93
  56.5 4.5 %collective-permute-done.2.refs_2_ = bf16[2,64,512]{2,1,0:T(8,128)(2,1)S(1)} collective-permute-done((bf16[2,64,512]{2,1,0:T(8,128)(2,1)S(1)}, bf16[2,64,512]{2,1,0:T(8,128)(2,1)S(1)}, u32[]{:S(2)}, u32[]{:S(2)}) %collective-permute-start.2) | collective-permute-done | bytes 131104 | tf_op jit(solution)/shard_map/ppermute | solution.py:93
  61.0 4.9 %collective-permute-done.3.refs_3_ = bf16[2,64,512]{2,1,0:T(8,128)(2,1)S(1)} collective-permute-done((bf16[2,64,512]{2,1,0:T(8,128)(2,1)S(1)}, bf16[2,64,512]{2,1,0:T(8,128)(2,1)S(1)}, u32[]{:S(2)}, u32[]{:S(2)}) %collective-permute-start.3) | collective-permute-done | bytes 131104 | tf_op jit(solution)/shard_map/ppermute | solution.py:93
  66.0 3.2 %collective-permute-done.5.refs_5_ = bf16[2,64,512]{2,1,0:T(8,128)(2,1)S(1)} collective-permute-done((bf16[2,64,512]{2,1,0:T(8,128)(2,1)S(1)}, bf16[2,64,512]{2,1,0:T(8,128)(2,1)S(1)}, u32[]{:S(2)}, u32[]{:S(2)}) %collective-permute-start.5) | collective-permute-done | bytes 131104 | tf_op jit(solution)/shard_map/ppermute | solution.py:93
  69.2 1.6 collective-permute-done.6.refs_6_
  70.8 2.5 %collective-permute-done.7.refs_7_ = bf16[2,64,512]{2,1,0:T(8,128)(2,1)S(1)} collective-permute-done((bf16[2,64,512]{2,1,0:T(8,128)(2,1)S(1)}, bf16[2,64,512]{2,1,0:T(8,128)(2,1)S(1)}, u32[]{:S(2)}, u32[]{:S(2)}) %collective-permute-start.7) | collective-permute-done | bytes 131104 | tf_op jit(solution)/shard_map/ppermute | solution.py:93
  73.3 4.2 %shard_map.50 = (f32[1032,512]{1,0:T(8,128)}, bf16[2,512,512]{2,1,0:T(8,128)(2,1)S(1)}) custom-call(bf16[8,2,128,512]{3,2,1,0:T(8,128)(2,1)S(1)} %bitcast.80, bf16[2,64,512]{2,1,0:T(8,128)(2,1)S(1)} %maximum_select_fusion.1.refs_0_, bf16[2,64,512]{2,1,0:T(8,128)(2,1)S(1)} %collective-permute-done.1.refs_1_, ...), custom_call_target="tpu_custom_call" | custom-call | flops 1073741824 | bytes 6291456 | tf_op jit(solution)/shard_map/pallas_call | solution.py:41
  77.6 1.0 copy-done
  78.6 0.1 iota_compare_fusion
  78.6 4.4 %collective-permute-done.8 = f32[1032,512]{1,0:T(8,128)} collective-permute-done((f32[1032,512]{1,0:T(8,128)}, f32[1032,512]{1,0:T(8,128)}, u32[]{:S(2)}, u32[]{:S(2)}) %collective-permute-start.8) | collective-permute-done | bytes 2113568 | tf_op jit(solution)/shard_map/ppermute | solution.py:57
  83.1 0.7 slice_maximum_fusion
  83.8 0.5 fusion.25
  84.3 3.9 %fusion.21 = (f32[512]{0:T(512)S(1)}, f32[1024]{0:T(1024)S(1)}, f32[1024,512]{1,0:T(8,128)}) fusion(f32[1032,512]{1,0:T(8,128)} %collective-permute-done.8, f32[1032,512]{1,0:T(8,128)} %get-tuple-element.5), kind=kLoop, calls=%fused_computation.81 | loop fusion | flops 2095616 | bytes 6297600 | tf_op jit(solution)/shard_map/reduce_max | solution.py:108
  88.2 0.1 broadcast_in_dim.99
  88.3 2.4 %exponential_reduce_fusion = (f32[512]{0:T(512)S(1)}, f32[1024]{0:T(1024)S(1)}) fusion(f32[1024,512]{1,0:T(8,128)} %get-tuple-element.20, f32[512]{0:T(512)S(1)} %get-tuple-element.8, f32[1024]{0:T(1024)S(1)} %get-tuple-element.9), kind=kLoop, calls=%fused_computation.7 | loop fusion | flops 2095616 | bytes 2109440 | tf_op jit(solution)/shard_map/reduce_sum | solution.py:109
  91.4 0.1 broadcast_in_dim.102
  91.5 0.1 select_reduce_fusion.1
  91.5 0.1 reshape.185
  92.4 0.7 broadcast_in_dim.106
  93.2 7.7 %all-to-all-start.1 = ((f32[16,8,512]{2,1,0:T(8,128)}), f32[16,8,512]{2,1,0:T(8,128)S(1)}, u32[]{:S(2)}, u32[]{:S(2)}) async-start(f32[16,8,512]{2,1,0:T(8,128)} %broadcast_in_dim.106), calls=%async_computation.1 | async-start | bytes 524288 | tf_op jit(solution)/shard_map/all_to_all | solution.py:133
  100.9 6.9 %all-to-all-done.1 = f32[16,8,512]{2,1,0:T(8,128)S(1)} async-done(((f32[16,8,512]{2,1,0:T(8,128)}), f32[16,8,512]{2,1,0:T(8,128)S(1)}, u32[]{:S(2)}, u32[]{:S(2)}) %all-to-all-start.1) | async-done | bytes 262176 | tf_op jit(solution)/shard_map/all_to_all | solution.py:133
  107.9 0.1 slice_reduce_fusion.2
  108.0 0.1 fusion.5
  108.2 0.1 add.160
  108.3 0.1 select_reduce_fusion
  108.4 0.1 reshape.188
  108.4 0.1 concatenate.21
  108.5 0.2 slice_reduce_fusion.1
  108.7 0.1 concatenate.20
  108.8 1.1 collective-permute-start.9
  110.0 0.1 add.170
  110.1 0.6 collective-permute-done.9
  110.8 2.3 %subtract_convert_fusion = bf16[1024,512]{1,0:T(8,128)(2,1)S(1)} fusion(f32[1024,512]{1,0:T(8,128)} %get-tuple-element.20, s32[512]{0:T(512)S(1)} %add.170, f32[512]{0:T(512)S(1)} %bitcast.92, f32[1024]{0:T(1024)S(1)} %bitcast.88, s32[1024]{0:T(1024)S(1)} %bitcast.89), kind=kLoop, calls=%fused_computation.6 | loop fusion | flops 4194304 | bytes 3158016 | tf_op jit(solution)/shard_map/convert_element_type | solution.py:167
  113.1 1.0 copy-done.2
  114.1 2.6 %fusion.2 = f16[8,2,128,512]{2,3,0,1:T(8,128)(2,1)} fusion(f32[]{:T(128)S(6)} %div.35, bf16[8,128,512,1]{2,1,0,3:T(8,128)(2,1)S(1)} %bitcast.85, bf16[2,512,512]{2,1,0:T(8,128)(2,1)S(1)} %copy-done.1), kind=kOutput, calls=%fused_computation.9 | convolution fusion | flops 1075838976 | bytes 4194308 | tf_op jit(solution)/shard_map/uij,xjk->uxik/dot_general | solution.py:180
  116.7 4.2 %copy.20 = f16[8,2,128,512]{3,2,1,0:T(8,128)(2,1)} copy(f16[8,2,128,512]{2,3,0,1:T(8,128)(2,1)} %fusion.2) | data formatting | bytes 4194304 | tf_op jit(solution)/shard_map/convert_element_type | solution.py:186
  120.9 6.7 %all-to-all-start.2 = ((f16[16,128,512]{2,1,0:T(8,128)(2,1)}), f16[16,128,512]{2,1,0:T(8,128)(2,1)}, u32[]{:S(2)}, u32[]{:S(2)}) async-start(f16[16,128,512]{2,1,0:T(8,128)(2,1)} %bitcast.82), calls=%async_computation.2 | async-start | bytes 4194304 | tf_op jit(solution)/shard_map/all_to_all | solution.py:187
  127.6 2.5 %fusion.1 = f16[512,2,512]{2,0,1:T(8,128)(2,1)S(1)} fusion(bf16[8,128,512,1]{2,1,3,0:T(8,128)(2,1)} %bitcast.86, bf16[8,2,128,512]{3,2,1,0:T(8,128)(2,1)S(1)} %bitcast.81, f32[]{:T(128)S(6)} %div.38), kind=kOutput, calls=%fused_computation.5 | convolution fusion | flops 1074790400 | bytes 4194308 | tf_op jit(solution)/shard_map/uij,uxik->jxk/dot_general | solution.py:169
  130.1 0.2 fusion.23
  130.3 1.2 collective-permute-start.16
  131.6 1.6 collective-permute-start.15
  133.2 1.1 collective-permute-start.14
  134.3 3.5 %collective-permute-start.13 = (f16[64,2,512]{2,0,1:T(8,128)(2,1)S(1)}, f16[64,2,512]{2,0,1:T(8,128)(2,1)S(1)}, u32[]{:S(2)}, u32[]{:S(2)}) collective-permute-start(f16[64,2,512]{2,0,1:T(8,128)(2,1)S(1)} %get-tuple-element.25), channel_id=1, source_target_pairs={{0,128},{32,160},{64,192},{96,224},{128,0},{160,32},{192,64},{224,... | collective-permute-start | bytes 393224 | tf_op jit(solution)/shard_map/ppermute | solution.py:177
  137.8 3.2 %collective-permute-start.12 = (f16[64,2,512]{2,0,1:T(8,128)(2,1)S(1)}, f16[64,2,512]{2,0,1:T(8,128)(2,1)S(1)}, u32[]{:S(2)}, u32[]{:S(2)}) collective-permute-start(f16[64,2,512]{2,0,1:T(8,128)(2,1)S(1)} %get-tuple-element.26), channel_id=1, source_target_pairs={{0,160},{32,192},{64,224},{96,0},{128,32},{160,64},{192,96},{224,1... | collective-permute-start | bytes 393224 | tf_op jit(solution)/shard_map/ppermute | solution.py:177
  141.0 1.7 %collective-permute-start.11 = (f16[64,2,512]{2,0,1:T(8,128)(2,1)S(1)}, f16[64,2,512]{2,0,1:T(8,128)(2,1)S(1)}, u32[]{:S(2)}, u32[]{:S(2)}) collective-permute-start(f16[64,2,512]{2,0,1:T(8,128)(2,1)S(1)} %get-tuple-element.27), channel_id=1, source_target_pairs={{0,192},{32,224},{64,0},{96,32},{128,64},{160,96},{192,128},{224,1... | collective-permute-start | bytes 393224 | tf_op jit(solution)/shard_map/ppermute | solution.py:177
  142.7 5.2 %collective-permute-done.15 = f16[64,2,512]{2,0,1:T(8,128)(2,1)S(1)} collective-permute-done((f16[64,2,512]{2,0,1:T(8,128)(2,1)S(1)}, f16[64,2,512]{2,0,1:T(8,128)(2,1)S(1)}, u32[]{:S(2)}, u32[]{:S(2)}) %collective-permute-start.15) | collective-permute-done | bytes 131104 | tf_op jit(solution)/shard_map/ppermute | solution.py:177
  148.0 0.7 fusion.11
  153.7 0.7 collective-permute-done.12
  154.5 4.9 %collective-permute-done.11 = f16[64,2,512]{2,0,1:T(8,128)(2,1)S(1)} collective-permute-done((f16[64,2,512]{2,0,1:T(8,128)(2,1)S(1)}, f16[64,2,512]{2,0,1:T(8,128)(2,1)S(1)}, u32[]{:S(2)}, u32[]{:S(2)}) %collective-permute-start.11) | collective-permute-done | bytes 131104 | tf_op jit(solution)/shard_map/ppermute | solution.py:177
  159.3 2.4 %collective-permute-done.10 = f16[64,2,512]{2,0,1:T(8,128)(2,1)S(1)} collective-permute-done((f16[64,2,512]{2,0,1:T(8,128)(2,1)S(1)}, f16[64,2,512]{2,0,1:T(8,128)(2,1)S(1)}, u32[]{:S(2)}, u32[]{:S(2)}) %collective-permute-start.10) | collective-permute-done | bytes 131104 | tf_op jit(solution)/shard_map/ppermute | solution.py:177
  161.8 0.2 multiply_add_fusion
  162.0 1.3 collective-permute-start.17
  163.3 3.8 %collective-permute-done.17 = f32[64,512]{1,0:T(8,128)S(1)} collective-permute-done((f32[64,512]{1,0:T(8,128)S(1)}, f32[64,512]{1,0:T(8,128)S(1)}, u32[]{:S(2)}, u32[]{:S(2)}) %collective-permute-start.17) | collective-permute-done | bytes 131104 | tf_op jit(solution)/shard_map/ppermute | solution.py:57
  167.0 0.7 maximum_select_fusion
  167.8 2.8 %multiply_reduce_fusion = f32[128,512]{1,0:T(8,128)} fusion(f16[16,128,512]{2,1,0:T(8,128)(2,1)} %all-to-all-done.2, f32[16]{0:T(128)S(1)} %fusion.20), kind=kLoop, calls=%fused_computation | loop fusion | flops 3080192 | bytes 2359360 | tf_op jit(solution)/shard_map/reduce_sum | solution.py:190
  (57 shorter events, 0.5 us)
Async XLA Ops:
  3.1 7.6 %copy-start.3 = (bf16[128,512]{1,0:T(8,128)(2,1)S(1)}, bf16[128,512]{1,0:T(8,128)(2,1)}, u32[]{:S(2)}) copy-start(bf16[128,512]{1,0:T(8,128)(2,1)} %param.4) | copy-start | bytes 393220
  3.1 70.2 %all-to-all-start = ((bf16[16,128,512]{2,1,0:T(8,128)(2,1)}), bf16[16,128,512]{2,1,0:T(8,128)(2,1)S(1)}, u32[]{:S(2)}, u32[]{:S(2)}) async-start(bf16[16,128,512]{2,1,0:T(8,128)(2,1)} %broadcast_in_dim.95), calls=%async_computation | async-start | bytes 4194304 | tf_op jit(solution)/shard_map/all_to_all | solution.py:95
  10.7 28.3 %collective-permute-start = (bf16[64,512]{1,0:T(8,128)(2,1)S(1)}, bf16[64,512]{1,0:T(8,128)(2,1)S(1)}, u32[]{:S(2)}, u32[]{:S(2)}) collective-permute-start(bf16[64,512]{1,0:T(8,128)(2,1)S(1)} %get-tuple-element.34), channel_id=1, source_target_pairs={{0,2},{2,0},{1,3},{3,1},{4,6},{6,4},{5,7},{7,5},{8,10},{10,8},{9,1... | collective-permute-start | bytes 196616 | tf_op jit(solution)/shard_map/ppermute | solution.py:57
  39.0 14.8 %collective-permute-start.1 = (bf16[2,64,512]{2,1,0:T(8,128)(2,1)S(1)}, bf16[2,64,512]{2,1,0:T(8,128)(2,1)S(1)}, u32[]{:S(2)}, u32[]{:S(2)}) collective-permute-start(bf16[2,64,512]{2,1,0:T(8,128)(2,1)S(1)} %maximum_select_fusion.1.refs_0_), channel_id=1, source_target_pairs={{0,32},{32,64},{64,96},{96,128},{128,160},{160,192},{192,224},{224... | collective-permute-start | bytes 393224 | tf_op jit(solution)/shard_map/ppermute | solution.py:93
  41.0 20.0 %collective-permute-start.2 = (bf16[2,64,512]{2,1,0:T(8,128)(2,1)S(1)}, bf16[2,64,512]{2,1,0:T(8,128)(2,1)S(1)}, u32[]{:S(2)}, u32[]{:S(2)}) collective-permute-start(bf16[2,64,512]{2,1,0:T(8,128)(2,1)S(1)} %maximum_select_fusion.1.refs_0_), channel_id=1, source_target_pairs={{0,64},{32,96},{64,128},{96,160},{128,192},{160,224},{192,0},{224,... | collective-permute-start | bytes 393224 | tf_op jit(solution)/shard_map/ppermute | solution.py:93
  44.3 21.6 %collective-permute-start.3 = (bf16[2,64,512]{2,1,0:T(8,128)(2,1)S(1)}, bf16[2,64,512]{2,1,0:T(8,128)(2,1)S(1)}, u32[]{:S(2)}, u32[]{:S(2)}) collective-permute-start(bf16[2,64,512]{2,1,0:T(8,128)(2,1)S(1)} %maximum_select_fusion.1.refs_0_), channel_id=1, source_target_pairs={{0,96},{32,128},{64,160},{96,192},{128,224},{160,0},{192,32},{224,... | collective-permute-start | bytes 393224 | tf_op jit(solution)/shard_map/ppermute | solution.py:93
  48.4 17.6 %collective-permute-start.4 = (bf16[2,64,512]{2,1,0:T(8,128)(2,1)S(1)}, bf16[2,64,512]{2,1,0:T(8,128)(2,1)S(1)}, u32[]{:S(2)}, u32[]{:S(2)}) collective-permute-start(bf16[2,64,512]{2,1,0:T(8,128)(2,1)S(1)} %maximum_select_fusion.1.refs_0_), channel_id=1, source_target_pairs={{0,128},{32,160},{64,192},{96,224},{128,0},{160,32},{192,64},{224,... | collective-permute-start | bytes 393224 | tf_op jit(solution)/shard_map/ppermute | solution.py:93
  48.9 20.3 %collective-permute-start.5 = (bf16[2,64,512]{2,1,0:T(8,128)(2,1)S(1)}, bf16[2,64,512]{2,1,0:T(8,128)(2,1)S(1)}, u32[]{:S(2)}, u32[]{:S(2)}) collective-permute-start(bf16[2,64,512]{2,1,0:T(8,128)(2,1)S(1)} %maximum_select_fusion.1.refs_0_), channel_id=1, source_target_pairs={{0,160},{32,192},{64,224},{96,0},{128,32},{160,64},{192,96},{224,1... | collective-permute-start | bytes 393224 | tf_op jit(solution)/shard_map/ppermute | solution.py:93
  53.8 17.0 %collective-permute-start.6 = (bf16[2,64,512]{2,1,0:T(8,128)(2,1)S(1)}, bf16[2,64,512]{2,1,0:T(8,128)(2,1)S(1)}, u32[]{:S(2)}, u32[]{:S(2)}) collective-permute-start(bf16[2,64,512]{2,1,0:T(8,128)(2,1)S(1)} %maximum_select_fusion.1.refs_0_), channel_id=1, source_target_pairs={{0,192},{32,224},{64,0},{96,32},{128,64},{160,96},{192,128},{224,1... | collective-permute-start | bytes 393224 | tf_op jit(solution)/shard_map/ppermute | solution.py:93
  61.0 12.3 %collective-permute-start.7 = (bf16[2,64,512]{2,1,0:T(8,128)(2,1)S(1)}, bf16[2,64,512]{2,1,0:T(8,128)(2,1)S(1)}, u32[]{:S(2)}, u32[]{:S(2)}) collective-permute-start(bf16[2,64,512]{2,1,0:T(8,128)(2,1)S(1)} %maximum_select_fusion.1.refs_0_), channel_id=1, source_target_pairs={{0,224},{32,0},{64,32},{96,64},{128,96},{160,128},{192,160},{224,1... | collective-permute-start | bytes 393224 | tf_op jit(solution)/shard_map/ppermute | solution.py:93
  77.6 1.0 copy-start
  78.6 4.5 %collective-permute-start.8 = (f32[1032,512]{1,0:T(8,128)}, f32[1032,512]{1,0:T(8,128)}, u32[]{:S(2)}, u32[]{:S(2)}) collective-permute-start(f32[1032,512]{1,0:T(8,128)} %get-tuple-element.5), channel_id=1, source_target_pairs={{0,1},{1,0},{2,3},{3,2},{4,5},{5,4},{6,7},{7,6},{8,9},{9,8},{10,11... | collective-permute-start | bytes 6340616 | tf_op jit(solution)/shard_map/ppermute | solution.py:57
  88.2 3.1 %copy-start.4 = (s32[128]{0:T(128)S(1)}, s32[128]{0:T(128)}, u32[]{:S(2)}) copy-start(s32[128]{0:T(128)} %param.5) | copy-start | bytes 1540
  93.2 14.6 %all-to-all-start.1 = ((f32[16,8,512]{2,1,0:T(8,128)}), f32[16,8,512]{2,1,0:T(8,128)S(1)}, u32[]{:S(2)}, u32[]{:S(2)}) async-start(f32[16,8,512]{2,1,0:T(8,128)} %broadcast_in_dim.106), calls=%async_computation.1 | async-start | bytes 524288 | tf_op jit(solution)/shard_map/all_to_all | solution.py:133
  107.8 6.3 %copy-start.1 = (bf16[2,512,512]{2,1,0:T(8,128)(2,1)S(1)}, bf16[2,512,512]{2,1,0:T(8,128)(2,1)}, u32[]{:S(2)}) copy-start(bf16[2,512,512]{2,1,0:T(8,128)(2,1)} %copy-done) | copy-start | bytes 3145732
  108.8 1.9 %collective-permute-start.9 = (f32[8,512]{1,0:T(8,128)S(1)}, f32[8,512]{1,0:T(8,128)S(1)}, u32[]{:S(2)}, u32[]{:S(2)}) collective-permute-start(f32[8,512]{1,0:T(8,128)S(1)} %select_n.187), channel_id=1, source_target_pairs={{0,1},{1,0},{2,3},{3,2},{4,5},{5,4},{6,7},{7,6},{8,9},{9,8},{10,11... | collective-permute-start | bytes 49160 | tf_op jit(solution)/shard_map/ppermute | solution.py:57
  113.1 1.0 copy-start.2
  120.9 46.9 %all-to-all-start.2 = ((f16[16,128,512]{2,1,0:T(8,128)(2,1)}), f16[16,128,512]{2,1,0:T(8,128)(2,1)}, u32[]{:S(2)}, u32[]{:S(2)}) async-start(f16[16,128,512]{2,1,0:T(8,128)(2,1)} %bitcast.82), calls=%async_computation.2 | async-start | bytes 4194304 | tf_op jit(solution)/shard_map/all_to_all | solution.py:187
  130.3 10.7 %collective-permute-start.16 = (f16[64,2,512]{2,0,1:T(8,128)(2,1)S(1)}, f16[64,2,512]{2,0,1:T(8,128)(2,1)S(1)}, u32[]{:S(2)}, u32[]{:S(2)}) collective-permute-start(f16[64,2,512]{2,0,1:T(8,128)(2,1)S(1)} %get-tuple-element.22), channel_id=1, source_target_pairs={{0,32},{32,64},{64,96},{96,128},{128,160},{160,192},{192,224},{224... | collective-permute-start | bytes 393224 | tf_op jit(solution)/shard_map/ppermute | solution.py:177
  131.6 16.4 %collective-permute-start.15 = (f16[64,2,512]{2,0,1:T(8,128)(2,1)S(1)}, f16[64,2,512]{2,0,1:T(8,128)(2,1)S(1)}, u32[]{:S(2)}, u32[]{:S(2)}) collective-permute-start(f16[64,2,512]{2,0,1:T(8,128)(2,1)S(1)} %get-tuple-element.23), channel_id=1, source_target_pairs={{0,64},{32,96},{64,128},{96,160},{128,192},{160,224},{192,0},{224,... | collective-permute-start | bytes 393224 | tf_op jit(solution)/shard_map/ppermute | solution.py:177
  133.2 20.5 %collective-permute-start.14 = (f16[64,2,512]{2,0,1:T(8,128)(2,1)S(1)}, f16[64,2,512]{2,0,1:T(8,128)(2,1)S(1)}, u32[]{:S(2)}, u32[]{:S(2)}) collective-permute-start(f16[64,2,512]{2,0,1:T(8,128)(2,1)S(1)} %get-tuple-element.24), channel_id=1, source_target_pairs={{0,96},{32,128},{64,160},{96,192},{128,224},{160,0},{192,32},{224,... | collective-permute-start | bytes 393224 | tf_op jit(solution)/shard_map/ppermute | solution.py:177
  134.3 19.4 %collective-permute-start.13 = (f16[64,2,512]{2,0,1:T(8,128)(2,1)S(1)}, f16[64,2,512]{2,0,1:T(8,128)(2,1)S(1)}, u32[]{:S(2)}, u32[]{:S(2)}) collective-permute-start(f16[64,2,512]{2,0,1:T(8,128)(2,1)S(1)} %get-tuple-element.25), channel_id=1, source_target_pairs={{0,128},{32,160},{64,192},{96,224},{128,0},{160,32},{192,64},{224,... | collective-permute-start | bytes 393224 | tf_op jit(solution)/shard_map/ppermute | solution.py:177
  137.8 16.7 %collective-permute-start.12 = (f16[64,2,512]{2,0,1:T(8,128)(2,1)S(1)}, f16[64,2,512]{2,0,1:T(8,128)(2,1)S(1)}, u32[]{:S(2)}, u32[]{:S(2)}) collective-permute-start(f16[64,2,512]{2,0,1:T(8,128)(2,1)S(1)} %get-tuple-element.26), channel_id=1, source_target_pairs={{0,160},{32,192},{64,224},{96,0},{128,32},{160,64},{192,96},{224,1... | collective-permute-start | bytes 393224 | tf_op jit(solution)/shard_map/ppermute | solution.py:177
  141.0 18.3 %collective-permute-start.11 = (f16[64,2,512]{2,0,1:T(8,128)(2,1)S(1)}, f16[64,2,512]{2,0,1:T(8,128)(2,1)S(1)}, u32[]{:S(2)}, u32[]{:S(2)}) collective-permute-start(f16[64,2,512]{2,0,1:T(8,128)(2,1)S(1)} %get-tuple-element.27), channel_id=1, source_target_pairs={{0,192},{32,224},{64,0},{96,32},{128,64},{160,96},{192,128},{224,1... | collective-permute-start | bytes 393224 | tf_op jit(solution)/shard_map/ppermute | solution.py:177
  148.0 13.8 %collective-permute-start.10 = (f16[64,2,512]{2,0,1:T(8,128)(2,1)S(1)}, f16[64,2,512]{2,0,1:T(8,128)(2,1)S(1)}, u32[]{:S(2)}, u32[]{:S(2)}) collective-permute-start(f16[64,2,512]{2,0,1:T(8,128)(2,1)S(1)} %get-tuple-element.21), channel_id=1, source_target_pairs={{0,224},{32,0},{64,32},{96,64},{128,96},{160,128},{192,160},{224,1... | collective-permute-start | bytes 393224 | tf_op jit(solution)/shard_map/ppermute | solution.py:177
  162.0 5.1 %collective-permute-start.17 = (f32[64,512]{1,0:T(8,128)S(1)}, f32[64,512]{1,0:T(8,128)S(1)}, u32[]{:S(2)}, u32[]{:S(2)}) collective-permute-start(f32[64,512]{1,0:T(8,128)S(1)} %get-tuple-element.29), channel_id=1, source_target_pairs={{0,2},{2,0},{1,3},{3,1},{4,6},{6,4},{5,7},{7,5},{8,10},{10,8},{9,1... | collective-permute-start | bytes 393224 | tf_op jit(solution)/shard_map/ppermute | solution.py:57

commit v2 on v0

v2 whole, which is shorter than its diff:
```python
import math

import jax
import jax.numpy as jnp
from jax import lax
from jax.experimental import pallas as pl
from jax.experimental.pallas import tpu as pltpu
from jax.sharding import Mesh
from jax.sharding import PartitionSpec as P

D = 2048
NZ, NY, NXH, NXL, NC = 8, 4, 2, 2, 2
PLANE = ("xl", "y", "xh")
COLUMN = ("xl", "z")
EVERY = ("z", "y", "xh", "xl", "core")
ROWS = 128
HALF = 64
WIDTH = 512
NI = NY * NXH * ROWS
NJ = NZ * HALF
LANES = 128
SCALE = 2.0 / math.sqrt(D)
VMEM = pl.BlockSpec(memory_space=pltpu.VMEM)
SMEM = pl.BlockSpec(memory_space=pltpu.SMEM)
LIMIT = pltpu.CompilerParams(vmem_limit_bytes=48 * 1024 * 1024)


def score_kernel(v1_ref, v2_ref, s_ref):
    contract = (((1,), (1,)), ((), ()))
    for u in range(NI // 256):
        rows = slice(u * 256, (u + 1) * 256)
        s_ref[rows, :] = lax.dot_general(
            v1_ref[0, rows, :], v2_ref[0], contract, preferred_element_type=jnp.float32
        ) + lax.dot_general(
            v1_ref[1, rows, :], v2_ref[1], contract, preferred_element_type=jnp.float32
        )


def partial_scores(v1_all, v2_all):
    return pl.pallas_call(
        score_kernel,
        out_shape=jax.ShapeDtypeStruct((NI, NJ), jnp.float32),
        in_specs=[VMEM, VMEM],
        out_specs=VMEM,
        compiler_params=LIMIT,
        cost_estimate=pl.CostEstimate(
            flops=2 * NI * NJ * NXL * WIDTH, bytes_accessed=5 * 2**20, transcendentals=0
        ),
    )(v1_all, v2_all)


def diagonal():
    shape = (LANES, LANES)
    return lax.broadcasted_iota(jnp.int32, shape, 0) == lax.broadcasted_iota(jnp.int32, shape, 1)


def stats_kernel(own_ref, other_ref, partner_ref, most_ref, s_ref, pack_ref):
    eye = diagonal()
    pack_ref[...] = jnp.zeros_like(pack_ref)
    col_highest = jnp.full((1, NJ), -jnp.inf, jnp.float32)
    col_total = jnp.zeros((1, NJ), jnp.float32)
    for u in range(NI // LANES):
        rows = slice(u * LANES, (u + 1) * LANES)
        s = SCALE * (own_ref[rows, :] + other_ref[rows, :])
        s_ref[rows, :] = s
        highest = jnp.max(s, axis=1, keepdims=True)
        lse = highest + jnp.log(jnp.sum(jnp.exp(s - highest), axis=1, keepdims=True))
        pack_ref[0, u : u + 1, :] = jnp.sum(jnp.where(eye, lse, 0.0), axis=0, keepdims=True)
        higher = jnp.maximum(col_highest, jnp.max(s, axis=0, keepdims=True))
        col_total = col_total * jnp.exp(col_highest - higher) + jnp.sum(
            jnp.exp(s - higher), axis=0, keepdims=True
        )
        col_highest = higher
    col_lse = col_highest + jnp.log(col_total)
    for t in range(NJ // LANES):
        pack_ref[1, t : t + 1, :] = col_lse[:, t * LANES : (t + 1) * LANES]
    pack_ref[0, 8:9, :] = partner_ref[...].astype(jnp.float32)
    pack_ref[0, 9:10, :] = most_ref[0:1, :]
    pack_ref[1, 9:10, :] = most_ref[1:2, :]


def local_stats(own, other, partner, most):
    return pl.pallas_call(
        stats_kernel,
        out_shape=(
            jax.ShapeDtypeStruct((NI, NJ), jnp.float32),
            jax.ShapeDtypeStruct((2, 16, LANES), jnp.float32),
        ),
        in_specs=[VMEM] * 4,
        out_specs=(VMEM, VMEM),
        compiler_params=LIMIT,
        cost_estimate=pl.CostEstimate(
            flops=10 * NI * NJ, bytes_accessed=6 * 2**20, transcendentals=2 * NI * NJ
        ),
    )(own, other, partner.reshape(1, ROWS), most)


def merged(lses):
    top = jnp.max(lses, axis=0)
    return top + jnp.log(jnp.sum(jnp.exp(lses - top[None]), axis=0))


def merge_kernel(place_ref, seen_ref, known_ref):
    core, xl = place_ref[0], place_ref[1]

    @pl.when(core == 0)
    def _():
        known_ref[0:8, :] = merged(seen_ref[:, 0:8, :])
        for u in range(8):
            known_ref[8 + u : 9 + u, :] = seen_ref[u, 8:9, :]
        for p in range(16):
            known_ref[16 + p : 17 + p, :] = seen_ref[p, 9:10, :]

    @pl.when(core != 0)
    def _():
        known_ref[...] = jnp.zeros_like(known_ref)
        known_ref[0:8, :] = merged(seen_ref[pl.ds(xl * NZ, NZ), 0:8, :])
        for p in range(16):
            known_ref[16 + p : 17 + p, :] = seen_ref[p, 9:10, :]


def merge_stats(place, seen):
    return pl.pallas_call(
        merge_kernel,
        out_shape=jax.ShapeDtypeStruct((32, LANES), jnp.float32),
        in_specs=[SMEM, VMEM],
        out_specs=VMEM,
        cost_estimate=pl.CostEstimate(flops=10**5, bytes_accessed=2**17, transcendentals=2**14),
    )(place, seen)


def swap(x, axis):
    return lax.ppermute(x, axis, [(0, 1), (1, 0)])


def stat_groups():
    def number(z, y, xh, xl, c):
        return (((z * NY + y) * NXH + xh) * NXL + xl) * NC + c

    planes = [
        [number(z, y, xh, xl, 0) for xl in range(NXL) for y in range(NY) for xh in range(NXH)]
        for z in range(NZ)
    ]
    columns = [
        [number(z, y, xh, xl, 1) for xl in range(NXL) for z in range(NZ)]
        for y in range(NY)
        for xh in range(NXH)
    ]
    return planes + columns


def on_device(view_one, view_two, partner):
    uhigh = lax.axis_index("y") * NXH + lax.axis_index("xh")
    xl = lax.axis_index("xl")
    core = lax.axis_index("core")

    v2_all = lax.all_to_all(
        jnp.broadcast_to(view_two.reshape(NXL, 1, HALF, WIDTH), (NXL, NZ, HALF, WIDTH)).reshape(
            NXL * NZ, HALF, WIDTH
        ),
        COLUMN,
        0,
        0,
        tiled=True,
    ).reshape(NXL, NJ, WIDTH)
    v1_all = lax.all_to_all(
        jnp.broadcast_to(view_one[None], (16, ROWS, WIDTH)), PLANE, 0, 0, tiled=True
    ).reshape(NXL, NI, WIDTH)

    own = partial_scores(v1_all, v2_all)
    other = swap(own, "core")
    most = jnp.stack([jnp.max(jnp.abs(v2_all)), jnp.max(jnp.abs(v1_all))]).astype(jnp.float32)
    most = jnp.broadcast_to(jnp.maximum(most, 1e-30)[:, None], (2, LANES))
    most = jnp.maximum(most, swap(most, "core"))

    scores, pack = local_stats(own, other, partner, most)
    pack = jnp.where(core == 0, pack[0], pack[1])
    seen = lax.all_to_all(
        jnp.broadcast_to(pack[None], (16, 16, LANES)),
        EVERY,
        0,
        0,
        axis_index_groups=stat_groups(),
        tiled=True,
    )
    known = merge_stats(jnp.stack([core, xl]).astype(jnp.int32), seen)
    told = swap(known, "core")
    rows = jnp.where(core == 0, known, told)
    cols = jnp.where(core == 0, told, known)
    row_lse = rows[0:8].reshape(NI)
    row_partner = rows[8:16].reshape(NI).astype(jnp.int32)
    two_most = rows[16:32, 0]
    col_lse = cols[0:4].reshape(NJ)
    one_most = cols[16:32, 0]

    block = jnp.arange(NZ)
    index = ((block * (NY * NXH) + uhigh) * ROWS + xl * HALF)[:, None] + jnp.arange(HALF)[None, :]
    positive = (index.reshape(1, NJ) == row_partner[:, None]).astype(jnp.float32)
    both = jnp.exp(scores - row_lse[:, None]) + jnp.exp(scores - col_lse[None, :])
    coupling = (0.5 * both - positive).astype(jnp.bfloat16)

    part_two = jnp.stack(
        [
            (
                lax.dot_general(
                    coupling, v1_all[x], (((0,), (0,)), ((), ())), preferred_element_type=jnp.float32
                )
                * (64.0 / most[1, 0])
            ).astype(jnp.float16)
            for x in range(NXL)
        ]
    )
    two_parts = lax.all_to_all(
        part_two.reshape(NXL * NZ, HALF, WIDTH), COLUMN, 0, 0, tiled=True
    )
    part_one = jnp.stack(
        [
            (
                jnp.dot(coupling, v2_all[x], preferred_element_type=jnp.float32)
                * (128.0 / most[0, 0])
            ).astype(jnp.float16)
            for x in range(NXL)
        ]
    )
    one_parts = lax.all_to_all(part_one.reshape(16, ROWS, WIDTH), PLANE, 0, 0, tiled=True)
    grad_two = jnp.sum(
        two_parts.reshape(NXL, NZ, HALF, WIDTH).astype(jnp.float32)
        * (one_most / 64.0).reshape(NXL, NZ, 1, 1),
        axis=1,
    ).reshape(ROWS, WIDTH)
    grad_one = jnp.sum(one_parts.astype(jnp.float32) * (two_most / 128.0)[:, None, None], axis=0)
    return (grad_one, grad_two)


def solution(mesh):
    fine = Mesh(mesh.devices.reshape(NZ, NY, NXH, NXL, NC), EVERY)
    users = P(("z", "y", "xh"))
    both = P(("z", "y", "xh"), ("xl", "core"))
    return jax.shard_map(
        on_device,
        mesh=fine,
        in_specs=(both, both, users),
        out_specs=(both, both),
        check_vma=False,
    )
```

time: 1050 us -> 174 us (0.17)
  waiting for transfers between devices: 622 us -> 51.3 us
  blocking collectives: 372 us -> 67.3 us
  matrix products: 22.7 us -> 2.88 us
  starting transfers between devices: 0.16 us -> 18.4 us
  between operations: 13.9 us -> 2.18 us
    reduce_scatter x2 -> x0, waiting for transfers between devices: 439 us -> none  [the longest x1 392 us: on_device(): lax.psum_scatter(jnp.dot(block_rows, view_one, preferred_element_type=jnp...]
    all_gather x4 -> x0, blocking collectives: 372 us -> none  [combined_all(): pieces = jax.tree.map(lambda part: lax.all_gather(part, axis), value)]
    all_gather x2 -> x0, waiting for transfers between devices: 182 us -> none  [the longest x1 155 us: on_device(): every_two = lax.all_gather(view_two, 'user', axis=0, tiled=True)]
    all_to_all x0 -> x2, blocking collectives: none -> 67.3 us  [the longest x1 33.8 us: on_device(): lax.all_to_all(jnp.broadcast_to(view_two.reshape(NXL, 1, HALF, WIDTH), (N...]
    all_to_all x0 -> x3, waiting for transfers between devices: none -> 51.2 us  [the longest x1 23.6 us: on_device(): lax.all_to_all(part_two.reshape(NXL * NZ, HALF, WIDTH), COLUMN, 0, 0, til...]
    dot_general x3 -> x4, matrix products: 22.7 us -> 2.88 us  [the longest x2 1.47 us: on_device(): lax.dot_general(coupling, v1_all[x], (((0,), (0,)), ((), ())), preferred_...]
    all_to_all x0 -> x3, starting transfers between devices: none -> 17.1 us  [the longest x1 6.06 us: on_device(): lax.all_to_all(jnp.broadcast_to(pack[None], (16, 16, LANES)), EVERY, 0, 0...]
  transfers between devices with their start and end apart: 4 -> 6, of which waited for: 4 -> 4; matrix products, arithmetic and copies ran while one was open for 1% -> 7% of each run, Pallas kernels for 0% -> 0%
where the time goes in v2:
time: 174 us; the launch traced here: 171 us
  blocking collectives  67.3 us (39%)
  waiting for transfers between devices  51.3 us (29%)
  starting transfers between devices  18.4 us (11%)
  other arithmetic  13.6 us (8%)
  local copies, waits for them, and re-layouts  7.73 us (4%)
  Pallas kernels  7.55 us (4%)
  matrix products  2.88 us (2%)
  between operations  2.18 us (1%)
    all_to_all x1, blocking collectives, on_device(): lax.all_to_all(jnp.broadcast_to(view_two.reshape(NXL, 1, HALF, WIDTH), (N...  33.8 us
    all_to_all x1, blocking collectives, on_device(): lax.all_to_all(jnp.broadcast_to(view_one[None], (16, ROWS, WIDTH)), PLANE...  33.5 us
    all_to_all x1, waiting for transfers between devices, on_device(): lax.all_to_all(part_two.reshape(NXL * NZ, HALF, WIDTH), COLUMN, 0, 0, til...  23.6 us
    all_to_all x1, waiting for transfers between devices, on_device(): lax.all_to_all(part_one.reshape(16, ROWS, WIDTH), PLANE, 0, 0, tiled=True)  23.4 us
    all_to_all x1, starting transfers between devices, on_device(): lax.all_to_all(jnp.broadcast_to(pack[None], (16, 16, LANES)), EVERY, 0, 0...  6.06 us
    all_to_all x1, starting transfers between devices, on_device(): lax.all_to_all(part_one.reshape(16, ROWS, WIDTH), PLANE, 0, 0, tiled=True)  5.78 us
    all_to_all x1, starting transfers between devices, on_device(): lax.all_to_all(part_two.reshape(NXL * NZ, HALF, WIDTH), COLUMN, 0, 0, til...  5.28 us
    all_to_all x1, waiting for transfers between devices, on_device(): lax.all_to_all(jnp.broadcast_to(pack[None], (16, 16, LANES)), EVERY, 0, 0...  4.22 us
  transfers between devices with their start and end apart: 6, of which 4 were waited for; matrix products, arithmetic and copies ran while one was open for 7% of the time, Pallas kernels for 0%

profile of v2, /device:TPU:4, one launch (start us, length us, event | category | flops | bytes accessed | tf_op | source)
XLA Modules:
  0.0 171.0 jit_solution(8542196151162425228)
XLA Ops:
  0.6 1.1 broadcast_in_dim.12
  1.7 0.0 copy-start.6
  1.7 33.5 %all_to_all.25 = bf16[16,128,512]{2,1,0:T(8,128)(2,1)S(1)} all-to-all(bf16[16,128,512]{2,1,0:T(8,128)(2,1)S(1)} %broadcast_in_dim.12), channel_id=1, replica_groups=mesh['z'=8,'y'=4,'xh'=2,'xl'=2,'core'=2] {'xl','y','xh'}, dimensions={0} | all-to-all | bytes 4194304 | tf_op jit(solution)/shard_map/all_to_all | solution.py:166
  35.2 0.0 copy-done.6
  35.2 0.1 broadcast_in_dim.14
  35.3 33.8 %all_to_all.26 = bf16[16,64,512]{2,1,0:T(8,128)(2,1)S(1)} all-to-all(bf16[16,64,512]{2,1,0:T(8,128)(2,1)S(1)} %bitcast.49), channel_id=1, replica_groups=mesh['z'=8,'y'=4,'xh'=2,'xl'=2,'core'=2] {'xl','z'}, dimensions={0} | all-to-all | bytes 2097152 | tf_op jit(solution)/shard_map/all_to_all | solution.py:157
  69.1 2.6 %shard_map.50.own_ref = f32[1024,512]{1,0:T(8,128)} custom-call(bf16[2,1024,512]{2,1,0:T(8,128)(2,1)S(1)} %bitcast.45, bf16[2,512,512]{2,1,0:T(8,128)(2,1)S(1)} %bitcast.46), custom_call_target="tpu_custom_call" | custom-call | flops 1073741824 | bytes 5242880 | tf_op jit(solution)/shard_map/pallas_call | solution.py:40
  71.7 0.0 copy-start.1
  71.7 0.0 collective-permute-start
  71.7 0.1 iota_add_fusion
  71.8 0.7 abs_reduce_fusion.1
  72.5 0.9 abs_reduce_fusion
  73.4 1.4 fusion.10
  74.8 0.1 broadcast_in_dim.15
  74.9 0.5 collective-permute-start.1
  75.4 0.7 pad_add_fusion.place_ref
  76.0 0.1 add.55
  76.1 0.1 collective-permute-done.1
  76.2 0.1 broadcast_maximum_fusion.most_ref
  76.3 0.0 collective-permute-done.other_ref
  76.3 0.0 copy-done.1
  76.3 3.4 %shard_map.51 = (f32[1024,512]{1,0:T(8,128)S(1)}, f32[2,16,128]{2,1,0:T(8,128)S(1)}) custom-call(f32[1024,512]{1,0:T(8,128)} %shard_map.50.own_ref, f32[1024,512]{1,0:T(8,128)} %collective-permute-done.other_ref, s32[1,128]{1,0:T(1,128)S(1)} %bitcast.47, f32[2,128]{1,0:T(2,128)S(1)} %broadcast_maximum_fusion.most_ref), custom_call_target="tpu_custom_call" | custom-call | flops 5242880 | bytes 6291456 | tf_op jit(solution)/shard_map/pallas_call | solution.py:83
  79.7 0.0 copy-start
  79.7 1.3 copy-done
  81.0 0.7 broadcast_in_dim.17
  81.7 6.1 %all-to-all-start.2 = ((f32[16,16,128]{2,1,0:T(8,128)}), f32[16,16,128]{2,1,0:T(8,128)S(1)}, u32[]{:S(2)}, u32[]{:S(2)}) async-start(f32[16,16,128]{2,1,0:T(8,128)} %broadcast_in_dim.17), calls=%async_computation.2 | async-start | bytes 262144 | tf_op jit(solution)/shard_map/all_to_all | solution.py:178
  87.7 1.5 fusion.11
  89.2 0.0 copy-start.4
  89.2 4.2 %all-to-all-done.2.seen_ref = f32[16,16,128]{2,1,0:T(8,128)S(1)} async-done(((f32[16,16,128]{2,1,0:T(8,128)}), f32[16,16,128]{2,1,0:T(8,128)S(1)}, u32[]{:S(2)}, u32[]{:S(2)}) %all-to-all-start.2) | async-done | bytes 131104 | tf_op jit(solution)/shard_map/all_to_all | solution.py:178
  93.5 0.0 copy-start.5
  93.5 0.7 copy-done.5
  94.1 1.6 shard_map.52
  95.7 0.8 collective-permute-start.2
  96.5 0.6 fusion.13
  97.8 0.0 collective-permute-done.2
  97.8 0.7 broadcast_select_fusion.1
  98.5 2.3 %subtract_convert_fusion = bf16[1024,512]{1,0:T(8,128)(2,1)S(1)} fusion(f32[1024,512]{1,0:T(8,128)} %copy-done, s32[512]{0:T(512)S(1)} %add.55, f32[512]{0:T(512)S(1)} %slice_bitcast_fusion.1, f32[1024]{0:T(1024)S(1)} %get-tuple-element.13, s32[1024]{0:T(1024)S(1)} %get-tuple-element.12), kind=kLoop, calls=%fused_computation.6 | loop fusion | flops 4194304 | bytes 3158016 | tf_op jit(solution)/shard_map/convert_element_type | solution.py:200
  100.8 0.0 copy-done.4
  100.8 0.0 copy-start.3
  100.8 0.7 fusion.6
  101.6 0.5 copy-done.3
  102.0 0.7 fusion.5
  102.8 1.2 pad_maximum_fusion.1
  104.0 5.3 %all-to-all-start.4 = ((f16[16,64,512]{2,1,0:T(8,128)(2,1)}), f16[16,64,512]{2,1,0:T(8,128)(2,1)S(1)}, u32[]{:S(2)}, u32[]{:S(2)}) async-start(f16[16,64,512]{2,1,0:T(8,128)(2,1)} %bitcast.24), calls=%async_computation.4 | async-start | bytes 2097152 | tf_op jit(solution)/shard_map/all_to_all | solution.py:213
  109.3 0.1 fusion.12
  110.1 0.7 fusion.1
  110.8 0.7 fusion.2
  111.6 1.9 %pad_maximum_fusion = f16[2,1024,512]{2,1,0:T(8,128)(2,1)} fusion(f16[1,1024,512]{2,1,0:T(8,128)(2,1)S(1)} %fusion.2, f16[1,1024,512]{2,1,0:T(8,128)(2,1)S(1)} %fusion.1), kind=kLoop, calls=%fused_computation.1 | loop fusion | flops 1048576 | bytes 4194304 | tf_op jit(solution)/shard_map/stack | solution.py:216
  113.5 23.6 %all-to-all-done.4 = f16[16,64,512]{2,1,0:T(8,128)(2,1)S(1)} async-done(((f16[16,64,512]{2,1,0:T(8,128)(2,1)}), f16[16,64,512]{2,1,0:T(8,128)(2,1)S(1)}, u32[]{:S(2)}, u32[]{:S(2)}) %all-to-all-start.4) | async-done | bytes 1048608 | tf_op jit(solution)/shard_map/all_to_all | solution.py:213
  137.1 0.0 copy-start.2
  137.1 1.0 copy-done.2
  138.1 5.8 %all-to-all-start.3 = ((f16[16,128,512]{2,1,0:T(8,128)(2,1)}), f16[16,128,512]{2,1,0:T(8,128)(2,1)S(1)}, u32[]{:S(2)}, u32[]{:S(2)}) async-start(f16[16,128,512]{2,1,0:T(8,128)(2,1)} %bitcast.48), calls=%async_computation.3 | async-start | bytes 4194304 | tf_op jit(solution)/shard_map/all_to_all | solution.py:225
  143.8 0.1 fusion.7
  143.9 0.1 div.31
  144.0 0.1 fusion.8
  144.1 2.2 %fusion = f32[2,64,512]{2,1,0:T(8,128)} fusion(f32[2,8]{1,0:T(2,128)S(1)} %div.31, f16[16,64,512]{2,1,0:T(8,128)(2,1)} %copy-done.2), kind=kLoop, calls=%fused_computation.3 | loop fusion | flops 1507328 | bytes 1310784 | tf_op jit(solution)/shard_map/reduce_sum | solution.py:226
  146.4 23.4 %all-to-all-done.3 = f16[16,128,512]{2,1,0:T(8,128)(2,1)S(1)} async-done(((f16[16,128,512]{2,1,0:T(8,128)(2,1)}), f16[16,128,512]{2,1,0:T(8,128)(2,1)S(1)}, u32[]{:S(2)}, u32[]{:S(2)}) %all-to-all-start.3) | async-done | bytes 2097184 | tf_op jit(solution)/shard_map/all_to_all | solution.py:225
  169.8 1.2 multiply_reduce_fusion
  (4 shorter events, 0.0 us)
Async XLA Ops:
  1.7 33.5 %copy-start.6 = (bf16[128,512]{1,0:T(8,128)(2,1)S(1)}, bf16[128,512]{1,0:T(8,128)(2,1)}, u32[]{:S(2)}) copy-start(bf16[128,512]{1,0:T(8,128)(2,1)} %param.4) | copy-start | bytes 393220
  71.7 4.5 %copy-start.1 = (s32[128]{0:T(128)S(1)}, s32[128]{0:T(128)}, u32[]{:S(2)}) copy-start(s32[128]{0:T(128)} %param.5) | copy-start | bytes 1540
  71.7 4.5 %collective-permute-start = (f32[1024,512]{1,0:T(8,128)}, f32[1024,512]{1,0:T(8,128)}, u32[]{:S(2)}, u32[]{:S(2)}) collective-permute-start(f32[1024,512]{1,0:T(8,128)} %shard_map.50.own_ref), channel_id=1, source_target_pairs={{0,1},{1,0},{2,3},{3,2},{4,5},{5,4},{6,7},{7,6},{8,9},{9,8},{10,11... | collective-permute-start | bytes 6291464 | tf_op jit(solution)/shard_map/ppermute | solution.py:133
  74.9 1.3 collective-permute-start.1
  79.7 1.3 copy-start
  81.7 11.8 %all-to-all-start.2 = ((f32[16,16,128]{2,1,0:T(8,128)}), f32[16,16,128]{2,1,0:T(8,128)S(1)}, u32[]{:S(2)}, u32[]{:S(2)}) async-start(f32[16,16,128]{2,1,0:T(8,128)} %broadcast_in_dim.17), calls=%async_computation.2 | async-start | bytes 262144 | tf_op jit(solution)/shard_map/all_to_all | solution.py:178
  89.2 11.6 %copy-start.4 = (bf16[8,128,512]{2,1,0:T(8,128)(2,1)S(1)}, bf16[8,128,512]{2,1,0:T(8,128)(2,1)}, u32[]{:S(2)}) copy-start(bf16[8,128,512]{2,1,0:T(8,128)(2,1)} %get-tuple-element.6) | copy-start | bytes 3145732
  93.5 0.7 copy-start.5
  95.7 2.1 %collective-permute-start.2 = (f32[32,128]{1,0:T(8,128)}, f32[32,128]{1,0:T(8,128)S(1)}, u32[]{:S(2)}, u32[]{:S(2)}) collective-permute-start(f32[32,128]{1,0:T(8,128)} %shard_map.52), channel_id=1, source_target_pairs={{0,1},{1,0},{2,3},{3,2},{4,5},{5,4},{6,7},{7,6},{8,9},{9,8},{10,11... | collective-permute-start | bytes 49160 | tf_op jit(solution)/shard_map/ppermute | solution.py:133
  100.8 1.2 copy-start.3
  104.0 33.1 %all-to-all-start.4 = ((f16[16,64,512]{2,1,0:T(8,128)(2,1)}), f16[16,64,512]{2,1,0:T(8,128)(2,1)S(1)}, u32[]{:S(2)}, u32[]{:S(2)}) async-start(f16[16,64,512]{2,1,0:T(8,128)(2,1)} %bitcast.24), calls=%async_computation.4 | async-start | bytes 2097152 | tf_op jit(solution)/shard_map/all_to_all | solution.py:213
  137.1 1.0 copy-start.2
  138.1 31.8 %all-to-all-start.3 = ((f16[16,128,512]{2,1,0:T(8,128)(2,1)}), f16[16,128,512]{2,1,0:T(8,128)(2,1)S(1)}, u32[]{:S(2)}, u32[]{:S(2)}) async-start(f16[16,128,512]{2,1,0:T(8,128)(2,1)} %bitcast.48), calls=%async_computation.3 | async-start | bytes 4194304 | tf_op jit(solution)/shard_map/all_to_all | solution.py:225

commit v3 on v2

v3 whole, which is shorter than its diff:
```python
import math

import jax
import jax.numpy as jnp
from jax import lax
from jax.experimental import pallas as pl
from jax.experimental.pallas import tpu as pltpu
from jax.sharding import Mesh
from jax.sharding import PartitionSpec as P

D = 2048
NZ, NY, NXH, NXL, NC = 8, 4, 2, 2, 2
PLANE = ("xl", "y", "xh")
PAIR = ("z", "xl")
OFFSETS = (0, -1, 1, -2)
GROUP = 128
EVERY = ("z", "y", "xh", "xl", "core")
ROWS = 128
HALF = 64
WIDTH = 512
NI = NY * NXH * ROWS
NJ = NZ * HALF
LANES = 128
SCALE = 2.0 / math.sqrt(D)
VMEM = pl.BlockSpec(memory_space=pltpu.VMEM)
SMEM = pl.BlockSpec(memory_space=pltpu.SMEM)
LIMIT = pltpu.CompilerParams(vmem_limit_bytes=16 * 1024 * 1024)


def score_kernel(v1_ref, *refs):
    group_refs, s_ref, v2_ref = refs[:4], refs[4], refs[5]
    for g in range(4):
        v2_ref[:, g * GROUP : (g + 1) * GROUP, :] = group_refs[g][...]
    contract = (((1,), (1,)), ((), ()))
    for u in range(NI // 256):
        rows = slice(u * 256, (u + 1) * 256)
        s_ref[rows, :] = lax.dot_general(
            v1_ref[0, rows, :], v2_ref[0], contract, preferred_element_type=jnp.float32
        ) + lax.dot_general(
            v1_ref[1, rows, :], v2_ref[1], contract, preferred_element_type=jnp.float32
        )


def partial_scores(v1_all, groups):
    return pl.pallas_call(
        score_kernel,
        out_shape=(
            jax.ShapeDtypeStruct((NI, NJ), jnp.float32),
            jax.ShapeDtypeStruct((NXL, NJ, WIDTH), jnp.bfloat16),
        ),
        in_specs=[VMEM] * 5,
        out_specs=(VMEM, VMEM),
        compiler_params=LIMIT,
        cost_estimate=pl.CostEstimate(
            flops=2 * NI * NJ * NXL * WIDTH, bytes_accessed=6 * 2**20, transcendentals=0
        ),
    )(v1_all, *groups)


def diagonal():
    shape = (LANES, LANES)
    return lax.broadcasted_iota(jnp.int32, shape, 0) == lax.broadcasted_iota(jnp.int32, shape, 1)


def placed(z, g):
    first = lax.rem(z + OFFSETS[g] + NZ, NZ)
    return lax.rem(first, 4), first >= 4


def turned(row, trade):
    return jnp.where(trade, pltpu.roll(row, HALF, 1), row)


def stats_kernel(place_ref, own_ref, other_ref, partner_ref, most_ref, s_ref, pack_ref):
    eye = diagonal()
    pack_ref[...] = jnp.zeros_like(pack_ref)
    col_highest = jnp.full((1, NJ), -jnp.inf, jnp.float32)
    col_total = jnp.zeros((1, NJ), jnp.float32)
    for u in range(NI // LANES):
        rows = slice(u * LANES, (u + 1) * LANES)
        s = SCALE * (own_ref[rows, :] + other_ref[rows, :])
        s_ref[rows, :] = s
        highest = jnp.max(s, axis=1, keepdims=True)
        lse = highest + jnp.log(jnp.sum(jnp.exp(s - highest), axis=1, keepdims=True))
        pack_ref[0, u : u + 1, :] = jnp.sum(jnp.where(eye, lse, 0.0), axis=0, keepdims=True)
        higher = jnp.maximum(col_highest, jnp.max(s, axis=0, keepdims=True))
        col_total = col_total * jnp.exp(col_highest - higher) + jnp.sum(
            jnp.exp(s - higher), axis=0, keepdims=True
        )
        col_highest = higher
    col_lse = col_highest + jnp.log(col_total)
    for g in range(4):
        row, trade = placed(place_ref[2], g)
        pack_ref[1, pl.ds(row, 1), :] = turned(col_lse[:, g * LANES : (g + 1) * LANES], trade)
    pack_ref[0, 8:9, :] = partner_ref[...].astype(jnp.float32)
    pack_ref[0, 9:10, :] = most_ref[0:1, :]
    pack_ref[1, 9:10, :] = most_ref[1:2, :]


def local_stats(place, own, other, partner, most):
    return pl.pallas_call(
        stats_kernel,
        out_shape=(
            jax.ShapeDtypeStruct((NI, NJ), jnp.float32),
            jax.ShapeDtypeStruct((2, 16, LANES), jnp.float32),
        ),
        in_specs=[SMEM] + [VMEM] * 4,
        out_specs=(VMEM, VMEM),
        compiler_params=LIMIT,
        cost_estimate=pl.CostEstimate(
            flops=10 * NI * NJ, bytes_accessed=6 * 2**20, transcendentals=2 * NI * NJ
        ),
    )(place, own, other, partner.reshape(1, ROWS), most)


def merged(lses):
    top = jnp.max(lses, axis=0)
    return top + jnp.log(jnp.sum(jnp.exp(lses - top[None]), axis=0))


def merge_kernel(place_ref, seen_ref, known_ref, cols_ref):
    core, xl = place_ref[0], place_ref[1]

    @pl.when(core == 0)
    def _():
        known_ref[0:8, :] = merged(seen_ref[:, 0:8, :])
        for u in range(8):
            known_ref[8 + u : 9 + u, :] = seen_ref[u, 8:9, :]
        known_ref[16:24, :] = jnp.broadcast_to(jnp.max(seen_ref[:, 9:10, :], axis=0), (8, LANES))

    @pl.when(core != 0)
    def _():
        known_ref[...] = jnp.zeros_like(known_ref)
        cols_ref[...] = merged(seen_ref[pl.ds(xl * NZ, NZ), 0:8, :])
        for g in range(4):
            row, trade = placed(place_ref[2], g)
            known_ref[g : g + 1, :] = turned(cols_ref[pl.ds(row, 1), :], trade)
        known_ref[16:24, :] = jnp.broadcast_to(jnp.max(seen_ref[:, 9:10, :], axis=0), (8, LANES))


def merge_stats(place, seen):
    return pl.pallas_call(
        merge_kernel,
        out_shape=jax.ShapeDtypeStruct((24, LANES), jnp.float32),
        in_specs=[SMEM, VMEM],
        out_specs=VMEM,
        scratch_shapes=[pltpu.VMEM((8, LANES), jnp.float32)],
        cost_estimate=pl.CostEstimate(flops=10**5, bytes_accessed=2**17, transcendentals=2**14),
    )(place, seen)


def swap(x, axis):
    return lax.ppermute(x, axis, [(0, 1), (1, 0)])


def stat_groups():
    def number(z, y, xh, xl, c):
        return (((z * NY + y) * NXH + xh) * NXL + xl) * NC + c

    planes = [
        [number(z, y, xh, xl, 0) for xl in range(NXL) for y in range(NY) for xh in range(NXH)]
        for z in range(NZ)
    ]
    columns = [
        [number(z, y, xh, xl, 1) for xl in range(NXL) for z in range(NZ)]
        for y in range(NY)
        for xh in range(NXH)
    ]
    return planes + columns


def to_pair(x, dz, dxl):
    steps = [(z * NXL + l, (z + dz) % NZ * NXL + (l + dxl) % NXL) for z in range(NZ) for l in range(NXL)]
    return lax.ppermute(x, PAIR, steps)


def to_plane(x, dz):
    return lax.ppermute(x, "z", [(z, (z + dz) % NZ) for z in range(NZ)])


def on_device(view_one, view_two, partner):
    z = lax.axis_index("z")
    uhigh = lax.axis_index("y") * NXH + lax.axis_index("xh")
    xl = lax.axis_index("xl")
    core = lax.axis_index("core")
    place = jnp.stack([core, xl, z]).astype(jnp.int32)

    keep = jnp.where(xl == 0, view_two[:HALF], view_two[HALF:])
    give = jnp.where(xl == 0, view_two[HALF:], view_two[:HALF])
    side, far, far_side = to_pair(give, 0, 1), to_pair(keep, 4, 0), to_pair(give, 4, 1)
    view_one, side, far, far_side = lax.optimization_barrier((view_one, side, far, far_side))
    here = jnp.concatenate([keep, far])
    there = jnp.concatenate([side, far_side])
    pair = jnp.where(xl == 0, jnp.stack([here, there]), jnp.stack([there, here]))
    groups = [pair] + [to_plane(pair, -dz) for dz in OFFSETS[1:]]
    v1_all = lax.all_to_all(
        jnp.broadcast_to(view_one[None], (16, ROWS, WIDTH)), PLANE, 0, 0, tiled=True
    ).reshape(NXL, NI, WIDTH)

    own, v2_all = partial_scores(v1_all, groups)
    other = swap(own, "core")
    most = jnp.stack([jnp.max(jnp.abs(v2_all)), jnp.max(jnp.abs(v1_all))]).astype(jnp.float32)
    most = jnp.broadcast_to(jnp.maximum(most, 1e-30)[:, None], (2, LANES))
    most = jnp.maximum(most, swap(most, "core"))

    scores, pack = local_stats(place, own, other, partner, most)
    pack = jnp.where(core == 0, pack[0], pack[1])
    seen = lax.all_to_all(
        jnp.broadcast_to(pack[None], (16, 16, LANES)),
        EVERY,
        0,
        0,
        axis_index_groups=stat_groups(),
        tiled=True,
    )
    known = merge_stats(place, seen)
    told = swap(known, "core")
    rows = jnp.where(core == 0, known, told)
    cols = jnp.where(core == 0, told, known)
    row_lse = rows[0:8].reshape(NI)
    row_partner = rows[8:16].reshape(NI).astype(jnp.int32)
    most_two = rows[16, 0]
    col_lse = cols[0:4].reshape(NJ)
    most_one = cols[16, 0]

    block = (z + jnp.array(OFFSETS)[:, None] + 4 * jnp.arange(2)[None, :] + NZ) % NZ
    index = ((block * (NY * NXH) + uhigh) * ROWS + xl * HALF)[:, :, None] + jnp.arange(HALF)
    positive = (index.reshape(1, NJ) == row_partner[:, None]).astype(jnp.float32)
    both = jnp.exp(scores - row_lse[:, None]) + jnp.exp(scores - col_lse[None, :])
    coupling = (0.5 * both - positive).astype(jnp.bfloat16)

    part_two = [
        (
            lax.dot_general(
                coupling, v1_all[x], (((0,), (0,)), ((), ())), preferred_element_type=jnp.float32
            )
            * (64.0 / most_one)
        ).astype(jnp.float16)
        for x in range(NXL)
    ]
    parts = [
        jnp.stack([part_two[x][g * GROUP : (g + 1) * GROUP] for x in range(NXL)])
        for g in range(4)
    ]
    parts = [parts[0]] + [to_plane(parts[g], OFFSETS[g]) for g in range(1, 4)]
    part_one = jnp.stack(
        [
            (
                jnp.dot(coupling, v2_all[x], preferred_element_type=jnp.float32)
                * (128.0 / most_two)
            ).astype(jnp.float16)
            for x in range(NXL)
        ]
    )
    one_parts = lax.all_to_all(part_one.reshape(16, ROWS, WIDTH), PLANE, 0, 0, tiled=True)

    joined = sum(part.astype(jnp.float32) for part in parts)
    here = jnp.where(xl == 0, joined[0], joined[1])
    there = (jnp.where(xl == 0, joined[1], joined[0]) * 0.25).astype(jnp.float16)
    here_far = (here[HALF:] * 0.25).astype(jnp.float16)
    side, far, far_side = (
        to_pair(there[:HALF], 0, 1),
        to_pair(here_far, 4, 0),
        to_pair(there[HALF:], 4, 1),
    )
    mine = (here[:HALF] + 4.0 * far.astype(jnp.float32)) * (most_one / 64.0)
    rest = (side.astype(jnp.float32) + far_side.astype(jnp.float32)) * (most_one / 16.0)
    grad_two = jnp.where(
        xl == 0, jnp.concatenate([mine, rest]), jnp.concatenate([rest, mine])
    )
    grad_one = jnp.sum(one_parts.astype(jnp.float32), axis=0) * (most_two / 128.0)
    return (grad_one, grad_two)


def solution(mesh):
    fine = Mesh(mesh.devices.reshape(NZ, NY, NXH, NXL, NC), EVERY)
    users = P(("z", "y", "xh"))
    both = P(("z", "y", "xh"), ("xl", "core"))
    return jax.shard_map(
        on_device,
        mesh=fine,
        in_specs=(both, both, users),
        out_specs=(both, both),
        check_vma=False,
    )
```

time: 174 us -> 141 us (0.81)
  blocking collectives: 67.3 us -> 0 us
  starting transfers between devices: 18.4 us -> 45.5 us
  waiting for transfers between devices: 51.3 us -> 57.5 us
  local copies, waits for them, and re-layouts: 7.73 us -> 11.8 us
  other arithmetic: 13.6 us -> 9.55 us
  between operations: 2.18 us -> 4.3 us
    all_to_all x2 -> x0, blocking collectives: 67.3 us -> none  [the longest x1 33.8 us: on_device(): lax.all_to_all(jnp.broadcast_to(view_two.reshape(NXL, 1, HALF, WIDTH), (N...]
    ppermute x0 -> x12, waiting for transfers between devices: none -> 40.4 us  [the longest x6 21.1 us: to_plane(): return lax.ppermute(x, 'z', [(z, (z + dz) % NZ) for z in range(NZ)])]
    ppermute x0 -> x12, starting transfers between devices: none -> 24.6 us  [the longest x6 16.3 us: to_pair(): return lax.ppermute(x, PAIR, steps)]
    all_to_all x1, waiting for transfers between devices: 23.4 us -> 0.01 us  [on_device(): lax.all_to_all(part_one.reshape(16, ROWS, WIDTH), PLANE, 0, 0, tiled=True)]
    all_to_all x1, waiting for transfers between devices: 23.6 us -> 9.87 us  [on_device(): lax.all_to_all(jnp.broadcast_to(view_one[None], (16, ROWS, WIDTH)), PLANE...]
    unnamed x14 -> x26, local copies, waits for them, and re-layouts: 3.46 us -> 6.97 us
    reduce_sum x2 -> x1, other arithmetic: 3.44 us -> 0.28 us  [on_device(): jnp.sum(one_parts.astype(jnp.float32), axis=0) * (most_two / 128.0)]
    ppermute x3, starting transfers between devices: 1.32 us -> 3.59 us  [swap(): return lax.ppermute(x, axis, [(0, 1), (1, 0)])]
  transfers between devices with their start and end apart: 6 -> 18, of which waited for: 4 -> 10; matrix products, arithmetic and copies ran while one was open for 7% -> 5% of each run, Pallas kernels for 0% -> 0%
where the time goes in v3:
time: 141 us; the launch traced here: 139 us
  waiting for transfers between devices  57.5 us (41%)
  starting transfers between devices  45.5 us (32%)
  local copies, waits for them, and re-layouts  11.8 us (8%)
  other arithmetic  9.55 us (7%)
  Pallas kernels  7.55 us (5%)
  between operations  4.3 us (3%)
  matrix products  2.88 us (2%)
    ppermute x6, waiting for transfers between devices, to_plane(): return lax.ppermute(x, 'z', [(z, (z + dz) % NZ) for z in range(NZ)])  21.1 us
    ppermute x6, waiting for transfers between devices, to_pair(): return lax.ppermute(x, PAIR, steps)  19.3 us
    ppermute x6, starting transfers between devices, to_pair(): return lax.ppermute(x, PAIR, steps)  16.3 us
    all_to_all x1, waiting for transfers between devices, on_device(): lax.all_to_all(jnp.broadcast_to(view_one[None], (16, ROWS, WIDTH)), PLANE...  9.87 us
    ppermute x6, starting transfers between devices, to_plane(): return lax.ppermute(x, 'z', [(z, (z + dz) % NZ) for z in range(NZ)])  8.31 us
    all_to_all x1, starting transfers between devices, on_device(): lax.all_to_all(jnp.broadcast_to(view_one[None], (16, ROWS, WIDTH)), PLANE...  7.45 us
    unnamed x26, local copies, waits for them, and re-layouts  6.97 us
    all_to_all x1, waiting for transfers between devices, on_device(): lax.all_to_all(jnp.broadcast_to(pack[None], (16, 16, LANES)), EVERY, 0, 0...  5.66 us
  transfers between devices with their start and end apart: 18, of which 10 were waited for; matrix products, arithmetic and copies ran while one was open for 5% of the time, Pallas kernels for 0%

profile of v3, /device:TPU:4, one launch (start us, length us, event | category | flops | bytes accessed | tf_op | source)
XLA Modules:
  0.0 139.1 jit_solution(14622550233131903543)
XLA Ops:
  0.6 0.9 broadcast_select_fusion
  1.5 1.3 collective-permute-start
  2.8 7.2 %collective-permute-start.1 = (bf16[64,512]{1,0:T(8,128)(2,1)S(1)}, bf16[64,512]{1,0:T(8,128)(2,1)S(1)}, u32[]{:S(2)}, u32[]{:S(2)}) collective-permute-start(bf16[64,512]{1,0:T(8,128)(2,1)S(1)} %get-tuple-element.32), channel_id=1, source_target_pairs={{0,128},{2,130},{32,160},{34,162},{64,192},{66,194},{96,224},{98,2... | collective-permute-start | bytes 196616 | tf_op jit(solution)/shard_map/ppermute | solution.py:174
  10.0 0.3 collective-permute-start.2
  10.3 2.2 %collective-permute-done.1 = bf16[64,512]{1,0:T(8,128)(2,1)S(1)} collective-permute-done((bf16[64,512]{1,0:T(8,128)(2,1)S(1)}, bf16[64,512]{1,0:T(8,128)(2,1)S(1)}, u32[]{:S(2)}, u32[]{:S(2)}) %collective-permute-start.1) | collective-permute-done | bytes 65568 | tf_op jit(solution)/shard_map/ppermute | solution.py:174
  12.5 6.6 %collective-permute-done.2 = bf16[64,512]{1,0:T(8,128)(2,1)S(1)} collective-permute-done((bf16[64,512]{1,0:T(8,128)(2,1)S(1)}, bf16[64,512]{1,0:T(8,128)(2,1)S(1)}, u32[]{:S(2)}, u32[]{:S(2)}) %collective-permute-start.2) | collective-permute-done | bytes 65568 | tf_op jit(solution)/shard_map/ppermute | solution.py:174
  19.1 2.4 %broadcast_in_dim.8 = bf16[16,128,512]{2,1,0:T(8,128)(2,1)} broadcast(bf16[128,512]{1,0:T(8,128)(2,1)} %param.4), dimensions={1,2} | broadcast | bytes 2228224 | tf_op jit(solution)/shard_map/broadcast_in_dim | solution.py:197
  21.5 7.4 %all-to-all-start = ((bf16[16,128,512]{2,1,0:T(8,128)(2,1)}), bf16[16,128,512]{2,1,0:T(8,128)(2,1)S(1)}, u32[]{:S(2)}, u32[]{:S(2)}) async-start(bf16[16,128,512]{2,1,0:T(8,128)(2,1)} %broadcast_in_dim.8), calls=%async_computation | async-start | bytes 4194304 | tf_op jit(solution)/shard_map/all_to_all | solution.py:196
  29.0 1.1 collective-permute-start.3
  30.1 2.2 %collective-permute-start.4 = (bf16[2,128,512]{2,1,0:T(8,128)(2,1)S(1)}, bf16[2,128,512]{2,1,0:T(8,128)(2,1)S(1)}, u32[]{:S(2)}, u32[]{:S(2)}) collective-permute-start(bf16[2,128,512]{2,1,0:T(8,128)(2,1)S(1)} %maximum_select_fusion.refs_0_), channel_id=1, source_target_pairs={{0,224},{32,0},{64,32},{96,64},{128,96},{160,128},{192,160},{224,1... | collective-permute-start | bytes 786440 | tf_op jit(solution)/shard_map/ppermute | solution.py:178
  32.4 0.3 collective-permute-start.5
  32.6 11.5 %collective-permute-done.3.refs_1_ = bf16[2,128,512]{2,1,0:T(8,128)(2,1)S(1)} collective-permute-done((bf16[2,128,512]{2,1,0:T(8,128)(2,1)S(1)}, bf16[2,128,512]{2,1,0:T(8,128)(2,1)S(1)}, u32[]{:S(2)}, u32[]{:S(2)}) %collective-permute-start.3) | collective-permute-done | bytes 262176 | tf_op jit(solution)/shard_map/ppermute | solution.py:178
  44.1 0.7 copy-done.4
  44.8 0.7 copy-done.6
  45.5 0.7 copy-done.8
  46.2 9.9 %all-to-all-done = bf16[16,128,512]{2,1,0:T(8,128)(2,1)S(1)} async-done(((bf16[16,128,512]{2,1,0:T(8,128)(2,1)}), bf16[16,128,512]{2,1,0:T(8,128)(2,1)S(1)}, u32[]{:S(2)}, u32[]{:S(2)}) %all-to-all-start) | async-done | bytes 2097184 | tf_op jit(solution)/shard_map/all_to_all | solution.py:196
  56.1 0.9 copy-done.5
  57.0 0.9 copy-done.7
  58.0 0.9 copy-done.9
  58.9 2.6 %shard_map.59 = (f32[1024,512]{1,0:T(8,128)}, bf16[2,512,512]{2,1,0:T(8,128)(2,1)S(1)}) custom-call(bf16[2,1024,512]{2,1,0:T(8,128)(2,1)S(1)} %bitcast.71, bf16[2,128,512]{2,1,0:T(8,128)(2,1)S(1)} %maximum_select_fusion.refs_0_, bf16[2,128,512]{2,1,0:T(8,128)(2,1)S(1)} %copy-done.5, bf16[2,128,512]{2,1,0:T(8,128)(2,1)S(1)} %copy-done.7, ...), custom_call_target="tpu_custom_call" | custom-call | flops 1073741824 | bytes 6291456 | tf_op jit(solution)/shard_map/pallas_call | solution.py:45
  61.6 0.8 abs_reduce_fusion.1
  62.4 0.9 abs_reduce_fusion
  63.3 1.3 fusion.18
  64.6 0.1 broadcast_in_dim.9
  64.7 0.5 collective-permute-start.7
  65.2 0.1 pad_add_fusion.place_ref
  65.3 0.7 collective-permute-done.7
  66.1 3.4 %shard_map.60 = (f32[1024,512]{1,0:T(8,128)S(1)}, f32[2,16,128]{2,1,0:T(8,128)S(1)}) custom-call(s32[3]{0:T(128)S(1)} %pad_add_fusion.place_ref, f32[1024,512]{1,0:T(8,128)} %get-tuple-element.14.own_ref, f32[1024,512]{1,0:T(8,128)} %collective-permute-done.6.other_ref, s32[1,128]{1,0:T(1,128)S(1)} %bitcast.72, f32[2,128]{1,0:T(2,128)S(1)} %broadcast_maximum_fusion.most_ref), custom_call_target="tpu_custom_call" | custom-call | flops 5242880 | bytes 6291456 | tf_op jit(solution)/shard_map/pallas_call | solution.py:101
  69.5 1.3 copy-done
  70.8 0.7 broadcast_in_dim.11
  71.5 5.1 %all-to-all-start.1 = ((f32[16,16,128]{2,1,0:T(8,128)}), f32[16,16,128]{2,1,0:T(8,128)S(1)}, u32[]{:S(2)}, u32[]{:S(2)}) async-start(f32[16,16,128]{2,1,0:T(8,128)} %broadcast_in_dim.11), calls=%async_computation.1 | async-start | bytes 262144 | tf_op jit(solution)/shard_map/all_to_all | solution.py:208
  76.5 0.1 fusion.17
  76.6 0.1 iota_add_fusion
  76.7 0.1 add.118
  76.8 5.7 %all-to-all-done.1.seen_ref = f32[16,16,128]{2,1,0:T(8,128)S(1)} async-done(((f32[16,16,128]{2,1,0:T(8,128)}), f32[16,16,128]{2,1,0:T(8,128)S(1)}, u32[]{:S(2)}, u32[]{:S(2)}) %all-to-all-start.1) | async-done | bytes 131104 | tf_op jit(solution)/shard_map/all_to_all | solution.py:208
  82.4 0.7 copy-done.10
  83.1 1.6 %shard_map.61 = f32[24,128]{1,0:T(8,128)} custom-call(s32[3]{0:T(128)} %copy-done.2, f32[16,16,128]{2,1,0:T(8,128)} %copy-done.10), custom_call_target="tpu_custom_call" | custom-call | flops 100000 | bytes 131072 | tf_op jit(solution)/shard_map/pallas_call | solution.py:142
  84.6 3.1 %collective-permute-start.8 = (f32[24,128]{1,0:T(8,128)}, f32[24,128]{1,0:T(8,128)S(1)}, u32[]{:S(2)}, u32[]{:S(2)}) collective-permute-start(f32[24,128]{1,0:T(8,128)} %shard_map.61), channel_id=1, source_target_pairs={{0,1},{1,0},{2,3},{3,2},{4,5},{5,4},{6,7},{7,6},{8,9},{9,8},{10,11... | collective-permute-start | bytes 36872 | tf_op jit(solution)/shard_map/ppermute | solution.py:153
  87.7 0.2 fusion.19
  87.9 0.8 collective-permute-done.8
  88.8 0.6 slice.132
  89.4 0.5 slice.130
  90.6 1.1 subtract_convert_fusion
  91.8 0.7 fusion
  92.5 0.7 fusion.1
  93.9 0.7 fusion.2
  94.7 0.1 slice_bitcast_fusion.8
  94.8 0.7 fusion.3
  95.5 0.1 slice_bitcast_fusion.7
  95.7 1.5 %collective-permute-start.9 = (f16[2,128,512]{2,1,0:T(8,128)(2,1)S(1)}, f16[2,128,512]{2,1,0:T(8,128)(2,1)S(1)}, u32[]{:S(2)}, u32[]{:S(2)}) collective-permute-start(f16[2,128,512]{2,1,0:T(8,128)(2,1)S(1)} %pad_maximum_fusion.1), channel_id=1, source_target_pairs={{0,224},{32,0},{64,32},{96,64},{128,96},{160,128},{192,160},{224,1... | collective-permute-start | bytes 786440 | tf_op jit(solution)/shard_map/ppermute | solution.py:178
  97.2 1.9 %pad_maximum_fusion = f16[2,1024,512]{2,1,0:T(8,128)(2,1)} fusion(f16[1,1024,512]{2,1,0:T(8,128)(2,1)S(1)} %fusion.1, f16[1,1024,512]{2,1,0:T(8,128)(2,1)S(1)} %fusion), kind=kLoop, calls=%fused_computation.1 | loop fusion | flops 1048576 | bytes 4194304 | tf_op jit(solution)/shard_map/stack | solution.py:246
  99.1 4.8 %all-to-all-start.2 = ((f16[16,128,512]{2,1,0:T(8,128)(2,1)}), f16[16,128,512]{2,1,0:T(8,128)(2,1)S(1)}, u32[]{:S(2)}, u32[]{:S(2)}) async-start(f16[16,128,512]{2,1,0:T(8,128)(2,1)} %bitcast.73), calls=%async_computation.2 | async-start | bytes 4194304 | tf_op jit(solution)/shard_map/all_to_all | solution.py:255
  104.0 0.7 collective-permute-start.10
  104.8 2.5 %collective-permute-start.11 = (f16[2,128,512]{2,1,0:T(8,128)(2,1)S(1)}, f16[2,128,512]{2,1,0:T(8,128)(2,1)S(1)}, u32[]{:S(2)}, u32[]{:S(2)}) collective-permute-start(f16[2,128,512]{2,1,0:T(8,128)(2,1)S(1)} %pad_maximum_fusion.3), channel_id=1, source_target_pairs={{0,192},{32,224},{64,0},{96,32},{128,64},{160,96},{192,128},{224,1... | collective-permute-start | bytes 786440 | tf_op jit(solution)/shard_map/ppermute | solution.py:178
  109.3 3.7 %collective-permute-done.10 = f16[2,128,512]{2,1,0:T(8,128)(2,1)S(1)} collective-permute-done((f16[2,128,512]{2,1,0:T(8,128)(2,1)S(1)}, f16[2,128,512]{2,1,0:T(8,128)(2,1)S(1)}, u32[]{:S(2)}, u32[]{:S(2)}) %collective-permute-start.10) | collective-permute-done | bytes 262176 | tf_op jit(solution)/shard_map/ppermute | solution.py:178
  113.0 6.0 %collective-permute-done.11 = f16[2,128,512]{2,1,0:T(8,128)(2,1)S(1)} collective-permute-done((f16[2,128,512]{2,1,0:T(8,128)(2,1)S(1)}, f16[2,128,512]{2,1,0:T(8,128)(2,1)S(1)}, u32[]{:S(2)}, u32[]{:S(2)}) %collective-permute-start.11) | collective-permute-done | bytes 262176 | tf_op jit(solution)/shard_map/ppermute | solution.py:178
  119.0 0.1 convert_add_fusion
  119.2 1.3 collective-permute-start.13
  120.5 2.6 %collective-permute-start.14 = (f16[64,512]{1,0:T(8,128)(2,1)S(1)}, f16[64,512]{1,0:T(8,128)(2,1)S(1)}, u32[]{:S(2)}, u32[]{:S(2)}) collective-permute-start(f16[64,512]{1,0:T(8,128)(2,1)S(1)} %get-tuple-element.31), channel_id=1, source_target_pairs={{0,130},{2,128},{32,162},{34,160},{64,194},{66,192},{96,226},{98,2... | collective-permute-start | bytes 196616 | tf_op jit(solution)/shard_map/ppermute | solution.py:174
  123.1 3.7 %collective-permute-start.12 = (f16[64,512]{1,0:T(8,128)(2,1)S(1)}, f16[64,512]{1,0:T(8,128)(2,1)S(1)}, u32[]{:S(2)}, u32[]{:S(2)}) collective-permute-start(f16[64,512]{1,0:T(8,128)(2,1)S(1)} %fusion.11), channel_id=1, source_target_pairs={{0,128},{2,130},{32,160},{34,162},{64,192},{66,194},{96,224},{98,2... | collective-permute-start | bytes 196616 | tf_op jit(solution)/shard_map/ppermute | solution.py:174
  126.8 10.4 %collective-permute-done.13 = f16[64,512]{1,0:T(8,128)(2,1)S(1)} collective-permute-done((f16[64,512]{1,0:T(8,128)(2,1)S(1)}, f16[64,512]{1,0:T(8,128)(2,1)S(1)}, u32[]{:S(2)}, u32[]{:S(2)}) %collective-permute-start.13) | collective-permute-done | bytes 65568 | tf_op jit(solution)/shard_map/ppermute | solution.py:174
  137.3 0.7 maximum_select_fusion.1
  138.1 0.3 convert_reduce_fusion
  138.3 0.7 broadcast_multiply_fusion
  (44 shorter events, 0.5 us)
Async XLA Ops:
  1.5 8.7 %collective-permute-start = (bf16[64,512]{1,0:T(8,128)(2,1)S(1)}, bf16[64,512]{1,0:T(8,128)(2,1)S(1)}, u32[]{:S(2)}, u32[]{:S(2)}) collective-permute-start(bf16[64,512]{1,0:T(8,128)(2,1)S(1)} %get-tuple-element.33), channel_id=1, source_target_pairs={{0,2},{2,0},{32,34},{34,32},{64,66},{66,64},{96,98},{98,96},{128,1... | collective-permute-start | bytes 196616 | tf_op jit(solution)/shard_map/ppermute | solution.py:174
  2.8 9.7 %collective-permute-start.1 = (bf16[64,512]{1,0:T(8,128)(2,1)S(1)}, bf16[64,512]{1,0:T(8,128)(2,1)S(1)}, u32[]{:S(2)}, u32[]{:S(2)}) collective-permute-start(bf16[64,512]{1,0:T(8,128)(2,1)S(1)} %get-tuple-element.32), channel_id=1, source_target_pairs={{0,128},{2,130},{32,160},{34,162},{64,192},{66,194},{96,224},{98,2... | collective-permute-start | bytes 196616 | tf_op jit(solution)/shard_map/ppermute | solution.py:174
  10.0 9.1 %collective-permute-start.2 = (bf16[64,512]{1,0:T(8,128)(2,1)S(1)}, bf16[64,512]{1,0:T(8,128)(2,1)S(1)}, u32[]{:S(2)}, u32[]{:S(2)}) collective-permute-start(bf16[64,512]{1,0:T(8,128)(2,1)S(1)} %get-tuple-element.33), channel_id=1, source_target_pairs={{0,130},{2,128},{32,162},{34,160},{64,194},{66,192},{96,226},{98,2... | collective-permute-start | bytes 196616 | tf_op jit(solution)/shard_map/ppermute | solution.py:174
  21.5 34.5 %all-to-all-start = ((bf16[16,128,512]{2,1,0:T(8,128)(2,1)}), bf16[16,128,512]{2,1,0:T(8,128)(2,1)S(1)}, u32[]{:S(2)}, u32[]{:S(2)}) async-start(bf16[16,128,512]{2,1,0:T(8,128)(2,1)} %broadcast_in_dim.8), calls=%async_computation | async-start | bytes 4194304 | tf_op jit(solution)/shard_map/all_to_all | solution.py:196
  29.0 32.5 %copy-start.12 = (s32[4]{0:T(128)S(1)}, s32[4]{0:T(128)}, u32[]{:S(2)}) copy-start(s32[4]{0:T(128)} %constant.75.clone) | copy-start | bytes 52
  29.0 15.0 %collective-permute-start.3 = (bf16[2,128,512]{2,1,0:T(8,128)(2,1)S(1)}, bf16[2,128,512]{2,1,0:T(8,128)(2,1)S(1)}, u32[]{:S(2)}, u32[]{:S(2)}) collective-permute-start(bf16[2,128,512]{2,1,0:T(8,128)(2,1)S(1)} %maximum_select_fusion.refs_0_), channel_id=1, source_target_pairs={{0,32},{32,64},{64,96},{96,128},{128,160},{160,192},{192,224},{224... | collective-permute-start | bytes 786440 | tf_op jit(solution)/shard_map/ppermute | solution.py:178
  30.1 14.7 %collective-permute-start.4 = (bf16[2,128,512]{2,1,0:T(8,128)(2,1)S(1)}, bf16[2,128,512]{2,1,0:T(8,128)(2,1)S(1)}, u32[]{:S(2)}, u32[]{:S(2)}) collective-permute-start(bf16[2,128,512]{2,1,0:T(8,128)(2,1)S(1)} %maximum_select_fusion.refs_0_), channel_id=1, source_target_pairs={{0,224},{32,0},{64,32},{96,64},{128,96},{160,128},{192,160},{224,1... | collective-permute-start | bytes 786440 | tf_op jit(solution)/shard_map/ppermute | solution.py:178
  32.4 13.1 %collective-permute-start.5 = (bf16[2,128,512]{2,1,0:T(8,128)(2,1)S(1)}, bf16[2,128,512]{2,1,0:T(8,128)(2,1)S(1)}, u32[]{:S(2)}, u32[]{:S(2)}) collective-permute-start(bf16[2,128,512]{2,1,0:T(8,128)(2,1)S(1)} %maximum_select_fusion.refs_0_), channel_id=1, source_target_pairs={{0,64},{32,96},{64,128},{96,160},{128,192},{160,224},{192,0},{224,... | collective-permute-start | bytes 786440 | tf_op jit(solution)/shard_map/ppermute | solution.py:178
  44.1 0.7 copy-start.4
  44.8 0.7 copy-start.6
  45.5 0.7 copy-start.8
  56.1 1.0 copy-start.5
  57.0 0.9 copy-start.7
  58.0 0.9 copy-start.9
  61.5 4.5 %copy-start.3 = (s32[128]{0:T(128)S(1)}, s32[128]{0:T(128)}, u32[]{:S(2)}) copy-start(s32[128]{0:T(128)} %param.6) | copy-start | bytes 1540
  61.5 4.5 %collective-permute-start.6 = (f32[1024,512]{1,0:T(8,128)}, f32[1024,512]{1,0:T(8,128)}, u32[]{:S(2)}, u32[]{:S(2)}) collective-permute-start(f32[1024,512]{1,0:T(8,128)} %get-tuple-element.14.own_ref), channel_id=1, source_target_pairs={{0,1},{1,0},{2,3},{3,2},{4,5},{5,4},{6,7},{7,6},{8,9},{9,8},{10,11... | collective-permute-start | bytes 6291464 | tf_op jit(solution)/shard_map/ppermute | solution.py:153
  64.7 1.3 collective-permute-start.7
  65.3 4.2 %copy-start.2 = (s32[3]{0:T(128)}, s32[3]{0:T(128)S(1)}, u32[]{:S(2)}) copy-start(s32[3]{0:T(128)S(1)} %pad_add_fusion.place_ref) | copy-start | bytes 40
  69.4 1.3 copy-start
  71.5 11.0 %all-to-all-start.1 = ((f32[16,16,128]{2,1,0:T(8,128)}), f32[16,16,128]{2,1,0:T(8,128)S(1)}, u32[]{:S(2)}, u32[]{:S(2)}) async-start(f32[16,16,128]{2,1,0:T(8,128)} %broadcast_in_dim.11), calls=%async_computation.1 | async-start | bytes 262144 | tf_op jit(solution)/shard_map/all_to_all | solution.py:208
  82.4 0.7 copy-start.10
  84.6 4.1 %copy-start.11 = (f32[24,128]{1,0:T(8,128)S(1)}, f32[24,128]{1,0:T(8,128)}, u32[]{:S(2)}) copy-start(f32[24,128]{1,0:T(8,128)} %shard_map.61) | copy-start | bytes 36868
  84.6 6.0 %copy-start.1 = (f32[1024,512]{1,0:T(8,128)S(1)}, f32[1024,512]{1,0:T(8,128)}, u32[]{:S(2)}) copy-start(f32[1024,512]{1,0:T(8,128)} %copy-done) | copy-start | bytes 6291460
  84.6 4.1 %collective-permute-start.8 = (f32[24,128]{1,0:T(8,128)}, f32[24,128]{1,0:T(8,128)S(1)}, u32[]{:S(2)}, u32[]{:S(2)}) collective-permute-start(f32[24,128]{1,0:T(8,128)} %shard_map.61), channel_id=1, source_target_pairs={{0,1},{1,0},{2,3},{3,2},{4,5},{5,4},{6,7},{7,6},{8,9},{9,8},{10,11... | collective-permute-start | bytes 36872 | tf_op jit(solution)/shard_map/ppermute | solution.py:153
  95.7 13.7 %collective-permute-start.9 = (f16[2,128,512]{2,1,0:T(8,128)(2,1)S(1)}, f16[2,128,512]{2,1,0:T(8,128)(2,1)S(1)}, u32[]{:S(2)}, u32[]{:S(2)}) collective-permute-start(f16[2,128,512]{2,1,0:T(8,128)(2,1)S(1)} %pad_maximum_fusion.1), channel_id=1, source_target_pairs={{0,224},{32,0},{64,32},{96,64},{128,96},{160,128},{192,160},{224,1... | collective-permute-start | bytes 786440 | tf_op jit(solution)/shard_map/ppermute | solution.py:178
  99.1 38.9 %all-to-all-start.2 = ((f16[16,128,512]{2,1,0:T(8,128)(2,1)}), f16[16,128,512]{2,1,0:T(8,128)(2,1)S(1)}, u32[]{:S(2)}, u32[]{:S(2)}) async-start(f16[16,128,512]{2,1,0:T(8,128)(2,1)} %bitcast.73), calls=%async_computation.2 | async-start | bytes 4194304 | tf_op jit(solution)/shard_map/all_to_all | solution.py:255
  104.0 9.0 %collective-permute-start.10 = (f16[2,128,512]{2,1,0:T(8,128)(2,1)S(1)}, f16[2,128,512]{2,1,0:T(8,128)(2,1)S(1)}, u32[]{:S(2)}, u32[]{:S(2)}) collective-permute-start(f16[2,128,512]{2,1,0:T(8,128)(2,1)S(1)} %pad_maximum_fusion.2), channel_id=1, source_target_pairs={{0,32},{32,64},{64,96},{96,128},{128,160},{160,192},{192,224},{224... | collective-permute-start | bytes 786440 | tf_op jit(solution)/shard_map/ppermute | solution.py:178
  104.8 14.2 %collective-permute-start.11 = (f16[2,128,512]{2,1,0:T(8,128)(2,1)S(1)}, f16[2,128,512]{2,1,0:T(8,128)(2,1)S(1)}, u32[]{:S(2)}, u32[]{:S(2)}) collective-permute-start(f16[2,128,512]{2,1,0:T(8,128)(2,1)S(1)} %pad_maximum_fusion.3), channel_id=1, source_target_pairs={{0,192},{32,224},{64,0},{96,32},{128,64},{160,96},{192,128},{224,1... | collective-permute-start | bytes 786440 | tf_op jit(solution)/shard_map/ppermute | solution.py:178
  119.2 18.0 %collective-permute-start.13 = (f16[64,512]{1,0:T(8,128)(2,1)S(1)}, f16[64,512]{1,0:T(8,128)(2,1)S(1)}, u32[]{:S(2)}, u32[]{:S(2)}) collective-permute-start(f16[64,512]{1,0:T(8,128)(2,1)S(1)} %get-tuple-element.30), channel_id=1, source_target_pairs={{0,2},{2,0},{32,34},{34,32},{64,66},{66,64},{96,98},{98,96},{128,1... | collective-permute-start | bytes 196616 | tf_op jit(solution)/shard_map/ppermute | solution.py:174
  120.5 16.8 %collective-permute-start.14 = (f16[64,512]{1,0:T(8,128)(2,1)S(1)}, f16[64,512]{1,0:T(8,128)(2,1)S(1)}, u32[]{:S(2)}, u32[]{:S(2)}) collective-permute-start(f16[64,512]{1,0:T(8,128)(2,1)S(1)} %get-tuple-element.31), channel_id=1, source_target_pairs={{0,130},{2,128},{32,162},{34,160},{64,194},{66,192},{96,226},{98,2... | collective-permute-start | bytes 196616 | tf_op jit(solution)/shard_map/ppermute | solution.py:174
  123.1 14.2 %collective-permute-start.12 = (f16[64,512]{1,0:T(8,128)(2,1)S(1)}, f16[64,512]{1,0:T(8,128)(2,1)S(1)}, u32[]{:S(2)}, u32[]{:S(2)}) collective-permute-start(f16[64,512]{1,0:T(8,128)(2,1)S(1)} %fusion.11), channel_id=1, source_target_pairs={{0,128},{2,130},{32,160},{34,162},{64,192},{66,194},{96,224},{98,2... | collective-permute-start | bytes 196616 | tf_op jit(solution)/shard_map/ppermute | solution.py:174

commit v4 on v3

v4 whole, which is shorter than its diff:
```python
import math

import jax
import jax.numpy as jnp
from jax import lax
from jax.experimental import pallas as pl
from jax.experimental.pallas import tpu as pltpu
from jax.sharding import Mesh
from jax.sharding import PartitionSpec as P

D = 2048
NZ, NY, NXH, NXL, NC = 8, 4, 2, 2, 2
PLANE = ("xl", "y", "xh")
OFFSETS = (0, -1, 1, -2)
GROUP = 128
EVERY = ("z", "y", "xh", "xl", "core")
ROWS = 128
HALF = 64
WIDTH = 512
NI = NY * NXH * ROWS
NJ = NZ * HALF
LANES = 128
SCALE = 2.0 / math.sqrt(D)
VMEM = pl.BlockSpec(memory_space=pltpu.VMEM)
SMEM = pl.BlockSpec(memory_space=pltpu.SMEM)


def limit(mib):
    return pltpu.CompilerParams(vmem_limit_bytes=mib * 1024 * 1024)


def score_kernel(v1_ref, *refs):
    group_refs, s_ref, v2_ref = refs[:4], refs[4], refs[5]
    for g in range(4):
        v2_ref[:, g * GROUP : (g + 1) * GROUP, :] = group_refs[g][...]
    contract = (((1,), (1,)), ((), ()))
    for u in range(NI // 256):
        rows = slice(u * 256, (u + 1) * 256)
        s_ref[rows, :] = lax.dot_general(
            v1_ref[0, rows, :], v2_ref[0], contract, preferred_element_type=jnp.float32
        ) + lax.dot_general(
            v1_ref[1, rows, :], v2_ref[1], contract, preferred_element_type=jnp.float32
        )


def partial_scores(v1_all, groups):
    return pl.pallas_call(
        score_kernel,
        out_shape=(
            jax.ShapeDtypeStruct((NI, NJ), jnp.float32),
            jax.ShapeDtypeStruct((NXL, NJ, WIDTH), jnp.bfloat16),
        ),
        in_specs=[VMEM] * 5,
        out_specs=(VMEM, VMEM),
        compiler_params=limit(8),
        cost_estimate=pl.CostEstimate(
            flops=2 * NI * NJ * NXL * WIDTH, bytes_accessed=6 * 2**20, transcendentals=0
        ),
    )(v1_all, *groups)


def diagonal():
    shape = (LANES, LANES)
    return lax.broadcasted_iota(jnp.int32, shape, 0) == lax.broadcasted_iota(jnp.int32, shape, 1)


def placed(z, g):
    first = lax.rem(z + OFFSETS[g] + NZ, NZ)
    return lax.rem(first, 4), first >= 4


def turned(row, trade):
    return jnp.where(trade, pltpu.roll(row, HALF, 1), row)


def stats_kernel(
    place_ref, own_ref, other_ref, partner_ref, most_ref, most_other_ref, s_ref, out_ref, pack_ref
):
    eye = diagonal()
    core = place_ref[0]
    pack_ref[...] = jnp.zeros_like(pack_ref)
    col_highest = jnp.full((1, NJ), -jnp.inf, jnp.float32)
    col_total = jnp.zeros((1, NJ), jnp.float32)
    for u in range(NI // LANES):
        rows = slice(u * LANES, (u + 1) * LANES)
        s = SCALE * (own_ref[rows, :] + other_ref[rows, :])
        s_ref[rows, :] = s
        highest = jnp.max(s, axis=1, keepdims=True)
        lse = highest + jnp.log(jnp.sum(jnp.exp(s - highest), axis=1, keepdims=True))
        pack_ref[0, u : u + 1, :] = jnp.sum(jnp.where(eye, lse, 0.0), axis=0, keepdims=True)
        higher = jnp.maximum(col_highest, jnp.max(s, axis=0, keepdims=True))
        col_total = col_total * jnp.exp(col_highest - higher) + jnp.sum(
            jnp.exp(s - higher), axis=0, keepdims=True
        )
        col_highest = higher
    col_lse = col_highest + jnp.log(col_total)
    for g in range(4):
        row, trade = placed(place_ref[2], g)
        pack_ref[1, pl.ds(row, 1), :] = turned(col_lse[:, g * LANES : (g + 1) * LANES], trade)
    most = jnp.max(jnp.maximum(most_ref[...], most_other_ref[...]), axis=1, keepdims=True)
    most = jnp.broadcast_to(jnp.maximum(most, 1e-30), (2, LANES))
    pack_ref[0, 8:9, :] = partner_ref[...].astype(jnp.float32)
    pack_ref[0, 9:10, :] = most[0:1, :]
    pack_ref[1, 9:10, :] = most[1:2, :]
    chosen = jnp.where(core == 0, pack_ref[0], pack_ref[1])
    for p in range(16):
        out_ref[p] = chosen


def local_stats(place, own, other, partner, most, most_other):
    return pl.pallas_call(
        stats_kernel,
        out_shape=(
            jax.ShapeDtypeStruct((NI, NJ), jnp.float32),
            jax.ShapeDtypeStruct((16, 16, LANES), jnp.float32),
        ),
        in_specs=[SMEM] + [VMEM] * 5,
        out_specs=(VMEM, VMEM),
        scratch_shapes=[pltpu.VMEM((2, 16, LANES), jnp.float32)],
        compiler_params=limit(8),
        cost_estimate=pl.CostEstimate(
            flops=10 * NI * NJ, bytes_accessed=6 * 2**20, transcendentals=2 * NI * NJ
        ),
    )(place, own, other, partner.reshape(1, ROWS), most, most_other)


def merged(lses):
    top = jnp.max(lses, axis=0)
    return top + jnp.log(jnp.sum(jnp.exp(lses - top[None]), axis=0))


def merge_kernel(place_ref, seen_ref, known_ref, cols_ref):
    core, xl = place_ref[0], place_ref[1]

    @pl.when(core == 0)
    def _():
        known_ref[0:8, :] = merged(seen_ref[:, 0:8, :])
        for u in range(8):
            known_ref[8 + u : 9 + u, :] = seen_ref[u, 8:9, :]

    @pl.when(core != 0)
    def _():
        known_ref[...] = jnp.zeros_like(known_ref)
        cols_ref[...] = merged(seen_ref[pl.ds(xl * NZ, NZ), 0:8, :])
        for g in range(4):
            row, trade = placed(place_ref[2], g)
            known_ref[g : g + 1, :] = turned(cols_ref[pl.ds(row, 1), :], trade)

    known_ref[16:24, :] = jnp.broadcast_to(jnp.max(seen_ref[:, 9:10, :], axis=0), (8, LANES))


def merge_stats(place, seen):
    return pl.pallas_call(
        merge_kernel,
        out_shape=jax.ShapeDtypeStruct((24, LANES), jnp.float32),
        in_specs=[SMEM, VMEM],
        out_specs=VMEM,
        scratch_shapes=[pltpu.VMEM((8, LANES), jnp.float32)],
        compiler_params=limit(2),
        cost_estimate=pl.CostEstimate(flops=10**5, bytes_accessed=2**17, transcendentals=2**14),
    )(place, seen)


def couple_kernel(place_ref, s_ref, known_ref, told_ref, c_ref, size_ref):
    core, xl, z, uhigh = place_ref[0], place_ref[1], place_ref[2], place_ref[3]
    rows = jnp.where(core == 0, known_ref[...], told_ref[...])
    cols = jnp.where(core == 0, told_ref[...], known_ref[...])
    eye = diagonal()
    lane = lax.broadcasted_iota(jnp.int32, (1, LANES), 1)
    index, col_lse = [], []
    for g in range(4):
        first = lax.rem(z + OFFSETS[g] + NZ, NZ)
        second = lax.rem(first + 4, NZ)
        user = jnp.where(lane < HALF, first, second) * (NY * NXH) + uhigh
        inside = jnp.where(lane < HALF, lane, lane - HALF)
        index.append((user * ROWS + xl * HALF + inside).astype(jnp.float32))
        col_lse.append(cols[g : g + 1, :])
    index = jnp.concatenate(index, axis=1)
    col_lse = jnp.concatenate(col_lse, axis=1)
    for u in range(NI // LANES):
        here = slice(u * LANES, (u + 1) * LANES)
        s = s_ref[here, :]
        row_lse = jnp.sum(jnp.where(eye, rows[u : u + 1, :], 0.0), axis=1, keepdims=True)
        partner = jnp.sum(jnp.where(eye, rows[8 + u : 9 + u, :], 0.0), axis=1, keepdims=True)
        both = jnp.exp(s - row_lse) + jnp.exp(s - col_lse)
        positive = (partner == index).astype(jnp.float32)
        c_ref[here, :] = (0.5 * both - positive).astype(jnp.bfloat16)
    size_ref[0:1, :] = rows[16:17, :]
    size_ref[1:2, :] = cols[16:17, :]


def coupling_of(place, scores, known, told):
    return pl.pallas_call(
        couple_kernel,
        out_shape=(
            jax.ShapeDtypeStruct((NI, NJ), jnp.bfloat16),
            jax.ShapeDtypeStruct((2, LANES), jnp.float32),
        ),
        in_specs=[SMEM] + [VMEM] * 3,
        out_specs=(VMEM, VMEM),
        compiler_params=limit(5),
        cost_estimate=pl.CostEstimate(
            flops=8 * NI * NJ, bytes_accessed=3 * 2**20, transcendentals=2 * NI * NJ
        ),
    )(place, scores, known, told)


def swap(x, axis):
    return lax.ppermute(x, axis, [(0, 1), (1, 0)])


def stat_groups():
    def number(z, y, xh, xl, c):
        return (((z * NY + y) * NXH + xh) * NXL + xl) * NC + c

    planes = [
        [number(z, y, xh, xl, 0) for xl in range(NXL) for y in range(NY) for xh in range(NXH)]
        for z in range(NZ)
    ]
    columns = [
        [number(z, y, xh, xl, 1) for xl in range(NXL) for z in range(NZ)]
        for y in range(NY)
        for xh in range(NXH)
    ]
    return planes + columns


def to_plane(x, dz):
    return lax.ppermute(x, "z", [(z, (z + dz) % NZ) for z in range(NZ)])


def largest(x):
    return jnp.max(jnp.abs(x), axis=(0, 1)).astype(jnp.float32)


def on_device(view_one, view_two, partner):
    z = lax.axis_index("z")
    uhigh = lax.axis_index("y") * NXH + lax.axis_index("xh")
    xl = lax.axis_index("xl")
    core = lax.axis_index("core")
    place = jnp.stack([core, xl, z, uhigh]).astype(jnp.int32)

    keep = jnp.where(xl == 0, view_two[:HALF], view_two[HALF:])
    give = jnp.where(xl == 0, view_two[HALF:], view_two[:HALF])
    side = swap(give, "xl")
    copies = jnp.broadcast_to(view_one[None], (16, ROWS, WIDTH))
    copies, side = lax.optimization_barrier((copies, side))
    here = jnp.where(xl == 0, jnp.stack([keep, side]), jnp.stack([side, keep]))
    pair = jnp.concatenate([here, to_plane(here, 4)], axis=1)
    groups = [pair] + [to_plane(pair, -dz) for dz in OFFSETS[1:]]
    v1_all = lax.all_to_all(copies, PLANE, 0, 0, tiled=True).reshape(NXL, NI, WIDTH)

    own, v2_all = partial_scores(v1_all, groups)
    other = swap(own, "core")
    most = jnp.stack([largest(v2_all), largest(v1_all)])
    most_other = swap(most, "core")

    scores, pack = local_stats(place, own, other, partner, most, most_other)
    seen = lax.all_to_all(
        pack, EVERY, 0, 0, axis_index_groups=stat_groups(), tiled=True
    )
    known = merge_stats(place, seen)
    coupling, sizes = coupling_of(place, scores, known, swap(known, "core"))
    most_two, most_one = sizes[0, 0], sizes[1, 0]

    part_one = (
        lax.dot_general(
            jnp.broadcast_to(coupling[None], (NXL, NI, NJ)),
            v2_all,
            (((2,), (1,)), ((0,), (0,))),
            preferred_element_type=jnp.float32,
        )
        * (128.0 / most_two)
    ).astype(jnp.float16)
    coupling, part_one = lax.optimization_barrier((coupling, part_one))
    one_parts = lax.all_to_all(part_one.reshape(16, ROWS, WIDTH), PLANE, 0, 0, tiled=True)
    part_two = (
        lax.dot_general(
            jnp.broadcast_to(coupling[None], (NXL, NI, NJ)),
            v1_all,
            (((1,), (1,)), ((0,), (0,))),
            preferred_element_type=jnp.float32,
        )
        * (64.0 / most_one)
    ).astype(jnp.float16)
    parts = [part_two[:, :GROUP]] + [
        to_plane(part_two[:, g * GROUP : (g + 1) * GROUP], OFFSETS[g]) for g in range(1, 4)
    ]
    joined = sum(part.astype(jnp.float32) for part in parts)
    far = to_plane((joined[:, HALF:] * 0.25).astype(jnp.float16), 4)
    total = (joined[:, :HALF] + 4.0 * far.astype(jnp.float32)) * (most_one / 64.0)
    stay = jnp.where(xl == 0, total[0], total[1])
    come = swap(jnp.where(xl == 0, total[1], total[0]), "xl")
    grad_two = jnp.where(
        xl == 0, jnp.concatenate([stay, come]), jnp.concatenate([come, stay])
    )
    grad_one = jnp.sum(one_parts.astype(jnp.float32), axis=0) * (most_two / 128.0)
    return (grad_one, grad_two)


def solution(mesh):
    fine = Mesh(mesh.devices.reshape(NZ, NY, NXH, NXL, NC), EVERY)
    users = P(("z", "y", "xh"))
    both = P(("z", "y", "xh"), ("xl", "core"))
    return jax.shard_map(
        on_device,
        mesh=fine,
        in_specs=(both, both, users),
        out_specs=(both, both),
        check_vma=False,
    )
```

time: 141 us -> 134 us (0.950)
  blocking collectives: 0 us -> 12.8 us
  starting transfers between devices: 45.5 us -> 38.8 us
  waiting for transfers between devices: 57.5 us -> 50.8 us
  other arithmetic: 9.55 us -> 4.97 us
  local copies, waits for them, and re-layouts: 11.8 us -> 9.5 us
  matrix products: 2.88 us -> 5.08 us
    ppermute x6 -> x8, waiting for transfers between devices: 21.1 us -> 40.4 us  [to_plane(): return lax.ppermute(x, 'z', [(z, (z + dz) % NZ) for z in range(NZ)])]
    ppermute x6 -> x0, waiting for transfers between devices: 19.3 us -> none  [to_pair(): return lax.ppermute(x, PAIR, steps)]
    ppermute x6 -> x0, starting transfers between devices: 16.3 us -> none  [to_pair(): return lax.ppermute(x, PAIR, steps)]
    all_to_all x2 -> x1, waiting for transfers between devices: 15.5 us -> 0.01 us  [on_device(): lax.all_to_all(copies, PLANE, 0, 0, tiled=True).reshape(NXL, NI, WIDTH)]
    all_to_all x0 -> x1, blocking collectives: none -> 12.8 us  [on_device(): lax.all_to_all(pack, EVERY, 0, 0, axis_index_groups=stat_groups(), tiled=...]
    ppermute x6 -> x8, starting transfers between devices: 8.31 us -> 18.6 us  [to_plane(): return lax.ppermute(x, 'z', [(z, (z + dz) % NZ) for z in range(NZ)])]
    ppermute x3 -> x5, waiting for transfers between devices: 1.58 us -> 10.4 us  [swap(): return lax.ppermute(x, axis, [(0, 1), (1, 0)])]
    all_to_all x2 -> x1, starting transfers between devices: 12.5 us -> 7.45 us  [on_device(): lax.all_to_all(copies, PLANE, 0, 0, tiled=True).reshape(NXL, NI, WIDTH)]
  transfers between devices with their start and end apart: 18 -> 15, of which waited for: 10 -> 11; matrix products, arithmetic and copies ran while one was open for 5% -> 4% of each run, Pallas kernels for 0% -> 0%
where the time goes in v4:
time: 134 us; the launch traced here: 133 us
  waiting for transfers between devices  50.8 us (38%)
  starting transfers between devices  38.8 us (29%)
  blocking collectives  12.8 us (10%)
  local copies, waits for them, and re-layouts  9.5 us (7%)
  Pallas kernels  7.98 us (6%)
  matrix products  5.08 us (4%)
  other arithmetic  4.97 us (4%)
  between operations  3.44 us (3%)
    ppermute x8, waiting for transfers between devices, to_plane(): return lax.ppermute(x, 'z', [(z, (z + dz) % NZ) for z in range(NZ)])  40.4 us
    ppermute x8, starting transfers between devices, to_plane(): return lax.ppermute(x, 'z', [(z, (z + dz) % NZ) for z in range(NZ)])  18.6 us
    all_to_all x1, blocking collectives, on_device(): lax.all_to_all(pack, EVERY, 0, 0, axis_index_groups=stat_groups(), tiled=...  12.8 us
    ppermute x5, waiting for transfers between devices, swap(): return lax.ppermute(x, axis, [(0, 1), (1, 0)])  10.4 us
    all_to_all x1, starting transfers between devices, on_device(): lax.all_to_all(copies, PLANE, 0, 0, tiled=True).reshape(NXL, NI, WIDTH)  7.45 us
    all_to_all x1, starting transfers between devices, on_device(): lax.all_to_all(part_one.reshape(16, ROWS, WIDTH), PLANE, 0, 0, tiled=True)  7.06 us
    ppermute x5, starting transfers between devices, swap(): return lax.ppermute(x, axis, [(0, 1), (1, 0)])  5.71 us
    unnamed x18, local copies, waits for them, and re-layouts  4.97 us
  transfers between devices with their start and end apart: 15, of which 11 were waited for; matrix products, arithmetic and copies ran while one was open for 4% of the time, Pallas kernels for 0%

profile of v4, /device:TPU:4, one launch (start us, length us, event | category | flops | bytes accessed | tf_op | source)
XLA Modules:
  0.0 133.4 jit_solution(8965808556421611880)
XLA Ops:
  0.6 0.9 select_bitcast_fusion.2
  1.5 1.3 collective-permute-start
  2.8 3.1 %collective-permute-done = bf16[64,512]{1,0:T(8,128)(2,1)S(1)} collective-permute-done((bf16[64,512]{1,0:T(8,128)(2,1)S(1)}, bf16[64,512]{1,0:T(8,128)(2,1)S(1)}, u32[]{:S(2)}, u32[]{:S(2)}) %collective-permute-start) | collective-permute-done | bytes 65568 | tf_op jit(solution)/shard_map/ppermute | solution.py:209
  5.9 2.4 %broadcast_in_dim.6 = bf16[16,128,512]{2,1,0:T(8,128)(2,1)} broadcast(bf16[128,512]{1,0:T(8,128)(2,1)} %param.3), dimensions={1,2} | broadcast | bytes 2228224 | tf_op jit(solution)/shard_map/broadcast_in_dim | solution.py:246
  8.3 7.4 %all-to-all-start = ((bf16[16,128,512]{2,1,0:T(8,128)(2,1)}), bf16[16,128,512]{2,1,0:T(8,128)(2,1)S(1)}, u32[]{:S(2)}, u32[]{:S(2)}) async-start(bf16[16,128,512]{2,1,0:T(8,128)(2,1)} %broadcast_in_dim.6), calls=%async_computation | async-start | bytes 4194304 | tf_op jit(solution)/shard_map/all_to_all | solution.py:251
  15.8 7.3 %collective-permute-start.1 = (bf16[2,64,512]{2,1,0:T(8,128)(2,1)S(1)}, bf16[2,64,512]{2,1,0:T(8,128)(2,1)S(1)}, u32[]{:S(2)}, u32[]{:S(2)}) collective-permute-start(bf16[2,64,512]{2,1,0:T(8,128)(2,1)S(1)} %maximum_select_fusion.1), channel_id=1, source_target_pairs={{0,128},{32,160},{64,192},{96,224},{128,0},{160,32},{192,64},{224,... | collective-permute-start | bytes 393224 | tf_op jit(solution)/shard_map/ppermute | solution.py:229
  23.1 3.5 %collective-permute-done.1 = bf16[2,64,512]{2,1,0:T(8,128)(2,1)S(1)} collective-permute-done((bf16[2,64,512]{2,1,0:T(8,128)(2,1)S(1)}, bf16[2,64,512]{2,1,0:T(8,128)(2,1)S(1)}, u32[]{:S(2)}, u32[]{:S(2)}) %collective-permute-start.1) | collective-permute-done | bytes 131104 | tf_op jit(solution)/shard_map/ppermute | solution.py:229
  26.6 3.1 %collective-permute-start.4 = (bf16[2,128,512]{2,1,0:T(8,128)(2,1)S(1)}, bf16[2,128,512]{2,1,0:T(8,128)(2,1)S(1)}, u32[]{:S(2)}, u32[]{:S(2)}) collective-permute-start(bf16[2,128,512]{2,1,0:T(8,128)(2,1)S(1)} %pad_maximum_fusion.refs_0_), channel_id=1, source_target_pairs={{0,64},{32,96},{64,128},{96,160},{128,192},{160,224},{192,0},{224,... | collective-permute-start | bytes 786440 | tf_op jit(solution)/shard_map/ppermute | solution.py:229
  29.7 2.0 %collective-permute-start.3 = (bf16[2,128,512]{2,1,0:T(8,128)(2,1)S(1)}, bf16[2,128,512]{2,1,0:T(8,128)(2,1)S(1)}, u32[]{:S(2)}, u32[]{:S(2)}) collective-permute-start(bf16[2,128,512]{2,1,0:T(8,128)(2,1)S(1)} %pad_maximum_fusion.refs_0_), channel_id=1, source_target_pairs={{0,224},{32,0},{64,32},{96,64},{128,96},{160,128},{192,160},{224,1... | collective-permute-start | bytes 786440 | tf_op jit(solution)/shard_map/ppermute | solution.py:229
  31.6 0.1 collective-permute-start.2
  31.7 12.2 %collective-permute-done.4.refs_3_ = bf16[2,128,512]{2,1,0:T(8,128)(2,1)S(1)} collective-permute-done((bf16[2,128,512]{2,1,0:T(8,128)(2,1)S(1)}, bf16[2,128,512]{2,1,0:T(8,128)(2,1)S(1)}, u32[]{:S(2)}, u32[]{:S(2)}) %collective-permute-start.4) | collective-permute-done | bytes 262176 | tf_op jit(solution)/shard_map/ppermute | solution.py:229
  43.9 0.0 copy-start.3
  43.9 0.7 copy-done.3
  44.6 0.0 collective-permute-done.3.refs_2_
  44.6 0.0 copy-start.5
  44.6 0.7 copy-done.5
  45.3 0.4 collective-permute-done.2.refs_1_
  45.7 0.0 copy-start.7
  45.7 0.7 copy-done.7
  46.4 0.0 all-to-all-done
  46.4 0.0 copy-start.4
  46.4 0.9 copy-done.4
  47.4 0.0 copy-start.6
  47.4 0.9 copy-done.6
  48.3 0.9 copy-done.8
  49.3 2.6 %shard_map.50 = (f32[1024,512]{1,0:T(8,128)}, bf16[2,512,512]{2,1,0:T(8,128)(2,1)S(1)}) custom-call(bf16[2,1024,512]{2,1,0:T(8,128)(2,1)S(1)} %bitcast.20, bf16[2,128,512]{2,1,0:T(8,128)(2,1)S(1)} %pad_maximum_fusion.refs_0_, bf16[2,128,512]{2,1,0:T(8,128)(2,1)S(1)} %copy-done.8, bf16[2,128,512]{2,1,0:T(8,128)(2,1)S(1)} %copy-done.6, ...), custom_call_target="tpu_custom_call" | custom-call | flops 1073741824 | bytes 6291456 | tf_op jit(solution)/shard_map/pallas_call | solution.py:47
  51.9 0.0 collective-permute-start.5
  51.9 0.2 abs_reduce_fusion
  52.1 0.1 abs_reduce_fusion.1
  52.3 0.6 collective-permute-start.6
  52.9 0.1 pad_add_fusion.place_ref
  53.0 3.1 %collective-permute-done.6.most_other_ref = f32[2,512]{1,0:T(2,128)S(1)} collective-permute-done((f32[2,512]{1,0:T(2,128)S(1)}, f32[2,512]{1,0:T(2,128)S(1)}, u32[]{:S(2)}, u32[]{:S(2)}) %collective-permute-start.6) | collective-permute-done | bytes 4128 | tf_op jit(solution)/shard_map/ppermute | solution.py:209
  56.1 0.3 collective-permute-done.5.other_ref
  56.4 0.0 copy-done.2
  56.4 3.4 %shard_map.51 = (f32[1024,512]{1,0:T(8,128)S(1)}, f32[16,16,128]{2,1,0:T(8,128)S(1)}) custom-call(s32[4]{0:T(128)S(1)} %pad_add_fusion.place_ref, f32[1024,512]{1,0:T(8,128)} %get-tuple-element.14.own_ref, f32[1024,512]{1,0:T(8,128)} %collective-permute-done.5.other_ref, s32[1,128]{1,0:T(1,128)S(1)} %bitcast.22, f32[2,512]{1,0:T(2,128)S(1)} %maximum_convert_fusion.most_ref, ...), custom_call_target="tpu_custom_call" | custom-call | flops 5242880 | bytes 6291456 | tf_op jit(solution)/shard_map/pallas_call | solution.py:111
  59.8 12.8 %all_to_all.15.seen_ref = f32[16,16,128]{2,1,0:T(8,128)S(1)} all-to-all(f32[16,16,128]{2,1,0:T(8,128)S(1)} %get-tuple-element.17), channel_id=1, replica_groups={{0,4,8,12,16,20,24,28,2,6,10,14,18,22,26,30},{32,36,40,44,48,52,56,60,3..., dimensions={0} | all-to-all | bytes 262144 | tf_op jit(solution)/shard_map/all_to_all | solution.py:259
  72.6 0.6 shard_map.52.known_ref
  73.2 2.5 %collective-permute-start.7 = (f32[24,128]{1,0:T(8,128)S(1)}, f32[24,128]{1,0:T(8,128)S(1)}, u32[]{:S(2)}, u32[]{:S(2)}) collective-permute-start(f32[24,128]{1,0:T(8,128)S(1)} %shard_map.52.known_ref), channel_id=1, source_target_pairs={{0,1},{1,0},{2,3},{3,2},{4,5},{5,4},{6,7},{7,6},{8,9},{9,8},{10,11... | collective-permute-start | bytes 36872 | tf_op jit(solution)/shard_map/ppermute | solution.py:209
  75.7 0.8 collective-permute-done.7.told_ref
  76.5 1.4 %shard_map.53 = (bf16[1024,512]{1,0:T(8,128)(2,1)S(1)}, f32[2,128]{1,0:T(2,128)S(1)}) custom-call(s32[4]{0:T(128)S(1)} %pad_add_fusion.place_ref, f32[1024,512]{1,0:T(8,128)S(1)} %get-tuple-element.16.s_ref, f32[24,128]{1,0:T(8,128)S(1)} %shard_map.52.known_ref, f32[24,128]{1,0:T(8,128)S(1)} %collective-permute-done.7.told_ref), custom_call_target="tpu_custom_call" | custom-call | flops 4194304 | bytes 3145728 | tf_op jit(solution)/shard_map/pallas_call | solution.py:193
  78.0 0.0 copy-start
  78.0 0.6 fusion.5
  79.2 2.6 %multiply_convert_fusion = f16[2,1024,512]{2,1,0:T(8,128)(2,1)} fusion(bf16[2,512,512]{2,1,0:T(8,128)(2,1)S(1)} %get-tuple-element.15, f32[]{:T(128)} %bitcast.8, bf16[1024,512]{1,0:T(8,128)(2,1)S(1)} %get-tuple-element.21), kind=kOutput, calls=%fused_computation.1 | convolution fusion | flops 1075838976 | bytes 4194308 | tf_op jit(solution)/shard_map/dot_general | solution.py:267
  81.8 0.0 copy-done
  81.8 7.1 %all-to-all-start.2 = ((f16[16,128,512]{2,1,0:T(8,128)(2,1)}), f16[16,128,512]{2,1,0:T(8,128)(2,1)}, u32[]{:S(2)}, u32[]{:S(2)}) async-start(f16[16,128,512]{2,1,0:T(8,128)(2,1)} %bitcast.23), calls=%async_computation.2 | async-start | bytes 4194304 | tf_op jit(solution)/shard_map/all_to_all | solution.py:276
  88.9 0.0 copy-done.1
  88.9 1.3 copy.5
  90.9 2.5 %multiply_convert_fusion.1 = f16[2,512,512]{2,1,0:T(8,128)(2,1)S(1)} fusion(bf16[2,1024,512]{2,1,0:T(8,128)(2,1)S(1)} %bitcast.21, f32[]{:T(128)} %bitcast.11, bf16[1024,512]{0,1:T(8,128)(2,1)} %copy.5), kind=kOutput, calls=%fused_computation.2 | convolution fusion | flops 1074790400 | bytes 4194308 | tf_op jit(solution)/shard_map/dot_general | solution.py:278
  93.4 0.2 fusion.4
  93.6 1.7 %collective-permute-start.8 = (f16[2,128,512]{2,1,0:T(8,128)(2,1)S(1)}, f16[2,128,512]{2,1,0:T(8,128)(2,1)S(1)}, u32[]{:S(2)}, u32[]{:S(2)}) collective-permute-start(f16[2,128,512]{2,1,0:T(8,128)(2,1)S(1)} %get-tuple-element.22), channel_id=1, source_target_pairs={{0,224},{32,0},{64,32},{96,64},{128,96},{160,128},{192,160},{224,1... | collective-permute-start | bytes 786440 | tf_op jit(solution)/shard_map/ppermute | solution.py:229
  95.3 1.1 collective-permute-start.10
  96.4 1.0 collective-permute-start.9
  97.4 6.4 %collective-permute-done.8 = f16[2,128,512]{2,1,0:T(8,128)(2,1)S(1)} collective-permute-done((f16[2,128,512]{2,1,0:T(8,128)(2,1)S(1)}, f16[2,128,512]{2,1,0:T(8,128)(2,1)S(1)}, u32[]{:S(2)}, u32[]{:S(2)}) %collective-permute-start.8) | collective-permute-done | bytes 262176 | tf_op jit(solution)/shard_map/ppermute | solution.py:229
  103.8 10.1 %collective-permute-done.10 = f16[2,128,512]{2,1,0:T(8,128)(2,1)S(1)} collective-permute-done((f16[2,128,512]{2,1,0:T(8,128)(2,1)S(1)}, f16[2,128,512]{2,1,0:T(8,128)(2,1)S(1)}, u32[]{:S(2)}, u32[]{:S(2)}) %collective-permute-start.10) | collective-permute-done | bytes 262176 | tf_op jit(solution)/shard_map/ppermute | solution.py:229
  113.9 0.0 collective-permute-done.9
  113.9 0.2 convert_add_fusion
  114.1 2.3 %collective-permute-start.11 = (f16[2,64,512]{2,1,0:T(8,128)(2,1)S(1)}, f16[2,64,512]{2,1,0:T(8,128)(2,1)S(1)}, u32[]{:S(2)}, u32[]{:S(2)}) collective-permute-start(f16[2,64,512]{2,1,0:T(8,128)(2,1)S(1)} %fusion.2), channel_id=1, source_target_pairs={{0,128},{32,160},{64,192},{96,224},{128,0},{160,32},{192,64},{224,... | collective-permute-start | bytes 393224 | tf_op jit(solution)/shard_map/ppermute | solution.py:229
  117.1 7.8 %collective-permute-done.11 = f16[2,64,512]{2,1,0:T(8,128)(2,1)S(1)} collective-permute-done((f16[2,64,512]{2,1,0:T(8,128)(2,1)S(1)}, f16[2,64,512]{2,1,0:T(8,128)(2,1)S(1)}, u32[]{:S(2)}, u32[]{:S(2)}) %collective-permute-start.11) | collective-permute-done | bytes 131104 | tf_op jit(solution)/shard_map/ppermute | solution.py:229
  125.0 1.3 collective-permute-start.12
  127.0 3.1 %collective-permute-done.12 = f32[64,512]{1,0:T(8,128)S(1)} collective-permute-done((f32[64,512]{1,0:T(8,128)S(1)}, f32[64,512]{1,0:T(8,128)S(1)}, u32[]{:S(2)}, u32[]{:S(2)}) %collective-permute-start.12) | collective-permute-done | bytes 131104 | tf_op jit(solution)/shard_map/ppermute | solution.py:209
  130.0 0.7 maximum_select_fusion
  130.8 0.0 all-to-all-done.2
  130.8 1.9 %convert_reduce_fusion = f32[128,512]{1,0:T(8,128)S(1)} fusion(f16[16,128,512]{2,1,0:T(8,128)(2,1)} %all-to-all-done.2), kind=kLoop, calls=%fused_computation | loop fusion | flops 2031616 | bytes 2359296 | tf_op jit(solution)/shard_map/reduce_sum | solution.py:297
  132.7 0.7 broadcast_multiply_fusion
  (11 shorter events, 0.1 us)
Async XLA Ops:
  1.5 4.4 %collective-permute-start = (bf16[64,512]{1,0:T(8,128)(2,1)S(1)}, bf16[64,512]{1,0:T(8,128)(2,1)S(1)}, u32[]{:S(2)}, u32[]{:S(2)}) collective-permute-start(bf16[64,512]{1,0:T(8,128)(2,1)S(1)} %get-tuple-element.28), channel_id=1, source_target_pairs={{0,2},{2,0},{1,3},{3,1},{4,6},{6,4},{5,7},{7,5},{8,10},{10,8},{9,1... | collective-permute-start | bytes 196616 | tf_op jit(solution)/shard_map/ppermute | solution.py:209
  8.3 38.1 %all-to-all-start = ((bf16[16,128,512]{2,1,0:T(8,128)(2,1)}), bf16[16,128,512]{2,1,0:T(8,128)(2,1)S(1)}, u32[]{:S(2)}, u32[]{:S(2)}) async-start(bf16[16,128,512]{2,1,0:T(8,128)(2,1)} %broadcast_in_dim.6), calls=%async_computation | async-start | bytes 4194304 | tf_op jit(solution)/shard_map/all_to_all | solution.py:251
  15.8 10.7 %collective-permute-start.1 = (bf16[2,64,512]{2,1,0:T(8,128)(2,1)S(1)}, bf16[2,64,512]{2,1,0:T(8,128)(2,1)S(1)}, u32[]{:S(2)}, u32[]{:S(2)}) collective-permute-start(bf16[2,64,512]{2,1,0:T(8,128)(2,1)S(1)} %maximum_select_fusion.1), channel_id=1, source_target_pairs={{0,128},{32,160},{64,192},{96,224},{128,0},{160,32},{192,64},{224,... | collective-permute-start | bytes 393224 | tf_op jit(solution)/shard_map/ppermute | solution.py:229
  26.6 17.4 %collective-permute-start.4 = (bf16[2,128,512]{2,1,0:T(8,128)(2,1)S(1)}, bf16[2,128,512]{2,1,0:T(8,128)(2,1)S(1)}, u32[]{:S(2)}, u32[]{:S(2)}) collective-permute-start(bf16[2,128,512]{2,1,0:T(8,128)(2,1)S(1)} %pad_maximum_fusion.refs_0_), channel_id=1, source_target_pairs={{0,64},{32,96},{64,128},{96,160},{128,192},{160,224},{192,0},{224,... | collective-permute-start | bytes 786440 | tf_op jit(solution)/shard_map/ppermute | solution.py:229
  29.7 15.0 %collective-permute-start.3 = (bf16[2,128,512]{2,1,0:T(8,128)(2,1)S(1)}, bf16[2,128,512]{2,1,0:T(8,128)(2,1)S(1)}, u32[]{:S(2)}, u32[]{:S(2)}) collective-permute-start(bf16[2,128,512]{2,1,0:T(8,128)(2,1)S(1)} %pad_maximum_fusion.refs_0_), channel_id=1, source_target_pairs={{0,224},{32,0},{64,32},{96,64},{128,96},{160,128},{192,160},{224,1... | collective-permute-start | bytes 786440 | tf_op jit(solution)/shard_map/ppermute | solution.py:229
  31.6 14.1 %collective-permute-start.2 = (bf16[2,128,512]{2,1,0:T(8,128)(2,1)S(1)}, bf16[2,128,512]{2,1,0:T(8,128)(2,1)S(1)}, u32[]{:S(2)}, u32[]{:S(2)}) collective-permute-start(bf16[2,128,512]{2,1,0:T(8,128)(2,1)S(1)} %pad_maximum_fusion.refs_0_), channel_id=1, source_target_pairs={{0,32},{32,64},{64,96},{96,128},{128,160},{160,192},{192,224},{224... | collective-permute-start | bytes 786440 | tf_op jit(solution)/shard_map/ppermute | solution.py:229
  43.9 0.7 copy-start.3
  44.6 0.7 copy-start.5
  45.7 0.7 copy-start.7
  46.4 1.0 copy-start.4
  47.4 0.9 copy-start.6
  48.3 0.9 copy-start.8
  51.9 4.5 %copy-start.2 = (s32[128]{0:T(128)S(1)}, s32[128]{0:T(128)}, u32[]{:S(2)}) copy-start(s32[128]{0:T(128)} %param.5) | copy-start | bytes 1540
  51.9 4.5 %collective-permute-start.5 = (f32[1024,512]{1,0:T(8,128)}, f32[1024,512]{1,0:T(8,128)}, u32[]{:S(2)}, u32[]{:S(2)}) collective-permute-start(f32[1024,512]{1,0:T(8,128)} %get-tuple-element.14.own_ref), channel_id=1, source_target_pairs={{0,1},{1,0},{2,3},{3,2},{4,5},{5,4},{6,7},{7,6},{8,9},{9,8},{10,11... | collective-permute-start | bytes 6291464 | tf_op jit(solution)/shard_map/ppermute | solution.py:209
  52.3 3.8 %collective-permute-start.6 = (f32[2,512]{1,0:T(2,128)S(1)}, f32[2,512]{1,0:T(2,128)S(1)}, u32[]{:S(2)}, u32[]{:S(2)}) collective-permute-start(f32[2,512]{1,0:T(2,128)S(1)} %maximum_convert_fusion.most_ref), channel_id=1, source_target_pairs={{0,1},{1,0},{2,3},{3,2},{4,5},{5,4},{6,7},{7,6},{8,9},{9,8},{10,11... | collective-permute-start | bytes 12296 | tf_op jit(solution)/shard_map/ppermute | solution.py:209
  73.2 3.4 %collective-permute-start.7 = (f32[24,128]{1,0:T(8,128)S(1)}, f32[24,128]{1,0:T(8,128)S(1)}, u32[]{:S(2)}, u32[]{:S(2)}) collective-permute-start(f32[24,128]{1,0:T(8,128)S(1)} %shard_map.52.known_ref), channel_id=1, source_target_pairs={{0,1},{1,0},{2,3},{3,2},{4,5},{5,4},{6,7},{7,6},{8,9},{9,8},{10,11... | collective-permute-start | bytes 36872 | tf_op jit(solution)/shard_map/ppermute | solution.py:209
  78.0 3.9 %copy-start = (bf16[1024,512]{1,0:T(8,128)(2,1)}, bf16[1024,512]{1,0:T(8,128)(2,1)S(1)}, u32[]{:S(2)}) copy-start(bf16[1024,512]{1,0:T(8,128)(2,1)S(1)} %get-tuple-element.21) | copy-start | bytes 3145732
  81.8 7.1 %copy-start.1 = (bf16[1024,512]{1,0:T(8,128)(2,1)S(1)}, bf16[1024,512]{1,0:T(8,128)(2,1)}, u32[]{:S(2)}) copy-start(bf16[1024,512]{1,0:T(8,128)(2,1)} %copy-done) | copy-start | bytes 3145732
  81.8 48.9 %all-to-all-start.2 = ((f16[16,128,512]{2,1,0:T(8,128)(2,1)}), f16[16,128,512]{2,1,0:T(8,128)(2,1)}, u32[]{:S(2)}, u32[]{:S(2)}) async-start(f16[16,128,512]{2,1,0:T(8,128)(2,1)} %bitcast.23), calls=%async_computation.2 | async-start | bytes 4194304 | tf_op jit(solution)/shard_map/all_to_all | solution.py:276
  93.6 10.2 %collective-permute-start.8 = (f16[2,128,512]{2,1,0:T(8,128)(2,1)S(1)}, f16[2,128,512]{2,1,0:T(8,128)(2,1)S(1)}, u32[]{:S(2)}, u32[]{:S(2)}) collective-permute-start(f16[2,128,512]{2,1,0:T(8,128)(2,1)S(1)} %get-tuple-element.22), channel_id=1, source_target_pairs={{0,224},{32,0},{64,32},{96,64},{128,96},{160,128},{192,160},{224,1... | collective-permute-start | bytes 786440 | tf_op jit(solution)/shard_map/ppermute | solution.py:229
  95.3 18.6 %collective-permute-start.10 = (f16[2,128,512]{2,1,0:T(8,128)(2,1)S(1)}, f16[2,128,512]{2,1,0:T(8,128)(2,1)S(1)}, u32[]{:S(2)}, u32[]{:S(2)}) collective-permute-start(f16[2,128,512]{2,1,0:T(8,128)(2,1)S(1)} %get-tuple-element.23), channel_id=1, source_target_pairs={{0,192},{32,224},{64,0},{96,32},{128,64},{160,96},{192,128},{224,1... | collective-permute-start | bytes 786440 | tf_op jit(solution)/shard_map/ppermute | solution.py:229
  96.4 17.5 %collective-permute-start.9 = (f16[2,128,512]{2,1,0:T(8,128)(2,1)S(1)}, f16[2,128,512]{2,1,0:T(8,128)(2,1)S(1)}, u32[]{:S(2)}, u32[]{:S(2)}) collective-permute-start(f16[2,128,512]{2,1,0:T(8,128)(2,1)S(1)} %get-tuple-element.24), channel_id=1, source_target_pairs={{0,32},{32,64},{64,96},{96,128},{128,160},{160,192},{192,224},{224... | collective-permute-start | bytes 786440 | tf_op jit(solution)/shard_map/ppermute | solution.py:229
  114.1 10.8 %collective-permute-start.11 = (f16[2,64,512]{2,1,0:T(8,128)(2,1)S(1)}, f16[2,64,512]{2,1,0:T(8,128)(2,1)S(1)}, u32[]{:S(2)}, u32[]{:S(2)}) collective-permute-start(f16[2,64,512]{2,1,0:T(8,128)(2,1)S(1)} %fusion.2), channel_id=1, source_target_pairs={{0,128},{32,160},{64,192},{96,224},{128,0},{160,32},{192,64},{224,... | collective-permute-start | bytes 393224 | tf_op jit(solution)/shard_map/ppermute | solution.py:229
  125.0 5.1 %collective-permute-start.12 = (f32[64,512]{1,0:T(8,128)S(1)}, f32[64,512]{1,0:T(8,128)S(1)}, u32[]{:S(2)}, u32[]{:S(2)}) collective-permute-start(f32[64,512]{1,0:T(8,128)S(1)} %get-tuple-element.26), channel_id=1, source_target_pairs={{0,2},{2,0},{1,3},{3,1},{4,6},{6,4},{5,7},{7,5},{8,10},{10,8},{9,1... | collective-permute-start | bytes 393224 | tf_op jit(solution)/shard_map/ppermute | solution.py:209

commit v5 on v4

--- a/solution.py
+++ b/solution.py
@@ -29,10 +29,57 @@
     return pltpu.CompilerParams(vmem_limit_bytes=mib * 1024 * 1024)
 
 
-def score_kernel(v1_ref, *refs):
-    group_refs, s_ref, v2_ref = refs[:4], refs[4], refs[5]
-    for g in range(4):
-        v2_ref[:, g * GROUP : (g + 1) * GROUP, :] = group_refs[g][...]
+def copies_kernel(x_ref, o_ref, sems):
+    copies = [pltpu.make_async_copy(x_ref, o_ref.at[p], sems.at[p]) for p in range(16)]
+    for copy in copies:
+        copy.start()
+    for copy in copies:
+        copy.wait()
+
+
+def sixteen_copies(x):
+    return pl.pallas_call(
+        copies_kernel,
+        out_shape=jax.ShapeDtypeStruct((16, ROWS, WIDTH), x.dtype),
+        in_specs=[VMEM],
+        out_specs=pl.BlockSpec(memory_space=pl.ANY),
+        scratch_shapes=[pltpu.SemaphoreType.DMA((16,))],
+        compiler_params=limit(1),
+        cost_estimate=pl.CostEstimate(flops=0, bytes_accessed=3 * 2**20, transcendentals=0),
+    )(x)
+
+
+def join_kernel(own_ref, next_ref, last_ref, two0_ref, two1_ref, v2_ref, most_ref):
+    v2_ref[:, :GROUP, :] = own_ref[...]
+    v2_ref[:, GROUP : 2 * GROUP, :] = next_ref[...]
+    v2_ref[:, 2 * GROUP : 3 * GROUP, :] = last_ref[...]
+    v2_ref[0, 3 * GROUP : 3 * GROUP + HALF, :] = two0_ref[HALF:, :]
+    v2_ref[0, 3 * GROUP + HALF :, :] = two0_ref[:HALF, :]
+    v2_ref[1, 3 * GROUP :, :] = two1_ref[...]
+    size = jnp.abs(jnp.maximum(jnp.abs(v2_ref[0]), jnp.abs(v2_ref[1])).astype(jnp.float32))
+    most_ref[...] = jnp.max(size, axis=0, keepdims=True)
+
+
+def join(parts):
+    return pl.pallas_call(
+        join_kernel,
+        out_shape=(
+            jax.ShapeDtypeStruct((NXL, NJ, WIDTH), jnp.bfloat16),
+            jax.ShapeDtypeStruct((1, WIDTH), jnp.float32),
+        ),
+        in_specs=[VMEM] * 5,
+        out_specs=(VMEM, VMEM),
+        compiler_params=limit(4),
+        cost_estimate=pl.CostEstimate(flops=2**20, bytes_accessed=2**21, transcendentals=0),
+    )(*parts)
+
+
+def score_kernel(v1_ref, v2_hbm, s_ref, v2_ref, sems):
+    copies = [pltpu.make_async_copy(v2_hbm.at[x], v2_ref.at[x], sems.at[x]) for x in range(NXL)]
+    for copy in copies:
+        copy.start()
+    for copy in copies:
+        copy.wait()
     contract = (((1,), (1,)), ((), ()))
     for u in range(NI // 256):
         rows = slice(u * 256, (u + 1) * 256)
@@ -43,20 +90,21 @@
         )
 
 
-def partial_scores(v1_all, groups):
+def partial_scores(v1_all, v2_all):
     return pl.pallas_call(
         score_kernel,
-        out_shape=(
-            jax.ShapeDtypeStruct((NI, NJ), jnp.float32),
-            jax.ShapeDtypeStruct((NXL, NJ, WIDTH), jnp.bfloat16),
-        ),
-        in_specs=[VMEM] * 5,
-        out_specs=(VMEM, VMEM),
+        out_shape=jax.ShapeDtypeStruct((NI, NJ), jnp.float32),
+        in_specs=[VMEM, pl.BlockSpec(memory_space=pl.ANY)],
+        out_specs=VMEM,
+        scratch_shapes=[
+            pltpu.VMEM((NXL, NJ, WIDTH), jnp.bfloat16),
+            pltpu.SemaphoreType.DMA((NXL,)),
+        ],
         compiler_params=limit(8),
         cost_estimate=pl.CostEstimate(
             flops=2 * NI * NJ * NXL * WIDTH, bytes_accessed=6 * 2**20, transcendentals=0
         ),
-    )(v1_all, *groups)
+    )(v1_all, v2_all)
 
 
 def diagonal():
@@ -243,16 +291,24 @@
     keep = jnp.where(xl == 0, view_two[:HALF], view_two[HALF:])
     give = jnp.where(xl == 0, view_two[HALF:], view_two[:HALF])
     side = swap(give, "xl")
-    copies = jnp.broadcast_to(view_one[None], (16, ROWS, WIDTH))
+    copies = sixteen_copies(view_one)
     copies, side = lax.optimization_barrier((copies, side))
     here = jnp.where(xl == 0, jnp.stack([keep, side]), jnp.stack([side, keep]))
     pair = jnp.concatenate([here, to_plane(here, 4)], axis=1)
-    groups = [pair] + [to_plane(pair, -dz) for dz in OFFSETS[1:]]
+    v2_all, most_v2 = join(
+        [
+            pair,
+            to_plane(pair, 1),
+            to_plane(pair, -1),
+            to_plane(pair[0], -2),
+            to_plane(pair[1], 2),
+        ]
+    )
     v1_all = lax.all_to_all(copies, PLANE, 0, 0, tiled=True).reshape(NXL, NI, WIDTH)
 
-    own, v2_all = partial_scores(v1_all, groups)
+    own = partial_scores(v1_all, v2_all)
     other = swap(own, "core")
-    most = jnp.stack([largest(v2_all), largest(v1_all)])
+    most = jnp.concatenate([most_v2, largest(v1_all)[None]])
     most_other = swap(most, "core")
 
     scores, pack = local_stats(place, own, other, partner, most, most_other)
@@ -263,6 +319,23 @@
     coupling, sizes = coupling_of(place, scores, known, swap(known, "core"))
     most_two, most_one = sizes[0, 0], sizes[1, 0]
 
+    part_two = [
+        (
+            lax.dot_general(
+                coupling, v1_all[x], (((0,), (0,)), ((), ())), preferred_element_type=jnp.float32
+            )
+            * (64.0 / most_one)
+        ).astype(jnp.float16)
+        for x in range(NXL)
+    ]
+    coupling, part_two = lax.optimization_barrier((coupling, part_two))
+
+    def group(g):
+        return jnp.stack([part[g * GROUP : (g + 1) * GROUP] for part in part_two])
+
+    before, after = to_plane(group(1), -1), to_plane(group(2), 1)
+    two0 = to_plane(part_two[0][3 * GROUP :], 2)
+    two1 = to_plane(part_two[1][3 * GROUP :], -2)
     part_one = (
         lax.dot_general(
             jnp.broadcast_to(coupling[None], (NXL, NI, NJ)),
@@ -272,21 +345,9 @@
         )
         * (128.0 / most_two)
     ).astype(jnp.float16)
-    coupling, part_one = lax.optimization_barrier((coupling, part_one))
     one_parts = lax.all_to_all(part_one.reshape(16, ROWS, WIDTH), PLANE, 0, 0, tiled=True)
-    part_two = (
-        lax.dot_general(
-            jnp.broadcast_to(coupling[None], (NXL, NI, NJ)),
-            v1_all,
-            (((1,), (1,)), ((0,), (0,))),
-            preferred_element_type=jnp.float32,
-        )
-        * (64.0 / most_one)
-    ).astype(jnp.float16)
-    parts = [part_two[:, :GROUP]] + [
-        to_plane(part_two[:, g * GROUP : (g + 1) * GROUP], OFFSETS[g]) for g in range(1, 4)
-    ]
-    joined = sum(part.astype(jnp.float32) for part in parts)
+    two = jnp.stack([jnp.concatenate([two0[HALF:], two0[:HALF]]), two1])
+    joined = sum(part.astype(jnp.float32) for part in (group(0), before, after, two))
     far = to_plane((joined[:, HALF:] * 0.25).astype(jnp.float16), 4)
     total = (joined[:, :HALF] + 4.0 * far.astype(jnp.float32)) * (most_one / 64.0)
     stay = jnp.where(xl == 0, total[0], total[1])
@@ -294,7 +355,7 @@
     grad_two = jnp.where(
         xl == 0, jnp.concatenate([stay, come]), jnp.concatenate([come, stay])
     )
-    grad_one = jnp.sum(one_parts.astype(jnp.float32), axis=0) * (most_two / 128.0)
+    grad_one = jnp.sum(one_parts.astype(jnp.float32) * (most_two / 128.0), axis=0)
     return (grad_one, grad_two)
 
 

time: 134 us -> 125 us (0.933)
  waiting for transfers between devices: 50.8 us -> 41.3 us
  local copies, waits for them, and re-layouts: 9.5 us -> 3.11 us
  starting transfers between devices: 38.8 us -> 44.1 us
  Pallas kernels: 7.98 us -> 11.1 us
  other arithmetic: 4.97 us -> 3.51 us
    ppermute x8 -> x10, waiting for transfers between devices: 40.4 us -> 32 us  [to_plane(): return lax.ppermute(x, 'z', [(z, (z + dz) % NZ) for z in range(NZ)])]
    ppermute x8 -> x10, starting transfers between devices: 18.6 us -> 24.7 us  [to_plane(): return lax.ppermute(x, 'z', [(z, (z + dz) % NZ) for z in range(NZ)])]
    pallas_call x1 -> x3, Pallas kernels: 2.63 us -> 5.69 us  [the longest x1 2.84 us: sixteen_copies(): pl.pallas_call(copies_kernel, out_shape=jax.ShapeDtypeStruct((16, ROWS, W...]
    unnamed x18 -> x6, local copies, waits for them, and re-layouts: 4.97 us -> 2.23 us
    broadcast_in_dim x1 -> x0, local copies, waits for them, and re-layouts: 2.45 us -> none  [on_device(): copies = jnp.broadcast_to(view_one[None], (16, ROWS, WIDTH))]
    all_to_all x1, starting transfers between devices: 7.06 us -> 5.38 us  [on_device(): lax.all_to_all(part_one.reshape(16, ROWS, WIDTH), PLANE, 0, 0, tiled=True)]
  transfers between devices with their start and end apart: 15 -> 17, of which waited for: 11 -> 9; matrix products, arithmetic and copies ran while one was open for 4% -> 2% of each run, Pallas kernels for 0% -> 2%
where the time goes in v5:
time: 125 us; the launch traced here: 124 us
  starting transfers between devices  44.1 us (35%)
  waiting for transfers between devices  41.3 us (33%)
  blocking collectives  12.7 us (10%)
  Pallas kernels  11.1 us (9%)
  matrix products  4.07 us (3%)
  between operations  3.53 us (3%)
  other arithmetic  3.51 us (3%)
  local copies, waits for them, and re-layouts  3.11 us (2%)
    ppermute x10, waiting for transfers between devices, to_plane(): return lax.ppermute(x, 'z', [(z, (z + dz) % NZ) for z in range(NZ)])  32 us
    ppermute x10, starting transfers between devices, to_plane(): return lax.ppermute(x, 'z', [(z, (z + dz) % NZ) for z in range(NZ)])  24.7 us
    all_to_all x1, blocking collectives, on_device(): lax.all_to_all(pack, EVERY, 0, 0, axis_index_groups=stat_groups(), tiled=...  12.7 us
    ppermute x5, waiting for transfers between devices, swap(): return lax.ppermute(x, axis, [(0, 1), (1, 0)])  9.32 us
    all_to_all x1, starting transfers between devices, on_device(): lax.all_to_all(copies, PLANE, 0, 0, tiled=True).reshape(NXL, NI, WIDTH)  7.45 us
    ppermute x5, starting transfers between devices, swap(): return lax.ppermute(x, axis, [(0, 1), (1, 0)])  6.53 us
    all_to_all x1, starting transfers between devices, on_device(): lax.all_to_all(part_one.reshape(16, ROWS, WIDTH), PLANE, 0, 0, tiled=True)  5.38 us
    pallas_call x1, Pallas kernels, local_stats(): pl.pallas_call(stats_kernel, out_shape=(jax.ShapeDtypeStruct((NI, NJ), jn...  3.39 us
  transfers between devices with their start and end apart: 17, of which 9 were waited for; matrix products, arithmetic and copies ran while one was open for 2% of the time, Pallas kernels for 2%

profile of v5, /device:TPU:4, one launch (start us, length us, event | category | flops | bytes accessed | tf_op | source)
XLA Modules:
  0.0 123.5 jit_solution(10336940424674008941)
XLA Ops:
  0.6 0.9 select_bitcast_fusion.2
  1.5 1.3 %collective-permute-start = (bf16[64,512]{1,0:T(8,128)(2,1)S(1)}, bf16[64,512]{1,0:T(8,128)(2,1)S(1)}, u32[]{:S(2)}, u32[]{:S(2)}) collective-permute-start(bf16[64,512]{1,0:T(8,128)(2,1)S(1)} %get-tuple-element.41), channel_id=1, source_target_pairs={{0,2},{2,0},{1,3},{3,1},{4,6},{6,4},{5,7},{7,5},{8,10},{10,8},{9,1... | collective-permute-start | bytes 196616 | tf_op jit(solution)/shard_map/ppermute | solution.py:257
  2.8 0.0 copy-start.1
  2.8 0.9 copy-done.1
  3.7 2.8 %shard_map.50 = bf16[16,128,512]{2,1,0:T(8,128)(2,1)S(1)} custom-call(bf16[128,512]{1,0:T(8,128)(2,1)S(1)} %copy-done.1), custom_call_target="tpu_custom_call" | custom-call | bytes 3145728 | tf_op jit(solution)/shard_map/pallas_call | solution.py:41
  6.6 0.0 copy-start
  6.6 1.3 %copy-done = bf16[16,128,512]{2,1,0:T(8,128)(2,1)} copy-done((bf16[16,128,512]{2,1,0:T(8,128)(2,1)}, bf16[16,128,512]{2,1,0:T(8,128)(2,1)S(1)}, u32[]{:S(2)}) %copy-start) | copy-done | bytes 2097176
  7.9 0.0 collective-permute-done
  7.9 7.4 %all-to-all-start = ((bf16[16,128,512]{2,1,0:T(8,128)(2,1)}), bf16[16,128,512]{2,1,0:T(8,128)(2,1)S(1)}, u32[]{:S(2)}, u32[]{:S(2)}) async-start(bf16[16,128,512]{2,1,0:T(8,128)(2,1)} %copy-done), calls=%async_computation | async-start | bytes 4194304 | tf_op jit(solution)/shard_map/all_to_all | solution.py:307
  15.4 7.3 %collective-permute-start.1 = (bf16[2,64,512]{2,1,0:T(8,128)(2,1)S(1)}, bf16[2,64,512]{2,1,0:T(8,128)(2,1)S(1)}, u32[]{:S(2)}, u32[]{:S(2)}) collective-permute-start(bf16[2,64,512]{2,1,0:T(8,128)(2,1)S(1)} %maximum_select_fusion.1), channel_id=1, source_target_pairs={{0,128},{32,160},{64,192},{96,224},{128,0},{160,32},{192,64},{224,... | collective-permute-start | bytes 393224 | tf_op jit(solution)/shard_map/ppermute | solution.py:277
  22.6 4.4 %collective-permute-done.1 = bf16[2,64,512]{2,1,0:T(8,128)(2,1)S(1)} collective-permute-done((bf16[2,64,512]{2,1,0:T(8,128)(2,1)S(1)}, bf16[2,64,512]{2,1,0:T(8,128)(2,1)S(1)}, u32[]{:S(2)}, u32[]{:S(2)}) %collective-permute-start.1) | collective-permute-done | bytes 131104 | tf_op jit(solution)/shard_map/ppermute | solution.py:277
  27.1 4.0 %collective-permute-start.3 = (bf16[2,128,512]{2,1,0:T(8,128)(2,1)S(1)}, bf16[2,128,512]{2,1,0:T(8,128)(2,1)S(1)}, u32[]{:S(2)}, u32[]{:S(2)}) collective-permute-start(bf16[2,128,512]{2,1,0:T(8,128)(2,1)S(1)} %pad_maximum_fusion.own_ref), channel_id=1, source_target_pairs={{0,224},{32,0},{64,32},{96,64},{128,96},{160,128},{192,160},{224,1... | collective-permute-start | bytes 786440 | tf_op jit(solution)/shard_map/ppermute | solution.py:277
  31.1 0.0 collective-permute-start.2
  31.1 1.1 collective-permute-start.5
  32.2 3.6 %collective-permute-start.4 = (bf16[128,512]{1,0:T(8,128)(2,1)S(1)}, bf16[128,512]{1,0:T(8,128)(2,1)S(1)}, u32[]{:S(2)}, u32[]{:S(2)}) collective-permute-start(bf16[128,512]{1,0:T(8,128)(2,1)S(1)} %get-tuple-element.37), channel_id=1, source_target_pairs={{0,192},{32,224},{64,0},{96,32},{128,64},{160,96},{192,128},{224,1... | collective-permute-start | bytes 393224 | tf_op jit(solution)/shard_map/ppermute | solution.py:277
  35.8 9.4 %collective-permute-done.5.two1_ref = bf16[128,512]{1,0:T(8,128)(2,1)S(1)} collective-permute-done((bf16[128,512]{1,0:T(8,128)(2,1)S(1)}, bf16[128,512]{1,0:T(8,128)(2,1)S(1)}, u32[]{:S(2)}, u32[]{:S(2)}) %collective-permute-start.5) | collective-permute-done | bytes 131104 | tf_op jit(solution)/shard_map/ppermute | solution.py:277
  45.1 0.0 collective-permute-done.4.two0_ref
  45.1 0.0 collective-permute-done.3.last_ref
  45.1 0.0 collective-permute-done.2.next_ref
  45.1 0.2 shard_map.51
  45.3 0.0 all-to-all-done
  45.3 2.7 %shard_map.52.own_ref = f32[1024,512]{1,0:T(8,128)} custom-call(bf16[2,1024,512]{2,1,0:T(8,128)(2,1)S(1)} %bitcast.45, bf16[2,512,512]{2,1,0:T(8,128)(2,1)S(1)} %get-tuple-element.15.v2_hbm), custom_call_target="tpu_custom_call" | custom-call | flops 1073741824 | bytes 6291456 | tf_op jit(solution)/shard_map/pallas_call | solution.py:94
  48.0 0.0 copy-start.2
  48.0 0.1 collective-permute-start.6
  48.1 0.2 abs_reduce_fusion
  48.4 0.6 collective-permute-start.7
  49.0 0.1 pad_add_fusion.place_ref
  49.0 3.2 %collective-permute-done.7.most_other_ref = f32[2,512]{1,0:T(2,128)S(1)} collective-permute-done((f32[2,512]{1,0:T(2,128)S(1)}, f32[2,512]{1,0:T(2,128)S(1)}, u32[]{:S(2)}, u32[]{:S(2)}) %collective-permute-start.7) | collective-permute-done | bytes 4128 | tf_op jit(solution)/shard_map/ppermute | solution.py:257
  52.3 0.3 collective-permute-done.6.other_ref
  52.6 0.0 copy-done.2
  52.6 3.4 %shard_map.53 = (f32[1024,512]{1,0:T(8,128)S(1)}, f32[16,16,128]{2,1,0:T(8,128)S(1)}) custom-call(s32[4]{0:T(128)S(1)} %pad_add_fusion.place_ref, f32[1024,512]{1,0:T(8,128)} %shard_map.52.own_ref, f32[1024,512]{1,0:T(8,128)} %collective-permute-done.6.other_ref, s32[1,128]{1,0:T(1,128)S(1)} %bitcast.46, f32[2,512]{1,0:T(2,128)S(1)} %pad_maximum_fusion.3.most_ref, ...), custom_call_target="tpu_custom_call" | custom-call | flops 5242880 | bytes 6291456 | tf_op jit(solution)/shard_map/pallas_call | solution.py:159
  56.0 12.7 %all_to_all.15.seen_ref = f32[16,16,128]{2,1,0:T(8,128)S(1)} all-to-all(f32[16,16,128]{2,1,0:T(8,128)S(1)} %get-tuple-element.18), channel_id=1, replica_groups={{0,4,8,12,16,20,24,28,2,6,10,14,18,22,26,30},{32,36,40,44,48,52,56,60,3..., dimensions={0} | all-to-all | bytes 262144 | tf_op jit(solution)/shard_map/all_to_all | solution.py:315
  68.8 0.6 shard_map.54.known_ref
  69.3 3.3 %collective-permute-start.8 = (f32[24,128]{1,0:T(8,128)S(1)}, f32[24,128]{1,0:T(8,128)S(1)}, u32[]{:S(2)}, u32[]{:S(2)}) collective-permute-start(f32[24,128]{1,0:T(8,128)S(1)} %shard_map.54.known_ref), channel_id=1, source_target_pairs={{0,1},{1,0},{2,3},{3,2},{4,5},{5,4},{6,7},{7,6},{8,9},{9,8},{10,11... | collective-permute-start | bytes 36872 | tf_op jit(solution)/shard_map/ppermute | solution.py:257
  72.6 0.1 fusion.9
  72.8 0.7 collective-permute-done.8.told_ref
  73.5 1.4 %shard_map.55 = (bf16[1024,512]{1,0:T(8,128)(2,1)S(1)}, f32[2,128]{1,0:T(2,128)S(1)}) custom-call(s32[4]{0:T(128)S(1)} %pad_add_fusion.place_ref, f32[1024,512]{1,0:T(8,128)S(1)} %get-tuple-element.17.s_ref, f32[24,128]{1,0:T(8,128)S(1)} %shard_map.54.known_ref, f32[24,128]{1,0:T(8,128)S(1)} %collective-permute-done.8.told_ref), custom_call_target="tpu_custom_call" | custom-call | flops 4194304 | bytes 3145728 | tf_op jit(solution)/shard_map/pallas_call | solution.py:241
  74.9 0.5 fusion.13
  76.1 0.7 fusion.1
  76.8 0.7 fusion
  78.3 2.6 %multiply_convert_fusion = f16[2,1024,512]{2,1,0:T(8,128)(2,1)} fusion(bf16[2,512,512]{2,1,0:T(8,128)(2,1)S(1)} %get-tuple-element.15.v2_hbm, f32[]{:T(128)} %bitcast.14, bf16[1024,512]{1,0:T(8,128)(2,1)S(1)} %get-tuple-element.21), kind=kOutput, calls=%fused_computation.1 | convolution fusion | flops 1075838976 | bytes 4194308 | tf_op jit(solution)/shard_map/dot_general | solution.py:340
  80.9 5.4 %all-to-all-start.2 = ((f16[16,128,512]{2,1,0:T(8,128)(2,1)}), f16[16,128,512]{2,1,0:T(8,128)(2,1)S(1)}, u32[]{:S(2)}, u32[]{:S(2)}) async-start(f16[16,128,512]{2,1,0:T(8,128)(2,1)} %bitcast.47), calls=%async_computation.2 | async-start | bytes 4194304 | tf_op jit(solution)/shard_map/all_to_all | solution.py:348
  86.2 0.1 fusion.10
  86.3 1.6 %collective-permute-start.11 = (f16[128,512]{1,0:T(8,128)(2,1)S(1)}, f16[128,512]{1,0:T(8,128)(2,1)S(1)}, u32[]{:S(2)}, u32[]{:S(2)}) collective-permute-start(f16[128,512]{1,0:T(8,128)(2,1)S(1)} %get-tuple-element.26), channel_id=1, source_target_pairs={{0,64},{32,96},{64,128},{96,160},{128,192},{160,224},{192,0},{224,... | collective-permute-start | bytes 393224 | tf_op jit(solution)/shard_map/ppermute | solution.py:277
  87.9 0.1 fusion.11
  88.0 2.7 %collective-permute-start.12 = (f16[128,512]{1,0:T(8,128)(2,1)S(1)}, f16[128,512]{1,0:T(8,128)(2,1)S(1)}, u32[]{:S(2)}, u32[]{:S(2)}) collective-permute-start(f16[128,512]{1,0:T(8,128)(2,1)S(1)} %get-tuple-element.30), channel_id=1, source_target_pairs={{0,192},{32,224},{64,0},{96,32},{128,64},{160,96},{192,128},{224,1... | collective-permute-start | bytes 393224 | tf_op jit(solution)/shard_map/ppermute | solution.py:277
  90.7 0.1 pad_maximum_fusion.1
  90.8 0.4 collective-permute-start.9
  91.2 0.1 pad_maximum_fusion.2
  91.3 1.8 %collective-permute-start.10 = (f16[2,128,512]{2,1,0:T(8,128)(2,1)S(1)}, f16[2,128,512]{2,1,0:T(8,128)(2,1)S(1)}, u32[]{:S(2)}, u32[]{:S(2)}) collective-permute-start(f16[2,128,512]{2,1,0:T(8,128)(2,1)S(1)} %pad_maximum_fusion.2), channel_id=1, source_target_pairs={{0,32},{32,64},{64,96},{96,128},{128,160},{160,192},{192,224},{224... | collective-permute-start | bytes 786440 | tf_op jit(solution)/shard_map/ppermute | solution.py:277
  93.1 4.2 %collective-permute-done.11 = f16[128,512]{1,0:T(8,128)(2,1)S(1)} collective-permute-done((f16[128,512]{1,0:T(8,128)(2,1)S(1)}, f16[128,512]{1,0:T(8,128)(2,1)S(1)}, u32[]{:S(2)}, u32[]{:S(2)}) %collective-permute-start.11) | collective-permute-done | bytes 131104 | tf_op jit(solution)/shard_map/ppermute | solution.py:277
  97.3 0.0 collective-permute-done.12
  97.3 6.0 %collective-permute-done.9 = f16[2,128,512]{2,1,0:T(8,128)(2,1)S(1)} collective-permute-done((f16[2,128,512]{2,1,0:T(8,128)(2,1)S(1)}, f16[2,128,512]{2,1,0:T(8,128)(2,1)S(1)}, u32[]{:S(2)}, u32[]{:S(2)}) %collective-permute-start.9) | collective-permute-done | bytes 262176 | tf_op jit(solution)/shard_map/ppermute | solution.py:277
  103.3 0.0 collective-permute-done.10
  103.3 0.2 convert_add_fusion
  103.5 2.3 %collective-permute-start.13 = (f16[2,64,512]{2,1,0:T(8,128)(2,1)S(1)}, f16[2,64,512]{2,1,0:T(8,128)(2,1)S(1)}, u32[]{:S(2)}, u32[]{:S(2)}) collective-permute-start(f16[2,64,512]{2,1,0:T(8,128)(2,1)S(1)} %fusion.3), channel_id=1, source_target_pairs={{0,128},{32,160},{64,192},{96,224},{128,0},{160,32},{192,64},{224,... | collective-permute-start | bytes 393224 | tf_op jit(solution)/shard_map/ppermute | solution.py:277
  106.5 8.1 %collective-permute-done.13 = f16[2,64,512]{2,1,0:T(8,128)(2,1)S(1)} collective-permute-done((f16[2,64,512]{2,1,0:T(8,128)(2,1)S(1)}, f16[2,64,512]{2,1,0:T(8,128)(2,1)S(1)}, u32[]{:S(2)}, u32[]{:S(2)}) %collective-permute-start.13) | collective-permute-done | bytes 131104 | tf_op jit(solution)/shard_map/ppermute | solution.py:277
  114.6 1.3 %collective-permute-start.14 = (f32[64,512]{1,0:T(8,128)S(1)}, f32[64,512]{1,0:T(8,128)S(1)}, u32[]{:S(2)}, u32[]{:S(2)}) collective-permute-start(f32[64,512]{1,0:T(8,128)S(1)} %get-tuple-element.35), channel_id=1, source_target_pairs={{0,2},{2,0},{1,3},{3,1},{4,6},{6,4},{5,7},{7,5},{8,10},{10,8},{9,1... | collective-permute-start | bytes 393224 | tf_op jit(solution)/shard_map/ppermute | solution.py:257
  116.6 5.0 %collective-permute-done.14 = f32[64,512]{1,0:T(8,128)S(1)} collective-permute-done((f32[64,512]{1,0:T(8,128)S(1)}, f32[64,512]{1,0:T(8,128)S(1)}, u32[]{:S(2)}, u32[]{:S(2)}) %collective-permute-start.14) | collective-permute-done | bytes 131104 | tf_op jit(solution)/shard_map/ppermute | solution.py:257
  121.6 0.7 maximum_select_fusion
  122.4 0.0 all-to-all-done.2
  122.4 1.1 multiply_reduce_fusion
  (10 shorter events, 0.2 us)
Async XLA Ops:
  1.5 6.4 %collective-permute-start = (bf16[64,512]{1,0:T(8,128)(2,1)S(1)}, bf16[64,512]{1,0:T(8,128)(2,1)S(1)}, u32[]{:S(2)}, u32[]{:S(2)}) collective-permute-start(bf16[64,512]{1,0:T(8,128)(2,1)S(1)} %get-tuple-element.41), channel_id=1, source_target_pairs={{0,2},{2,0},{1,3},{3,1},{4,6},{6,4},{5,7},{7,5},{8,10},{10,8},{9,1... | collective-permute-start | bytes 196616 | tf_op jit(solution)/shard_map/ppermute | solution.py:257
  2.8 0.9 copy-start.1
  6.6 1.3 %copy-start = (bf16[16,128,512]{2,1,0:T(8,128)(2,1)}, bf16[16,128,512]{2,1,0:T(8,128)(2,1)S(1)}, u32[]{:S(2)}) copy-start(bf16[16,128,512]{2,1,0:T(8,128)(2,1)S(1)} %shard_map.50) | copy-start | bytes 6291460
  7.9 37.4 %all-to-all-start = ((bf16[16,128,512]{2,1,0:T(8,128)(2,1)}), bf16[16,128,512]{2,1,0:T(8,128)(2,1)S(1)}, u32[]{:S(2)}, u32[]{:S(2)}) async-start(bf16[16,128,512]{2,1,0:T(8,128)(2,1)} %copy-done), calls=%async_computation | async-start | bytes 4194304 | tf_op jit(solution)/shard_map/all_to_all | solution.py:307
  15.4 11.7 %collective-permute-start.1 = (bf16[2,64,512]{2,1,0:T(8,128)(2,1)S(1)}, bf16[2,64,512]{2,1,0:T(8,128)(2,1)S(1)}, u32[]{:S(2)}, u32[]{:S(2)}) collective-permute-start(bf16[2,64,512]{2,1,0:T(8,128)(2,1)S(1)} %maximum_select_fusion.1), channel_id=1, source_target_pairs={{0,128},{32,160},{64,192},{96,224},{128,0},{160,32},{192,64},{224,... | collective-permute-start | bytes 393224 | tf_op jit(solution)/shard_map/ppermute | solution.py:277
  27.1 18.1 %collective-permute-start.3 = (bf16[2,128,512]{2,1,0:T(8,128)(2,1)S(1)}, bf16[2,128,512]{2,1,0:T(8,128)(2,1)S(1)}, u32[]{:S(2)}, u32[]{:S(2)}) collective-permute-start(bf16[2,128,512]{2,1,0:T(8,128)(2,1)S(1)} %pad_maximum_fusion.own_ref), channel_id=1, source_target_pairs={{0,224},{32,0},{64,32},{96,64},{128,96},{160,128},{192,160},{224,1... | collective-permute-start | bytes 786440 | tf_op jit(solution)/shard_map/ppermute | solution.py:277
  31.1 14.1 %collective-permute-start.2 = (bf16[2,128,512]{2,1,0:T(8,128)(2,1)S(1)}, bf16[2,128,512]{2,1,0:T(8,128)(2,1)S(1)}, u32[]{:S(2)}, u32[]{:S(2)}) collective-permute-start(bf16[2,128,512]{2,1,0:T(8,128)(2,1)S(1)} %pad_maximum_fusion.own_ref), channel_id=1, source_target_pairs={{0,32},{32,64},{64,96},{96,128},{128,160},{160,192},{192,224},{224... | collective-permute-start | bytes 786440 | tf_op jit(solution)/shard_map/ppermute | solution.py:277
  31.1 14.0 %collective-permute-start.5 = (bf16[128,512]{1,0:T(8,128)(2,1)S(1)}, bf16[128,512]{1,0:T(8,128)(2,1)S(1)}, u32[]{:S(2)}, u32[]{:S(2)}) collective-permute-start(bf16[128,512]{1,0:T(8,128)(2,1)S(1)} %get-tuple-element.36), channel_id=1, source_target_pairs={{0,64},{32,96},{64,128},{96,160},{128,192},{160,224},{192,0},{224,... | collective-permute-start | bytes 393224 | tf_op jit(solution)/shard_map/ppermute | solution.py:277
  32.2 13.0 %collective-permute-start.4 = (bf16[128,512]{1,0:T(8,128)(2,1)S(1)}, bf16[128,512]{1,0:T(8,128)(2,1)S(1)}, u32[]{:S(2)}, u32[]{:S(2)}) collective-permute-start(bf16[128,512]{1,0:T(8,128)(2,1)S(1)} %get-tuple-element.37), channel_id=1, source_target_pairs={{0,192},{32,224},{64,0},{96,32},{128,64},{160,96},{192,128},{224,1... | collective-permute-start | bytes 393224 | tf_op jit(solution)/shard_map/ppermute | solution.py:277
  48.0 4.6 %copy-start.2 = (s32[128]{0:T(128)S(1)}, s32[128]{0:T(128)}, u32[]{:S(2)}) copy-start(s32[128]{0:T(128)} %param.5) | copy-start | bytes 1540
  48.0 4.6 %collective-permute-start.6 = (f32[1024,512]{1,0:T(8,128)}, f32[1024,512]{1,0:T(8,128)}, u32[]{:S(2)}, u32[]{:S(2)}) collective-permute-start(f32[1024,512]{1,0:T(8,128)} %shard_map.52.own_ref), channel_id=1, source_target_pairs={{0,1},{1,0},{2,3},{3,2},{4,5},{5,4},{6,7},{7,6},{8,9},{9,8},{10,11... | collective-permute-start | bytes 6291464 | tf_op jit(solution)/shard_map/ppermute | solution.py:257
  48.4 3.9 %collective-permute-start.7 = (f32[2,512]{1,0:T(2,128)S(1)}, f32[2,512]{1,0:T(2,128)S(1)}, u32[]{:S(2)}, u32[]{:S(2)}) collective-permute-start(f32[2,512]{1,0:T(2,128)S(1)} %pad_maximum_fusion.3.most_ref), channel_id=1, source_target_pairs={{0,1},{1,0},{2,3},{3,2},{4,5},{5,4},{6,7},{7,6},{8,9},{9,8},{10,11... | collective-permute-start | bytes 12296 | tf_op jit(solution)/shard_map/ppermute | solution.py:257
  69.3 4.1 %collective-permute-start.8 = (f32[24,128]{1,0:T(8,128)S(1)}, f32[24,128]{1,0:T(8,128)S(1)}, u32[]{:S(2)}, u32[]{:S(2)}) collective-permute-start(f32[24,128]{1,0:T(8,128)S(1)} %shard_map.54.known_ref), channel_id=1, source_target_pairs={{0,1},{1,0},{2,3},{3,2},{4,5},{5,4},{6,7},{7,6},{8,9},{9,8},{10,11... | collective-permute-start | bytes 36872 | tf_op jit(solution)/shard_map/ppermute | solution.py:257
  80.9 41.5 %all-to-all-start.2 = ((f16[16,128,512]{2,1,0:T(8,128)(2,1)}), f16[16,128,512]{2,1,0:T(8,128)(2,1)S(1)}, u32[]{:S(2)}, u32[]{:S(2)}) async-start(f16[16,128,512]{2,1,0:T(8,128)(2,1)} %bitcast.47), calls=%async_computation.2 | async-start | bytes 4194304 | tf_op jit(solution)/shard_map/all_to_all | solution.py:348
  86.3 10.9 %collective-permute-start.11 = (f16[128,512]{1,0:T(8,128)(2,1)S(1)}, f16[128,512]{1,0:T(8,128)(2,1)S(1)}, u32[]{:S(2)}, u32[]{:S(2)}) collective-permute-start(f16[128,512]{1,0:T(8,128)(2,1)S(1)} %get-tuple-element.26), channel_id=1, source_target_pairs={{0,64},{32,96},{64,128},{96,160},{128,192},{160,224},{192,0},{224,... | collective-permute-start | bytes 393224 | tf_op jit(solution)/shard_map/ppermute | solution.py:277
  88.0 9.3 %collective-permute-start.12 = (f16[128,512]{1,0:T(8,128)(2,1)S(1)}, f16[128,512]{1,0:T(8,128)(2,1)S(1)}, u32[]{:S(2)}, u32[]{:S(2)}) collective-permute-start(f16[128,512]{1,0:T(8,128)(2,1)S(1)} %get-tuple-element.30), channel_id=1, source_target_pairs={{0,192},{32,224},{64,0},{96,32},{128,64},{160,96},{192,128},{224,1... | collective-permute-start | bytes 393224 | tf_op jit(solution)/shard_map/ppermute | solution.py:277
  90.8 12.5 %collective-permute-start.9 = (f16[2,128,512]{2,1,0:T(8,128)(2,1)S(1)}, f16[2,128,512]{2,1,0:T(8,128)(2,1)S(1)}, u32[]{:S(2)}, u32[]{:S(2)}) collective-permute-start(f16[2,128,512]{2,1,0:T(8,128)(2,1)S(1)} %pad_maximum_fusion.1), channel_id=1, source_target_pairs={{0,224},{32,0},{64,32},{96,64},{128,96},{160,128},{192,160},{224,1... | collective-permute-start | bytes 786440 | tf_op jit(solution)/shard_map/ppermute | solution.py:277
  91.3 12.0 %collective-permute-start.10 = (f16[2,128,512]{2,1,0:T(8,128)(2,1)S(1)}, f16[2,128,512]{2,1,0:T(8,128)(2,1)S(1)}, u32[]{:S(2)}, u32[]{:S(2)}) collective-permute-start(f16[2,128,512]{2,1,0:T(8,128)(2,1)S(1)} %pad_maximum_fusion.2), channel_id=1, source_target_pairs={{0,32},{32,64},{64,96},{96,128},{128,160},{160,192},{192,224},{224... | collective-permute-start | bytes 786440 | tf_op jit(solution)/shard_map/ppermute | solution.py:277
  103.5 11.1 %collective-permute-start.13 = (f16[2,64,512]{2,1,0:T(8,128)(2,1)S(1)}, f16[2,64,512]{2,1,0:T(8,128)(2,1)S(1)}, u32[]{:S(2)}, u32[]{:S(2)}) collective-permute-start(f16[2,64,512]{2,1,0:T(8,128)(2,1)S(1)} %fusion.3), channel_id=1, source_target_pairs={{0,128},{32,160},{64,192},{96,224},{128,0},{160,32},{192,64},{224,... | collective-permute-start | bytes 393224 | tf_op jit(solution)/shard_map/ppermute | solution.py:277
  114.6 7.0 %collective-permute-start.14 = (f32[64,512]{1,0:T(8,128)S(1)}, f32[64,512]{1,0:T(8,128)S(1)}, u32[]{:S(2)}, u32[]{:S(2)}) collective-permute-start(f32[64,512]{1,0:T(8,128)S(1)} %get-tuple-element.35), channel_id=1, source_target_pairs={{0,2},{2,0},{1,3},{3,1},{4,6},{6,4},{5,7},{7,5},{8,10},{10,8},{9,1... | collective-permute-start | bytes 393224 | tf_op jit(solution)/shard_map/ppermute | solution.py:257

commit v6 on v5

--- a/solution.py
+++ b/solution.py
@@ -1,3 +1,4 @@
+import functools
 import math
 
 import jax
@@ -19,6 +20,7 @@
 WIDTH = 512
 NI = NY * NXH * ROWS
 NJ = NZ * HALF
+NP = NI // 2
 LANES = 128
 SCALE = 2.0 / math.sqrt(D)
 VMEM = pl.BlockSpec(memory_space=pltpu.VMEM)
@@ -41,8 +43,8 @@
     return pl.pallas_call(
         copies_kernel,
         out_shape=jax.ShapeDtypeStruct((16, ROWS, WIDTH), x.dtype),
-        in_specs=[VMEM],
-        out_specs=pl.BlockSpec(memory_space=pl.ANY),
+        in_specs=[pl.BlockSpec(memory_space=pltpu.HBM)],
+        out_specs=pl.BlockSpec(memory_space=pltpu.HBM),
         scratch_shapes=[pltpu.SemaphoreType.DMA((16,))],
         compiler_params=limit(1),
         cost_estimate=pl.CostEstimate(flops=0, bytes_accessed=3 * 2**20, transcendentals=0),
@@ -74,35 +76,36 @@
     )(*parts)
 
 
-def score_kernel(v1_ref, v2_hbm, s_ref, v2_ref, sems):
+def score_kernel(part, v1_ref, v2_hbm, s_ref, v2_ref, sems):
     copies = [pltpu.make_async_copy(v2_hbm.at[x], v2_ref.at[x], sems.at[x]) for x in range(NXL)]
     for copy in copies:
         copy.start()
     for copy in copies:
         copy.wait()
     contract = (((1,), (1,)), ((), ()))
-    for u in range(NI // 256):
+    for u in range(NP // 256):
         rows = slice(u * 256, (u + 1) * 256)
+        users = slice(part * NP + u * 256, part * NP + (u + 1) * 256)
         s_ref[rows, :] = lax.dot_general(
-            v1_ref[0, rows, :], v2_ref[0], contract, preferred_element_type=jnp.float32
+            v1_ref[0, users, :], v2_ref[0], contract, preferred_element_type=jnp.float32
         ) + lax.dot_general(
-            v1_ref[1, rows, :], v2_ref[1], contract, preferred_element_type=jnp.float32
+            v1_ref[1, users, :], v2_ref[1], contract, preferred_element_type=jnp.float32
         )
 
 
-def partial_scores(v1_all, v2_all):
-    return pl.pallas_call(
-        score_kernel,
-        out_shape=jax.ShapeDtypeStruct((NI, NJ), jnp.float32),
+def partial_scores(part, v1_all, v2_all):
+    return pl.pallas_call(
+        functools.partial(score_kernel, part),
+        out_shape=jax.ShapeDtypeStruct((NP, NJ), jnp.float32),
         in_specs=[VMEM, pl.BlockSpec(memory_space=pl.ANY)],
         out_specs=VMEM,
         scratch_shapes=[
             pltpu.VMEM((NXL, NJ, WIDTH), jnp.bfloat16),
             pltpu.SemaphoreType.DMA((NXL,)),
         ],
-        compiler_params=limit(8),
+        compiler_params=limit(6),
         cost_estimate=pl.CostEstimate(
-            flops=2 * NI * NJ * NXL * WIDTH, bytes_accessed=6 * 2**20, transcendentals=0
+            flops=2 * NP * NJ * NXL * WIDTH, bytes_accessed=3 * 2**20, transcendentals=0
         ),
     )(v1_all, v2_all)
 
@@ -121,26 +124,77 @@
     return jnp.where(trade, pltpu.roll(row, HALF, 1), row)
 
 
-def stats_kernel(
-    place_ref, own_ref, other_ref, partner_ref, most_ref, most_other_ref, s_ref, out_ref, pack_ref
-):
+def block_stats(own_ref, other_ref, s_ref, row_ref, col_highest, col_total):
     eye = diagonal()
-    core = place_ref[0]
-    pack_ref[...] = jnp.zeros_like(pack_ref)
-    col_highest = jnp.full((1, NJ), -jnp.inf, jnp.float32)
-    col_total = jnp.zeros((1, NJ), jnp.float32)
-    for u in range(NI // LANES):
+    for u in range(NP // LANES):
         rows = slice(u * LANES, (u + 1) * LANES)
         s = SCALE * (own_ref[rows, :] + other_ref[rows, :])
         s_ref[rows, :] = s
         highest = jnp.max(s, axis=1, keepdims=True)
         lse = highest + jnp.log(jnp.sum(jnp.exp(s - highest), axis=1, keepdims=True))
-        pack_ref[0, u : u + 1, :] = jnp.sum(jnp.where(eye, lse, 0.0), axis=0, keepdims=True)
+        row_ref[u : u + 1, :] = jnp.sum(jnp.where(eye, lse, 0.0), axis=0, keepdims=True)
         higher = jnp.maximum(col_highest, jnp.max(s, axis=0, keepdims=True))
         col_total = col_total * jnp.exp(col_highest - higher) + jnp.sum(
             jnp.exp(s - higher), axis=0, keepdims=True
         )
         col_highest = higher
+    return col_highest, col_total
+
+
+def first_kernel(own_ref, other_ref, s_ref, row_ref, col_ref):
+    highest, total = block_stats(
+        own_ref,
+        other_ref,
+        s_ref,
+        row_ref,
+        jnp.full((1, NJ), -jnp.inf, jnp.float32),
+        jnp.zeros((1, NJ), jnp.float32),
+    )
+    col_ref[0:1, :] = highest
+    col_ref[1:2, :] = total
+
+
+def first_stats(own, other):
+    return pl.pallas_call(
+        first_kernel,
+        out_shape=(
+            jax.ShapeDtypeStruct((NP, NJ), jnp.float32),
+            jax.ShapeDtypeStruct((NP // LANES, LANES), jnp.float32),
+            jax.ShapeDtypeStruct((2, NJ), jnp.float32),
+        ),
+        in_specs=[VMEM] * 2,
+        out_specs=(VMEM,) * 3,
+        compiler_params=limit(4),
+        cost_estimate=pl.CostEstimate(
+            flops=10 * NP * NJ, bytes_accessed=3 * 2**20, transcendentals=2 * NP * NJ
+        ),
+    )(own, other)
+
+
+def second_kernel(
+    place_ref,
+    own_ref,
+    other_ref,
+    first_ref,
+    col_ref,
+    partner_ref,
+    most_ref,
+    most_other_ref,
+    s_ref,
+    out_ref,
+    pack_ref,
+):
+    half = NP // LANES
+    pack_ref[...] = jnp.zeros_like(pack_ref)
+    pack_ref[0, 0:half, :] = first_ref[...]
+    col_highest, col_total = block_stats(
+        own_ref,
+        other_ref,
+        s_ref,
+        pack_ref.at[0, half : 2 * half, :],
+        col_ref[0:1, :],
+        col_ref[1:2, :],
+    )
     col_lse = col_highest + jnp.log(col_total)
     for g in range(4):
         row, trade = placed(place_ref[2], g)
@@ -150,26 +204,26 @@
     pack_ref[0, 8:9, :] = partner_ref[...].astype(jnp.float32)
     pack_ref[0, 9:10, :] = most[0:1, :]
     pack_ref[1, 9:10, :] = most[1:2, :]
-    chosen = jnp.where(core == 0, pack_ref[0], pack_ref[1])
+    chosen = jnp.where(place_ref[0] == 0, pack_ref[0], pack_ref[1])
     for p in range(16):
         out_ref[p] = chosen
 
 
-def local_stats(place, own, other, partner, most, most_other):
-    return pl.pallas_call(
-        stats_kernel,
+def second_stats(place, own, other, first, cols, partner, most, most_other):
+    return pl.pallas_call(
+        second_kernel,
         out_shape=(
-            jax.ShapeDtypeStruct((NI, NJ), jnp.float32),
+            jax.ShapeDtypeStruct((NP, NJ), jnp.float32),
             jax.ShapeDtypeStruct((16, 16, LANES), jnp.float32),
         ),
-        in_specs=[SMEM] + [VMEM] * 5,
+        in_specs=[SMEM] + [VMEM] * 7,
         out_specs=(VMEM, VMEM),
         scratch_shapes=[pltpu.VMEM((2, 16, LANES), jnp.float32)],
-        compiler_params=limit(8),
+        compiler_params=limit(4),
         cost_estimate=pl.CostEstimate(
-            flops=10 * NI * NJ, bytes_accessed=6 * 2**20, transcendentals=2 * NI * NJ
-        ),
-    )(place, own, other, partner.reshape(1, ROWS), most, most_other)
+            flops=10 * NP * NJ, bytes_accessed=3 * 2**20, transcendentals=2 * NP * NJ
+        ),
+    )(place, own, other, first, cols, partner.reshape(1, ROWS), most, most_other)
 
 
 def merged(lses):
@@ -209,7 +263,18 @@
     )(place, seen)
 
 
-def couple_kernel(place_ref, s_ref, known_ref, told_ref, c_ref, size_ref):
+def couple_kernel(
+    place_ref,
+    s0_ref,
+    s1_ref,
+    known_ref,
+    told_ref,
+    c_ref,
+    give_one_ref,
+    give_two_ref,
+    take_one_ref,
+    take_two_ref,
+):
     core, xl, z, uhigh = place_ref[0], place_ref[1], place_ref[2], place_ref[3]
     rows = jnp.where(core == 0, known_ref[...], told_ref[...])
     cols = jnp.where(core == 0, told_ref[...], known_ref[...])
@@ -227,30 +292,36 @@
     col_lse = jnp.concatenate(col_lse, axis=1)
     for u in range(NI // LANES):
         here = slice(u * LANES, (u + 1) * LANES)
-        s = s_ref[here, :]
+        half_ref = s0_ref if u < NP // LANES else s1_ref
+        start = u * LANES % NP
+        s = half_ref[start : start + LANES, :]
         row_lse = jnp.sum(jnp.where(eye, rows[u : u + 1, :], 0.0), axis=1, keepdims=True)
         partner = jnp.sum(jnp.where(eye, rows[8 + u : 9 + u, :], 0.0), axis=1, keepdims=True)
         both = jnp.exp(s - row_lse) + jnp.exp(s - col_lse)
         positive = (partner == index).astype(jnp.float32)
         c_ref[here, :] = (0.5 * both - positive).astype(jnp.bfloat16)
-    size_ref[0:1, :] = rows[16:17, :]
-    size_ref[1:2, :] = cols[16:17, :]
-
-
-def coupling_of(place, scores, known, told):
+    most_two = jnp.concatenate([rows[16:17, :]] * 4, axis=1)
+    most_one = jnp.concatenate([cols[16:17, :]] * 4, axis=1)
+    give_one_ref[...] = 128.0 / most_two
+    take_one_ref[...] = most_two / 128.0
+    give_two_ref[...] = 64.0 / most_one
+    take_two_ref[...] = most_one / 64.0
+
+
+def coupling_of(place, scores0, scores1, known, told):
     return pl.pallas_call(
         couple_kernel,
         out_shape=(
             jax.ShapeDtypeStruct((NI, NJ), jnp.bfloat16),
-            jax.ShapeDtypeStruct((2, LANES), jnp.float32),
-        ),
-        in_specs=[SMEM] + [VMEM] * 3,
-        out_specs=(VMEM, VMEM),
+        )
+        + (jax.ShapeDtypeStruct((1, WIDTH), jnp.float32),) * 4,
+        in_specs=[SMEM] + [VMEM] * 4,
+        out_specs=(VMEM,) * 5,
         compiler_params=limit(5),
         cost_estimate=pl.CostEstimate(
             flops=8 * NI * NJ, bytes_accessed=3 * 2**20, transcendentals=2 * NI * NJ
         ),
-    )(place, scores, known, told)
+    )(place, scores0, scores1, known, told)
 
 
 def swap(x, axis):
@@ -306,25 +377,29 @@
     )
     v1_all = lax.all_to_all(copies, PLANE, 0, 0, tiled=True).reshape(NXL, NI, WIDTH)
 
-    own = partial_scores(v1_all, v2_all)
-    other = swap(own, "core")
+    own0 = partial_scores(0, v1_all, v2_all)
+    other0 = swap(own0, "core")
+    own1 = partial_scores(1, v1_all, v2_all)
+    other1 = swap(own1, "core")
     most = jnp.concatenate([most_v2, largest(v1_all)[None]])
     most_other = swap(most, "core")
 
-    scores, pack = local_stats(place, own, other, partner, most, most_other)
+    scores0, first, cols = first_stats(own0, other0)
+    scores1, pack = second_stats(place, own1, other1, first, cols, partner, most, most_other)
     seen = lax.all_to_all(
         pack, EVERY, 0, 0, axis_index_groups=stat_groups(), tiled=True
     )
     known = merge_stats(place, seen)
-    coupling, sizes = coupling_of(place, scores, known, swap(known, "core"))
-    most_two, most_one = sizes[0, 0], sizes[1, 0]
+    coupling, give_one, give_two, take_one, take_two = coupling_of(
+        place, scores0, scores1, known, swap(known, "core")
+    )
 
     part_two = [
         (
             lax.dot_general(
                 coupling, v1_all[x], (((0,), (0,)), ((), ())), preferred_element_type=jnp.float32
             )
-            * (64.0 / most_one)
+            * give_two
         ).astype(jnp.float16)
         for x in range(NXL)
     ]
@@ -343,19 +418,20 @@
             (((2,), (1,)), ((0,), (0,))),
             preferred_element_type=jnp.float32,
         )
-        * (128.0 / most_two)
+        * give_one
     ).astype(jnp.float16)
     one_parts = lax.all_to_all(part_one.reshape(16, ROWS, WIDTH), PLANE, 0, 0, tiled=True)
     two = jnp.stack([jnp.concatenate([two0[HALF:], two0[:HALF]]), two1])
     joined = sum(part.astype(jnp.float32) for part in (group(0), before, after, two))
     far = to_plane((joined[:, HALF:] * 0.25).astype(jnp.float16), 4)
-    total = (joined[:, :HALF] + 4.0 * far.astype(jnp.float32)) * (most_one / 64.0)
+    total = (joined[:, :HALF] + 4.0 * far.astype(jnp.float32)) * take_two
     stay = jnp.where(xl == 0, total[0], total[1])
     come = swap(jnp.where(xl == 0, total[1], total[0]), "xl")
+    grad_one = jnp.sum(one_parts.astype(jnp.float32) * take_one, axis=0)
+    come, grad_one = lax.optimization_barrier((come, grad_one))
     grad_two = jnp.where(
         xl == 0, jnp.concatenate([stay, come]), jnp.concatenate([come, stay])
     )
-    grad_one = jnp.sum(one_parts.astype(jnp.float32) * (most_two / 128.0), axis=0)
     return (grad_one, grad_two)
 
 

time: 125 us -> 122 us (0.976)
  waiting for transfers between devices: 41.3 us -> 38 us
  between operations: 3.53 us -> 0.89 us
  local copies, waits for them, and re-layouts: 3.11 us -> 4.36 us
    ppermute x5 -> x6, waiting for transfers between devices: 9.32 us -> 3.2 us  [swap(): return lax.ppermute(x, axis, [(0, 1), (1, 0)])]
    all_to_all x1, waiting for transfers between devices: 0.01 us -> 2.33 us  [on_device(): lax.all_to_all(part_one.reshape(16, ROWS, WIDTH), PLANE, 0, 0, tiled=True)]
    unnamed x6 -> x12, local copies, waits for them, and re-layouts: 2.23 us -> 3.93 us
    ppermute x5 -> x6, starting transfers between devices: 6.53 us -> 7.16 us  [swap(): return lax.ppermute(x, axis, [(0, 1), (1, 0)])]
    pallas_call x2 -> x4, Pallas kernels: 6.1 us -> 6.64 us  [the longest x2 2.65 us: partial_scores(): pl.pallas_call(functools.partial(score_kernel, part), out_shape=jax.Shape...]
  transfers between devices with their start and end apart: 17 -> 18, of which waited for: 9 -> 8; matrix products, arithmetic and copies ran while one was open for 2% -> 2% of each run, Pallas kernels for 2% -> 5%
where the time goes in v6:
time: 122 us; the launch traced here: 120 us
  starting transfers between devices  44.4 us (36%)
  waiting for transfers between devices  38 us (31%)
  blocking collectives  12.7 us (10%)
  Pallas kernels  11.6 us (10%)
  local copies, waits for them, and re-layouts  4.36 us (4%)
  matrix products  4.09 us (3%)
  other arithmetic  3.51 us (3%)
    ppermute x10, waiting for transfers between devices, to_plane(): return lax.ppermute(x, 'z', [(z, (z + dz) % NZ) for z in range(NZ)])  32.5 us
    ppermute x10, starting transfers between devices, to_plane(): return lax.ppermute(x, 'z', [(z, (z + dz) % NZ) for z in range(NZ)])  24.6 us
    all_to_all x1, blocking collectives, on_device(): lax.all_to_all(pack, EVERY, 0, 0, axis_index_groups=stat_groups(), tiled=...  12.7 us
    all_to_all x1, starting transfers between devices, on_device(): lax.all_to_all(copies, PLANE, 0, 0, tiled=True).reshape(NXL, NI, WIDTH)  7.45 us
    ppermute x6, starting transfers between devices, swap(): return lax.ppermute(x, axis, [(0, 1), (1, 0)])  7.16 us
    all_to_all x1, starting transfers between devices, on_device(): lax.all_to_all(part_one.reshape(16, ROWS, WIDTH), PLANE, 0, 0, tiled=True)  5.2 us
    unnamed x12, local copies, waits for them, and re-layouts  3.93 us
    ppermute x6, waiting for transfers between devices, swap(): return lax.ppermute(x, axis, [(0, 1), (1, 0)])  3.2 us
  transfers between devices with their start and end apart: 18, of which 8 were waited for; matrix products, arithmetic and copies ran while one was open for 2% of the time, Pallas kernels for 5%

profile of v6, /device:TPU:4, one launch (start us, length us, event | category | flops | bytes accessed | tf_op | source)
XLA Modules:
  0.0 119.7 jit_solution(6256909548132481213)
XLA Ops:
  0.6 0.9 select_bitcast_fusion.2
  1.5 1.3 %collective-permute-start = (bf16[64,512]{1,0:T(8,128)(2,1)S(1)}, bf16[64,512]{1,0:T(8,128)(2,1)S(1)}, u32[]{:S(2)}, u32[]{:S(2)}) collective-permute-start(bf16[64,512]{1,0:T(8,128)(2,1)S(1)} %get-tuple-element.57), channel_id=1, source_target_pairs={{0,2},{2,0},{1,3},{3,1},{4,6},{6,4},{5,7},{7,5},{8,10},{10,8},{9,1... | collective-permute-start | bytes 196616 | tf_op jit(solution)/shard_map/ppermute | solution.py:328
  2.8 0.9 copy-done.4
  3.7 2.8 %shard_map.50 = bf16[16,128,512]{2,1,0:T(8,128)(2,1)S(1)} custom-call(bf16[128,512]{1,0:T(8,128)(2,1)S(1)} %copy-done.4), custom_call_target="tpu_custom_call" | custom-call | bytes 3145728 | tf_op jit(solution)/shard_map/pallas_call | solution.py:43
  6.6 1.3 %copy-done = bf16[16,128,512]{2,1,0:T(8,128)(2,1)} copy-done((bf16[16,128,512]{2,1,0:T(8,128)(2,1)}, bf16[16,128,512]{2,1,0:T(8,128)(2,1)S(1)}, u32[]{:S(2)}) %copy-start) | copy-done | bytes 2097176
  7.9 0.0 collective-permute-done
  7.9 7.4 %all-to-all-start = ((bf16[16,128,512]{2,1,0:T(8,128)(2,1)}), bf16[16,128,512]{2,1,0:T(8,128)(2,1)S(1)}, u32[]{:S(2)}, u32[]{:S(2)}) async-start(bf16[16,128,512]{2,1,0:T(8,128)(2,1)} %copy-done), calls=%async_computation | async-start | bytes 4194304 | tf_op jit(solution)/shard_map/all_to_all | solution.py:378
  15.4 7.3 %collective-permute-start.1 = (bf16[2,64,512]{2,1,0:T(8,128)(2,1)S(1)}, bf16[2,64,512]{2,1,0:T(8,128)(2,1)S(1)}, u32[]{:S(2)}, u32[]{:S(2)}) collective-permute-start(bf16[2,64,512]{2,1,0:T(8,128)(2,1)S(1)} %maximum_select_fusion.1), channel_id=1, source_target_pairs={{0,128},{32,160},{64,192},{96,224},{128,0},{160,32},{192,64},{224,... | collective-permute-start | bytes 393224 | tf_op jit(solution)/shard_map/ppermute | solution.py:348
  22.7 4.4 %collective-permute-done.1 = bf16[2,64,512]{2,1,0:T(8,128)(2,1)S(1)} collective-permute-done((bf16[2,64,512]{2,1,0:T(8,128)(2,1)S(1)}, bf16[2,64,512]{2,1,0:T(8,128)(2,1)S(1)}, u32[]{:S(2)}, u32[]{:S(2)}) %collective-permute-start.1) | collective-permute-done | bytes 131104 | tf_op jit(solution)/shard_map/ppermute | solution.py:348
  27.1 4.0 %collective-permute-start.3 = (bf16[2,128,512]{2,1,0:T(8,128)(2,1)S(1)}, bf16[2,128,512]{2,1,0:T(8,128)(2,1)S(1)}, u32[]{:S(2)}, u32[]{:S(2)}) collective-permute-start(bf16[2,128,512]{2,1,0:T(8,128)(2,1)S(1)} %pad_maximum_fusion.own_ref), channel_id=1, source_target_pairs={{0,224},{32,0},{64,32},{96,64},{128,96},{160,128},{192,160},{224,1... | collective-permute-start | bytes 786440 | tf_op jit(solution)/shard_map/ppermute | solution.py:348
  31.1 0.0 collective-permute-start.2
  31.1 1.1 collective-permute-start.5
  32.2 3.6 %collective-permute-start.4 = (bf16[128,512]{1,0:T(8,128)(2,1)S(1)}, bf16[128,512]{1,0:T(8,128)(2,1)S(1)}, u32[]{:S(2)}, u32[]{:S(2)}) collective-permute-start(bf16[128,512]{1,0:T(8,128)(2,1)S(1)} %get-tuple-element.53), channel_id=1, source_target_pairs={{0,192},{32,224},{64,0},{96,32},{128,64},{160,96},{192,128},{224,1... | collective-permute-start | bytes 393224 | tf_op jit(solution)/shard_map/ppermute | solution.py:348
  35.8 9.4 %collective-permute-done.5.two1_ref = bf16[128,512]{1,0:T(8,128)(2,1)S(1)} collective-permute-done((bf16[128,512]{1,0:T(8,128)(2,1)S(1)}, bf16[128,512]{1,0:T(8,128)(2,1)S(1)}, u32[]{:S(2)}, u32[]{:S(2)}) %collective-permute-start.5) | collective-permute-done | bytes 131104 | tf_op jit(solution)/shard_map/ppermute | solution.py:348
  45.1 0.0 collective-permute-done.4.two0_ref
  45.1 0.0 collective-permute-done.3.last_ref
  45.1 0.0 collective-permute-done.2.next_ref
  45.1 0.2 shard_map.51
  45.3 0.0 copy-start.1
  45.3 0.0 all-to-all-done
  45.3 1.8 %shard_map.52.own_ref = f32[512,512]{1,0:T(8,128)} custom-call(bf16[2,1024,512]{2,1,0:T(8,128)(2,1)S(1)} %bitcast.45, bf16[2,512,512]{2,1,0:T(8,128)(2,1)S(1)} %get-tuple-element.23.v2_hbm), custom_call_target="tpu_custom_call" | custom-call | flops 536870912 | bytes 3145728 | tf_op jit(solution)/shard_map/pallas_call | solution.py:97
  47.2 0.1 collective-permute-start.6
  47.3 1.2 %copy-done.2 = bf16[2,512,512]{2,1,0:T(8,128)(2,1)S(1)} copy-done((bf16[2,512,512]{2,1,0:T(8,128)(2,1)S(1)}, bf16[2,512,512]{2,1,0:T(8,128)(2,1)}, u32[]{:S(2)}) %copy-start.2) | copy-done | bytes 1048600
  48.5 0.8 shard_map.54.own_ref
  49.3 0.6 collective-permute-start.7
  49.9 0.2 abs_reduce_fusion
  50.2 0.1 collective-permute-start.8
  50.3 0.1 pad_add_fusion.place_ref
  50.4 0.0 collective-permute-done.6.other_ref
  50.4 2.1 %shard_map.53 = (f32[512,512]{1,0:T(8,128)S(1)}, f32[4,128]{1,0:T(4,128)S(1)}, f32[2,512]{1,0:T(2,128)S(1)}) custom-call(f32[512,512]{1,0:T(8,128)} %shard_map.52.own_ref, f32[512,512]{1,0:T(8,128)} %collective-permute-done.6.other_ref), custom_call_target="tpu_custom_call" | custom-call | flops 2621440 | bytes 3145728 | tf_op jit(solution)/shard_map/pallas_call | solution.py:158
  52.5 0.0 collective-permute-done.8.most_other_ref
  52.5 0.0 collective-permute-done.7.other_ref
  52.5 1.8 %shard_map.55 = (f32[512,512]{1,0:T(8,128)S(1)}, f32[16,16,128]{2,1,0:T(8,128)S(1)}) custom-call(s32[4]{0:T(128)S(1)} %pad_add_fusion.place_ref, f32[512,512]{1,0:T(8,128)S(1)} %shard_map.54.own_ref, f32[512,512]{1,0:T(8,128)} %collective-permute-done.7.other_ref, f32[4,128]{1,0:T(4,128)S(1)} %get-tuple-element.25.first_ref, ...), custom_call_target="tpu_custom_call" | custom-call | flops 2621440 | bytes 3145728 | tf_op jit(solution)/shard_map/pallas_call | solution.py:213
  54.4 12.7 %all_to_all.15.seen_ref = f32[16,16,128]{2,1,0:T(8,128)S(1)} all-to-all(f32[16,16,128]{2,1,0:T(8,128)S(1)} %get-tuple-element.29), channel_id=1, replica_groups={{0,4,8,12,16,20,24,28,2,6,10,14,18,22,26,30},{32,36,40,44,48,52,56,60,3..., dimensions={0} | all-to-all | bytes 262144 | tf_op jit(solution)/shard_map/all_to_all | solution.py:389
  67.1 0.6 shard_map.56.known_ref
  67.7 3.8 %collective-permute-start.9 = (f32[24,128]{1,0:T(8,128)S(1)}, f32[24,128]{1,0:T(8,128)S(1)}, u32[]{:S(2)}, u32[]{:S(2)}) collective-permute-start(f32[24,128]{1,0:T(8,128)S(1)} %shard_map.56.known_ref), channel_id=1, source_target_pairs={{0,1},{1,0},{2,3},{3,2},{4,5},{5,4},{6,7},{7,6},{8,9},{9,8},{10,11... | collective-permute-start | bytes 36872 | tf_op jit(solution)/shard_map/ppermute | solution.py:328
  71.5 0.2 fusion.9
  71.7 0.6 collective-permute-done.9.told_ref
  72.3 1.4 %shard_map.57 = (bf16[1024,512]{1,0:T(8,128)(2,1)S(1)}, f32[1,512]{1,0:T(1,128)S(1)}, f32[1,512]{1,0:T(1,128)S(1)}, f32[1,512]{1,0:T(1,128)S(1)}, f32[1,512]{1,0:T(1,128)S(1)}) custom-call(s32[4]{0:T(128)S(1)} %pad_add_fusion.place_ref, f32[512,512]{1,0:T(8,128)S(1)} %get-tuple-element.24.s0_ref, f32[512,512]{1,0:T(8,128)S(1)} %get-tuple-element.28.s1_ref, ...), custom_call_target="tpu_custom_call" | custom-call | flops 4194304 | bytes 3145728 | tf_op jit(solution)/shard_map/pallas_call | solution.py:312
  73.8 0.7 fusion.1
  74.5 0.7 fusion
  75.3 0.5 copy-done.3
  75.7 2.6 %multiply_convert_fusion = f16[2,1024,512]{2,1,0:T(8,128)(2,1)} fusion(bf16[2,512,512]{2,1,0:T(8,128)(2,1)S(1)} %copy-done.3, f32[512]{0:T(512)S(1)} %bitcast.50, bf16[1024,512]{1,0:T(8,128)(2,1)S(1)} %get-tuple-element.35), kind=kOutput, calls=%fused_computation.1 | convolution fusion | flops 1075838976 | bytes 4196352 | tf_op jit(solution)/shard_map/dot_general | solution.py:415
  78.3 5.2 %all-to-all-start.2 = ((f16[16,128,512]{2,1,0:T(8,128)(2,1)}), f16[16,128,512]{2,1,0:T(8,128)(2,1)S(1)}, u32[]{:S(2)}, u32[]{:S(2)}) async-start(f16[16,128,512]{2,1,0:T(8,128)(2,1)} %bitcast.53), calls=%async_computation.2 | async-start | bytes 4194304 | tf_op jit(solution)/shard_map/all_to_all | solution.py:423
  83.5 0.1 fusion.10
  83.6 1.6 %collective-permute-start.12 = (f16[128,512]{1,0:T(8,128)(2,1)S(1)}, f16[128,512]{1,0:T(8,128)(2,1)S(1)}, u32[]{:S(2)}, u32[]{:S(2)}) collective-permute-start(f16[128,512]{1,0:T(8,128)(2,1)S(1)} %get-tuple-element.42), channel_id=1, source_target_pairs={{0,64},{32,96},{64,128},{96,160},{128,192},{160,224},{192,0},{224,... | collective-permute-start | bytes 393224 | tf_op jit(solution)/shard_map/ppermute | solution.py:348
  85.2 0.1 fusion.11
  85.3 2.7 %collective-permute-start.13 = (f16[128,512]{1,0:T(8,128)(2,1)S(1)}, f16[128,512]{1,0:T(8,128)(2,1)S(1)}, u32[]{:S(2)}, u32[]{:S(2)}) collective-permute-start(f16[128,512]{1,0:T(8,128)(2,1)S(1)} %get-tuple-element.46), channel_id=1, source_target_pairs={{0,192},{32,224},{64,0},{96,32},{128,64},{160,96},{192,128},{224,1... | collective-permute-start | bytes 393224 | tf_op jit(solution)/shard_map/ppermute | solution.py:348
  88.0 0.1 pad_maximum_fusion.1
  88.1 0.3 collective-permute-start.10
  88.4 0.1 pad_maximum_fusion.2
  88.5 1.9 %collective-permute-start.11 = (f16[2,128,512]{2,1,0:T(8,128)(2,1)S(1)}, f16[2,128,512]{2,1,0:T(8,128)(2,1)S(1)}, u32[]{:S(2)}, u32[]{:S(2)}) collective-permute-start(f16[2,128,512]{2,1,0:T(8,128)(2,1)S(1)} %pad_maximum_fusion.2), channel_id=1, source_target_pairs={{0,32},{32,64},{64,96},{96,128},{128,160},{160,192},{192,224},{224... | collective-permute-start | bytes 786440 | tf_op jit(solution)/shard_map/ppermute | solution.py:348
  90.3 4.1 %collective-permute-done.12 = f16[128,512]{1,0:T(8,128)(2,1)S(1)} collective-permute-done((f16[128,512]{1,0:T(8,128)(2,1)S(1)}, f16[128,512]{1,0:T(8,128)(2,1)S(1)}, u32[]{:S(2)}, u32[]{:S(2)}) %collective-permute-start.12) | collective-permute-done | bytes 131104 | tf_op jit(solution)/shard_map/ppermute | solution.py:348
  94.5 0.0 collective-permute-done.13
  94.6 6.0 %collective-permute-done.10 = f16[2,128,512]{2,1,0:T(8,128)(2,1)S(1)} collective-permute-done((f16[2,128,512]{2,1,0:T(8,128)(2,1)S(1)}, f16[2,128,512]{2,1,0:T(8,128)(2,1)S(1)}, u32[]{:S(2)}, u32[]{:S(2)}) %collective-permute-start.10) | collective-permute-done | bytes 262176 | tf_op jit(solution)/shard_map/ppermute | solution.py:348
  100.6 0.0 collective-permute-done.11
  100.6 0.2 convert_add_fusion
  100.8 2.2 %collective-permute-start.14 = (f16[2,64,512]{2,1,0:T(8,128)(2,1)S(1)}, f16[2,64,512]{2,1,0:T(8,128)(2,1)S(1)}, u32[]{:S(2)}, u32[]{:S(2)}) collective-permute-start(f16[2,64,512]{2,1,0:T(8,128)(2,1)S(1)} %fusion.3), channel_id=1, source_target_pairs={{0,128},{32,160},{64,192},{96,224},{128,0},{160,32},{192,64},{224,... | collective-permute-start | bytes 393224 | tf_op jit(solution)/shard_map/ppermute | solution.py:348
  103.0 8.5 %collective-permute-done.14 = f16[2,64,512]{2,1,0:T(8,128)(2,1)S(1)} collective-permute-done((f16[2,64,512]{2,1,0:T(8,128)(2,1)S(1)}, f16[2,64,512]{2,1,0:T(8,128)(2,1)S(1)}, u32[]{:S(2)}, u32[]{:S(2)}) %collective-permute-start.14) | collective-permute-done | bytes 131104 | tf_op jit(solution)/shard_map/ppermute | solution.py:348
  111.6 1.3 %collective-permute-start.15 = (f32[64,512]{1,0:T(8,128)S(1)}, f32[64,512]{1,0:T(8,128)S(1)}, u32[]{:S(2)}, u32[]{:S(2)}) collective-permute-start(f32[64,512]{1,0:T(8,128)S(1)} %get-tuple-element.51), channel_id=1, source_target_pairs={{0,2},{2,0},{1,3},{3,1},{4,6},{6,4},{5,7},{7,5},{8,10},{10,8},{9,1... | collective-permute-start | bytes 393224 | tf_op jit(solution)/shard_map/ppermute | solution.py:328
  112.9 2.3 %all-to-all-done.2 = f16[16,128,512]{2,1,0:T(8,128)(2,1)S(1)} async-done(((f16[16,128,512]{2,1,0:T(8,128)(2,1)}), f16[16,128,512]{2,1,0:T(8,128)(2,1)S(1)}, u32[]{:S(2)}, u32[]{:S(2)}) %all-to-all-start.2) | async-done | bytes 2097184 | tf_op jit(solution)/shard_map/all_to_all | solution.py:423
  115.2 1.1 multiply_reduce_fusion
  116.4 2.6 %collective-permute-done.15 = f32[64,512]{1,0:T(8,128)S(1)} collective-permute-done((f32[64,512]{1,0:T(8,128)S(1)}, f32[64,512]{1,0:T(8,128)S(1)}, u32[]{:S(2)}, u32[]{:S(2)}) %collective-permute-start.15) | collective-permute-done | bytes 131104 | tf_op jit(solution)/shard_map/ppermute | solution.py:328
  118.9 0.7 maximum_select_fusion
  (17 shorter events, 0.2 us)
Async XLA Ops:
  1.5 6.4 %collective-permute-start = (bf16[64,512]{1,0:T(8,128)(2,1)S(1)}, bf16[64,512]{1,0:T(8,128)(2,1)S(1)}, u32[]{:S(2)}, u32[]{:S(2)}) collective-permute-start(bf16[64,512]{1,0:T(8,128)(2,1)S(1)} %get-tuple-element.57), channel_id=1, source_target_pairs={{0,2},{2,0},{1,3},{3,1},{4,6},{6,4},{5,7},{7,5},{8,10},{10,8},{9,1... | collective-permute-start | bytes 196616 | tf_op jit(solution)/shard_map/ppermute | solution.py:328
  2.8 0.9 copy-start.4
  6.6 1.3 %copy-start = (bf16[16,128,512]{2,1,0:T(8,128)(2,1)}, bf16[16,128,512]{2,1,0:T(8,128)(2,1)S(1)}, u32[]{:S(2)}) copy-start(bf16[16,128,512]{2,1,0:T(8,128)(2,1)S(1)} %shard_map.50) | copy-start | bytes 6291460
  7.9 37.4 %all-to-all-start = ((bf16[16,128,512]{2,1,0:T(8,128)(2,1)}), bf16[16,128,512]{2,1,0:T(8,128)(2,1)S(1)}, u32[]{:S(2)}, u32[]{:S(2)}) async-start(bf16[16,128,512]{2,1,0:T(8,128)(2,1)} %copy-done), calls=%async_computation | async-start | bytes 4194304 | tf_op jit(solution)/shard_map/all_to_all | solution.py:378
  15.4 11.7 %collective-permute-start.1 = (bf16[2,64,512]{2,1,0:T(8,128)(2,1)S(1)}, bf16[2,64,512]{2,1,0:T(8,128)(2,1)S(1)}, u32[]{:S(2)}, u32[]{:S(2)}) collective-permute-start(bf16[2,64,512]{2,1,0:T(8,128)(2,1)S(1)} %maximum_select_fusion.1), channel_id=1, source_target_pairs={{0,128},{32,160},{64,192},{96,224},{128,0},{160,32},{192,64},{224,... | collective-permute-start | bytes 393224 | tf_op jit(solution)/shard_map/ppermute | solution.py:348
  27.1 18.1 %collective-permute-start.3 = (bf16[2,128,512]{2,1,0:T(8,128)(2,1)S(1)}, bf16[2,128,512]{2,1,0:T(8,128)(2,1)S(1)}, u32[]{:S(2)}, u32[]{:S(2)}) collective-permute-start(bf16[2,128,512]{2,1,0:T(8,128)(2,1)S(1)} %pad_maximum_fusion.own_ref), channel_id=1, source_target_pairs={{0,224},{32,0},{64,32},{96,64},{128,96},{160,128},{192,160},{224,1... | collective-permute-start | bytes 786440 | tf_op jit(solution)/shard_map/ppermute | solution.py:348
  31.1 14.1 %collective-permute-start.2 = (bf16[2,128,512]{2,1,0:T(8,128)(2,1)S(1)}, bf16[2,128,512]{2,1,0:T(8,128)(2,1)S(1)}, u32[]{:S(2)}, u32[]{:S(2)}) collective-permute-start(bf16[2,128,512]{2,1,0:T(8,128)(2,1)S(1)} %pad_maximum_fusion.own_ref), channel_id=1, source_target_pairs={{0,32},{32,64},{64,96},{96,128},{128,160},{160,192},{192,224},{224... | collective-permute-start | bytes 786440 | tf_op jit(solution)/shard_map/ppermute | solution.py:348
  31.1 14.0 %collective-permute-start.5 = (bf16[128,512]{1,0:T(8,128)(2,1)S(1)}, bf16[128,512]{1,0:T(8,128)(2,1)S(1)}, u32[]{:S(2)}, u32[]{:S(2)}) collective-permute-start(bf16[128,512]{1,0:T(8,128)(2,1)S(1)} %get-tuple-element.52), channel_id=1, source_target_pairs={{0,64},{32,96},{64,128},{96,160},{128,192},{160,224},{192,0},{224,... | collective-permute-start | bytes 393224 | tf_op jit(solution)/shard_map/ppermute | solution.py:348
  32.2 13.0 %collective-permute-start.4 = (bf16[128,512]{1,0:T(8,128)(2,1)S(1)}, bf16[128,512]{1,0:T(8,128)(2,1)S(1)}, u32[]{:S(2)}, u32[]{:S(2)}) collective-permute-start(bf16[128,512]{1,0:T(8,128)(2,1)S(1)} %get-tuple-element.53), channel_id=1, source_target_pairs={{0,192},{32,224},{64,0},{96,32},{128,64},{160,96},{192,128},{224,1... | collective-permute-start | bytes 393224 | tf_op jit(solution)/shard_map/ppermute | solution.py:348
  45.3 1.8 %copy-start.1 = (bf16[2,512,512]{2,1,0:T(8,128)(2,1)}, bf16[2,512,512]{2,1,0:T(8,128)(2,1)S(1)}, u32[]{:S(2)}) copy-start(bf16[2,512,512]{2,1,0:T(8,128)(2,1)S(1)} %get-tuple-element.23.v2_hbm) | copy-start | bytes 3145732
  47.2 3.2 %collective-permute-start.6 = (f32[512,512]{1,0:T(8,128)}, f32[512,512]{1,0:T(8,128)}, u32[]{:S(2)}, u32[]{:S(2)}) collective-permute-start(f32[512,512]{1,0:T(8,128)} %shard_map.52.own_ref), channel_id=1, source_target_pairs={{0,1},{1,0},{2,3},{3,2},{4,5},{5,4},{6,7},{7,6},{8,9},{9,8},{10,11... | collective-permute-start | bytes 3145736 | tf_op jit(solution)/shard_map/ppermute | solution.py:328
  47.3 1.2 %copy-start.2 = (bf16[2,512,512]{2,1,0:T(8,128)(2,1)S(1)}, bf16[2,512,512]{2,1,0:T(8,128)(2,1)}, u32[]{:S(2)}) copy-start(bf16[2,512,512]{2,1,0:T(8,128)(2,1)} %copy-done.1) | copy-start | bytes 3145732
  49.3 3.2 %collective-permute-start.7 = (f32[512,512]{1,0:T(8,128)S(1)}, f32[512,512]{1,0:T(8,128)}, u32[]{:S(2)}, u32[]{:S(2)}) collective-permute-start(f32[512,512]{1,0:T(8,128)S(1)} %shard_map.54.own_ref), channel_id=1, source_target_pairs={{0,1},{1,0},{2,3},{3,2},{4,5},{5,4},{6,7},{7,6},{8,9},{9,8},{10,11... | collective-permute-start | bytes 3145736 | tf_op jit(solution)/shard_map/ppermute | solution.py:328
  49.9 2.6 %copy-start.5 = (s32[128]{0:T(128)S(1)}, s32[128]{0:T(128)}, u32[]{:S(2)}) copy-start(s32[128]{0:T(128)} %param.5) | copy-start | bytes 1540
  50.2 2.4 %collective-permute-start.8 = (f32[2,512]{1,0:T(2,128)S(1)}, f32[2,512]{1,0:T(2,128)S(1)}, u32[]{:S(2)}, u32[]{:S(2)}) collective-permute-start(f32[2,512]{1,0:T(2,128)S(1)} %pad_maximum_fusion.3.most_ref), channel_id=1, source_target_pairs={{0,1},{1,0},{2,3},{3,2},{4,5},{5,4},{6,7},{7,6},{8,9},{9,8},{10,11... | collective-permute-start | bytes 12296 | tf_op jit(solution)/shard_map/ppermute | solution.py:328
  67.7 4.6 %collective-permute-start.9 = (f32[24,128]{1,0:T(8,128)S(1)}, f32[24,128]{1,0:T(8,128)S(1)}, u32[]{:S(2)}, u32[]{:S(2)}) collective-permute-start(f32[24,128]{1,0:T(8,128)S(1)} %shard_map.56.known_ref), channel_id=1, source_target_pairs={{0,1},{1,0},{2,3},{3,2},{4,5},{5,4},{6,7},{7,6},{8,9},{9,8},{10,11... | collective-permute-start | bytes 36872 | tf_op jit(solution)/shard_map/ppermute | solution.py:328
  74.5 1.2 %copy-start.3 = (bf16[2,512,512]{2,1,0:T(8,128)(2,1)S(1)}, bf16[2,512,512]{2,1,0:T(8,128)(2,1)}, u32[]{:S(2)}) copy-start(bf16[2,512,512]{2,1,0:T(8,128)(2,1)} %copy-done.1) | copy-start | bytes 3145732
  78.3 36.9 %all-to-all-start.2 = ((f16[16,128,512]{2,1,0:T(8,128)(2,1)}), f16[16,128,512]{2,1,0:T(8,128)(2,1)S(1)}, u32[]{:S(2)}, u32[]{:S(2)}) async-start(f16[16,128,512]{2,1,0:T(8,128)(2,1)} %bitcast.53), calls=%async_computation.2 | async-start | bytes 4194304 | tf_op jit(solution)/shard_map/all_to_all | solution.py:423
  83.6 10.8 %collective-permute-start.12 = (f16[128,512]{1,0:T(8,128)(2,1)S(1)}, f16[128,512]{1,0:T(8,128)(2,1)S(1)}, u32[]{:S(2)}, u32[]{:S(2)}) collective-permute-start(f16[128,512]{1,0:T(8,128)(2,1)S(1)} %get-tuple-element.42), channel_id=1, source_target_pairs={{0,64},{32,96},{64,128},{96,160},{128,192},{160,224},{192,0},{224,... | collective-permute-start | bytes 393224 | tf_op jit(solution)/shard_map/ppermute | solution.py:348
  85.3 9.2 %collective-permute-start.13 = (f16[128,512]{1,0:T(8,128)(2,1)S(1)}, f16[128,512]{1,0:T(8,128)(2,1)S(1)}, u32[]{:S(2)}, u32[]{:S(2)}) collective-permute-start(f16[128,512]{1,0:T(8,128)(2,1)S(1)} %get-tuple-element.46), channel_id=1, source_target_pairs={{0,192},{32,224},{64,0},{96,32},{128,64},{160,96},{192,128},{224,1... | collective-permute-start | bytes 393224 | tf_op jit(solution)/shard_map/ppermute | solution.py:348
  88.1 12.5 %collective-permute-start.10 = (f16[2,128,512]{2,1,0:T(8,128)(2,1)S(1)}, f16[2,128,512]{2,1,0:T(8,128)(2,1)S(1)}, u32[]{:S(2)}, u32[]{:S(2)}) collective-permute-start(f16[2,128,512]{2,1,0:T(8,128)(2,1)S(1)} %pad_maximum_fusion.1), channel_id=1, source_target_pairs={{0,224},{32,0},{64,32},{96,64},{128,96},{160,128},{192,160},{224,1... | collective-permute-start | bytes 786440 | tf_op jit(solution)/shard_map/ppermute | solution.py:348
  88.5 12.1 %collective-permute-start.11 = (f16[2,128,512]{2,1,0:T(8,128)(2,1)S(1)}, f16[2,128,512]{2,1,0:T(8,128)(2,1)S(1)}, u32[]{:S(2)}, u32[]{:S(2)}) collective-permute-start(f16[2,128,512]{2,1,0:T(8,128)(2,1)S(1)} %pad_maximum_fusion.2), channel_id=1, source_target_pairs={{0,32},{32,64},{64,96},{96,128},{128,160},{160,192},{192,224},{224... | collective-permute-start | bytes 786440 | tf_op jit(solution)/shard_map/ppermute | solution.py:348
  100.8 10.7 %collective-permute-start.14 = (f16[2,64,512]{2,1,0:T(8,128)(2,1)S(1)}, f16[2,64,512]{2,1,0:T(8,128)(2,1)S(1)}, u32[]{:S(2)}, u32[]{:S(2)}) collective-permute-start(f16[2,64,512]{2,1,0:T(8,128)(2,1)S(1)} %fusion.3), channel_id=1, source_target_pairs={{0,128},{32,160},{64,192},{96,224},{128,0},{160,32},{192,64},{224,... | collective-permute-start | bytes 393224 | tf_op jit(solution)/shard_map/ppermute | solution.py:348
  111.6 7.3 %collective-permute-start.15 = (f32[64,512]{1,0:T(8,128)S(1)}, f32[64,512]{1,0:T(8,128)S(1)}, u32[]{:S(2)}, u32[]{:S(2)}) collective-permute-start(f32[64,512]{1,0:T(8,128)S(1)} %get-tuple-element.51), channel_id=1, source_target_pairs={{0,2},{2,0},{1,3},{3,1},{4,6},{6,4},{5,7},{7,5},{8,10},{10,8},{9,1... | collective-permute-start | bytes 393224 | tf_op jit(solution)/shard_map/ppermute | solution.py:328

commit v7 on v6

--- a/solution.py
+++ b/solution.py
@@ -11,8 +11,8 @@
 
 D = 2048
 NZ, NY, NXH, NXL, NC = 8, 4, 2, 2, 2
-PLANE = ("xl", "y", "xh")
-OFFSETS = (0, -1, 1, -2)
+PLANE = ("xl", "xh", "y")
+OFFSETS = (0, 4, 2, -2, 1, 3, -1, -3)
 GROUP = 128
 EVERY = ("z", "y", "xh", "xl", "core")
 ROWS = 128
@@ -31,73 +31,88 @@
     return pltpu.CompilerParams(vmem_limit_bytes=mib * 1024 * 1024)
 
 
-def copies_kernel(x_ref, o_ref, sems):
-    copies = [pltpu.make_async_copy(x_ref, o_ref.at[p], sems.at[p]) for p in range(16)]
+def block_of(core, x, u):
+    return jnp.where(core == 0, x * 8 + u, u % 4 * 4 + x * 2 + u // 4)
+
+
+def arrange_kernel(place_ref, v1_ref, o_ref, sems):
+    copies = [
+        pltpu.make_async_copy(
+            v1_ref.at[block_of(place_ref[0], x, u)], o_ref.at[x, u], sems.at[x * 8 + u]
+        )
+        for x in range(NXL)
+        for u in range(8)
+    ]
     for copy in copies:
         copy.start()
     for copy in copies:
         copy.wait()
 
 
-def sixteen_copies(x):
-    return pl.pallas_call(
-        copies_kernel,
-        out_shape=jax.ShapeDtypeStruct((16, ROWS, WIDTH), x.dtype),
-        in_specs=[pl.BlockSpec(memory_space=pltpu.HBM)],
-        out_specs=pl.BlockSpec(memory_space=pltpu.HBM),
+def arranged(place, v1_all):
+    return pl.pallas_call(
+        arrange_kernel,
+        out_shape=jax.ShapeDtypeStruct((NXL, 8, ROWS, WIDTH), v1_all.dtype),
+        in_specs=[SMEM, pl.BlockSpec(memory_space=pl.ANY)],
+        out_specs=pl.BlockSpec(memory_space=pl.ANY),
         scratch_shapes=[pltpu.SemaphoreType.DMA((16,))],
         compiler_params=limit(1),
-        cost_estimate=pl.CostEstimate(flops=0, bytes_accessed=3 * 2**20, transcendentals=0),
-    )(x)
-
-
-def join_kernel(own_ref, next_ref, last_ref, two0_ref, two1_ref, v2_ref, most_ref):
-    v2_ref[:, :GROUP, :] = own_ref[...]
-    v2_ref[:, GROUP : 2 * GROUP, :] = next_ref[...]
-    v2_ref[:, 2 * GROUP : 3 * GROUP, :] = last_ref[...]
-    v2_ref[0, 3 * GROUP : 3 * GROUP + HALF, :] = two0_ref[HALF:, :]
-    v2_ref[0, 3 * GROUP + HALF :, :] = two0_ref[:HALF, :]
-    v2_ref[1, 3 * GROUP :, :] = two1_ref[...]
-    size = jnp.abs(jnp.maximum(jnp.abs(v2_ref[0]), jnp.abs(v2_ref[1])).astype(jnp.float32))
+        cost_estimate=pl.CostEstimate(flops=0, bytes_accessed=2**22, transcendentals=0),
+    )(place, v1_all)
+
+
+def join_kernel(own, four0, four1, up2, down2, up, down, v2_ref, most_ref):
+    v2_ref[:, :HALF, :] = own[...]
+    v2_ref[0, HALF : 2 * HALF, :] = four0[...]
+    v2_ref[1, HALF : 2 * HALF, :] = four1[...]
+    v2_ref[:, 2 * HALF : 3 * HALF, :] = up2[...]
+    v2_ref[:, 3 * HALF : 4 * HALF, :] = down2[...]
+    v2_ref[:, 4 * HALF : 6 * HALF, :] = up[...]
+    v2_ref[:, 6 * HALF :, :] = down[...]
+    size = jnp.maximum(jnp.abs(v2_ref[0]), jnp.abs(v2_ref[1])).astype(jnp.float32)
     most_ref[...] = jnp.max(size, axis=0, keepdims=True)
 
 
-def join(parts):
+def join(*parts):
     return pl.pallas_call(
         join_kernel,
         out_shape=(
             jax.ShapeDtypeStruct((NXL, NJ, WIDTH), jnp.bfloat16),
             jax.ShapeDtypeStruct((1, WIDTH), jnp.float32),
         ),
-        in_specs=[VMEM] * 5,
+        in_specs=[VMEM] * 7,
         out_specs=(VMEM, VMEM),
         compiler_params=limit(4),
         cost_estimate=pl.CostEstimate(flops=2**20, bytes_accessed=2**21, transcendentals=0),
     )(*parts)
 
 
-def score_kernel(part, v1_ref, v2_hbm, s_ref, v2_ref, sems):
+def score_kernel(part, place_ref, v1_ref, v2_hbm, s_ref, v2_ref, sems):
     copies = [pltpu.make_async_copy(v2_hbm.at[x], v2_ref.at[x], sems.at[x]) for x in range(NXL)]
     for copy in copies:
         copy.start()
     for copy in copies:
         copy.wait()
     contract = (((1,), (1,)), ((), ()))
-    for u in range(NP // 256):
-        rows = slice(u * 256, (u + 1) * 256)
-        users = slice(part * NP + u * 256, part * NP + (u + 1) * 256)
-        s_ref[rows, :] = lax.dot_general(
-            v1_ref[0, users, :], v2_ref[0], contract, preferred_element_type=jnp.float32
-        ) + lax.dot_general(
-            v1_ref[1, users, :], v2_ref[1], contract, preferred_element_type=jnp.float32
+    for u in range(NP // ROWS):
+        rows = slice(u * ROWS, (u + 1) * ROWS)
+        user = part * (NP // ROWS) + u
+        s_ref[rows, :] = sum(
+            lax.dot_general(
+                v1_ref[block_of(place_ref[0], x, user)],
+                v2_ref[x],
+                contract,
+                preferred_element_type=jnp.float32,
+            )
+            for x in range(NXL)
         )
 
 
-def partial_scores(part, v1_all, v2_all):
+def partial_scores(part, place, v1_all, v2_all):
     return pl.pallas_call(
         functools.partial(score_kernel, part),
         out_shape=jax.ShapeDtypeStruct((NP, NJ), jnp.float32),
-        in_specs=[VMEM, pl.BlockSpec(memory_space=pl.ANY)],
+        in_specs=[SMEM, VMEM, pl.BlockSpec(memory_space=pl.ANY)],
         out_specs=VMEM,
         scratch_shapes=[
             pltpu.VMEM((NXL, NJ, WIDTH), jnp.bfloat16),
@@ -107,7 +122,7 @@
         cost_estimate=pl.CostEstimate(
             flops=2 * NP * NJ * NXL * WIDTH, bytes_accessed=3 * 2**20, transcendentals=0
         ),
-    )(v1_all, v2_all)
+    )(place, v1_all, v2_all)
 
 
 def diagonal():
@@ -115,13 +130,18 @@
     return lax.broadcasted_iota(jnp.int32, shape, 0) == lax.broadcasted_iota(jnp.int32, shape, 1)
 
 
-def placed(z, g):
-    first = lax.rem(z + OFFSETS[g] + NZ, NZ)
-    return lax.rem(first, 4), first >= 4
+def placed(z, k):
+    plane = lax.rem(z + OFFSETS[k] + NZ, NZ)
+    half = plane // 4
+    return plane % 4, half, half != k % 2
 
 
 def turned(row, trade):
     return jnp.where(trade, pltpu.roll(row, HALF, 1), row)
+
+
+def lane_half():
+    return lax.broadcasted_iota(jnp.int32, (1, LANES), 1) // HALF
 
 
 def block_stats(own_ref, other_ref, s_ref, row_ref, col_highest, col_total):
@@ -196,9 +216,12 @@
         col_ref[1:2, :],
     )
     col_lse = col_highest + jnp.log(col_total)
-    for g in range(4):
-        row, trade = placed(place_ref[2], g)
-        pack_ref[1, pl.ds(row, 1), :] = turned(col_lse[:, g * LANES : (g + 1) * LANES], trade)
+    for k in range(NZ):
+        row, half, trade = placed(place_ref[2], k)
+        g = k // 2
+        here = turned(col_lse[:, g * LANES : (g + 1) * LANES], trade)
+        there = pack_ref[1, pl.ds(row, 1), :]
+        pack_ref[1, pl.ds(row, 1), :] = jnp.where(lane_half() == half, here, there)
     most = jnp.max(jnp.maximum(most_ref[...], most_other_ref[...]), axis=1, keepdims=True)
     most = jnp.broadcast_to(jnp.maximum(most, 1e-30), (2, LANES))
     pack_ref[0, 8:9, :] = partner_ref[...].astype(jnp.float32)
@@ -245,8 +268,13 @@
         known_ref[...] = jnp.zeros_like(known_ref)
         cols_ref[...] = merged(seen_ref[pl.ds(xl * NZ, NZ), 0:8, :])
         for g in range(4):
-            row, trade = placed(place_ref[2], g)
-            known_ref[g : g + 1, :] = turned(cols_ref[pl.ds(row, 1), :], trade)
+            row0, _, trade0 = placed(place_ref[2], 2 * g)
+            row1, _, trade1 = placed(place_ref[2], 2 * g + 1)
+            known_ref[g : g + 1, :] = jnp.where(
+                lane_half() == 0,
+                turned(cols_ref[pl.ds(row0, 1), :], trade0),
+                turned(cols_ref[pl.ds(row1, 1), :], trade1),
+            )
 
     known_ref[16:24, :] = jnp.broadcast_to(jnp.max(seen_ref[:, 9:10, :], axis=0), (8, LANES))
 
@@ -282,8 +310,8 @@
     lane = lax.broadcasted_iota(jnp.int32, (1, LANES), 1)
     index, col_lse = [], []
     for g in range(4):
-        first = lax.rem(z + OFFSETS[g] + NZ, NZ)
-        second = lax.rem(first + 4, NZ)
+        first = lax.rem(z + OFFSETS[2 * g] + NZ, NZ)
+        second = lax.rem(z + OFFSETS[2 * g + 1] + NZ, NZ)
         user = jnp.where(lane < HALF, first, second) * (NY * NXH) + uhigh
         inside = jnp.where(lane < HALF, lane, lane - HALF)
         index.append((user * ROWS + xl * HALF + inside).astype(jnp.float32))
@@ -328,12 +356,39 @@
     return lax.ppermute(x, axis, [(0, 1), (1, 0)])
 
 
+def number(z, y, xh, xl, c):
+    return (((z * NY + y) * NXH + xh) * NXL + xl) * NC + c
+
+
+def line_groups(turn):
+    alongs_y = [
+        [number(z, y, xh, xl, turn) for y in range(NY)]
+        for z in range(NZ)
+        for xl in range(NXL)
+        for xh in range(NXH)
+    ]
+    alongs_x = [
+        [number(z, y, xh, xl, 1 - turn) for xl in range(NXL) for xh in range(NXH)]
+        for z in range(NZ)
+        for y in range(NY)
+    ]
+    return alongs_y + alongs_x
+
+
+def spread(x, turn):
+    return lax.all_to_all(
+        jnp.broadcast_to(x[None], (4,) + x.shape),
+        EVERY,
+        0,
+        0,
+        axis_index_groups=line_groups(turn),
+        tiled=True,
+    )
+
+
 def stat_groups():
-    def number(z, y, xh, xl, c):
-        return (((z * NY + y) * NXH + xh) * NXL + xl) * NC + c
-
     planes = [
-        [number(z, y, xh, xl, 0) for xl in range(NXL) for y in range(NY) for xh in range(NXH)]
+        [number(z, y, xh, xl, 0) for xl in range(NXL) for xh in range(NXH) for y in range(NY)]
         for z in range(NZ)
     ]
     columns = [
@@ -362,24 +417,19 @@
     keep = jnp.where(xl == 0, view_two[:HALF], view_two[HALF:])
     give = jnp.where(xl == 0, view_two[HALF:], view_two[:HALF])
     side = swap(give, "xl")
-    copies = sixteen_copies(view_one)
-    copies, side = lax.optimization_barrier((copies, side))
+    lines = spread(view_one, 0)
     here = jnp.where(xl == 0, jnp.stack([keep, side]), jnp.stack([side, keep]))
-    pair = jnp.concatenate([here, to_plane(here, 4)], axis=1)
+    up2, down2 = to_plane(here, -2), to_plane(here, 2)
+    v1_all = spread(lines, 1).reshape(16, ROWS, WIDTH)
+    up = to_plane(jnp.concatenate([here, up2], axis=1), -1)
+    down = to_plane(jnp.concatenate([here, down2], axis=1), 1)
     v2_all, most_v2 = join(
-        [
-            pair,
-            to_plane(pair, 1),
-            to_plane(pair, -1),
-            to_plane(pair[0], -2),
-            to_plane(pair[1], 2),
-        ]
-    )
-    v1_all = lax.all_to_all(copies, PLANE, 0, 0, tiled=True).reshape(NXL, NI, WIDTH)
-
-    own0 = partial_scores(0, v1_all, v2_all)
+        here, to_plane(up2[0], -2), to_plane(down2[1], 2), up2, down2, up, down
+    )
+
+    own0 = partial_scores(0, place, v1_all, v2_all)
     other0 = swap(own0, "core")
-    own1 = partial_scores(1, v1_all, v2_all)
+    own1 = partial_scores(1, place, v1_all, v2_all)
     other1 = swap(own1, "core")
     most = jnp.concatenate([most_v2, largest(v1_all)[None]])
     most_other = swap(most, "core")
@@ -389,28 +439,12 @@
     seen = lax.all_to_all(
         pack, EVERY, 0, 0, axis_index_groups=stat_groups(), tiled=True
     )
+    v1_rows = arranged(place, v1_all).reshape(NXL, NI, WIDTH)
     known = merge_stats(place, seen)
     coupling, give_one, give_two, take_one, take_two = coupling_of(
         place, scores0, scores1, known, swap(known, "core")
     )
 
-    part_two = [
-        (
-            lax.dot_general(
-                coupling, v1_all[x], (((0,), (0,)), ((), ())), preferred_element_type=jnp.float32
-            )
-            * give_two
-        ).astype(jnp.float16)
-        for x in range(NXL)
-    ]
-    coupling, part_two = lax.optimization_barrier((coupling, part_two))
-
-    def group(g):
-        return jnp.stack([part[g * GROUP : (g + 1) * GROUP] for part in part_two])
-
-    before, after = to_plane(group(1), -1), to_plane(group(2), 1)
-    two0 = to_plane(part_two[0][3 * GROUP :], 2)
-    two1 = to_plane(part_two[1][3 * GROUP :], -2)
     part_one = (
         lax.dot_general(
             jnp.broadcast_to(coupling[None], (NXL, NI, NJ)),
@@ -420,11 +454,34 @@
         )
         * give_one
     ).astype(jnp.float16)
+    coupling, part_one = lax.optimization_barrier((coupling, part_one))
     one_parts = lax.all_to_all(part_one.reshape(16, ROWS, WIDTH), PLANE, 0, 0, tiled=True)
-    two = jnp.stack([jnp.concatenate([two0[HALF:], two0[:HALF]]), two1])
-    joined = sum(part.astype(jnp.float32) for part in (group(0), before, after, two))
-    far = to_plane((joined[:, HALF:] * 0.25).astype(jnp.float16), 4)
-    total = (joined[:, :HALF] + 4.0 * far.astype(jnp.float32)) * take_two
+    part_two = [
+        (
+            lax.dot_general(
+                coupling, v1_rows[x], (((0,), (0,)), ((), ())), preferred_element_type=jnp.float32
+            )
+            * give_two
+        ).astype(jnp.float16)
+        for x in range(NXL)
+    ]
+
+    def blocks(start, stop):
+        return jnp.stack([part[start * HALF : stop * HALF] for part in part_two])
+
+    from_below, from_above = to_plane(blocks(4, 6), 1), to_plane(blocks(6, 8), -1)
+    four0 = to_plane(part_two[0][HALF : 2 * HALF], 2)
+    four1 = to_plane(part_two[1][HALF : 2 * HALF], -2)
+    wide = [x.astype(jnp.float32) for x in (from_below, from_above, four0, four1)]
+    up2 = blocks(2, 3).astype(jnp.float32) + wide[0][:, HALF:]
+    up2 = jnp.stack([up2[0] + wide[2], up2[1]])
+    down2 = blocks(3, 4).astype(jnp.float32) + wide[1][:, HALF:]
+    down2 = jnp.stack([down2[0], down2[1] + wide[3]])
+    from_up = to_plane((up2 * 0.25).astype(jnp.float16), 2)
+    from_down = to_plane((down2 * 0.25).astype(jnp.float16), -2)
+    total = blocks(0, 1).astype(jnp.float32) + wide[0][:, :HALF] + wide[1][:, :HALF]
+    total = total + 4.0 * (from_up.astype(jnp.float32) + from_down.astype(jnp.float32))
+    total = total * take_two
     stay = jnp.where(xl == 0, total[0], total[1])
     come = swap(jnp.where(xl == 0, total[1], total[0]), "xl")
     grad_one = jnp.sum(one_parts.astype(jnp.float32) * take_one, axis=0)

time: 122 us -> 127 us (1.041)
  waiting for transfers between devices: 38 us -> 43.1 us
  local copies, waits for them, and re-layouts: 4.36 us -> 7.72 us
  starting transfers between devices: 44.4 us -> 42.7 us
    ppermute x6, waiting for transfers between devices: 3.2 us -> 14.7 us  [swap(): return lax.ppermute(x, axis, [(0, 1), (1, 0)])]
    ppermute x10 -> x12, waiting for transfers between devices: 32.5 us -> 23.8 us  [to_plane(): return lax.ppermute(x, 'z', [(z, (z + dz) % NZ) for z in range(NZ)])]
    ppermute x6, starting transfers between devices: 7.16 us -> 3.91 us  [swap(): return lax.ppermute(x, axis, [(0, 1), (1, 0)])]
    all_to_all x1 -> x2, starting transfers between devices: 7.45 us -> 10.4 us  [the longest x1 5.43 us: on_device(): lax.all_to_all(pack, EVERY, 0, 0, axis_index_groups=stat_groups(), tiled=...]
    broadcast_in_dim x0 -> x2, local copies, waits for them, and re-layouts: none -> 2.49 us  [spread(): jnp.broadcast_to(x[None], (4,) + x.shape)]
    ppermute x10 -> x12, starting transfers between devices: 24.6 us -> 22.2 us  [to_plane(): return lax.ppermute(x, 'z', [(z, (z + dz) % NZ) for z in range(NZ)])]
    pallas_call x2, Pallas kernels: 2.65 us -> 4.2 us  [partial_scores(): pl.pallas_call(functools.partial(score_kernel, part), out_shape=jax.Shape...]
    pallas_call x1, Pallas kernels: 2.15 us -> 0.61 us  [first_stats(): pl.pallas_call(first_kernel, out_shape=(jax.ShapeDtypeStruct((NP, NJ), jn...]
  transfers between devices with their start and end apart: 18 -> 21, of which waited for: 8 -> 13; matrix products, arithmetic and copies ran while one was open for 2% -> 3% of each run, Pallas kernels for 5% -> 5%
where the time goes in v7:
time: 127 us; the launch traced here: 126 us
  waiting for transfers between devices  43.1 us (34%)
  starting transfers between devices  42.7 us (34%)
  blocking collectives  12.3 us (10%)
  Pallas kernels  12.3 us (10%)
  local copies, waits for them, and re-layouts  7.72 us (6%)
  matrix products  4.1 us (3%)
  other arithmetic  2.76 us (2%)
    ppermute x12, waiting for transfers between devices, to_plane(): return lax.ppermute(x, 'z', [(z, (z + dz) % NZ) for z in range(NZ)])  23.8 us
    ppermute x12, starting transfers between devices, to_plane(): return lax.ppermute(x, 'z', [(z, (z + dz) % NZ) for z in range(NZ)])  22.2 us
    ppermute x6, waiting for transfers between devices, swap(): return lax.ppermute(x, axis, [(0, 1), (1, 0)])  14.7 us
    all_to_all x1, blocking collectives, spread(): lax.all_to_all(jnp.broadcast_to(x[None], (4,) + x.shape), EVERY, 0, 0, ax...  12.3 us
    all_to_all x1, starting transfers between devices, on_device(): lax.all_to_all(part_one.reshape(16, ROWS, WIDTH), PLANE, 0, 0, tiled=True)  6.24 us
    all_to_all x1, starting transfers between devices, on_device(): lax.all_to_all(pack, EVERY, 0, 0, axis_index_groups=stat_groups(), tiled=...  5.43 us
    all_to_all x1, starting transfers between devices, spread(): lax.all_to_all(jnp.broadcast_to(x[None], (4,) + x.shape), EVERY, 0, 0, ax...  4.93 us
    pallas_call x2, Pallas kernels, partial_scores(): pl.pallas_call(functools.partial(score_kernel, part), out_shape=jax.Shape...  4.2 us
  transfers between devices with their start and end apart: 21, of which 13 were waited for; matrix products, arithmetic and copies ran while one was open for 3% of the time, Pallas kernels for 5%

profile of v7, /device:TPU:4, one launch (start us, length us, event | category | flops | bytes accessed | tf_op | source)
XLA Modules:
  0.0 125.9 jit_solution(2099799870898015784)
XLA Ops:
  0.6 0.9 broadcast_in_dim.6
  1.6 12.3 %all_to_all.20 = bf16[4,128,512]{2,1,0:T(8,128)(2,1)S(1)} all-to-all(bf16[4,128,512]{2,1,0:T(8,128)(2,1)S(1)} %broadcast_in_dim.6), channel_id=1, replica_groups={{0,8,16,24},{4,12,20,28},{2,10,18,26},{6,14,22,30},{32,40,48,56},{36,44..., dimensions={0} | all-to-all | bytes 1048576 | tf_op jit(solution)/shard_map/all_to_all | solution.py:379
  13.9 1.5 %broadcast_in_dim.7 = bf16[4,4,128,512]{3,2,1,0:T(8,128)(2,1)} broadcast(bf16[4,128,512]{2,1,0:T(8,128)(2,1)S(1)} %all_to_all.20), dimensions={1,2,3} | broadcast | bytes 2621440 | tf_op jit(solution)/shard_map/broadcast_in_dim | solution.py:380
  15.5 4.9 %all-to-all-start.1 = ((bf16[4,4,128,512]{3,2,1,0:T(8,128)(2,1)}), bf16[4,4,128,512]{3,2,1,0:T(8,128)(2,1)S(1)}, u32[]{:S(2)}, u32[]{:S(2)}) async-start(bf16[4,4,128,512]{3,2,1,0:T(8,128)(2,1)} %broadcast_in_dim.7), calls=%async_computation.1 | async-start | bytes 4194304 | tf_op jit(solution)/shard_map/all_to_all | solution.py:379
  20.4 1.3 collective-permute-start
  21.7 13.6 %collective-permute-done = bf16[64,512]{1,0:T(8,128)(2,1)S(1)} collective-permute-done((bf16[64,512]{1,0:T(8,128)(2,1)S(1)}, bf16[64,512]{1,0:T(8,128)(2,1)S(1)}, u32[]{:S(2)}, u32[]{:S(2)}) %collective-permute-start) | collective-permute-done | bytes 65568 | tf_op jit(solution)/shard_map/ppermute | solution.py:356
  35.3 3.3 %collective-permute-start.3 = (bf16[2,64,512]{2,1,0:T(8,128)(2,1)S(1)}, bf16[2,64,512]{2,1,0:T(8,128)(2,1)S(1)}, u32[]{:S(2)}, u32[]{:S(2)}) collective-permute-start(bf16[2,64,512]{2,1,0:T(8,128)(2,1)S(1)} %maximum_select_fusion.1.own), channel_id=1, source_target_pairs={{0,64},{32,96},{64,128},{96,160},{128,192},{160,224},{192,0},{224,... | collective-permute-start | bytes 393224 | tf_op jit(solution)/shard_map/ppermute | solution.py:403
  38.7 3.1 %collective-permute-start.1 = (bf16[2,64,512]{2,1,0:T(8,128)(2,1)S(1)}, bf16[2,64,512]{2,1,0:T(8,128)(2,1)S(1)}, u32[]{:S(2)}, u32[]{:S(2)}) collective-permute-start(bf16[2,64,512]{2,1,0:T(8,128)(2,1)S(1)} %maximum_select_fusion.1.own), channel_id=1, source_target_pairs={{0,192},{32,224},{64,0},{96,32},{128,64},{160,96},{192,128},{224,1... | collective-permute-start | bytes 393224 | tf_op jit(solution)/shard_map/ppermute | solution.py:403
  41.8 2.9 %collective-permute-done.3.down2 = bf16[2,64,512]{2,1,0:T(8,128)(2,1)S(1)} collective-permute-done((bf16[2,64,512]{2,1,0:T(8,128)(2,1)S(1)}, bf16[2,64,512]{2,1,0:T(8,128)(2,1)S(1)}, u32[]{:S(2)}, u32[]{:S(2)}) %collective-permute-start.3) | collective-permute-done | bytes 131104 | tf_op jit(solution)/shard_map/ppermute | solution.py:403
  44.8 1.6 %collective-permute-start.4 = (bf16[64,512]{1,0:T(8,128)(2,1)S(1)}, bf16[64,512]{1,0:T(8,128)(2,1)S(1)}, u32[]{:S(2)}, u32[]{:S(2)}) collective-permute-start(bf16[64,512]{1,0:T(8,128)(2,1)S(1)} %slice_bitcast_fusion.12), channel_id=1, source_target_pairs={{0,64},{32,96},{64,128},{96,160},{128,192},{160,224},{192,0},{224,... | collective-permute-start | bytes 196616 | tf_op jit(solution)/shard_map/ppermute | solution.py:403
  46.4 1.1 collective-permute-done.1.up2
  47.5 0.1 collective-permute-start.6
  47.6 3.2 %collective-permute-start.5 = (bf16[2,128,512]{2,1,0:T(8,128)(2,1)S(1)}, bf16[2,128,512]{2,1,0:T(8,128)(2,1)S(1)}, u32[]{:S(2)}, u32[]{:S(2)}) collective-permute-start(bf16[2,128,512]{2,1,0:T(8,128)(2,1)S(1)} %get-tuple-element.51), channel_id=1, source_target_pairs={{0,224},{32,0},{64,32},{96,64},{128,96},{160,128},{192,160},{224,1... | collective-permute-start | bytes 786440 | tf_op jit(solution)/shard_map/ppermute | solution.py:403
  50.9 1.6 %collective-permute-start.2 = (bf16[64,512]{1,0:T(8,128)(2,1)S(1)}, bf16[64,512]{1,0:T(8,128)(2,1)S(1)}, u32[]{:S(2)}, u32[]{:S(2)}) collective-permute-start(bf16[64,512]{1,0:T(8,128)(2,1)S(1)} %slice_bitcast_fusion.13), channel_id=1, source_target_pairs={{0,192},{32,224},{64,0},{96,32},{128,64},{160,96},{192,128},{224,1... | collective-permute-start | bytes 196616 | tf_op jit(solution)/shard_map/ppermute | solution.py:403
  52.4 0.1 pad_add_fusion.place_ref
  52.5 7.0 %collective-permute-done.2.four0 = bf16[64,512]{1,0:T(8,128)(2,1)S(1)} collective-permute-done((bf16[64,512]{1,0:T(8,128)(2,1)S(1)}, bf16[64,512]{1,0:T(8,128)(2,1)S(1)}, u32[]{:S(2)}, u32[]{:S(2)}) %collective-permute-start.2) | collective-permute-done | bytes 65568 | tf_op jit(solution)/shard_map/ppermute | solution.py:403
  59.5 0.0 collective-permute-done.6.down
  59.5 0.2 shard_map.50
  59.7 2.1 %shard_map.51.own_ref = f32[512,512]{1,0:T(8,128)S(1)} custom-call(s32[4]{0:T(128)S(1)} %pad_add_fusion.place_ref, bf16[16,128,512]{2,1,0:T(8,128)(2,1)S(1)} %bitcast.66, bf16[2,512,512]{2,1,0:T(8,128)(2,1)S(1)} %get-tuple-element.18.v2_hbm), custom_call_target="tpu_custom_call" | custom-call | flops 536870912 | bytes 3145728 | tf_op jit(solution)/shard_map/pallas_call | solution.py:112
  61.8 0.1 collective-permute-start.7
  61.9 2.1 %shard_map.53.own_ref = f32[512,512]{1,0:T(8,128)S(1)} custom-call(s32[4]{0:T(128)S(1)} %pad_add_fusion.place_ref, bf16[16,128,512]{2,1,0:T(8,128)(2,1)S(1)} %bitcast.67, bf16[2,512,512]{2,1,0:T(8,128)(2,1)S(1)} %get-tuple-element.18.v2_hbm), custom_call_target="tpu_custom_call" | custom-call | flops 536870912 | bytes 3145728 | tf_op jit(solution)/shard_map/pallas_call | solution.py:112
  64.0 0.0 copy-start.5
  64.0 0.6 collective-permute-start.8
  64.6 0.2 abs_reduce_fusion
  64.9 0.1 collective-permute-start.9
  65.0 0.6 shard_map.52
  65.6 1.0 copy-done.1
  66.6 0.3 collective-permute-done.9.most_other_ref
  66.9 1.8 %shard_map.54 = (f32[512,512]{1,0:T(8,128)S(1)}, f32[16,16,128]{2,1,0:T(8,128)}) custom-call(s32[4]{0:T(128)S(1)} %pad_add_fusion.place_ref, f32[512,512]{1,0:T(8,128)S(1)} %shard_map.53.own_ref, f32[512,512]{1,0:T(8,128)S(1)} %collective-permute-done.8.other_ref, f32[4,128]{1,0:T(4,128)S(1)} %get-tuple-element.20.first_ref, ...), custom_call_target="tpu_custom_call" | custom-call | flops 2621440 | bytes 3145728 | tf_op jit(solution)/shard_map/pallas_call | solution.py:236
  68.8 1.0 copy-done.3
  69.7 5.4 %all-to-all-start.2 = ((f32[16,16,128]{2,1,0:T(8,128)}), f32[16,16,128]{2,1,0:T(8,128)S(1)}, u32[]{:S(2)}, u32[]{:S(2)}) async-start(f32[16,16,128]{2,1,0:T(8,128)} %get-tuple-element.24), calls=%async_computation.2 | async-start | bytes 262144 | tf_op jit(solution)/shard_map/all_to_all | solution.py:439
  75.2 3.4 %shard_map.57 = bf16[2,8,128,512]{3,2,1,0:T(8,128)(2,1)S(1)} custom-call(s32[4]{0:T(128)S(1)} %pad_add_fusion.place_ref, bf16[16,128,512]{2,1,0:T(8,128)(2,1)S(1)} %bitcast.68), custom_call_target="tpu_custom_call" | custom-call | bytes 4194304 | tf_op jit(solution)/shard_map/pallas_call | solution.py:53
  78.6 1.3 %copy-done = bf16[2,8,128,512]{3,2,1,0:T(8,128)(2,1)} copy-done((bf16[2,8,128,512]{3,2,1,0:T(8,128)(2,1)}, bf16[2,8,128,512]{3,2,1,0:T(8,128)(2,1)S(1)}, u32[]{:S(2)}) %copy-start) | copy-done | bytes 2097176
  80.0 0.8 all-to-all-done.2.seen_ref
  80.8 0.6 shard_map.55.known_ref
  81.4 0.6 collective-permute-start.10
  82.0 1.7 %fusion.11 = (bf16[1,8,128,512]{3,2,1,0:T(8,128)(2,1)S(1)}, bf16[1,8,128,512]{3,2,1,0:T(8,128)(2,1)S(1)}) fusion(bf16[2,8,128,512]{3,2,1,0:T(8,128)(2,1)} %copy-done), kind=kLoop, calls=%fused_computation.48 | loop fusion | bytes 4194304 | tf_op jit(solution)/shard_map/slice | solution.py:462
  83.7 1.4 %shard_map.56 = (bf16[1024,512]{1,0:T(8,128)(2,1)S(1)}, f32[1,512]{1,0:T(1,128)S(1)}, f32[1,512]{1,0:T(1,128)S(1)}, f32[1,512]{1,0:T(1,128)S(1)}, f32[1,512]{1,0:T(1,128)S(1)}) custom-call(s32[4]{0:T(128)S(1)} %pad_add_fusion.place_ref, f32[512,512]{1,0:T(8,128)S(1)} %copy-done.2, f32[512,512]{1,0:T(8,128)S(1)} %copy-done.4, ...), custom_call_target="tpu_custom_call" | custom-call | flops 4194304 | bytes 3145728 | tf_op jit(solution)/shard_map/pallas_call | solution.py:340
  85.1 2.6 %multiply_convert_fusion = f16[2,1024,512]{2,1,0:T(8,128)(2,1)} fusion(bf16[2,512,512]{2,1,0:T(8,128)(2,1)S(1)} %get-tuple-element.18.v2_hbm, f32[512]{0:T(512)S(1)} %bitcast.74, bf16[1024,512]{1,0:T(8,128)(2,1)S(1)} %get-tuple-element.27), kind=kOutput, calls=%fused_computation.1 | convolution fusion | flops 1075838976 | bytes 4196352 | tf_op jit(solution)/shard_map/dot_general | solution.py:449
  87.8 0.7 fusion.1
  88.5 0.7 fusion
  89.3 6.2 %all-to-all-start.3 = ((f16[16,128,512]{2,1,0:T(8,128)(2,1)}), f16[16,128,512]{2,1,0:T(8,128)(2,1)S(1)}, u32[]{:S(2)}, u32[]{:S(2)}) async-start(f16[16,128,512]{2,1,0:T(8,128)(2,1)} %bitcast.75), calls=%async_computation.3 | async-start | bytes 4194304 | tf_op jit(solution)/shard_map/all_to_all | solution.py:458
  95.6 0.1 slice_bitcast_fusion.4
  95.7 0.1 pad_maximum_fusion.3
  95.7 1.0 collective-permute-start.12
  96.8 0.9 collective-permute-start.15
  97.7 2.1 %collective-permute-start.13 = (f16[64,512]{1,0:T(8,128)(2,1)S(1)}, f16[64,512]{1,0:T(8,128)(2,1)S(1)}, u32[]{:S(2)}, u32[]{:S(2)}) collective-permute-start(f16[64,512]{1,0:T(8,128)(2,1)S(1)} %get-tuple-element.38), channel_id=1, source_target_pairs={{0,64},{32,96},{64,128},{96,160},{128,192},{160,224},{192,0},{224,... | collective-permute-start | bytes 196616 | tf_op jit(solution)/shard_map/ppermute | solution.py:403
  99.8 0.1 pad_maximum_fusion.2
  99.9 1.1 collective-permute-start.11
  101.0 4.2 %collective-permute-done.12 = f16[2,128,512]{2,1,0:T(8,128)(2,1)S(1)} collective-permute-done((f16[2,128,512]{2,1,0:T(8,128)(2,1)S(1)}, f16[2,128,512]{2,1,0:T(8,128)(2,1)S(1)}, u32[]{:S(2)}, u32[]{:S(2)}) %collective-permute-start.12) | collective-permute-done | bytes 262176 | tf_op jit(solution)/shard_map/ppermute | solution.py:403
  105.2 0.1 convert_element_type.65
  105.3 0.7 collective-permute-done.15
  106.1 2.9 %collective-permute-start.16 = (f16[2,64,512]{2,1,0:T(8,128)(2,1)S(1)}, f16[2,64,512]{2,1,0:T(8,128)(2,1)S(1)}, u32[]{:S(2)}, u32[]{:S(2)}) collective-permute-start(f16[2,64,512]{2,1,0:T(8,128)(2,1)S(1)} %fusion.6), channel_id=1, source_target_pairs={{0,192},{32,224},{64,0},{96,32},{128,64},{160,96},{192,128},{224,1... | collective-permute-start | bytes 393224 | tf_op jit(solution)/shard_map/ppermute | solution.py:403
  108.9 0.8 collective-permute-done.11
  109.7 0.1 convert_element_type.64
  109.9 1.2 collective-permute-start.14
  111.1 3.5 %collective-permute-done.16 = f16[2,64,512]{2,1,0:T(8,128)(2,1)S(1)} collective-permute-done((f16[2,64,512]{2,1,0:T(8,128)(2,1)S(1)}, f16[2,64,512]{2,1,0:T(8,128)(2,1)S(1)}, u32[]{:S(2)}, u32[]{:S(2)}) %collective-permute-start.16) | collective-permute-done | bytes 131104 | tf_op jit(solution)/shard_map/ppermute | solution.py:403
  114.6 3.6 %collective-permute-done.14 = f16[2,64,512]{2,1,0:T(8,128)(2,1)S(1)} collective-permute-done((f16[2,64,512]{2,1,0:T(8,128)(2,1)S(1)}, f16[2,64,512]{2,1,0:T(8,128)(2,1)S(1)}, u32[]{:S(2)}, u32[]{:S(2)}) %collective-permute-start.14) | collective-permute-done | bytes 131104 | tf_op jit(solution)/shard_map/ppermute | solution.py:403
  118.2 0.1 fusion.4
  118.3 1.3 %collective-permute-start.17 = (f32[64,512]{1,0:T(8,128)S(1)}, f32[64,512]{1,0:T(8,128)S(1)}, u32[]{:S(2)}, u32[]{:S(2)}) collective-permute-start(f32[64,512]{1,0:T(8,128)S(1)} %get-tuple-element.49), channel_id=1, source_target_pairs={{0,2},{2,0},{1,3},{3,1},{4,6},{6,4},{5,7},{7,5},{8,10},{10,8},{9,1... | collective-permute-start | bytes 393224 | tf_op jit(solution)/shard_map/ppermute | solution.py:356
  119.6 3.8 %all-to-all-done.3 = f16[16,128,512]{2,1,0:T(8,128)(2,1)S(1)} async-done(((f16[16,128,512]{2,1,0:T(8,128)(2,1)}), f16[16,128,512]{2,1,0:T(8,128)(2,1)S(1)}, u32[]{:S(2)}, u32[]{:S(2)}) %all-to-all-start.3) | async-done | bytes 2097184 | tf_op jit(solution)/shard_map/all_to_all | solution.py:458
  123.3 1.1 multiply_reduce_fusion
  124.5 0.7 collective-permute-done.17
  125.2 0.7 maximum_select_fusion
  (35 shorter events, 0.4 us)
Async XLA Ops:
  15.5 4.9 %copy-start.6 = (bf16[128,512]{1,0:T(8,128)(2,1)S(1)}, bf16[128,512]{1,0:T(8,128)(2,1)}, u32[]{:S(2)}) copy-start(bf16[128,512]{1,0:T(8,128)(2,1)} %param.4) | copy-start | bytes 393220
  15.5 44.2 %all-to-all-start.1 = ((bf16[4,4,128,512]{3,2,1,0:T(8,128)(2,1)}), bf16[4,4,128,512]{3,2,1,0:T(8,128)(2,1)S(1)}, u32[]{:S(2)}, u32[]{:S(2)}) async-start(bf16[4,4,128,512]{3,2,1,0:T(8,128)(2,1)} %broadcast_in_dim.7), calls=%async_computation.1 | async-start | bytes 4194304 | tf_op jit(solution)/shard_map/all_to_all | solution.py:379
  20.4 14.9 %collective-permute-start = (bf16[64,512]{1,0:T(8,128)(2,1)S(1)}, bf16[64,512]{1,0:T(8,128)(2,1)S(1)}, u32[]{:S(2)}, u32[]{:S(2)}) collective-permute-start(bf16[64,512]{1,0:T(8,128)(2,1)S(1)} %get-tuple-element.53), channel_id=1, source_target_pairs={{0,2},{2,0},{1,3},{3,1},{4,6},{6,4},{5,7},{7,5},{8,10},{10,8},{9,1... | collective-permute-start | bytes 196616 | tf_op jit(solution)/shard_map/ppermute | solution.py:356
  35.3 9.4 %collective-permute-start.3 = (bf16[2,64,512]{2,1,0:T(8,128)(2,1)S(1)}, bf16[2,64,512]{2,1,0:T(8,128)(2,1)S(1)}, u32[]{:S(2)}, u32[]{:S(2)}) collective-permute-start(bf16[2,64,512]{2,1,0:T(8,128)(2,1)S(1)} %maximum_select_fusion.1.own), channel_id=1, source_target_pairs={{0,64},{32,96},{64,128},{96,160},{128,192},{160,224},{192,0},{224,... | collective-permute-start | bytes 393224 | tf_op jit(solution)/shard_map/ppermute | solution.py:403
  38.7 8.8 %collective-permute-start.1 = (bf16[2,64,512]{2,1,0:T(8,128)(2,1)S(1)}, bf16[2,64,512]{2,1,0:T(8,128)(2,1)S(1)}, u32[]{:S(2)}, u32[]{:S(2)}) collective-permute-start(bf16[2,64,512]{2,1,0:T(8,128)(2,1)S(1)} %maximum_select_fusion.1.own), channel_id=1, source_target_pairs={{0,192},{32,224},{64,0},{96,32},{128,64},{160,96},{192,128},{224,1... | collective-permute-start | bytes 393224 | tf_op jit(solution)/shard_map/ppermute | solution.py:403
  44.8 7.8 %collective-permute-start.4 = (bf16[64,512]{1,0:T(8,128)(2,1)S(1)}, bf16[64,512]{1,0:T(8,128)(2,1)S(1)}, u32[]{:S(2)}, u32[]{:S(2)}) collective-permute-start(bf16[64,512]{1,0:T(8,128)(2,1)S(1)} %slice_bitcast_fusion.12), channel_id=1, source_target_pairs={{0,64},{32,96},{64,128},{96,160},{128,192},{160,224},{192,0},{224,... | collective-permute-start | bytes 196616 | tf_op jit(solution)/shard_map/ppermute | solution.py:403
  47.5 12.0 %collective-permute-start.6 = (bf16[2,128,512]{2,1,0:T(8,128)(2,1)S(1)}, bf16[2,128,512]{2,1,0:T(8,128)(2,1)S(1)}, u32[]{:S(2)}, u32[]{:S(2)}) collective-permute-start(bf16[2,128,512]{2,1,0:T(8,128)(2,1)S(1)} %get-tuple-element.50), channel_id=1, source_target_pairs={{0,32},{32,64},{64,96},{96,128},{128,160},{160,192},{192,224},{224... | collective-permute-start | bytes 786440 | tf_op jit(solution)/shard_map/ppermute | solution.py:403
  47.6 11.9 %collective-permute-start.5 = (bf16[2,128,512]{2,1,0:T(8,128)(2,1)S(1)}, bf16[2,128,512]{2,1,0:T(8,128)(2,1)S(1)}, u32[]{:S(2)}, u32[]{:S(2)}) collective-permute-start(bf16[2,128,512]{2,1,0:T(8,128)(2,1)S(1)} %get-tuple-element.51), channel_id=1, source_target_pairs={{0,224},{32,0},{64,32},{96,64},{128,96},{160,128},{192,160},{224,1... | collective-permute-start | bytes 786440 | tf_op jit(solution)/shard_map/ppermute | solution.py:403
  50.9 8.7 %collective-permute-start.2 = (bf16[64,512]{1,0:T(8,128)(2,1)S(1)}, bf16[64,512]{1,0:T(8,128)(2,1)S(1)}, u32[]{:S(2)}, u32[]{:S(2)}) collective-permute-start(bf16[64,512]{1,0:T(8,128)(2,1)S(1)} %slice_bitcast_fusion.13), channel_id=1, source_target_pairs={{0,192},{32,224},{64,0},{96,32},{128,64},{160,96},{192,128},{224,1... | collective-permute-start | bytes 196616 | tf_op jit(solution)/shard_map/ppermute | solution.py:403
  61.8 3.2 %collective-permute-start.7 = (f32[512,512]{1,0:T(8,128)S(1)}, f32[512,512]{1,0:T(8,128)S(1)}, u32[]{:S(2)}, u32[]{:S(2)}) collective-permute-start(f32[512,512]{1,0:T(8,128)S(1)} %shard_map.51.own_ref), channel_id=1, source_target_pairs={{0,1},{1,0},{2,3},{3,2},{4,5},{5,4},{6,7},{7,6},{8,9},{9,8},{10,11... | collective-permute-start | bytes 3145736 | tf_op jit(solution)/shard_map/ppermute | solution.py:356
  64.0 2.9 %copy-start.5 = (s32[128]{0:T(128)S(1)}, s32[128]{0:T(128)}, u32[]{:S(2)}) copy-start(s32[128]{0:T(128)} %param.5) | copy-start | bytes 1540
  64.0 2.9 %collective-permute-start.8 = (f32[512,512]{1,0:T(8,128)S(1)}, f32[512,512]{1,0:T(8,128)S(1)}, u32[]{:S(2)}, u32[]{:S(2)}) collective-permute-start(f32[512,512]{1,0:T(8,128)S(1)} %shard_map.53.own_ref), channel_id=1, source_target_pairs={{0,1},{1,0},{2,3},{3,2},{4,5},{5,4},{6,7},{7,6},{8,9},{9,8},{10,11... | collective-permute-start | bytes 3145736 | tf_op jit(solution)/shard_map/ppermute | solution.py:356
  64.9 2.0 %collective-permute-start.9 = (f32[2,512]{1,0:T(2,128)S(1)}, f32[2,512]{1,0:T(2,128)S(1)}, u32[]{:S(2)}, u32[]{:S(2)}) collective-permute-start(f32[2,512]{1,0:T(2,128)S(1)} %pad_maximum_fusion.4.most_ref), channel_id=1, source_target_pairs={{0,1},{1,0},{2,3},{3,2},{4,5},{5,4},{6,7},{7,6},{8,9},{9,8},{10,11... | collective-permute-start | bytes 12296 | tf_op jit(solution)/shard_map/ppermute | solution.py:356
  65.6 1.0 copy-start.1
  68.8 1.0 copy-start.3
  69.7 11.0 %all-to-all-start.2 = ((f32[16,16,128]{2,1,0:T(8,128)}), f32[16,16,128]{2,1,0:T(8,128)S(1)}, u32[]{:S(2)}, u32[]{:S(2)}) async-start(f32[16,16,128]{2,1,0:T(8,128)} %get-tuple-element.24), calls=%async_computation.2 | async-start | bytes 262144 | tf_op jit(solution)/shard_map/all_to_all | solution.py:439
  78.6 1.3 %copy-start = (bf16[2,8,128,512]{3,2,1,0:T(8,128)(2,1)}, bf16[2,8,128,512]{3,2,1,0:T(8,128)(2,1)S(1)}, u32[]{:S(2)}) copy-start(bf16[2,8,128,512]{3,2,1,0:T(8,128)(2,1)S(1)} %shard_map.57) | copy-start | bytes 6291460
  81.4 2.3 %copy-start.2 = (f32[512,512]{1,0:T(8,128)S(1)}, f32[512,512]{1,0:T(8,128)}, u32[]{:S(2)}) copy-start(f32[512,512]{1,0:T(8,128)} %copy-done.1) | copy-start | bytes 3145732
  81.4 2.3 %copy-start.4 = (f32[512,512]{1,0:T(8,128)S(1)}, f32[512,512]{1,0:T(8,128)}, u32[]{:S(2)}) copy-start(f32[512,512]{1,0:T(8,128)} %copy-done.3) | copy-start | bytes 3145732
  81.4 2.3 %collective-permute-start.10 = (f32[24,128]{1,0:T(8,128)S(1)}, f32[24,128]{1,0:T(8,128)S(1)}, u32[]{:S(2)}, u32[]{:S(2)}) collective-permute-start(f32[24,128]{1,0:T(8,128)S(1)} %shard_map.55.known_ref), channel_id=1, source_target_pairs={{0,1},{1,0},{2,3},{3,2},{4,5},{5,4},{6,7},{7,6},{8,9},{9,8},{10,11... | collective-permute-start | bytes 36872 | tf_op jit(solution)/shard_map/ppermute | solution.py:356
  89.3 34.1 %all-to-all-start.3 = ((f16[16,128,512]{2,1,0:T(8,128)(2,1)}), f16[16,128,512]{2,1,0:T(8,128)(2,1)S(1)}, u32[]{:S(2)}, u32[]{:S(2)}) async-start(f16[16,128,512]{2,1,0:T(8,128)(2,1)} %bitcast.75), calls=%async_computation.3 | async-start | bytes 4194304 | tf_op jit(solution)/shard_map/all_to_all | solution.py:458
  95.7 9.5 %collective-permute-start.12 = (f16[2,128,512]{2,1,0:T(8,128)(2,1)S(1)}, f16[2,128,512]{2,1,0:T(8,128)(2,1)S(1)}, u32[]{:S(2)}, u32[]{:S(2)}) collective-permute-start(f16[2,128,512]{2,1,0:T(8,128)(2,1)S(1)} %pad_maximum_fusion.3), channel_id=1, source_target_pairs={{0,224},{32,0},{64,32},{96,64},{128,96},{160,128},{192,160},{224,1... | collective-permute-start | bytes 786440 | tf_op jit(solution)/shard_map/ppermute | solution.py:403
  96.8 9.2 %collective-permute-start.15 = (f16[64,512]{1,0:T(8,128)(2,1)S(1)}, f16[64,512]{1,0:T(8,128)(2,1)S(1)}, u32[]{:S(2)}, u32[]{:S(2)}) collective-permute-start(f16[64,512]{1,0:T(8,128)(2,1)S(1)} %get-tuple-element.41), channel_id=1, source_target_pairs={{0,192},{32,224},{64,0},{96,32},{128,64},{160,96},{192,128},{224,1... | collective-permute-start | bytes 196616 | tf_op jit(solution)/shard_map/ppermute | solution.py:403
  97.7 12.1 %collective-permute-start.13 = (f16[64,512]{1,0:T(8,128)(2,1)S(1)}, f16[64,512]{1,0:T(8,128)(2,1)S(1)}, u32[]{:S(2)}, u32[]{:S(2)}) collective-permute-start(f16[64,512]{1,0:T(8,128)(2,1)S(1)} %get-tuple-element.38), channel_id=1, source_target_pairs={{0,64},{32,96},{64,128},{96,160},{128,192},{160,224},{192,0},{224,... | collective-permute-start | bytes 196616 | tf_op jit(solution)/shard_map/ppermute | solution.py:403
  99.9 9.8 %collective-permute-start.11 = (f16[2,128,512]{2,1,0:T(8,128)(2,1)S(1)}, f16[2,128,512]{2,1,0:T(8,128)(2,1)S(1)}, u32[]{:S(2)}, u32[]{:S(2)}) collective-permute-start(f16[2,128,512]{2,1,0:T(8,128)(2,1)S(1)} %pad_maximum_fusion.2), channel_id=1, source_target_pairs={{0,32},{32,64},{64,96},{96,128},{128,160},{160,192},{192,224},{224... | collective-permute-start | bytes 786440 | tf_op jit(solution)/shard_map/ppermute | solution.py:403
  106.1 8.5 %collective-permute-start.16 = (f16[2,64,512]{2,1,0:T(8,128)(2,1)S(1)}, f16[2,64,512]{2,1,0:T(8,128)(2,1)S(1)}, u32[]{:S(2)}, u32[]{:S(2)}) collective-permute-start(f16[2,64,512]{2,1,0:T(8,128)(2,1)S(1)} %fusion.6), channel_id=1, source_target_pairs={{0,192},{32,224},{64,0},{96,32},{128,64},{160,96},{192,128},{224,1... | collective-permute-start | bytes 393224 | tf_op jit(solution)/shard_map/ppermute | solution.py:403
  109.9 8.3 %collective-permute-start.14 = (f16[2,64,512]{2,1,0:T(8,128)(2,1)S(1)}, f16[2,64,512]{2,1,0:T(8,128)(2,1)S(1)}, u32[]{:S(2)}, u32[]{:S(2)}) collective-permute-start(f16[2,64,512]{2,1,0:T(8,128)(2,1)S(1)} %fusion.5), channel_id=1, source_target_pairs={{0,64},{32,96},{64,128},{96,160},{128,192},{160,224},{192,0},{224,... | collective-permute-start | bytes 393224 | tf_op jit(solution)/shard_map/ppermute | solution.py:403
  118.3 6.9 %collective-permute-start.17 = (f32[64,512]{1,0:T(8,128)S(1)}, f32[64,512]{1,0:T(8,128)S(1)}, u32[]{:S(2)}, u32[]{:S(2)}) collective-permute-start(f32[64,512]{1,0:T(8,128)S(1)} %get-tuple-element.49), channel_id=1, source_target_pairs={{0,2},{2,0},{1,3},{3,1},{4,6},{6,4},{5,7},{7,5},{8,10},{10,8},{9,1... | collective-permute-start | bytes 393224 | tf_op jit(solution)/shard_map/ppermute | solution.py:356

commit v8 on v7

--- a/solution.py
+++ b/solution.py
@@ -35,28 +35,19 @@
     return jnp.where(core == 0, x * 8 + u, u % 4 * 4 + x * 2 + u // 4)
 
 
-def arrange_kernel(place_ref, v1_ref, o_ref, sems):
-    copies = [
-        pltpu.make_async_copy(
-            v1_ref.at[block_of(place_ref[0], x, u)], o_ref.at[x, u], sems.at[x * 8 + u]
-        )
-        for x in range(NXL)
-        for u in range(8)
-    ]
-    for copy in copies:
-        copy.start()
-    for copy in copies:
-        copy.wait()
+def arrange_kernel(place_ref, v1_ref, *o_refs):
+    for x in range(NXL):
+        for u in range(8):
+            o_refs[x][u * ROWS : (u + 1) * ROWS, :] = v1_ref[block_of(place_ref[0], x, u)]
 
 
 def arranged(place, v1_all):
     return pl.pallas_call(
         arrange_kernel,
-        out_shape=jax.ShapeDtypeStruct((NXL, 8, ROWS, WIDTH), v1_all.dtype),
-        in_specs=[SMEM, pl.BlockSpec(memory_space=pl.ANY)],
-        out_specs=pl.BlockSpec(memory_space=pl.ANY),
-        scratch_shapes=[pltpu.SemaphoreType.DMA((16,))],
-        compiler_params=limit(1),
+        out_shape=(jax.ShapeDtypeStruct((NI, WIDTH), v1_all.dtype),) * NXL,
+        in_specs=[SMEM, VMEM],
+        out_specs=(VMEM,) * NXL,
+        compiler_params=limit(5),
         cost_estimate=pl.CostEstimate(flops=0, bytes_accessed=2**22, transcendentals=0),
     )(place, v1_all)
 
@@ -87,37 +78,26 @@
     )(*parts)
 
 
-def score_kernel(part, place_ref, v1_ref, v2_hbm, s_ref, v2_ref, sems):
-    copies = [pltpu.make_async_copy(v2_hbm.at[x], v2_ref.at[x], sems.at[x]) for x in range(NXL)]
-    for copy in copies:
-        copy.start()
-    for copy in copies:
-        copy.wait()
+def score_kernel(part, place_ref, v1_ref, v2_ref, s_ref):
+    users = range(part * (NP // ROWS), (part + 1) * (NP // ROWS))
     contract = (((1,), (1,)), ((), ()))
-    for u in range(NP // ROWS):
-        rows = slice(u * ROWS, (u + 1) * ROWS)
-        user = part * (NP // ROWS) + u
-        s_ref[rows, :] = sum(
-            lax.dot_general(
-                v1_ref[block_of(place_ref[0], x, user)],
-                v2_ref[x],
-                contract,
-                preferred_element_type=jnp.float32,
-            )
-            for x in range(NXL)
+    s_ref[...] = sum(
+        lax.dot_general(
+            jnp.concatenate([v1_ref[block_of(place_ref[0], x, u)] for u in users]),
+            v2_ref[x],
+            contract,
+            preferred_element_type=jnp.float32,
         )
+        for x in range(NXL)
+    )
 
 
 def partial_scores(part, place, v1_all, v2_all):
     return pl.pallas_call(
         functools.partial(score_kernel, part),
         out_shape=jax.ShapeDtypeStruct((NP, NJ), jnp.float32),
-        in_specs=[SMEM, VMEM, pl.BlockSpec(memory_space=pl.ANY)],
+        in_specs=[SMEM, VMEM, VMEM],
         out_specs=VMEM,
-        scratch_shapes=[
-            pltpu.VMEM((NXL, NJ, WIDTH), jnp.bfloat16),
-            pltpu.SemaphoreType.DMA((NXL,)),
-        ],
         compiler_params=limit(6),
         cost_estimate=pl.CostEstimate(
             flops=2 * NP * NJ * NXL * WIDTH, bytes_accessed=3 * 2**20, transcendentals=0
@@ -418,6 +398,7 @@
     give = jnp.where(xl == 0, view_two[HALF:], view_two[:HALF])
     side = swap(give, "xl")
     lines = spread(view_one, 0)
+    lines, side = lax.optimization_barrier((lines, side))
     here = jnp.where(xl == 0, jnp.stack([keep, side]), jnp.stack([side, keep]))
     up2, down2 = to_plane(here, -2), to_plane(here, 2)
     v1_all = spread(lines, 1).reshape(16, ROWS, WIDTH)
@@ -439,7 +420,7 @@
     seen = lax.all_to_all(
         pack, EVERY, 0, 0, axis_index_groups=stat_groups(), tiled=True
     )
-    v1_rows = arranged(place, v1_all).reshape(NXL, NI, WIDTH)
+    v1_rows = arranged(place, v1_all)
     known = merge_stats(place, seen)
     coupling, give_one, give_two, take_one, take_two = coupling_of(
         place, scores0, scores1, known, swap(known, "core")

time: 127 us -> 111 us (0.87)
  waiting for transfers between devices: 43.1 us -> 37.4 us
  Pallas kernels: 12.3 us -> 7.2 us
  local copies, waits for them, and re-layouts: 7.72 us -> 3.56 us
  starting transfers between devices: 42.7 us -> 39.1 us
  blocking collectives: 12.3 us -> 14.4 us
    ppermute x6, waiting for transfers between devices: 14.7 us -> 6.78 us  [swap(): return lax.ppermute(x, axis, [(0, 1), (1, 0)])]
    all_to_all x1 -> x0, starting transfers between devices: 5.43 us -> none  [on_device(): lax.all_to_all(pack, EVERY, 0, 0, axis_index_groups=stat_groups(), tiled=...]
    all_to_all x1 -> x2, starting transfers between devices: 4.93 us -> 9.26 us  [spread(): lax.all_to_all(jnp.broadcast_to(x[None], (4,) + x.shape), EVERY, 0, 0, ax...]
    unnamed x14 -> x2, local copies, waits for them, and re-layouts: 3.3 us -> 0.01 us
    pallas_call x1, Pallas kernels: 3.43 us -> 0.68 us  [arranged(): pl.pallas_call(arrange_kernel, out_shape=(jax.ShapeDtypeStruct((NI, WIDTH...]
    ppermute x12, waiting for transfers between devices: 23.8 us -> 26.1 us  [to_plane(): return lax.ppermute(x, 'z', [(z, (z + dz) % NZ) for z in range(NZ)])]
    ppermute x12, starting transfers between devices: 22.2 us -> 20.1 us  [to_plane(): return lax.ppermute(x, 'z', [(z, (z + dz) % NZ) for z in range(NZ)])]
    all_to_all x1 -> x2, waiting for transfers between devices: 0.01 us -> 2.08 us  [spread(): lax.all_to_all(jnp.broadcast_to(x[None], (4,) + x.shape), EVERY, 0, 0, ax...]
  transfers between devices with their start and end apart: 21 -> 21, of which waited for: 13 -> 14; matrix products, arithmetic and copies ran while one was open for 3% -> 3% of each run, Pallas kernels for 5% -> 2%
where the time goes in v8:
time: 111 us; the launch traced here: 110 us
  starting transfers between devices  39.1 us (35%)
  waiting for transfers between devices  37.4 us (34%)
  blocking collectives  14.4 us (13%)
  Pallas kernels  7.2 us (6%)
  matrix products  4.11 us (4%)
  other arithmetic  3.63 us (3%)
  local copies, waits for them, and re-layouts  3.56 us (3%)
    ppermute x12, waiting for transfers between devices, to_plane(): return lax.ppermute(x, 'z', [(z, (z + dz) % NZ) for z in range(NZ)])  26.1 us
    ppermute x12, starting transfers between devices, to_plane(): return lax.ppermute(x, 'z', [(z, (z + dz) % NZ) for z in range(NZ)])  20.1 us
    all_to_all x1, blocking collectives, on_device(): lax.all_to_all(pack, EVERY, 0, 0, axis_index_groups=stat_groups(), tiled=...  14.4 us
    all_to_all x2, starting transfers between devices, spread(): lax.all_to_all(jnp.broadcast_to(x[None], (4,) + x.shape), EVERY, 0, 0, ax...  9.26 us
    ppermute x6, waiting for transfers between devices, swap(): return lax.ppermute(x, axis, [(0, 1), (1, 0)])  6.78 us
    all_to_all x1, starting transfers between devices, on_device(): lax.all_to_all(part_one.reshape(16, ROWS, WIDTH), PLANE, 0, 0, tiled=True)  6.06 us
    ppermute x6, starting transfers between devices, swap(): return lax.ppermute(x, axis, [(0, 1), (1, 0)])  3.65 us
    broadcast_in_dim x2, local copies, waits for them, and re-layouts, spread(): jnp.broadcast_to(x[None], (4,) + x.shape)  3.33 us
  transfers between devices with their start and end apart: 21, of which 14 were waited for; matrix products, arithmetic and copies ran while one was open for 3% of the time, Pallas kernels for 2%

profile of v8, /device:TPU:4, one launch (start us, length us, event | category | flops | bytes accessed | tf_op | source)
XLA Modules:
  0.0 110.3 jit_solution(8290795743116767124)
XLA Ops:
  0.6 1.8 %broadcast_in_dim.6 = bf16[4,128,512]{2,1,0:T(8,128)(2,1)} broadcast(bf16[128,512]{1,0:T(8,128)(2,1)} %param.3), dimensions={1,2} | broadcast | bytes 655360 | tf_op jit(solution)/shard_map/broadcast_in_dim | solution.py:360
  2.4 4.5 %all-to-all-start = ((bf16[4,128,512]{2,1,0:T(8,128)(2,1)}), bf16[4,128,512]{2,1,0:T(8,128)(2,1)S(1)}, u32[]{:S(2)}, u32[]{:S(2)}) async-start(bf16[4,128,512]{2,1,0:T(8,128)(2,1)} %broadcast_in_dim.6), calls=%async_computation | async-start | bytes 1048576 | tf_op jit(solution)/shard_map/all_to_all | solution.py:359
  6.9 0.9 select_bitcast_fusion.2
  7.7 1.3 %collective-permute-start = (bf16[64,512]{1,0:T(8,128)(2,1)S(1)}, bf16[64,512]{1,0:T(8,128)(2,1)S(1)}, u32[]{:S(2)}, u32[]{:S(2)}) collective-permute-start(bf16[64,512]{1,0:T(8,128)(2,1)S(1)} %get-tuple-element.59), channel_id=1, source_target_pairs={{0,2},{2,0},{1,3},{3,1},{4,6},{6,4},{5,7},{7,5},{8,10},{10,8},{9,1... | collective-permute-start | bytes 196616 | tf_op jit(solution)/shard_map/ppermute | solution.py:336
  9.0 3.8 %collective-permute-done = bf16[64,512]{1,0:T(8,128)(2,1)S(1)} collective-permute-done((bf16[64,512]{1,0:T(8,128)(2,1)S(1)}, bf16[64,512]{1,0:T(8,128)(2,1)S(1)}, u32[]{:S(2)}, u32[]{:S(2)}) %collective-permute-start) | collective-permute-done | bytes 65568 | tf_op jit(solution)/shard_map/ppermute | solution.py:336
  12.9 2.1 %all-to-all-done = bf16[4,128,512]{2,1,0:T(8,128)(2,1)S(1)} async-done(((bf16[4,128,512]{2,1,0:T(8,128)(2,1)}), bf16[4,128,512]{2,1,0:T(8,128)(2,1)S(1)}, u32[]{:S(2)}, u32[]{:S(2)}) %all-to-all-start) | async-done | bytes 524320 | tf_op jit(solution)/shard_map/all_to_all | solution.py:359
  14.9 1.6 %broadcast_in_dim.7 = bf16[4,4,128,512]{3,2,1,0:T(8,128)(2,1)} broadcast(bf16[4,128,512]{2,1,0:T(8,128)(2,1)S(1)} %all-to-all-done), dimensions={1,2,3} | broadcast | bytes 2621440 | tf_op jit(solution)/shard_map/broadcast_in_dim | solution.py:360
  16.5 4.8 %all-to-all-start.1 = ((bf16[4,4,128,512]{3,2,1,0:T(8,128)(2,1)}), bf16[4,4,128,512]{3,2,1,0:T(8,128)(2,1)S(1)}, u32[]{:S(2)}, u32[]{:S(2)}) async-start(bf16[4,4,128,512]{3,2,1,0:T(8,128)(2,1)} %broadcast_in_dim.7), calls=%async_computation.1 | async-start | bytes 4194304 | tf_op jit(solution)/shard_map/all_to_all | solution.py:359
  21.3 3.3 %collective-permute-start.3 = (bf16[2,64,512]{2,1,0:T(8,128)(2,1)S(1)}, bf16[2,64,512]{2,1,0:T(8,128)(2,1)S(1)}, u32[]{:S(2)}, u32[]{:S(2)}) collective-permute-start(bf16[2,64,512]{2,1,0:T(8,128)(2,1)S(1)} %maximum_select_fusion.1.own), channel_id=1, source_target_pairs={{0,64},{32,96},{64,128},{96,160},{128,192},{160,224},{192,0},{224,... | collective-permute-start | bytes 393224 | tf_op jit(solution)/shard_map/ppermute | solution.py:383
  24.7 3.1 %collective-permute-start.1 = (bf16[2,64,512]{2,1,0:T(8,128)(2,1)S(1)}, bf16[2,64,512]{2,1,0:T(8,128)(2,1)S(1)}, u32[]{:S(2)}, u32[]{:S(2)}) collective-permute-start(bf16[2,64,512]{2,1,0:T(8,128)(2,1)S(1)} %maximum_select_fusion.1.own), channel_id=1, source_target_pairs={{0,192},{32,224},{64,0},{96,32},{128,64},{160,96},{192,128},{224,1... | collective-permute-start | bytes 393224 | tf_op jit(solution)/shard_map/ppermute | solution.py:383
  27.8 4.4 %collective-permute-done.3.down2 = bf16[2,64,512]{2,1,0:T(8,128)(2,1)S(1)} collective-permute-done((bf16[2,64,512]{2,1,0:T(8,128)(2,1)S(1)}, bf16[2,64,512]{2,1,0:T(8,128)(2,1)S(1)}, u32[]{:S(2)}, u32[]{:S(2)}) %collective-permute-start.3) | collective-permute-done | bytes 131104 | tf_op jit(solution)/shard_map/ppermute | solution.py:383
  32.2 0.6 collective-permute-start.4
  32.8 0.7 collective-permute-done.1.up2
  33.5 0.5 collective-permute-start.6
  34.1 2.8 %collective-permute-start.5 = (bf16[2,128,512]{2,1,0:T(8,128)(2,1)S(1)}, bf16[2,128,512]{2,1,0:T(8,128)(2,1)S(1)}, u32[]{:S(2)}, u32[]{:S(2)}) collective-permute-start(bf16[2,128,512]{2,1,0:T(8,128)(2,1)S(1)} %get-tuple-element.57), channel_id=1, source_target_pairs={{0,224},{32,0},{64,32},{96,64},{128,96},{160,128},{192,160},{224,1... | collective-permute-start | bytes 786440 | tf_op jit(solution)/shard_map/ppermute | solution.py:383
  36.9 1.6 %collective-permute-start.2 = (bf16[64,512]{1,0:T(8,128)(2,1)S(1)}, bf16[64,512]{1,0:T(8,128)(2,1)S(1)}, u32[]{:S(2)}, u32[]{:S(2)}) collective-permute-start(bf16[64,512]{1,0:T(8,128)(2,1)S(1)} %slice_bitcast_fusion.13), channel_id=1, source_target_pairs={{0,192},{32,224},{64,0},{96,32},{128,64},{160,96},{192,128},{224,1... | collective-permute-start | bytes 196616 | tf_op jit(solution)/shard_map/ppermute | solution.py:383
  38.5 0.1 pad_add_fusion.place_ref
  38.6 0.0 collective-permute-done.4.four1
  38.6 6.0 %collective-permute-done.2.four0 = bf16[64,512]{1,0:T(8,128)(2,1)S(1)} collective-permute-done((bf16[64,512]{1,0:T(8,128)(2,1)S(1)}, bf16[64,512]{1,0:T(8,128)(2,1)S(1)}, u32[]{:S(2)}, u32[]{:S(2)}) %collective-permute-start.2) | collective-permute-done | bytes 65568 | tf_op jit(solution)/shard_map/ppermute | solution.py:383
  44.6 0.0 collective-permute-done.6.down
  44.6 0.0 collective-permute-done.5.up
  44.6 0.2 shard_map.50
  44.8 1.3 %shard_map.51.own_ref = f32[512,512]{1,0:T(8,128)S(1)} custom-call(s32[4]{0:T(128)S(1)} %pad_add_fusion.place_ref, bf16[16,128,512]{2,1,0:T(8,128)(2,1)S(1)} %bitcast.64, bf16[2,512,512]{2,1,0:T(8,128)(2,1)S(1)} %get-tuple-element.24.v2_ref), custom_call_target="tpu_custom_call" | custom-call | flops 536870912 | bytes 3145728 | tf_op jit(solution)/shard_map/pallas_call | solution.py:96
  46.1 0.1 collective-permute-start.7
  46.2 1.3 %shard_map.53.own_ref = f32[512,512]{1,0:T(8,128)S(1)} custom-call(s32[4]{0:T(128)S(1)} %pad_add_fusion.place_ref, bf16[16,128,512]{2,1,0:T(8,128)(2,1)S(1)} %bitcast.65, bf16[2,512,512]{2,1,0:T(8,128)(2,1)S(1)} %get-tuple-element.24.v2_ref), custom_call_target="tpu_custom_call" | custom-call | flops 536870912 | bytes 3145728 | tf_op jit(solution)/shard_map/pallas_call | solution.py:96
  47.4 0.0 copy-start
  47.5 0.6 collective-permute-start.8
  48.0 0.2 abs_reduce_fusion
  48.3 0.1 collective-permute-start.9
  48.4 0.4 collective-permute-done.7.other_ref
  48.8 0.6 shard_map.52
  49.4 0.9 collective-permute-done.9.most_other_ref
  50.3 1.2 %shard_map.54 = (f32[512,512]{1,0:T(8,128)S(1)}, f32[16,16,128]{2,1,0:T(8,128)S(1)}) custom-call(s32[4]{0:T(128)S(1)} %pad_add_fusion.place_ref, f32[512,512]{1,0:T(8,128)S(1)} %shard_map.53.own_ref, f32[512,512]{1,0:T(8,128)S(1)} %collective-permute-done.8.other_ref, f32[4,128]{1,0:T(4,128)S(1)} %get-tuple-element.26.first_ref, ...), custom_call_target="tpu_custom_call" | custom-call | flops 2621440 | bytes 3145728 | tf_op jit(solution)/shard_map/pallas_call | solution.py:216
  51.5 14.4 %all_to_all.20.seen_ref = f32[16,16,128]{2,1,0:T(8,128)S(1)} all-to-all(f32[16,16,128]{2,1,0:T(8,128)S(1)} %get-tuple-element.30), channel_id=1, replica_groups={{0,8,16,24,4,12,20,28,2,10,18,26,6,14,22,30},{32,40,48,56,36,44,52,60,3..., dimensions={0} | all-to-all | bytes 262144 | tf_op jit(solution)/shard_map/all_to_all | solution.py:420
  65.9 0.6 shard_map.55.known_ref
  66.5 0.3 collective-permute-start.10
  66.8 0.7 shard_map.57
  67.5 0.5 collective-permute-done.10.told_ref
  68.0 1.4 %shard_map.56 = (bf16[1024,512]{1,0:T(8,128)(2,1)S(1)}, f32[1,512]{1,0:T(1,128)S(1)}, f32[1,512]{1,0:T(1,128)S(1)}, f32[1,512]{1,0:T(1,128)S(1)}, f32[1,512]{1,0:T(1,128)S(1)}) custom-call(s32[4]{0:T(128)S(1)} %pad_add_fusion.place_ref, f32[512,512]{1,0:T(8,128)S(1)} %get-tuple-element.25.s0_ref, f32[512,512]{1,0:T(8,128)S(1)} %get-tuple-element.29.s1_ref, ...), custom_call_target="tpu_custom_call" | custom-call | flops 4194304 | bytes 3145728 | tf_op jit(solution)/shard_map/pallas_call | solution.py:320
  69.4 2.6 %multiply_convert_fusion = f16[2,1024,512]{2,1,0:T(8,128)(2,1)} fusion(bf16[2,512,512]{2,1,0:T(8,128)(2,1)S(1)} %get-tuple-element.24.v2_ref, f32[512]{0:T(512)S(1)} %bitcast.72, bf16[1024,512]{1,0:T(8,128)(2,1)S(1)} %get-tuple-element.33), kind=kOutput, calls=%fused_computation.1 | convolution fusion | flops 1075838976 | bytes 4196352 | tf_op jit(solution)/shard_map/dot_general | solution.py:430
  72.0 0.7 fusion.1
  72.8 0.7 fusion
  73.5 6.1 %all-to-all-start.3 = ((f16[16,128,512]{2,1,0:T(8,128)(2,1)}), f16[16,128,512]{2,1,0:T(8,128)(2,1)S(1)}, u32[]{:S(2)}, u32[]{:S(2)}) async-start(f16[16,128,512]{2,1,0:T(8,128)(2,1)} %bitcast.73), calls=%async_computation.3 | async-start | bytes 4194304 | tf_op jit(solution)/shard_map/all_to_all | solution.py:439
  79.6 0.1 slice_bitcast_fusion.4
  79.7 0.1 pad_maximum_fusion.3
  79.8 0.9 collective-permute-start.12
  80.7 1.4 %collective-permute-start.15 = (f16[64,512]{1,0:T(8,128)(2,1)S(1)}, f16[64,512]{1,0:T(8,128)(2,1)S(1)}, u32[]{:S(2)}, u32[]{:S(2)}) collective-permute-start(f16[64,512]{1,0:T(8,128)(2,1)S(1)} %get-tuple-element.47), channel_id=1, source_target_pairs={{0,192},{32,224},{64,0},{96,32},{128,64},{160,96},{192,128},{224,1... | collective-permute-start | bytes 196616 | tf_op jit(solution)/shard_map/ppermute | solution.py:383
  82.1 1.6 %collective-permute-start.13 = (f16[64,512]{1,0:T(8,128)(2,1)S(1)}, f16[64,512]{1,0:T(8,128)(2,1)S(1)}, u32[]{:S(2)}, u32[]{:S(2)}) collective-permute-start(f16[64,512]{1,0:T(8,128)(2,1)S(1)} %get-tuple-element.44), channel_id=1, source_target_pairs={{0,64},{32,96},{64,128},{96,160},{128,192},{160,224},{192,0},{224,... | collective-permute-start | bytes 196616 | tf_op jit(solution)/shard_map/ppermute | solution.py:383
  83.7 0.1 pad_maximum_fusion.2
  83.8 1.3 %collective-permute-start.11 = (f16[2,128,512]{2,1,0:T(8,128)(2,1)S(1)}, f16[2,128,512]{2,1,0:T(8,128)(2,1)S(1)}, u32[]{:S(2)}, u32[]{:S(2)}) collective-permute-start(f16[2,128,512]{2,1,0:T(8,128)(2,1)S(1)} %pad_maximum_fusion.2), channel_id=1, source_target_pairs={{0,32},{32,64},{64,96},{96,128},{128,160},{160,192},{192,224},{224... | collective-permute-start | bytes 786440 | tf_op jit(solution)/shard_map/ppermute | solution.py:383
  85.1 5.0 %collective-permute-done.12 = f16[2,128,512]{2,1,0:T(8,128)(2,1)S(1)} collective-permute-done((f16[2,128,512]{2,1,0:T(8,128)(2,1)S(1)}, f16[2,128,512]{2,1,0:T(8,128)(2,1)S(1)}, u32[]{:S(2)}, u32[]{:S(2)}) %collective-permute-start.12) | collective-permute-done | bytes 262176 | tf_op jit(solution)/shard_map/ppermute | solution.py:383
  90.1 0.1 convert_element_type.65
  90.3 2.9 %collective-permute-start.16 = (f16[2,64,512]{2,1,0:T(8,128)(2,1)S(1)}, f16[2,64,512]{2,1,0:T(8,128)(2,1)S(1)}, u32[]{:S(2)}, u32[]{:S(2)}) collective-permute-start(f16[2,64,512]{2,1,0:T(8,128)(2,1)S(1)} %fusion.6), channel_id=1, source_target_pairs={{0,192},{32,224},{64,0},{96,32},{128,64},{160,96},{192,128},{224,1... | collective-permute-start | bytes 393224 | tf_op jit(solution)/shard_map/ppermute | solution.py:383
  93.1 2.0 %collective-permute-done.11 = f16[2,128,512]{2,1,0:T(8,128)(2,1)S(1)} collective-permute-done((f16[2,128,512]{2,1,0:T(8,128)(2,1)S(1)}, f16[2,128,512]{2,1,0:T(8,128)(2,1)S(1)}, u32[]{:S(2)}, u32[]{:S(2)}) %collective-permute-start.11) | collective-permute-done | bytes 262176 | tf_op jit(solution)/shard_map/ppermute | solution.py:383
  95.1 0.1 convert_element_type.64
  95.3 0.1 collective-permute-start.14
  95.4 3.4 %collective-permute-done.16 = f16[2,64,512]{2,1,0:T(8,128)(2,1)S(1)} collective-permute-done((f16[2,64,512]{2,1,0:T(8,128)(2,1)S(1)}, f16[2,64,512]{2,1,0:T(8,128)(2,1)S(1)}, u32[]{:S(2)}, u32[]{:S(2)}) %collective-permute-start.16) | collective-permute-done | bytes 131104 | tf_op jit(solution)/shard_map/ppermute | solution.py:383
  98.8 4.6 %collective-permute-done.14 = f16[2,64,512]{2,1,0:T(8,128)(2,1)S(1)} collective-permute-done((f16[2,64,512]{2,1,0:T(8,128)(2,1)S(1)}, f16[2,64,512]{2,1,0:T(8,128)(2,1)S(1)}, u32[]{:S(2)}, u32[]{:S(2)}) %collective-permute-start.14) | collective-permute-done | bytes 131104 | tf_op jit(solution)/shard_map/ppermute | solution.py:383
  103.4 0.1 fusion.4
  103.5 1.3 %collective-permute-start.17 = (f32[64,512]{1,0:T(8,128)S(1)}, f32[64,512]{1,0:T(8,128)S(1)}, u32[]{:S(2)}, u32[]{:S(2)}) collective-permute-start(f32[64,512]{1,0:T(8,128)S(1)} %get-tuple-element.55), channel_id=1, source_target_pairs={{0,2},{2,0},{1,3},{3,1},{4,6},{6,4},{5,7},{7,5},{8,10},{10,8},{9,1... | collective-permute-start | bytes 393224 | tf_op jit(solution)/shard_map/ppermute | solution.py:336
  104.8 2.5 %all-to-all-done.3 = f16[16,128,512]{2,1,0:T(8,128)(2,1)S(1)} async-done(((f16[16,128,512]{2,1,0:T(8,128)(2,1)}), f16[16,128,512]{2,1,0:T(8,128)(2,1)S(1)}, u32[]{:S(2)}, u32[]{:S(2)}) %all-to-all-start.3) | async-done | bytes 2097184 | tf_op jit(solution)/shard_map/all_to_all | solution.py:439
  107.3 1.1 %multiply_reduce_fusion = f32[128,512]{1,0:T(8,128)} fusion(f16[16,128,512]{2,1,0:T(8,128)(2,1)S(1)} %all-to-all-done.3, f32[512]{0:T(512)S(1)} %bitcast.68), kind=kLoop, calls=%fused_computation | loop fusion | flops 3080192 | bytes 2361344 | tf_op jit(solution)/shard_map/reduce_sum | solution.py:468
  108.4 1.1 %collective-permute-done.17 = f32[64,512]{1,0:T(8,128)S(1)} collective-permute-done((f32[64,512]{1,0:T(8,128)S(1)}, f32[64,512]{1,0:T(8,128)S(1)}, u32[]{:S(2)}, u32[]{:S(2)}) %collective-permute-start.17) | collective-permute-done | bytes 131104 | tf_op jit(solution)/shard_map/ppermute | solution.py:336
  109.6 0.7 maximum_select_fusion
  (22 shorter events, 0.4 us)
Async XLA Ops:
  2.4 12.5 %all-to-all-start = ((bf16[4,128,512]{2,1,0:T(8,128)(2,1)}), bf16[4,128,512]{2,1,0:T(8,128)(2,1)S(1)}, u32[]{:S(2)}, u32[]{:S(2)}) async-start(bf16[4,128,512]{2,1,0:T(8,128)(2,1)} %broadcast_in_dim.6), calls=%async_computation | async-start | bytes 1048576 | tf_op jit(solution)/shard_map/all_to_all | solution.py:359
  7.7 5.1 %collective-permute-start = (bf16[64,512]{1,0:T(8,128)(2,1)S(1)}, bf16[64,512]{1,0:T(8,128)(2,1)S(1)}, u32[]{:S(2)}, u32[]{:S(2)}) collective-permute-start(bf16[64,512]{1,0:T(8,128)(2,1)S(1)} %get-tuple-element.59), channel_id=1, source_target_pairs={{0,2},{2,0},{1,3},{3,1},{4,6},{6,4},{5,7},{7,5},{8,10},{10,8},{9,1... | collective-permute-start | bytes 196616 | tf_op jit(solution)/shard_map/ppermute | solution.py:336
  16.5 28.3 %all-to-all-start.1 = ((bf16[4,4,128,512]{3,2,1,0:T(8,128)(2,1)}), bf16[4,4,128,512]{3,2,1,0:T(8,128)(2,1)S(1)}, u32[]{:S(2)}, u32[]{:S(2)}) async-start(bf16[4,4,128,512]{3,2,1,0:T(8,128)(2,1)} %broadcast_in_dim.7), calls=%async_computation.1 | async-start | bytes 4194304 | tf_op jit(solution)/shard_map/all_to_all | solution.py:359
  21.3 10.9 %collective-permute-start.3 = (bf16[2,64,512]{2,1,0:T(8,128)(2,1)S(1)}, bf16[2,64,512]{2,1,0:T(8,128)(2,1)S(1)}, u32[]{:S(2)}, u32[]{:S(2)}) collective-permute-start(bf16[2,64,512]{2,1,0:T(8,128)(2,1)S(1)} %maximum_select_fusion.1.own), channel_id=1, source_target_pairs={{0,64},{32,96},{64,128},{96,160},{128,192},{160,224},{192,0},{224,... | collective-permute-start | bytes 393224 | tf_op jit(solution)/shard_map/ppermute | solution.py:383
  24.7 8.8 %collective-permute-start.1 = (bf16[2,64,512]{2,1,0:T(8,128)(2,1)S(1)}, bf16[2,64,512]{2,1,0:T(8,128)(2,1)S(1)}, u32[]{:S(2)}, u32[]{:S(2)}) collective-permute-start(bf16[2,64,512]{2,1,0:T(8,128)(2,1)S(1)} %maximum_select_fusion.1.own), channel_id=1, source_target_pairs={{0,192},{32,224},{64,0},{96,32},{128,64},{160,96},{192,128},{224,1... | collective-permute-start | bytes 393224 | tf_op jit(solution)/shard_map/ppermute | solution.py:383
  32.2 6.4 %collective-permute-start.4 = (bf16[64,512]{1,0:T(8,128)(2,1)S(1)}, bf16[64,512]{1,0:T(8,128)(2,1)S(1)}, u32[]{:S(2)}, u32[]{:S(2)}) collective-permute-start(bf16[64,512]{1,0:T(8,128)(2,1)S(1)} %slice_bitcast_fusion.12), channel_id=1, source_target_pairs={{0,64},{32,96},{64,128},{96,160},{128,192},{160,224},{192,0},{224,... | collective-permute-start | bytes 196616 | tf_op jit(solution)/shard_map/ppermute | solution.py:383
  33.5 11.1 %collective-permute-start.6 = (bf16[2,128,512]{2,1,0:T(8,128)(2,1)S(1)}, bf16[2,128,512]{2,1,0:T(8,128)(2,1)S(1)}, u32[]{:S(2)}, u32[]{:S(2)}) collective-permute-start(bf16[2,128,512]{2,1,0:T(8,128)(2,1)S(1)} %get-tuple-element.56), channel_id=1, source_target_pairs={{0,32},{32,64},{64,96},{96,128},{128,160},{160,192},{192,224},{224... | collective-permute-start | bytes 786440 | tf_op jit(solution)/shard_map/ppermute | solution.py:383
  34.1 10.5 %collective-permute-start.5 = (bf16[2,128,512]{2,1,0:T(8,128)(2,1)S(1)}, bf16[2,128,512]{2,1,0:T(8,128)(2,1)S(1)}, u32[]{:S(2)}, u32[]{:S(2)}) collective-permute-start(bf16[2,128,512]{2,1,0:T(8,128)(2,1)S(1)} %get-tuple-element.57), channel_id=1, source_target_pairs={{0,224},{32,0},{64,32},{96,64},{128,96},{160,128},{192,160},{224,1... | collective-permute-start | bytes 786440 | tf_op jit(solution)/shard_map/ppermute | solution.py:383
  36.9 7.7 %collective-permute-start.2 = (bf16[64,512]{1,0:T(8,128)(2,1)S(1)}, bf16[64,512]{1,0:T(8,128)(2,1)S(1)}, u32[]{:S(2)}, u32[]{:S(2)}) collective-permute-start(bf16[64,512]{1,0:T(8,128)(2,1)S(1)} %slice_bitcast_fusion.13), channel_id=1, source_target_pairs={{0,192},{32,224},{64,0},{96,32},{128,64},{160,96},{192,128},{224,1... | collective-permute-start | bytes 196616 | tf_op jit(solution)/shard_map/ppermute | solution.py:383
  46.1 2.7 %collective-permute-start.7 = (f32[512,512]{1,0:T(8,128)S(1)}, f32[512,512]{1,0:T(8,128)S(1)}, u32[]{:S(2)}, u32[]{:S(2)}) collective-permute-start(f32[512,512]{1,0:T(8,128)S(1)} %shard_map.51.own_ref), channel_id=1, source_target_pairs={{0,1},{1,0},{2,3},{3,2},{4,5},{5,4},{6,7},{7,6},{8,9},{9,8},{10,11... | collective-permute-start | bytes 3145736 | tf_op jit(solution)/shard_map/ppermute | solution.py:336
  47.4 2.9 %copy-start = (s32[128]{0:T(128)S(1)}, s32[128]{0:T(128)}, u32[]{:S(2)}) copy-start(s32[128]{0:T(128)} %param.5) | copy-start | bytes 1540
  47.5 2.9 %collective-permute-start.8 = (f32[512,512]{1,0:T(8,128)S(1)}, f32[512,512]{1,0:T(8,128)S(1)}, u32[]{:S(2)}, u32[]{:S(2)}) collective-permute-start(f32[512,512]{1,0:T(8,128)S(1)} %shard_map.53.own_ref), channel_id=1, source_target_pairs={{0,1},{1,0},{2,3},{3,2},{4,5},{5,4},{6,7},{7,6},{8,9},{9,8},{10,11... | collective-permute-start | bytes 3145736 | tf_op jit(solution)/shard_map/ppermute | solution.py:336
  48.3 2.0 %collective-permute-start.9 = (f32[2,512]{1,0:T(2,128)S(1)}, f32[2,512]{1,0:T(2,128)S(1)}, u32[]{:S(2)}, u32[]{:S(2)}) collective-permute-start(f32[2,512]{1,0:T(2,128)S(1)} %pad_maximum_fusion.4.most_ref), channel_id=1, source_target_pairs={{0,1},{1,0},{2,3},{3,2},{4,5},{5,4},{6,7},{7,6},{8,9},{9,8},{10,11... | collective-permute-start | bytes 12296 | tf_op jit(solution)/shard_map/ppermute | solution.py:336
  66.5 1.4 %collective-permute-start.10 = (f32[24,128]{1,0:T(8,128)S(1)}, f32[24,128]{1,0:T(8,128)S(1)}, u32[]{:S(2)}, u32[]{:S(2)}) collective-permute-start(f32[24,128]{1,0:T(8,128)S(1)} %shard_map.55.known_ref), channel_id=1, source_target_pairs={{0,1},{1,0},{2,3},{3,2},{4,5},{5,4},{6,7},{7,6},{8,9},{9,8},{10,11... | collective-permute-start | bytes 36872 | tf_op jit(solution)/shard_map/ppermute | solution.py:336
  73.5 33.8 %all-to-all-start.3 = ((f16[16,128,512]{2,1,0:T(8,128)(2,1)}), f16[16,128,512]{2,1,0:T(8,128)(2,1)S(1)}, u32[]{:S(2)}, u32[]{:S(2)}) async-start(f16[16,128,512]{2,1,0:T(8,128)(2,1)} %bitcast.73), calls=%async_computation.3 | async-start | bytes 4194304 | tf_op jit(solution)/shard_map/all_to_all | solution.py:439
  79.8 10.3 %collective-permute-start.12 = (f16[2,128,512]{2,1,0:T(8,128)(2,1)S(1)}, f16[2,128,512]{2,1,0:T(8,128)(2,1)S(1)}, u32[]{:S(2)}, u32[]{:S(2)}) collective-permute-start(f16[2,128,512]{2,1,0:T(8,128)(2,1)S(1)} %pad_maximum_fusion.3), channel_id=1, source_target_pairs={{0,224},{32,0},{64,32},{96,64},{128,96},{160,128},{192,160},{224,1... | collective-permute-start | bytes 786440 | tf_op jit(solution)/shard_map/ppermute | solution.py:383
  80.7 9.5 %collective-permute-start.15 = (f16[64,512]{1,0:T(8,128)(2,1)S(1)}, f16[64,512]{1,0:T(8,128)(2,1)S(1)}, u32[]{:S(2)}, u32[]{:S(2)}) collective-permute-start(f16[64,512]{1,0:T(8,128)(2,1)S(1)} %get-tuple-element.47), channel_id=1, source_target_pairs={{0,192},{32,224},{64,0},{96,32},{128,64},{160,96},{192,128},{224,1... | collective-permute-start | bytes 196616 | tf_op jit(solution)/shard_map/ppermute | solution.py:383
  82.1 13.1 %collective-permute-start.13 = (f16[64,512]{1,0:T(8,128)(2,1)S(1)}, f16[64,512]{1,0:T(8,128)(2,1)S(1)}, u32[]{:S(2)}, u32[]{:S(2)}) collective-permute-start(f16[64,512]{1,0:T(8,128)(2,1)S(1)} %get-tuple-element.44), channel_id=1, source_target_pairs={{0,64},{32,96},{64,128},{96,160},{128,192},{160,224},{192,0},{224,... | collective-permute-start | bytes 196616 | tf_op jit(solution)/shard_map/ppermute | solution.py:383
  83.8 11.3 %collective-permute-start.11 = (f16[2,128,512]{2,1,0:T(8,128)(2,1)S(1)}, f16[2,128,512]{2,1,0:T(8,128)(2,1)S(1)}, u32[]{:S(2)}, u32[]{:S(2)}) collective-permute-start(f16[2,128,512]{2,1,0:T(8,128)(2,1)S(1)} %pad_maximum_fusion.2), channel_id=1, source_target_pairs={{0,32},{32,64},{64,96},{96,128},{128,160},{160,192},{192,224},{224... | collective-permute-start | bytes 786440 | tf_op jit(solution)/shard_map/ppermute | solution.py:383
  90.3 8.5 %collective-permute-start.16 = (f16[2,64,512]{2,1,0:T(8,128)(2,1)S(1)}, f16[2,64,512]{2,1,0:T(8,128)(2,1)S(1)}, u32[]{:S(2)}, u32[]{:S(2)}) collective-permute-start(f16[2,64,512]{2,1,0:T(8,128)(2,1)S(1)} %fusion.6), channel_id=1, source_target_pairs={{0,192},{32,224},{64,0},{96,32},{128,64},{160,96},{192,128},{224,1... | collective-permute-start | bytes 393224 | tf_op jit(solution)/shard_map/ppermute | solution.py:383
  95.3 8.1 %collective-permute-start.14 = (f16[2,64,512]{2,1,0:T(8,128)(2,1)S(1)}, f16[2,64,512]{2,1,0:T(8,128)(2,1)S(1)}, u32[]{:S(2)}, u32[]{:S(2)}) collective-permute-start(f16[2,64,512]{2,1,0:T(8,128)(2,1)S(1)} %fusion.5), channel_id=1, source_target_pairs={{0,64},{32,96},{64,128},{96,160},{128,192},{160,224},{192,0},{224,... | collective-permute-start | bytes 393224 | tf_op jit(solution)/shard_map/ppermute | solution.py:383
  103.5 6.1 %collective-permute-start.17 = (f32[64,512]{1,0:T(8,128)S(1)}, f32[64,512]{1,0:T(8,128)S(1)}, u32[]{:S(2)}, u32[]{:S(2)}) collective-permute-start(f32[64,512]{1,0:T(8,128)S(1)} %get-tuple-element.55), channel_id=1, source_target_pairs={{0,2},{2,0},{1,3},{3,1},{4,6},{6,4},{5,7},{7,5},{8,10},{10,8},{9,1... | collective-permute-start | bytes 393224 | tf_op jit(solution)/shard_map/ppermute | solution.py:336

commit v9 on v8

--- a/solution.py
+++ b/solution.py
@@ -74,7 +74,7 @@
         in_specs=[VMEM] * 7,
         out_specs=(VMEM, VMEM),
         compiler_params=limit(4),
-        cost_estimate=pl.CostEstimate(flops=2**20, bytes_accessed=2**21, transcendentals=0),
+        cost_estimate=pl.CostEstimate(flops=12 * 2**30, bytes_accessed=2**21, transcendentals=0),
     )(*parts)
 
 
@@ -415,12 +415,13 @@
     most = jnp.concatenate([most_v2, largest(v1_all)[None]])
     most_other = swap(most, "core")
 
+    v1_rows = arranged(place, v1_all)
+    other0, v1_rows = lax.optimization_barrier((other0, v1_rows))
     scores0, first, cols = first_stats(own0, other0)
     scores1, pack = second_stats(place, own1, other1, first, cols, partner, most, most_other)
     seen = lax.all_to_all(
         pack, EVERY, 0, 0, axis_index_groups=stat_groups(), tiled=True
     )
-    v1_rows = arranged(place, v1_all)
     known = merge_stats(place, seen)
     coupling, give_one, give_two, take_one, take_two = coupling_of(
         place, scores0, scores1, known, swap(known, "core")

time: 111 us -> 107 us (0.964)
  waiting for transfers between devices: 37.4 us -> 33.3 us
  starting transfers between devices: 39.1 us -> 41.5 us
  blocking collectives: 14.4 us -> 12.1 us
    ppermute x12, waiting for transfers between devices: 26.1 us -> 21.6 us  [to_plane(): return lax.ppermute(x, 'z', [(z, (z + dz) % NZ) for z in range(NZ)])]
    all_to_all x1, blocking collectives: 14.4 us -> 12.1 us  [on_device(): lax.all_to_all(pack, EVERY, 0, 0, axis_index_groups=stat_groups(), tiled=...]
    ppermute x6, starting transfers between devices: 3.65 us -> 5.52 us  [swap(): return lax.ppermute(x, axis, [(0, 1), (1, 0)])]
    all_to_all x2, waiting for transfers between devices: 2.08 us -> 3.32 us  [spread(): lax.all_to_all(jnp.broadcast_to(x[None], (4,) + x.shape), EVERY, 0, 0, ax...]
  transfers between devices with their start and end apart: 21 -> 21, of which waited for: 14 -> 14; matrix products, arithmetic and copies ran while one was open for 3% -> 4% of each run, Pallas kernels for 2% -> 3%
where the time goes in v9:
time: 107 us; the launch traced here: 106 us
  starting transfers between devices  41.5 us (39%)
  waiting for transfers between devices  33.3 us (31%)
  blocking collectives  12.1 us (11%)
  Pallas kernels  7.22 us (7%)
  matrix products  4.07 us (4%)
  other arithmetic  3.63 us (3%)
  local copies, waits for them, and re-layouts  3.56 us (3%)
    ppermute x12, waiting for transfers between devices, to_plane(): return lax.ppermute(x, 'z', [(z, (z + dz) % NZ) for z in range(NZ)])  21.6 us
    ppermute x12, starting transfers between devices, to_plane(): return lax.ppermute(x, 'z', [(z, (z + dz) % NZ) for z in range(NZ)])  21.2 us
    all_to_all x1, blocking collectives, on_device(): lax.all_to_all(pack, EVERY, 0, 0, axis_index_groups=stat_groups(), tiled=...  12.1 us
    all_to_all x2, starting transfers between devices, spread(): lax.all_to_all(jnp.broadcast_to(x[None], (4,) + x.shape), EVERY, 0, 0, ax...  9.26 us
    ppermute x6, waiting for transfers between devices, swap(): return lax.ppermute(x, axis, [(0, 1), (1, 0)])  6.54 us
    ppermute x6, starting transfers between devices, swap(): return lax.ppermute(x, axis, [(0, 1), (1, 0)])  5.52 us
    all_to_all x1, starting transfers between devices, on_device(): lax.all_to_all(part_one.reshape(16, ROWS, WIDTH), PLANE, 0, 0, tiled=True)  5.47 us
    broadcast_in_dim x2, local copies, waits for them, and re-layouts, spread(): jnp.broadcast_to(x[None], (4,) + x.shape)  3.33 us
  transfers between devices with their start and end apart: 21, of which 14 were waited for; matrix products, arithmetic and copies ran while one was open for 4% of the time, Pallas kernels for 3%

profile of v9, /device:TPU:4, one launch (start us, length us, event | category | flops | bytes accessed | tf_op | source)
XLA Modules:
  0.0 106.2 jit_solution(13163744858815452381)
XLA Ops:
  0.6 1.8 %broadcast_in_dim.6 = bf16[4,128,512]{2,1,0:T(8,128)(2,1)} broadcast(bf16[128,512]{1,0:T(8,128)(2,1)} %param.3), dimensions={1,2} | broadcast | bytes 655360 | tf_op jit(solution)/shard_map/broadcast_in_dim | solution.py:360
  2.4 4.5 %all-to-all-start = ((bf16[4,128,512]{2,1,0:T(8,128)(2,1)}), bf16[4,128,512]{2,1,0:T(8,128)(2,1)S(1)}, u32[]{:S(2)}, u32[]{:S(2)}) async-start(bf16[4,128,512]{2,1,0:T(8,128)(2,1)} %broadcast_in_dim.6), calls=%async_computation | async-start | bytes 1048576 | tf_op jit(solution)/shard_map/all_to_all | solution.py:359
  6.9 0.9 select_bitcast_fusion.2
  7.7 1.3 %collective-permute-start = (bf16[64,512]{1,0:T(8,128)(2,1)S(1)}, bf16[64,512]{1,0:T(8,128)(2,1)S(1)}, u32[]{:S(2)}, u32[]{:S(2)}) collective-permute-start(bf16[64,512]{1,0:T(8,128)(2,1)S(1)} %get-tuple-element.65), channel_id=1, source_target_pairs={{0,2},{2,0},{1,3},{3,1},{4,6},{6,4},{5,7},{7,5},{8,10},{10,8},{9,1... | collective-permute-start | bytes 196616 | tf_op jit(solution)/shard_map/ppermute | solution.py:336
  9.0 3.8 %collective-permute-done = bf16[64,512]{1,0:T(8,128)(2,1)S(1)} collective-permute-done((bf16[64,512]{1,0:T(8,128)(2,1)S(1)}, bf16[64,512]{1,0:T(8,128)(2,1)S(1)}, u32[]{:S(2)}, u32[]{:S(2)}) %collective-permute-start) | collective-permute-done | bytes 65568 | tf_op jit(solution)/shard_map/ppermute | solution.py:336
  12.9 2.1 %all-to-all-done = bf16[4,128,512]{2,1,0:T(8,128)(2,1)S(1)} async-done(((bf16[4,128,512]{2,1,0:T(8,128)(2,1)}), bf16[4,128,512]{2,1,0:T(8,128)(2,1)S(1)}, u32[]{:S(2)}, u32[]{:S(2)}) %all-to-all-start) | async-done | bytes 524320 | tf_op jit(solution)/shard_map/all_to_all | solution.py:359
  15.0 3.3 %collective-permute-start.3 = (bf16[2,64,512]{2,1,0:T(8,128)(2,1)S(1)}, bf16[2,64,512]{2,1,0:T(8,128)(2,1)S(1)}, u32[]{:S(2)}, u32[]{:S(2)}) collective-permute-start(bf16[2,64,512]{2,1,0:T(8,128)(2,1)S(1)} %maximum_select_fusion.1.own), channel_id=1, source_target_pairs={{0,64},{32,96},{64,128},{96,160},{128,192},{160,224},{192,0},{224,... | collective-permute-start | bytes 393224 | tf_op jit(solution)/shard_map/ppermute | solution.py:383
  18.3 3.1 %collective-permute-start.1 = (bf16[2,64,512]{2,1,0:T(8,128)(2,1)S(1)}, bf16[2,64,512]{2,1,0:T(8,128)(2,1)S(1)}, u32[]{:S(2)}, u32[]{:S(2)}) collective-permute-start(bf16[2,64,512]{2,1,0:T(8,128)(2,1)S(1)} %maximum_select_fusion.1.own), channel_id=1, source_target_pairs={{0,192},{32,224},{64,0},{96,32},{128,64},{160,96},{192,128},{224,1... | collective-permute-start | bytes 393224 | tf_op jit(solution)/shard_map/ppermute | solution.py:383
  21.4 1.6 %broadcast_in_dim.7 = bf16[4,4,128,512]{3,2,1,0:T(8,128)(2,1)} broadcast(bf16[4,128,512]{2,1,0:T(8,128)(2,1)S(1)} %all-to-all-done), dimensions={1,2,3} | broadcast | bytes 2621440 | tf_op jit(solution)/shard_map/broadcast_in_dim | solution.py:360
  23.0 4.8 %all-to-all-start.1 = ((bf16[4,4,128,512]{3,2,1,0:T(8,128)(2,1)}), bf16[4,4,128,512]{3,2,1,0:T(8,128)(2,1)S(1)}, u32[]{:S(2)}, u32[]{:S(2)}) async-start(bf16[4,4,128,512]{3,2,1,0:T(8,128)(2,1)} %broadcast_in_dim.7), calls=%async_computation.1 | async-start | bytes 4194304 | tf_op jit(solution)/shard_map/all_to_all | solution.py:359
  27.8 0.0 collective-permute-done.3.down2
  27.8 1.4 %collective-permute-start.4 = (bf16[64,512]{1,0:T(8,128)(2,1)S(1)}, bf16[64,512]{1,0:T(8,128)(2,1)S(1)}, u32[]{:S(2)}, u32[]{:S(2)}) collective-permute-start(bf16[64,512]{1,0:T(8,128)(2,1)S(1)} %slice_bitcast_fusion.12), channel_id=1, source_target_pairs={{0,64},{32,96},{64,128},{96,160},{128,192},{160,224},{192,0},{224,... | collective-permute-start | bytes 196616 | tf_op jit(solution)/shard_map/ppermute | solution.py:383
  29.3 1.1 %collective-permute-start.6 = (bf16[2,128,512]{2,1,0:T(8,128)(2,1)S(1)}, bf16[2,128,512]{2,1,0:T(8,128)(2,1)S(1)}, u32[]{:S(2)}, u32[]{:S(2)}) collective-permute-start(bf16[2,128,512]{2,1,0:T(8,128)(2,1)S(1)} %get-tuple-element.62), channel_id=1, source_target_pairs={{0,32},{32,64},{64,96},{96,128},{128,160},{160,192},{192,224},{224... | collective-permute-start | bytes 786440 | tf_op jit(solution)/shard_map/ppermute | solution.py:383
  30.4 2.2 %collective-permute-start.5 = (bf16[2,128,512]{2,1,0:T(8,128)(2,1)S(1)}, bf16[2,128,512]{2,1,0:T(8,128)(2,1)S(1)}, u32[]{:S(2)}, u32[]{:S(2)}) collective-permute-start(bf16[2,128,512]{2,1,0:T(8,128)(2,1)S(1)} %get-tuple-element.63), channel_id=1, source_target_pairs={{0,224},{32,0},{64,32},{96,64},{128,96},{160,128},{192,160},{224,1... | collective-permute-start | bytes 786440 | tf_op jit(solution)/shard_map/ppermute | solution.py:383
  32.6 1.6 %collective-permute-start.2 = (bf16[64,512]{1,0:T(8,128)(2,1)S(1)}, bf16[64,512]{1,0:T(8,128)(2,1)S(1)}, u32[]{:S(2)}, u32[]{:S(2)}) collective-permute-start(bf16[64,512]{1,0:T(8,128)(2,1)S(1)} %slice_bitcast_fusion.13), channel_id=1, source_target_pairs={{0,192},{32,224},{64,0},{96,32},{128,64},{160,96},{192,128},{224,1... | collective-permute-start | bytes 196616 | tf_op jit(solution)/shard_map/ppermute | solution.py:383
  34.2 0.1 pad_add_fusion.place_ref
  34.3 1.0 collective-permute-done.4.four1
  35.2 5.4 %collective-permute-done.2.four0 = bf16[64,512]{1,0:T(8,128)(2,1)S(1)} collective-permute-done((bf16[64,512]{1,0:T(8,128)(2,1)S(1)}, bf16[64,512]{1,0:T(8,128)(2,1)S(1)}, u32[]{:S(2)}, u32[]{:S(2)}) %collective-permute-start.2) | collective-permute-done | bytes 65568 | tf_op jit(solution)/shard_map/ppermute | solution.py:383
  40.6 0.0 collective-permute-done.6.down
  40.6 0.0 collective-permute-done.5.up
  40.6 0.2 shard_map.50
  40.8 1.2 %all-to-all-done.1 = bf16[4,4,128,512]{3,2,1,0:T(8,128)(2,1)S(1)} async-done(((bf16[4,4,128,512]{3,2,1,0:T(8,128)(2,1)}), bf16[4,4,128,512]{3,2,1,0:T(8,128)(2,1)S(1)}, u32[]{:S(2)}, u32[]{:S(2)}) %all-to-all-start.1) | async-done | bytes 2097184 | tf_op jit(solution)/shard_map/all_to_all | solution.py:359
  42.0 1.3 %shard_map.51.own_ref = f32[512,512]{1,0:T(8,128)S(1)} custom-call(s32[4]{0:T(128)S(1)} %pad_add_fusion.place_ref, bf16[16,128,512]{2,1,0:T(8,128)(2,1)S(1)} %bitcast.64, bf16[2,512,512]{2,1,0:T(8,128)(2,1)S(1)} %get-tuple-element.27.v2_ref), custom_call_target="tpu_custom_call" | custom-call | flops 536870912 | bytes 3145728 | tf_op jit(solution)/shard_map/pallas_call | solution.py:96
  43.3 0.1 collective-permute-start.7
  43.4 1.3 %shard_map.54.own_ref = f32[512,512]{1,0:T(8,128)S(1)} custom-call(s32[4]{0:T(128)S(1)} %pad_add_fusion.place_ref, bf16[16,128,512]{2,1,0:T(8,128)(2,1)S(1)} %bitcast.65, bf16[2,512,512]{2,1,0:T(8,128)(2,1)S(1)} %get-tuple-element.27.v2_ref), custom_call_target="tpu_custom_call" | custom-call | flops 536870912 | bytes 3145728 | tf_op jit(solution)/shard_map/pallas_call | solution.py:96
  44.7 0.6 collective-permute-start.8
  45.2 0.2 abs_reduce_fusion
  45.5 0.0 copy-start
  45.5 0.1 collective-permute-start.9
  45.6 0.7 shard_map.52
  46.3 0.6 shard_map.53
  46.9 0.6 collective-permute-done.9.most_other_ref
  47.5 1.2 %shard_map.55 = (f32[512,512]{1,0:T(8,128)S(1)}, f32[16,16,128]{2,1,0:T(8,128)S(1)}) custom-call(s32[4]{0:T(128)S(1)} %pad_add_fusion.place_ref, f32[512,512]{1,0:T(8,128)S(1)} %shard_map.54.own_ref, f32[512,512]{1,0:T(8,128)S(1)} %collective-permute-done.8.other_ref, f32[4,128]{1,0:T(4,128)S(1)} %get-tuple-element.32.first_ref, ...), custom_call_target="tpu_custom_call" | custom-call | flops 2621440 | bytes 3145728 | tf_op jit(solution)/shard_map/pallas_call | solution.py:216
  48.7 12.1 %all_to_all.20.seen_ref = f32[16,16,128]{2,1,0:T(8,128)S(1)} all-to-all(f32[16,16,128]{2,1,0:T(8,128)S(1)} %get-tuple-element.36), channel_id=1, replica_groups={{0,8,16,24,4,12,20,28,2,10,18,26,6,14,22,30},{32,40,48,56,36,44,52,60,3..., dimensions={0} | all-to-all | bytes 262144 | tf_op jit(solution)/shard_map/all_to_all | solution.py:422
  60.9 0.6 shard_map.56.known_ref
  61.5 2.1 %collective-permute-start.10 = (f32[24,128]{1,0:T(8,128)S(1)}, f32[24,128]{1,0:T(8,128)S(1)}, u32[]{:S(2)}, u32[]{:S(2)}) collective-permute-start(f32[24,128]{1,0:T(8,128)S(1)} %shard_map.56.known_ref), channel_id=1, source_target_pairs={{0,1},{1,0},{2,3},{3,2},{4,5},{5,4},{6,7},{7,6},{8,9},{9,8},{10,11... | collective-permute-start | bytes 36872 | tf_op jit(solution)/shard_map/ppermute | solution.py:336
  63.6 0.8 collective-permute-done.10.told_ref
  64.4 1.4 %shard_map.57 = (bf16[1024,512]{1,0:T(8,128)(2,1)S(1)}, f32[1,512]{1,0:T(1,128)S(1)}, f32[1,512]{1,0:T(1,128)S(1)}, f32[1,512]{1,0:T(1,128)S(1)}, f32[1,512]{1,0:T(1,128)S(1)}) custom-call(s32[4]{0:T(128)S(1)} %pad_add_fusion.place_ref, f32[512,512]{1,0:T(8,128)S(1)} %get-tuple-element.31.s0_ref, f32[512,512]{1,0:T(8,128)S(1)} %get-tuple-element.35.s1_ref, ...), custom_call_target="tpu_custom_call" | custom-call | flops 4194304 | bytes 3145728 | tf_op jit(solution)/shard_map/pallas_call | solution.py:320
  65.8 2.6 %multiply_convert_fusion = f16[2,1024,512]{2,1,0:T(8,128)(2,1)} fusion(bf16[2,512,512]{2,1,0:T(8,128)(2,1)S(1)} %get-tuple-element.27.v2_ref, f32[512]{0:T(512)S(1)} %bitcast.72, bf16[1024,512]{1,0:T(8,128)(2,1)S(1)} %get-tuple-element.39), kind=kOutput, calls=%fused_computation.1 | convolution fusion | flops 1075838976 | bytes 4196352 | tf_op jit(solution)/shard_map/dot_general | solution.py:431
  68.5 0.7 fusion.1
  69.2 0.7 fusion
  69.9 5.5 %all-to-all-start.3 = ((f16[16,128,512]{2,1,0:T(8,128)(2,1)}), f16[16,128,512]{2,1,0:T(8,128)(2,1)S(1)}, u32[]{:S(2)}, u32[]{:S(2)}) async-start(f16[16,128,512]{2,1,0:T(8,128)(2,1)} %bitcast.73), calls=%async_computation.3 | async-start | bytes 4194304 | tf_op jit(solution)/shard_map/all_to_all | solution.py:440
  75.5 0.1 slice_bitcast_fusion.4
  75.6 0.1 pad_maximum_fusion.3
  75.6 1.5 %collective-permute-start.12 = (f16[2,128,512]{2,1,0:T(8,128)(2,1)S(1)}, f16[2,128,512]{2,1,0:T(8,128)(2,1)S(1)}, u32[]{:S(2)}, u32[]{:S(2)}) collective-permute-start(f16[2,128,512]{2,1,0:T(8,128)(2,1)S(1)} %pad_maximum_fusion.3), channel_id=1, source_target_pairs={{0,224},{32,0},{64,32},{96,64},{128,96},{160,128},{192,160},{224,1... | collective-permute-start | bytes 786440 | tf_op jit(solution)/shard_map/ppermute | solution.py:383
  77.2 1.6 %collective-permute-start.15 = (f16[64,512]{1,0:T(8,128)(2,1)S(1)}, f16[64,512]{1,0:T(8,128)(2,1)S(1)}, u32[]{:S(2)}, u32[]{:S(2)}) collective-permute-start(f16[64,512]{1,0:T(8,128)(2,1)S(1)} %get-tuple-element.53), channel_id=1, source_target_pairs={{0,192},{32,224},{64,0},{96,32},{128,64},{160,96},{192,128},{224,1... | collective-permute-start | bytes 196616 | tf_op jit(solution)/shard_map/ppermute | solution.py:383
  78.8 1.4 %collective-permute-start.13 = (f16[64,512]{1,0:T(8,128)(2,1)S(1)}, f16[64,512]{1,0:T(8,128)(2,1)S(1)}, u32[]{:S(2)}, u32[]{:S(2)}) collective-permute-start(f16[64,512]{1,0:T(8,128)(2,1)S(1)} %get-tuple-element.50), channel_id=1, source_target_pairs={{0,64},{32,96},{64,128},{96,160},{128,192},{160,224},{192,0},{224,... | collective-permute-start | bytes 196616 | tf_op jit(solution)/shard_map/ppermute | solution.py:383
  80.2 0.1 pad_maximum_fusion.2
  80.3 0.7 collective-permute-start.11
  80.9 4.0 %collective-permute-done.12 = f16[2,128,512]{2,1,0:T(8,128)(2,1)S(1)} collective-permute-done((f16[2,128,512]{2,1,0:T(8,128)(2,1)S(1)}, f16[2,128,512]{2,1,0:T(8,128)(2,1)S(1)}, u32[]{:S(2)}, u32[]{:S(2)}) %collective-permute-start.12) | collective-permute-done | bytes 262176 | tf_op jit(solution)/shard_map/ppermute | solution.py:383
  84.9 0.1 convert_element_type.65
  85.0 2.4 %collective-permute-done.15 = f16[64,512]{1,0:T(8,128)(2,1)S(1)} collective-permute-done((f16[64,512]{1,0:T(8,128)(2,1)S(1)}, f16[64,512]{1,0:T(8,128)(2,1)S(1)}, u32[]{:S(2)}, u32[]{:S(2)}) %collective-permute-start.15) | collective-permute-done | bytes 65568 | tf_op jit(solution)/shard_map/ppermute | solution.py:383
  87.4 2.9 %collective-permute-start.16 = (f16[2,64,512]{2,1,0:T(8,128)(2,1)S(1)}, f16[2,64,512]{2,1,0:T(8,128)(2,1)S(1)}, u32[]{:S(2)}, u32[]{:S(2)}) collective-permute-start(f16[2,64,512]{2,1,0:T(8,128)(2,1)S(1)} %fusion.6), channel_id=1, source_target_pairs={{0,192},{32,224},{64,0},{96,32},{128,64},{160,96},{192,128},{224,1... | collective-permute-start | bytes 393224 | tf_op jit(solution)/shard_map/ppermute | solution.py:383
  90.3 0.3 collective-permute-done.11
  90.6 0.1 convert_element_type.64
  90.8 0.4 collective-permute-start.14
  91.1 3.5 %collective-permute-done.16 = f16[2,64,512]{2,1,0:T(8,128)(2,1)S(1)} collective-permute-done((f16[2,64,512]{2,1,0:T(8,128)(2,1)S(1)}, f16[2,64,512]{2,1,0:T(8,128)(2,1)S(1)}, u32[]{:S(2)}, u32[]{:S(2)}) %collective-permute-start.16) | collective-permute-done | bytes 131104 | tf_op jit(solution)/shard_map/ppermute | solution.py:383
  94.6 5.2 %collective-permute-done.14 = f16[2,64,512]{2,1,0:T(8,128)(2,1)S(1)} collective-permute-done((f16[2,64,512]{2,1,0:T(8,128)(2,1)S(1)}, f16[2,64,512]{2,1,0:T(8,128)(2,1)S(1)}, u32[]{:S(2)}, u32[]{:S(2)}) %collective-permute-start.14) | collective-permute-done | bytes 131104 | tf_op jit(solution)/shard_map/ppermute | solution.py:383
  99.8 0.1 fusion.4
  99.9 1.3 %collective-permute-start.17 = (f32[64,512]{1,0:T(8,128)S(1)}, f32[64,512]{1,0:T(8,128)S(1)}, u32[]{:S(2)}, u32[]{:S(2)}) collective-permute-start(f32[64,512]{1,0:T(8,128)S(1)} %get-tuple-element.61), channel_id=1, source_target_pairs={{0,2},{2,0},{1,3},{3,1},{4,6},{6,4},{5,7},{7,5},{8,10},{10,8},{9,1... | collective-permute-start | bytes 393224 | tf_op jit(solution)/shard_map/ppermute | solution.py:336
  101.3 1.8 %all-to-all-done.3 = f16[16,128,512]{2,1,0:T(8,128)(2,1)S(1)} async-done(((f16[16,128,512]{2,1,0:T(8,128)(2,1)}), f16[16,128,512]{2,1,0:T(8,128)(2,1)S(1)}, u32[]{:S(2)}, u32[]{:S(2)}) %all-to-all-start.3) | async-done | bytes 2097184 | tf_op jit(solution)/shard_map/all_to_all | solution.py:440
  103.1 1.1 %multiply_reduce_fusion = f32[128,512]{1,0:T(8,128)} fusion(f16[16,128,512]{2,1,0:T(8,128)(2,1)S(1)} %all-to-all-done.3, f32[512]{0:T(512)S(1)} %bitcast.68), kind=kLoop, calls=%fused_computation | loop fusion | flops 3080192 | bytes 2361344 | tf_op jit(solution)/shard_map/reduce_sum | solution.py:469
  104.2 1.3 %collective-permute-done.17 = f32[64,512]{1,0:T(8,128)S(1)} collective-permute-done((f32[64,512]{1,0:T(8,128)S(1)}, f32[64,512]{1,0:T(8,128)S(1)}, u32[]{:S(2)}, u32[]{:S(2)}) %collective-permute-start.17) | collective-permute-done | bytes 131104 | tf_op jit(solution)/shard_map/ppermute | solution.py:336
  105.5 0.7 maximum_select_fusion
  (22 shorter events, 0.4 us)
Async XLA Ops:
  2.4 12.5 %all-to-all-start = ((bf16[4,128,512]{2,1,0:T(8,128)(2,1)}), bf16[4,128,512]{2,1,0:T(8,128)(2,1)S(1)}, u32[]{:S(2)}, u32[]{:S(2)}) async-start(bf16[4,128,512]{2,1,0:T(8,128)(2,1)} %broadcast_in_dim.6), calls=%async_computation | async-start | bytes 1048576 | tf_op jit(solution)/shard_map/all_to_all | solution.py:359
  7.7 5.1 %collective-permute-start = (bf16[64,512]{1,0:T(8,128)(2,1)S(1)}, bf16[64,512]{1,0:T(8,128)(2,1)S(1)}, u32[]{:S(2)}, u32[]{:S(2)}) collective-permute-start(bf16[64,512]{1,0:T(8,128)(2,1)S(1)} %get-tuple-element.65), channel_id=1, source_target_pairs={{0,2},{2,0},{1,3},{3,1},{4,6},{6,4},{5,7},{7,5},{8,10},{10,8},{9,1... | collective-permute-start | bytes 196616 | tf_op jit(solution)/shard_map/ppermute | solution.py:336
  15.0 12.8 %collective-permute-start.3 = (bf16[2,64,512]{2,1,0:T(8,128)(2,1)S(1)}, bf16[2,64,512]{2,1,0:T(8,128)(2,1)S(1)}, u32[]{:S(2)}, u32[]{:S(2)}) collective-permute-start(bf16[2,64,512]{2,1,0:T(8,128)(2,1)S(1)} %maximum_select_fusion.1.own), channel_id=1, source_target_pairs={{0,64},{32,96},{64,128},{96,160},{128,192},{160,224},{192,0},{224,... | collective-permute-start | bytes 393224 | tf_op jit(solution)/shard_map/ppermute | solution.py:383
  18.3 10.9 %collective-permute-start.1 = (bf16[2,64,512]{2,1,0:T(8,128)(2,1)S(1)}, bf16[2,64,512]{2,1,0:T(8,128)(2,1)S(1)}, u32[]{:S(2)}, u32[]{:S(2)}) collective-permute-start(bf16[2,64,512]{2,1,0:T(8,128)(2,1)S(1)} %maximum_select_fusion.1.own), channel_id=1, source_target_pairs={{0,192},{32,224},{64,0},{96,32},{128,64},{160,96},{192,128},{224,1... | collective-permute-start | bytes 393224 | tf_op jit(solution)/shard_map/ppermute | solution.py:383
  23.0 19.0 %all-to-all-start.1 = ((bf16[4,4,128,512]{3,2,1,0:T(8,128)(2,1)}), bf16[4,4,128,512]{3,2,1,0:T(8,128)(2,1)S(1)}, u32[]{:S(2)}, u32[]{:S(2)}) async-start(bf16[4,4,128,512]{3,2,1,0:T(8,128)(2,1)} %broadcast_in_dim.7), calls=%async_computation.1 | async-start | bytes 4194304 | tf_op jit(solution)/shard_map/all_to_all | solution.py:359
  27.8 7.4 %collective-permute-start.4 = (bf16[64,512]{1,0:T(8,128)(2,1)S(1)}, bf16[64,512]{1,0:T(8,128)(2,1)S(1)}, u32[]{:S(2)}, u32[]{:S(2)}) collective-permute-start(bf16[64,512]{1,0:T(8,128)(2,1)S(1)} %slice_bitcast_fusion.12), channel_id=1, source_target_pairs={{0,64},{32,96},{64,128},{96,160},{128,192},{160,224},{192,0},{224,... | collective-permute-start | bytes 196616 | tf_op jit(solution)/shard_map/ppermute | solution.py:383
  29.3 11.3 %collective-permute-start.6 = (bf16[2,128,512]{2,1,0:T(8,128)(2,1)S(1)}, bf16[2,128,512]{2,1,0:T(8,128)(2,1)S(1)}, u32[]{:S(2)}, u32[]{:S(2)}) collective-permute-start(bf16[2,128,512]{2,1,0:T(8,128)(2,1)S(1)} %get-tuple-element.62), channel_id=1, source_target_pairs={{0,32},{32,64},{64,96},{96,128},{128,160},{160,192},{192,224},{224... | collective-permute-start | bytes 786440 | tf_op jit(solution)/shard_map/ppermute | solution.py:383
  30.4 10.2 %collective-permute-start.5 = (bf16[2,128,512]{2,1,0:T(8,128)(2,1)S(1)}, bf16[2,128,512]{2,1,0:T(8,128)(2,1)S(1)}, u32[]{:S(2)}, u32[]{:S(2)}) collective-permute-start(bf16[2,128,512]{2,1,0:T(8,128)(2,1)S(1)} %get-tuple-element.63), channel_id=1, source_target_pairs={{0,224},{32,0},{64,32},{96,64},{128,96},{160,128},{192,160},{224,1... | collective-permute-start | bytes 786440 | tf_op jit(solution)/shard_map/ppermute | solution.py:383
  32.6 8.0 %collective-permute-start.2 = (bf16[64,512]{1,0:T(8,128)(2,1)S(1)}, bf16[64,512]{1,0:T(8,128)(2,1)S(1)}, u32[]{:S(2)}, u32[]{:S(2)}) collective-permute-start(bf16[64,512]{1,0:T(8,128)(2,1)S(1)} %slice_bitcast_fusion.13), channel_id=1, source_target_pairs={{0,192},{32,224},{64,0},{96,32},{128,64},{160,96},{192,128},{224,1... | collective-permute-start | bytes 196616 | tf_op jit(solution)/shard_map/ppermute | solution.py:383
  43.3 3.0 %collective-permute-start.7 = (f32[512,512]{1,0:T(8,128)S(1)}, f32[512,512]{1,0:T(8,128)S(1)}, u32[]{:S(2)}, u32[]{:S(2)}) collective-permute-start(f32[512,512]{1,0:T(8,128)S(1)} %shard_map.51.own_ref), channel_id=1, source_target_pairs={{0,1},{1,0},{2,3},{3,2},{4,5},{5,4},{6,7},{7,6},{8,9},{9,8},{10,11... | collective-permute-start | bytes 3145736 | tf_op jit(solution)/shard_map/ppermute | solution.py:336
  44.7 2.9 %collective-permute-start.8 = (f32[512,512]{1,0:T(8,128)S(1)}, f32[512,512]{1,0:T(8,128)S(1)}, u32[]{:S(2)}, u32[]{:S(2)}) collective-permute-start(f32[512,512]{1,0:T(8,128)S(1)} %shard_map.54.own_ref), channel_id=1, source_target_pairs={{0,1},{1,0},{2,3},{3,2},{4,5},{5,4},{6,7},{7,6},{8,9},{9,8},{10,11... | collective-permute-start | bytes 3145736 | tf_op jit(solution)/shard_map/ppermute | solution.py:336
  45.5 2.1 %copy-start = (s32[128]{0:T(128)S(1)}, s32[128]{0:T(128)}, u32[]{:S(2)}) copy-start(s32[128]{0:T(128)} %param.5) | copy-start | bytes 1540
  45.5 2.0 %collective-permute-start.9 = (f32[2,512]{1,0:T(2,128)S(1)}, f32[2,512]{1,0:T(2,128)S(1)}, u32[]{:S(2)}, u32[]{:S(2)}) collective-permute-start(f32[2,512]{1,0:T(2,128)S(1)} %pad_maximum_fusion.4.most_ref), channel_id=1, source_target_pairs={{0,1},{1,0},{2,3},{3,2},{4,5},{5,4},{6,7},{7,6},{8,9},{9,8},{10,11... | collective-permute-start | bytes 12296 | tf_op jit(solution)/shard_map/ppermute | solution.py:336
  61.5 3.0 %collective-permute-start.10 = (f32[24,128]{1,0:T(8,128)S(1)}, f32[24,128]{1,0:T(8,128)S(1)}, u32[]{:S(2)}, u32[]{:S(2)}) collective-permute-start(f32[24,128]{1,0:T(8,128)S(1)} %shard_map.56.known_ref), channel_id=1, source_target_pairs={{0,1},{1,0},{2,3},{3,2},{4,5},{5,4},{6,7},{7,6},{8,9},{9,8},{10,11... | collective-permute-start | bytes 36872 | tf_op jit(solution)/shard_map/ppermute | solution.py:336
  69.9 33.1 %all-to-all-start.3 = ((f16[16,128,512]{2,1,0:T(8,128)(2,1)}), f16[16,128,512]{2,1,0:T(8,128)(2,1)S(1)}, u32[]{:S(2)}, u32[]{:S(2)}) async-start(f16[16,128,512]{2,1,0:T(8,128)(2,1)} %bitcast.73), calls=%async_computation.3 | async-start | bytes 4194304 | tf_op jit(solution)/shard_map/all_to_all | solution.py:440
  75.6 9.3 %collective-permute-start.12 = (f16[2,128,512]{2,1,0:T(8,128)(2,1)S(1)}, f16[2,128,512]{2,1,0:T(8,128)(2,1)S(1)}, u32[]{:S(2)}, u32[]{:S(2)}) collective-permute-start(f16[2,128,512]{2,1,0:T(8,128)(2,1)S(1)} %pad_maximum_fusion.3), channel_id=1, source_target_pairs={{0,224},{32,0},{64,32},{96,64},{128,96},{160,128},{192,160},{224,1... | collective-permute-start | bytes 786440 | tf_op jit(solution)/shard_map/ppermute | solution.py:383
  77.2 10.2 %collective-permute-start.15 = (f16[64,512]{1,0:T(8,128)(2,1)S(1)}, f16[64,512]{1,0:T(8,128)(2,1)S(1)}, u32[]{:S(2)}, u32[]{:S(2)}) collective-permute-start(f16[64,512]{1,0:T(8,128)(2,1)S(1)} %get-tuple-element.53), channel_id=1, source_target_pairs={{0,192},{32,224},{64,0},{96,32},{128,64},{160,96},{192,128},{224,1... | collective-permute-start | bytes 196616 | tf_op jit(solution)/shard_map/ppermute | solution.py:383
  78.8 11.9 %collective-permute-start.13 = (f16[64,512]{1,0:T(8,128)(2,1)S(1)}, f16[64,512]{1,0:T(8,128)(2,1)S(1)}, u32[]{:S(2)}, u32[]{:S(2)}) collective-permute-start(f16[64,512]{1,0:T(8,128)(2,1)S(1)} %get-tuple-element.50), channel_id=1, source_target_pairs={{0,64},{32,96},{64,128},{96,160},{128,192},{160,224},{192,0},{224,... | collective-permute-start | bytes 196616 | tf_op jit(solution)/shard_map/ppermute | solution.py:383
  80.3 10.3 %collective-permute-start.11 = (f16[2,128,512]{2,1,0:T(8,128)(2,1)S(1)}, f16[2,128,512]{2,1,0:T(8,128)(2,1)S(1)}, u32[]{:S(2)}, u32[]{:S(2)}) collective-permute-start(f16[2,128,512]{2,1,0:T(8,128)(2,1)S(1)} %pad_maximum_fusion.2), channel_id=1, source_target_pairs={{0,32},{32,64},{64,96},{96,128},{128,160},{160,192},{192,224},{224... | collective-permute-start | bytes 786440 | tf_op jit(solution)/shard_map/ppermute | solution.py:383
  87.4 7.2 %collective-permute-start.16 = (f16[2,64,512]{2,1,0:T(8,128)(2,1)S(1)}, f16[2,64,512]{2,1,0:T(8,128)(2,1)S(1)}, u32[]{:S(2)}, u32[]{:S(2)}) collective-permute-start(f16[2,64,512]{2,1,0:T(8,128)(2,1)S(1)} %fusion.6), channel_id=1, source_target_pairs={{0,192},{32,224},{64,0},{96,32},{128,64},{160,96},{192,128},{224,1... | collective-permute-start | bytes 393224 | tf_op jit(solution)/shard_map/ppermute | solution.py:383
  90.8 9.0 %collective-permute-start.14 = (f16[2,64,512]{2,1,0:T(8,128)(2,1)S(1)}, f16[2,64,512]{2,1,0:T(8,128)(2,1)S(1)}, u32[]{:S(2)}, u32[]{:S(2)}) collective-permute-start(f16[2,64,512]{2,1,0:T(8,128)(2,1)S(1)} %fusion.5), channel_id=1, source_target_pairs={{0,64},{32,96},{64,128},{96,160},{128,192},{160,224},{192,0},{224,... | collective-permute-start | bytes 393224 | tf_op jit(solution)/shard_map/ppermute | solution.py:383
  99.9 5.5 %collective-permute-start.17 = (f32[64,512]{1,0:T(8,128)S(1)}, f32[64,512]{1,0:T(8,128)S(1)}, u32[]{:S(2)}, u32[]{:S(2)}) collective-permute-start(f32[64,512]{1,0:T(8,128)S(1)} %get-tuple-element.61), channel_id=1, source_target_pairs={{0,2},{2,0},{1,3},{3,1},{4,6},{6,4},{5,7},{7,5},{8,10},{10,8},{9,1... | collective-permute-start | bytes 393224 | tf_op jit(solution)/shard_map/ppermute | solution.py:336

commit v10 on v8

--- a/solution.py
+++ b/solution.py
@@ -74,7 +74,7 @@
         in_specs=[VMEM] * 7,
         out_specs=(VMEM, VMEM),
         compiler_params=limit(4),
-        cost_estimate=pl.CostEstimate(flops=2**20, bytes_accessed=2**21, transcendentals=0),
+        cost_estimate=pl.CostEstimate(flops=12 * 2**30, bytes_accessed=2**21, transcendentals=0),
     )(*parts)
 
 
@@ -462,12 +462,13 @@
     from_down = to_plane((down2 * 0.25).astype(jnp.float16), -2)
     total = blocks(0, 1).astype(jnp.float32) + wide[0][:, :HALF] + wide[1][:, :HALF]
     total = total + 4.0 * (from_up.astype(jnp.float32) + from_down.astype(jnp.float32))
-    total = total * take_two
     stay = jnp.where(xl == 0, total[0], total[1])
-    come = swap(jnp.where(xl == 0, total[1], total[0]), "xl")
+    leave = jnp.where(xl == 0, total[1], total[0])
+    come = swap((leave * 0.125).astype(jnp.float16), "xl")
     grad_one = jnp.sum(one_parts.astype(jnp.float32) * take_one, axis=0)
     come, grad_one = lax.optimization_barrier((come, grad_one))
-    grad_two = jnp.where(
+    come = 8.0 * come.astype(jnp.float32)
+    grad_two = take_two * jnp.where(
         xl == 0, jnp.concatenate([stay, come]), jnp.concatenate([come, stay])
     )
     return (grad_one, grad_two)

time: 111 us -> 107 us (0.964); the launches traced: 110 us -> 105 us
  waiting for transfers between devices: 37.4 us -> 32.1 us
  blocking collectives: 14.4 us -> 12.1 us
  starting transfers between devices: 39.1 us -> 41.4 us
    ppermute x12, waiting for transfers between devices: 26.1 us -> 21.6 us  [to_plane(): return lax.ppermute(x, 'z', [(z, (z + dz) % NZ) for z in range(NZ)])]
    all_to_all x1, blocking collectives: 14.4 us -> 12.1 us  [on_device(): lax.all_to_all(pack, EVERY, 0, 0, axis_index_groups=stat_groups(), tiled=...]
    ppermute x6, starting transfers between devices: 3.65 us -> 5.51 us  [swap(): return lax.ppermute(x, axis, [(0, 1), (1, 0)])]
    ppermute x6, waiting for transfers between devices: 6.78 us -> 5.36 us  [swap(): return lax.ppermute(x, axis, [(0, 1), (1, 0)])]
    all_to_all x2, waiting for transfers between devices: 2.08 us -> 3.32 us  [spread(): lax.all_to_all(jnp.broadcast_to(x[None], (4,) + x.shape), EVERY, 0, 0, ax...]
  transfers between devices with their start and end apart: 21 -> 21, of which waited for: 14 -> 15; matrix products, arithmetic and copies ran while one was open for 3% -> 4% of each run, Pallas kernels for 2% -> 3%
where the time goes in v10:
time: 107 us; the launch traced here: 105 us
  starting transfers between devices  41.4 us (39%)
  waiting for transfers between devices  32.1 us (30%)
  blocking collectives  12.1 us (11%)
  Pallas kernels  7.2 us (7%)
  matrix products  4.11 us (4%)
  other arithmetic  3.65 us (3%)
  local copies, waits for them, and re-layouts  3.56 us (3%)
    ppermute x12, waiting for transfers between devices, to_plane(): return lax.ppermute(x, 'z', [(z, (z + dz) % NZ) for z in range(NZ)])  21.6 us
    ppermute x12, starting transfers between devices, to_plane(): return lax.ppermute(x, 'z', [(z, (z + dz) % NZ) for z in range(NZ)])  21.2 us
    all_to_all x1, blocking collectives, on_device(): lax.all_to_all(pack, EVERY, 0, 0, axis_index_groups=stat_groups(), tiled=...  12.1 us
    all_to_all x2, starting transfers between devices, spread(): lax.all_to_all(jnp.broadcast_to(x[None], (4,) + x.shape), EVERY, 0, 0, ax...  9.26 us
    ppermute x6, starting transfers between devices, swap(): return lax.ppermute(x, axis, [(0, 1), (1, 0)])  5.51 us
    all_to_all x1, starting transfers between devices, on_device(): lax.all_to_all(part_one.reshape(16, ROWS, WIDTH), PLANE, 0, 0, tiled=True)  5.48 us
    ppermute x6, waiting for transfers between devices, swap(): return lax.ppermute(x, axis, [(0, 1), (1, 0)])  5.36 us
    broadcast_in_dim x2, local copies, waits for them, and re-layouts, spread(): jnp.broadcast_to(x[None], (4,) + x.shape)  3.33 us
  transfers between devices with their start and end apart: 21, of which 15 were waited for; matrix products, arithmetic and copies ran while one was open for 4% of the time, Pallas kernels for 3%

profile of v10, /device:TPU:4, one launch (start us, length us, event | category | flops | bytes accessed | tf_op | source)
XLA Modules:
  0.0 105.1 jit_solution(4335557432444077978)
XLA Ops:
  0.6 1.8 %broadcast_in_dim.6 = bf16[4,128,512]{2,1,0:T(8,128)(2,1)} broadcast(bf16[128,512]{1,0:T(8,128)(2,1)} %param.3), dimensions={1,2} | broadcast | bytes 655360 | tf_op jit(solution)/shard_map/broadcast_in_dim | solution.py:360
  2.4 4.5 %all-to-all-start = ((bf16[4,128,512]{2,1,0:T(8,128)(2,1)}), bf16[4,128,512]{2,1,0:T(8,128)(2,1)S(1)}, u32[]{:S(2)}, u32[]{:S(2)}) async-start(bf16[4,128,512]{2,1,0:T(8,128)(2,1)} %broadcast_in_dim.6), calls=%async_computation | async-start | bytes 1048576 | tf_op jit(solution)/shard_map/all_to_all | solution.py:359
  6.9 0.9 select_bitcast_fusion.1
  7.7 1.3 %collective-permute-start = (bf16[64,512]{1,0:T(8,128)(2,1)S(1)}, bf16[64,512]{1,0:T(8,128)(2,1)S(1)}, u32[]{:S(2)}, u32[]{:S(2)}) collective-permute-start(bf16[64,512]{1,0:T(8,128)(2,1)S(1)} %get-tuple-element.59), channel_id=1, source_target_pairs={{0,2},{2,0},{1,3},{3,1},{4,6},{6,4},{5,7},{7,5},{8,10},{10,8},{9,1... | collective-permute-start | bytes 196616 | tf_op jit(solution)/shard_map/ppermute | solution.py:336
  9.0 3.8 %collective-permute-done = bf16[64,512]{1,0:T(8,128)(2,1)S(1)} collective-permute-done((bf16[64,512]{1,0:T(8,128)(2,1)S(1)}, bf16[64,512]{1,0:T(8,128)(2,1)S(1)}, u32[]{:S(2)}, u32[]{:S(2)}) %collective-permute-start) | collective-permute-done | bytes 65568 | tf_op jit(solution)/shard_map/ppermute | solution.py:336
  12.9 2.1 %all-to-all-done = bf16[4,128,512]{2,1,0:T(8,128)(2,1)S(1)} async-done(((bf16[4,128,512]{2,1,0:T(8,128)(2,1)}), bf16[4,128,512]{2,1,0:T(8,128)(2,1)S(1)}, u32[]{:S(2)}, u32[]{:S(2)}) %all-to-all-start) | async-done | bytes 524320 | tf_op jit(solution)/shard_map/all_to_all | solution.py:359
  15.0 3.3 %collective-permute-start.3 = (bf16[2,64,512]{2,1,0:T(8,128)(2,1)S(1)}, bf16[2,64,512]{2,1,0:T(8,128)(2,1)S(1)}, u32[]{:S(2)}, u32[]{:S(2)}) collective-permute-start(bf16[2,64,512]{2,1,0:T(8,128)(2,1)S(1)} %maximum_select_fusion.1.own), channel_id=1, source_target_pairs={{0,64},{32,96},{64,128},{96,160},{128,192},{160,224},{192,0},{224,... | collective-permute-start | bytes 393224 | tf_op jit(solution)/shard_map/ppermute | solution.py:383
  18.3 3.1 %collective-permute-start.1 = (bf16[2,64,512]{2,1,0:T(8,128)(2,1)S(1)}, bf16[2,64,512]{2,1,0:T(8,128)(2,1)S(1)}, u32[]{:S(2)}, u32[]{:S(2)}) collective-permute-start(bf16[2,64,512]{2,1,0:T(8,128)(2,1)S(1)} %maximum_select_fusion.1.own), channel_id=1, source_target_pairs={{0,192},{32,224},{64,0},{96,32},{128,64},{160,96},{192,128},{224,1... | collective-permute-start | bytes 393224 | tf_op jit(solution)/shard_map/ppermute | solution.py:383
  21.4 1.6 %broadcast_in_dim.7 = bf16[4,4,128,512]{3,2,1,0:T(8,128)(2,1)} broadcast(bf16[4,128,512]{2,1,0:T(8,128)(2,1)S(1)} %all-to-all-done), dimensions={1,2,3} | broadcast | bytes 2621440 | tf_op jit(solution)/shard_map/broadcast_in_dim | solution.py:360
  23.0 4.8 %all-to-all-start.1 = ((bf16[4,4,128,512]{3,2,1,0:T(8,128)(2,1)}), bf16[4,4,128,512]{3,2,1,0:T(8,128)(2,1)S(1)}, u32[]{:S(2)}, u32[]{:S(2)}) async-start(bf16[4,4,128,512]{3,2,1,0:T(8,128)(2,1)} %broadcast_in_dim.7), calls=%async_computation.1 | async-start | bytes 4194304 | tf_op jit(solution)/shard_map/all_to_all | solution.py:359
  27.8 0.0 collective-permute-done.3.down2
  27.8 1.4 %collective-permute-start.4 = (bf16[64,512]{1,0:T(8,128)(2,1)S(1)}, bf16[64,512]{1,0:T(8,128)(2,1)S(1)}, u32[]{:S(2)}, u32[]{:S(2)}) collective-permute-start(bf16[64,512]{1,0:T(8,128)(2,1)S(1)} %slice_bitcast_fusion.12), channel_id=1, source_target_pairs={{0,64},{32,96},{64,128},{96,160},{128,192},{160,224},{192,0},{224,... | collective-permute-start | bytes 196616 | tf_op jit(solution)/shard_map/ppermute | solution.py:383
  29.2 0.0 collective-permute-done.1.up2
  29.3 1.1 %collective-permute-start.6 = (bf16[2,128,512]{2,1,0:T(8,128)(2,1)S(1)}, bf16[2,128,512]{2,1,0:T(8,128)(2,1)S(1)}, u32[]{:S(2)}, u32[]{:S(2)}) collective-permute-start(bf16[2,128,512]{2,1,0:T(8,128)(2,1)S(1)} %get-tuple-element.56), channel_id=1, source_target_pairs={{0,32},{32,64},{64,96},{96,128},{128,160},{160,192},{192,224},{224... | collective-permute-start | bytes 786440 | tf_op jit(solution)/shard_map/ppermute | solution.py:383
  30.4 2.2 %collective-permute-start.5 = (bf16[2,128,512]{2,1,0:T(8,128)(2,1)S(1)}, bf16[2,128,512]{2,1,0:T(8,128)(2,1)S(1)}, u32[]{:S(2)}, u32[]{:S(2)}) collective-permute-start(bf16[2,128,512]{2,1,0:T(8,128)(2,1)S(1)} %get-tuple-element.57), channel_id=1, source_target_pairs={{0,224},{32,0},{64,32},{96,64},{128,96},{160,128},{192,160},{224,1... | collective-permute-start | bytes 786440 | tf_op jit(solution)/shard_map/ppermute | solution.py:383
  32.6 1.6 %collective-permute-start.2 = (bf16[64,512]{1,0:T(8,128)(2,1)S(1)}, bf16[64,512]{1,0:T(8,128)(2,1)S(1)}, u32[]{:S(2)}, u32[]{:S(2)}) collective-permute-start(bf16[64,512]{1,0:T(8,128)(2,1)S(1)} %slice_bitcast_fusion.13), channel_id=1, source_target_pairs={{0,192},{32,224},{64,0},{96,32},{128,64},{160,96},{192,128},{224,1... | collective-permute-start | bytes 196616 | tf_op jit(solution)/shard_map/ppermute | solution.py:383
  34.2 0.1 pad_add_fusion.place_ref
  34.3 1.0 collective-permute-done.4.four1
  35.2 5.4 %collective-permute-done.2.four0 = bf16[64,512]{1,0:T(8,128)(2,1)S(1)} collective-permute-done((bf16[64,512]{1,0:T(8,128)(2,1)S(1)}, bf16[64,512]{1,0:T(8,128)(2,1)S(1)}, u32[]{:S(2)}, u32[]{:S(2)}) %collective-permute-start.2) | collective-permute-done | bytes 65568 | tf_op jit(solution)/shard_map/ppermute | solution.py:383
  40.6 0.2 shard_map.50
  40.8 1.2 %all-to-all-done.1 = bf16[4,4,128,512]{3,2,1,0:T(8,128)(2,1)S(1)} async-done(((bf16[4,4,128,512]{3,2,1,0:T(8,128)(2,1)}), bf16[4,4,128,512]{3,2,1,0:T(8,128)(2,1)S(1)}, u32[]{:S(2)}, u32[]{:S(2)}) %all-to-all-start.1) | async-done | bytes 2097184 | tf_op jit(solution)/shard_map/all_to_all | solution.py:359
  42.0 1.3 %shard_map.51.own_ref = f32[512,512]{1,0:T(8,128)S(1)} custom-call(s32[4]{0:T(128)S(1)} %pad_add_fusion.place_ref, bf16[16,128,512]{2,1,0:T(8,128)(2,1)S(1)} %bitcast.64, bf16[2,512,512]{2,1,0:T(8,128)(2,1)S(1)} %get-tuple-element.24.v2_ref), custom_call_target="tpu_custom_call" | custom-call | flops 536870912 | bytes 3145728 | tf_op jit(solution)/shard_map/pallas_call | solution.py:96
  43.3 0.1 collective-permute-start.7
  43.4 1.3 %shard_map.53.own_ref = f32[512,512]{1,0:T(8,128)S(1)} custom-call(s32[4]{0:T(128)S(1)} %pad_add_fusion.place_ref, bf16[16,128,512]{2,1,0:T(8,128)(2,1)S(1)} %bitcast.65, bf16[2,512,512]{2,1,0:T(8,128)(2,1)S(1)} %get-tuple-element.24.v2_ref), custom_call_target="tpu_custom_call" | custom-call | flops 536870912 | bytes 3145728 | tf_op jit(solution)/shard_map/pallas_call | solution.py:96
  44.7 0.0 copy-start
  44.7 0.6 collective-permute-start.8
  45.2 0.2 abs_reduce_fusion
  45.5 0.1 collective-permute-start.9
  45.6 0.4 collective-permute-done.7.other_ref
  46.0 0.6 shard_map.52
  46.6 0.9 collective-permute-done.9.most_other_ref
  47.5 1.2 %shard_map.54 = (f32[512,512]{1,0:T(8,128)S(1)}, f32[16,16,128]{2,1,0:T(8,128)S(1)}) custom-call(s32[4]{0:T(128)S(1)} %pad_add_fusion.place_ref, f32[512,512]{1,0:T(8,128)S(1)} %shard_map.53.own_ref, f32[512,512]{1,0:T(8,128)S(1)} %collective-permute-done.8.other_ref, f32[4,128]{1,0:T(4,128)S(1)} %get-tuple-element.26.first_ref, ...), custom_call_target="tpu_custom_call" | custom-call | flops 2621440 | bytes 3145728 | tf_op jit(solution)/shard_map/pallas_call | solution.py:216
  48.7 12.1 %all_to_all.20.seen_ref = f32[16,16,128]{2,1,0:T(8,128)S(1)} all-to-all(f32[16,16,128]{2,1,0:T(8,128)S(1)} %get-tuple-element.30), channel_id=1, replica_groups={{0,8,16,24,4,12,20,28,2,10,18,26,6,14,22,30},{32,40,48,56,36,44,52,60,3..., dimensions={0} | all-to-all | bytes 262144 | tf_op jit(solution)/shard_map/all_to_all | solution.py:420
  60.9 0.6 shard_map.55.known_ref
  61.5 2.1 %collective-permute-start.10 = (f32[24,128]{1,0:T(8,128)S(1)}, f32[24,128]{1,0:T(8,128)S(1)}, u32[]{:S(2)}, u32[]{:S(2)}) collective-permute-start(f32[24,128]{1,0:T(8,128)S(1)} %shard_map.55.known_ref), channel_id=1, source_target_pairs={{0,1},{1,0},{2,3},{3,2},{4,5},{5,4},{6,7},{7,6},{8,9},{9,8},{10,11... | collective-permute-start | bytes 36872 | tf_op jit(solution)/shard_map/ppermute | solution.py:336
  63.6 0.7 shard_map.57
  64.3 0.2 collective-permute-done.10.told_ref
  64.4 1.4 %shard_map.56 = (bf16[1024,512]{1,0:T(8,128)(2,1)S(1)}, f32[1,512]{1,0:T(1,128)S(1)}, f32[1,512]{1,0:T(1,128)S(1)}, f32[1,512]{1,0:T(1,128)S(1)}, f32[1,512]{1,0:T(1,128)S(1)}) custom-call(s32[4]{0:T(128)S(1)} %pad_add_fusion.place_ref, f32[512,512]{1,0:T(8,128)S(1)} %get-tuple-element.25.s0_ref, f32[512,512]{1,0:T(8,128)S(1)} %get-tuple-element.29.s1_ref, ...), custom_call_target="tpu_custom_call" | custom-call | flops 4194304 | bytes 3145728 | tf_op jit(solution)/shard_map/pallas_call | solution.py:320
  65.9 2.6 %multiply_convert_fusion = f16[2,1024,512]{2,1,0:T(8,128)(2,1)} fusion(bf16[2,512,512]{2,1,0:T(8,128)(2,1)S(1)} %get-tuple-element.24.v2_ref, f32[512]{0:T(512)S(1)} %bitcast.72, bf16[1024,512]{1,0:T(8,128)(2,1)S(1)} %get-tuple-element.33), kind=kOutput, calls=%fused_computation.1 | convolution fusion | flops 1075838976 | bytes 4196352 | tf_op jit(solution)/shard_map/dot_general | solution.py:430
  68.5 0.7 fusion.1
  69.2 0.7 fusion
  70.0 5.5 %all-to-all-start.3 = ((f16[16,128,512]{2,1,0:T(8,128)(2,1)}), f16[16,128,512]{2,1,0:T(8,128)(2,1)S(1)}, u32[]{:S(2)}, u32[]{:S(2)}) async-start(f16[16,128,512]{2,1,0:T(8,128)(2,1)} %bitcast.73), calls=%async_computation.3 | async-start | bytes 4194304 | tf_op jit(solution)/shard_map/all_to_all | solution.py:439
  75.5 0.1 slice_bitcast_fusion.4
  75.6 0.1 pad_maximum_fusion.3
  75.7 1.5 %collective-permute-start.12 = (f16[2,128,512]{2,1,0:T(8,128)(2,1)S(1)}, f16[2,128,512]{2,1,0:T(8,128)(2,1)S(1)}, u32[]{:S(2)}, u32[]{:S(2)}) collective-permute-start(f16[2,128,512]{2,1,0:T(8,128)(2,1)S(1)} %pad_maximum_fusion.3), channel_id=1, source_target_pairs={{0,224},{32,0},{64,32},{96,64},{128,96},{160,128},{192,160},{224,1... | collective-permute-start | bytes 786440 | tf_op jit(solution)/shard_map/ppermute | solution.py:383
  77.3 1.6 %collective-permute-start.15 = (f16[64,512]{1,0:T(8,128)(2,1)S(1)}, f16[64,512]{1,0:T(8,128)(2,1)S(1)}, u32[]{:S(2)}, u32[]{:S(2)}) collective-permute-start(f16[64,512]{1,0:T(8,128)(2,1)S(1)} %get-tuple-element.47), channel_id=1, source_target_pairs={{0,192},{32,224},{64,0},{96,32},{128,64},{160,96},{192,128},{224,1... | collective-permute-start | bytes 196616 | tf_op jit(solution)/shard_map/ppermute | solution.py:383
  78.9 1.4 %collective-permute-start.13 = (f16[64,512]{1,0:T(8,128)(2,1)S(1)}, f16[64,512]{1,0:T(8,128)(2,1)S(1)}, u32[]{:S(2)}, u32[]{:S(2)}) collective-permute-start(f16[64,512]{1,0:T(8,128)(2,1)S(1)} %get-tuple-element.44), channel_id=1, source_target_pairs={{0,64},{32,96},{64,128},{96,160},{128,192},{160,224},{192,0},{224,... | collective-permute-start | bytes 196616 | tf_op jit(solution)/shard_map/ppermute | solution.py:383
  80.3 0.1 pad_maximum_fusion.2
  80.3 0.7 collective-permute-start.11
  81.0 4.0 %collective-permute-done.12 = f16[2,128,512]{2,1,0:T(8,128)(2,1)S(1)} collective-permute-done((f16[2,128,512]{2,1,0:T(8,128)(2,1)S(1)}, f16[2,128,512]{2,1,0:T(8,128)(2,1)S(1)}, u32[]{:S(2)}, u32[]{:S(2)}) %collective-permute-start.12) | collective-permute-done | bytes 262176 | tf_op jit(solution)/shard_map/ppermute | solution.py:383
  85.0 0.1 convert_element_type.74
  85.1 2.3 %collective-permute-done.15 = f16[64,512]{1,0:T(8,128)(2,1)S(1)} collective-permute-done((f16[64,512]{1,0:T(8,128)(2,1)S(1)}, f16[64,512]{1,0:T(8,128)(2,1)S(1)}, u32[]{:S(2)}, u32[]{:S(2)}) %collective-permute-start.15) | collective-permute-done | bytes 65568 | tf_op jit(solution)/shard_map/ppermute | solution.py:383
  87.5 2.9 %collective-permute-start.16 = (f16[2,64,512]{2,1,0:T(8,128)(2,1)S(1)}, f16[2,64,512]{2,1,0:T(8,128)(2,1)S(1)}, u32[]{:S(2)}, u32[]{:S(2)}) collective-permute-start(f16[2,64,512]{2,1,0:T(8,128)(2,1)S(1)} %fusion.5), channel_id=1, source_target_pairs={{0,192},{32,224},{64,0},{96,32},{128,64},{160,96},{192,128},{224,1... | collective-permute-start | bytes 393224 | tf_op jit(solution)/shard_map/ppermute | solution.py:383
  90.4 0.3 collective-permute-done.11
  90.6 0.1 convert_element_type.73
  90.8 0.4 collective-permute-start.14
  91.2 3.5 %collective-permute-done.16 = f16[2,64,512]{2,1,0:T(8,128)(2,1)S(1)} collective-permute-done((f16[2,64,512]{2,1,0:T(8,128)(2,1)S(1)}, f16[2,64,512]{2,1,0:T(8,128)(2,1)S(1)}, u32[]{:S(2)}, u32[]{:S(2)}) %collective-permute-start.16) | collective-permute-done | bytes 131104 | tf_op jit(solution)/shard_map/ppermute | solution.py:383
  94.7 5.1 %collective-permute-done.14 = f16[2,64,512]{2,1,0:T(8,128)(2,1)S(1)} collective-permute-done((f16[2,64,512]{2,1,0:T(8,128)(2,1)S(1)}, f16[2,64,512]{2,1,0:T(8,128)(2,1)S(1)}, u32[]{:S(2)}, u32[]{:S(2)}) %collective-permute-start.14) | collective-permute-done | bytes 131104 | tf_op jit(solution)/shard_map/ppermute | solution.py:383
  99.9 0.1 fusion.3
  100.0 1.3 %collective-permute-start.17 = (f16[64,512]{1,0:T(8,128)(2,1)S(1)}, f16[64,512]{1,0:T(8,128)(2,1)S(1)}, u32[]{:S(2)}, u32[]{:S(2)}) collective-permute-start(f16[64,512]{1,0:T(8,128)(2,1)S(1)} %get-tuple-element.55), channel_id=1, source_target_pairs={{0,2},{2,0},{1,3},{3,1},{4,6},{6,4},{5,7},{7,5},{8,10},{10,8},{9,1... | collective-permute-start | bytes 196616 | tf_op jit(solution)/shard_map/ppermute | solution.py:336
  101.3 1.9 %all-to-all-done.3 = f16[16,128,512]{2,1,0:T(8,128)(2,1)S(1)} async-done(((f16[16,128,512]{2,1,0:T(8,128)(2,1)}), f16[16,128,512]{2,1,0:T(8,128)(2,1)S(1)}, u32[]{:S(2)}, u32[]{:S(2)}) %all-to-all-start.3) | async-done | bytes 2097184 | tf_op jit(solution)/shard_map/all_to_all | solution.py:439
  103.2 1.1 %multiply_reduce_fusion = f32[128,512]{1,0:T(8,128)} fusion(f16[16,128,512]{2,1,0:T(8,128)(2,1)S(1)} %all-to-all-done.3, f32[512]{0:T(512)S(1)} %bitcast.68), kind=kLoop, calls=%fused_computation | loop fusion | flops 3080192 | bytes 2361344 | tf_op jit(solution)/shard_map/reduce_sum | solution.py:468
  104.3 0.1 collective-permute-done.17
  104.4 0.7 fusion.6
  (23 shorter events, 0.4 us)
Async XLA Ops:
  2.4 12.5 %all-to-all-start = ((bf16[4,128,512]{2,1,0:T(8,128)(2,1)}), bf16[4,128,512]{2,1,0:T(8,128)(2,1)S(1)}, u32[]{:S(2)}, u32[]{:S(2)}) async-start(bf16[4,128,512]{2,1,0:T(8,128)(2,1)} %broadcast_in_dim.6), calls=%async_computation | async-start | bytes 1048576 | tf_op jit(solution)/shard_map/all_to_all | solution.py:359
  7.7 5.1 %collective-permute-start = (bf16[64,512]{1,0:T(8,128)(2,1)S(1)}, bf16[64,512]{1,0:T(8,128)(2,1)S(1)}, u32[]{:S(2)}, u32[]{:S(2)}) collective-permute-start(bf16[64,512]{1,0:T(8,128)(2,1)S(1)} %get-tuple-element.59), channel_id=1, source_target_pairs={{0,2},{2,0},{1,3},{3,1},{4,6},{6,4},{5,7},{7,5},{8,10},{10,8},{9,1... | collective-permute-start | bytes 196616 | tf_op jit(solution)/shard_map/ppermute | solution.py:336
  15.0 12.8 %collective-permute-start.3 = (bf16[2,64,512]{2,1,0:T(8,128)(2,1)S(1)}, bf16[2,64,512]{2,1,0:T(8,128)(2,1)S(1)}, u32[]{:S(2)}, u32[]{:S(2)}) collective-permute-start(bf16[2,64,512]{2,1,0:T(8,128)(2,1)S(1)} %maximum_select_fusion.1.own), channel_id=1, source_target_pairs={{0,64},{32,96},{64,128},{96,160},{128,192},{160,224},{192,0},{224,... | collective-permute-start | bytes 393224 | tf_op jit(solution)/shard_map/ppermute | solution.py:383
  18.3 10.9 %collective-permute-start.1 = (bf16[2,64,512]{2,1,0:T(8,128)(2,1)S(1)}, bf16[2,64,512]{2,1,0:T(8,128)(2,1)S(1)}, u32[]{:S(2)}, u32[]{:S(2)}) collective-permute-start(bf16[2,64,512]{2,1,0:T(8,128)(2,1)S(1)} %maximum_select_fusion.1.own), channel_id=1, source_target_pairs={{0,192},{32,224},{64,0},{96,32},{128,64},{160,96},{192,128},{224,1... | collective-permute-start | bytes 393224 | tf_op jit(solution)/shard_map/ppermute | solution.py:383
  23.0 19.0 %all-to-all-start.1 = ((bf16[4,4,128,512]{3,2,1,0:T(8,128)(2,1)}), bf16[4,4,128,512]{3,2,1,0:T(8,128)(2,1)S(1)}, u32[]{:S(2)}, u32[]{:S(2)}) async-start(bf16[4,4,128,512]{3,2,1,0:T(8,128)(2,1)} %broadcast_in_dim.7), calls=%async_computation.1 | async-start | bytes 4194304 | tf_op jit(solution)/shard_map/all_to_all | solution.py:359
  27.8 7.4 %collective-permute-start.4 = (bf16[64,512]{1,0:T(8,128)(2,1)S(1)}, bf16[64,512]{1,0:T(8,128)(2,1)S(1)}, u32[]{:S(2)}, u32[]{:S(2)}) collective-permute-start(bf16[64,512]{1,0:T(8,128)(2,1)S(1)} %slice_bitcast_fusion.12), channel_id=1, source_target_pairs={{0,64},{32,96},{64,128},{96,160},{128,192},{160,224},{192,0},{224,... | collective-permute-start | bytes 196616 | tf_op jit(solution)/shard_map/ppermute | solution.py:383
  29.3 11.3 %collective-permute-start.6 = (bf16[2,128,512]{2,1,0:T(8,128)(2,1)S(1)}, bf16[2,128,512]{2,1,0:T(8,128)(2,1)S(1)}, u32[]{:S(2)}, u32[]{:S(2)}) collective-permute-start(bf16[2,128,512]{2,1,0:T(8,128)(2,1)S(1)} %get-tuple-element.56), channel_id=1, source_target_pairs={{0,32},{32,64},{64,96},{96,128},{128,160},{160,192},{192,224},{224... | collective-permute-start | bytes 786440 | tf_op jit(solution)/shard_map/ppermute | solution.py:383
  30.4 10.2 %collective-permute-start.5 = (bf16[2,128,512]{2,1,0:T(8,128)(2,1)S(1)}, bf16[2,128,512]{2,1,0:T(8,128)(2,1)S(1)}, u32[]{:S(2)}, u32[]{:S(2)}) collective-permute-start(bf16[2,128,512]{2,1,0:T(8,128)(2,1)S(1)} %get-tuple-element.57), channel_id=1, source_target_pairs={{0,224},{32,0},{64,32},{96,64},{128,96},{160,128},{192,160},{224,1... | collective-permute-start | bytes 786440 | tf_op jit(solution)/shard_map/ppermute | solution.py:383
  32.6 8.0 %collective-permute-start.2 = (bf16[64,512]{1,0:T(8,128)(2,1)S(1)}, bf16[64,512]{1,0:T(8,128)(2,1)S(1)}, u32[]{:S(2)}, u32[]{:S(2)}) collective-permute-start(bf16[64,512]{1,0:T(8,128)(2,1)S(1)} %slice_bitcast_fusion.13), channel_id=1, source_target_pairs={{0,192},{32,224},{64,0},{96,32},{128,64},{160,96},{192,128},{224,1... | collective-permute-start | bytes 196616 | tf_op jit(solution)/shard_map/ppermute | solution.py:383
  43.3 2.7 %collective-permute-start.7 = (f32[512,512]{1,0:T(8,128)S(1)}, f32[512,512]{1,0:T(8,128)S(1)}, u32[]{:S(2)}, u32[]{:S(2)}) collective-permute-start(f32[512,512]{1,0:T(8,128)S(1)} %shard_map.51.own_ref), channel_id=1, source_target_pairs={{0,1},{1,0},{2,3},{3,2},{4,5},{5,4},{6,7},{7,6},{8,9},{9,8},{10,11... | collective-permute-start | bytes 3145736 | tf_op jit(solution)/shard_map/ppermute | solution.py:336
  44.7 2.9 %copy-start = (s32[128]{0:T(128)S(1)}, s32[128]{0:T(128)}, u32[]{:S(2)}) copy-start(s32[128]{0:T(128)} %param.5) | copy-start | bytes 1540
  44.7 2.9 %collective-permute-start.8 = (f32[512,512]{1,0:T(8,128)S(1)}, f32[512,512]{1,0:T(8,128)S(1)}, u32[]{:S(2)}, u32[]{:S(2)}) collective-permute-start(f32[512,512]{1,0:T(8,128)S(1)} %shard_map.53.own_ref), channel_id=1, source_target_pairs={{0,1},{1,0},{2,3},{3,2},{4,5},{5,4},{6,7},{7,6},{8,9},{9,8},{10,11... | collective-permute-start | bytes 3145736 | tf_op jit(solution)/shard_map/ppermute | solution.py:336
  45.5 2.0 %collective-permute-start.9 = (f32[2,512]{1,0:T(2,128)S(1)}, f32[2,512]{1,0:T(2,128)S(1)}, u32[]{:S(2)}, u32[]{:S(2)}) collective-permute-start(f32[2,512]{1,0:T(2,128)S(1)} %pad_maximum_fusion.4.most_ref), channel_id=1, source_target_pairs={{0,1},{1,0},{2,3},{3,2},{4,5},{5,4},{6,7},{7,6},{8,9},{9,8},{10,11... | collective-permute-start | bytes 12296 | tf_op jit(solution)/shard_map/ppermute | solution.py:336
  61.5 3.0 %collective-permute-start.10 = (f32[24,128]{1,0:T(8,128)S(1)}, f32[24,128]{1,0:T(8,128)S(1)}, u32[]{:S(2)}, u32[]{:S(2)}) collective-permute-start(f32[24,128]{1,0:T(8,128)S(1)} %shard_map.55.known_ref), channel_id=1, source_target_pairs={{0,1},{1,0},{2,3},{3,2},{4,5},{5,4},{6,7},{7,6},{8,9},{9,8},{10,11... | collective-permute-start | bytes 36872 | tf_op jit(solution)/shard_map/ppermute | solution.py:336
  70.0 33.2 %all-to-all-start.3 = ((f16[16,128,512]{2,1,0:T(8,128)(2,1)}), f16[16,128,512]{2,1,0:T(8,128)(2,1)S(1)}, u32[]{:S(2)}, u32[]{:S(2)}) async-start(f16[16,128,512]{2,1,0:T(8,128)(2,1)} %bitcast.73), calls=%async_computation.3 | async-start | bytes 4194304 | tf_op jit(solution)/shard_map/all_to_all | solution.py:439
  75.7 9.3 %collective-permute-start.12 = (f16[2,128,512]{2,1,0:T(8,128)(2,1)S(1)}, f16[2,128,512]{2,1,0:T(8,128)(2,1)S(1)}, u32[]{:S(2)}, u32[]{:S(2)}) collective-permute-start(f16[2,128,512]{2,1,0:T(8,128)(2,1)S(1)} %pad_maximum_fusion.3), channel_id=1, source_target_pairs={{0,224},{32,0},{64,32},{96,64},{128,96},{160,128},{192,160},{224,1... | collective-permute-start | bytes 786440 | tf_op jit(solution)/shard_map/ppermute | solution.py:383
  77.3 10.2 %collective-permute-start.15 = (f16[64,512]{1,0:T(8,128)(2,1)S(1)}, f16[64,512]{1,0:T(8,128)(2,1)S(1)}, u32[]{:S(2)}, u32[]{:S(2)}) collective-permute-start(f16[64,512]{1,0:T(8,128)(2,1)S(1)} %get-tuple-element.47), channel_id=1, source_target_pairs={{0,192},{32,224},{64,0},{96,32},{128,64},{160,96},{192,128},{224,1... | collective-permute-start | bytes 196616 | tf_op jit(solution)/shard_map/ppermute | solution.py:383
  78.9 11.9 %collective-permute-start.13 = (f16[64,512]{1,0:T(8,128)(2,1)S(1)}, f16[64,512]{1,0:T(8,128)(2,1)S(1)}, u32[]{:S(2)}, u32[]{:S(2)}) collective-permute-start(f16[64,512]{1,0:T(8,128)(2,1)S(1)} %get-tuple-element.44), channel_id=1, source_target_pairs={{0,64},{32,96},{64,128},{96,160},{128,192},{160,224},{192,0},{224,... | collective-permute-start | bytes 196616 | tf_op jit(solution)/shard_map/ppermute | solution.py:383
  80.3 10.3 %collective-permute-start.11 = (f16[2,128,512]{2,1,0:T(8,128)(2,1)S(1)}, f16[2,128,512]{2,1,0:T(8,128)(2,1)S(1)}, u32[]{:S(2)}, u32[]{:S(2)}) collective-permute-start(f16[2,128,512]{2,1,0:T(8,128)(2,1)S(1)} %pad_maximum_fusion.2), channel_id=1, source_target_pairs={{0,32},{32,64},{64,96},{96,128},{128,160},{160,192},{192,224},{224... | collective-permute-start | bytes 786440 | tf_op jit(solution)/shard_map/ppermute | solution.py:383
  87.5 7.2 %collective-permute-start.16 = (f16[2,64,512]{2,1,0:T(8,128)(2,1)S(1)}, f16[2,64,512]{2,1,0:T(8,128)(2,1)S(1)}, u32[]{:S(2)}, u32[]{:S(2)}) collective-permute-start(f16[2,64,512]{2,1,0:T(8,128)(2,1)S(1)} %fusion.5), channel_id=1, source_target_pairs={{0,192},{32,224},{64,0},{96,32},{128,64},{160,96},{192,128},{224,1... | collective-permute-start | bytes 393224 | tf_op jit(solution)/shard_map/ppermute | solution.py:383
  90.8 9.0 %collective-permute-start.14 = (f16[2,64,512]{2,1,0:T(8,128)(2,1)S(1)}, f16[2,64,512]{2,1,0:T(8,128)(2,1)S(1)}, u32[]{:S(2)}, u32[]{:S(2)}) collective-permute-start(f16[2,64,512]{2,1,0:T(8,128)(2,1)S(1)} %fusion.4), channel_id=1, source_target_pairs={{0,64},{32,96},{64,128},{96,160},{128,192},{160,224},{192,0},{224,... | collective-permute-start | bytes 393224 | tf_op jit(solution)/shard_map/ppermute | solution.py:383
  100.0 4.4 %collective-permute-start.17 = (f16[64,512]{1,0:T(8,128)(2,1)S(1)}, f16[64,512]{1,0:T(8,128)(2,1)S(1)}, u32[]{:S(2)}, u32[]{:S(2)}) collective-permute-start(f16[64,512]{1,0:T(8,128)(2,1)S(1)} %get-tuple-element.55), channel_id=1, source_target_pairs={{0,2},{2,0},{1,3},{3,1},{4,6},{6,4},{5,7},{7,5},{8,10},{10,8},{9,1... | collective-permute-start | bytes 196616 | tf_op jit(solution)/shard_map/ppermute | solution.py:336

commit v11 on v8

--- a/solution.py
+++ b/solution.py
@@ -52,6 +52,21 @@
     )(place, v1_all)
 
 
+def number_kernel(partner_ref, o_ref):
+    o_ref[...] = partner_ref[...].astype(jnp.float32)
+
+
+def numbers(partner):
+    return pl.pallas_call(
+        number_kernel,
+        out_shape=jax.ShapeDtypeStruct((1, ROWS), jnp.float32),
+        in_specs=[VMEM],
+        out_specs=VMEM,
+        compiler_params=limit(1),
+        cost_estimate=pl.CostEstimate(flops=8 * 2**30, bytes_accessed=2**10, transcendentals=0),
+    )(partner.reshape(1, ROWS))
+
+
 def join_kernel(own, four0, four1, up2, down2, up, down, v2_ref, most_ref):
     v2_ref[:, :HALF, :] = own[...]
     v2_ref[0, HALF : 2 * HALF, :] = four0[...]
@@ -74,7 +89,7 @@
         in_specs=[VMEM] * 7,
         out_specs=(VMEM, VMEM),
         compiler_params=limit(4),
-        cost_estimate=pl.CostEstimate(flops=2**20, bytes_accessed=2**21, transcendentals=0),
+        cost_estimate=pl.CostEstimate(flops=12 * 2**30, bytes_accessed=2**21, transcendentals=0),
     )(*parts)
 
 
@@ -204,7 +219,7 @@
         pack_ref[1, pl.ds(row, 1), :] = jnp.where(lane_half() == half, here, there)
     most = jnp.max(jnp.maximum(most_ref[...], most_other_ref[...]), axis=1, keepdims=True)
     most = jnp.broadcast_to(jnp.maximum(most, 1e-30), (2, LANES))
-    pack_ref[0, 8:9, :] = partner_ref[...].astype(jnp.float32)
+    pack_ref[0, 8:9, :] = partner_ref[...]
     pack_ref[0, 9:10, :] = most[0:1, :]
     pack_ref[1, 9:10, :] = most[1:2, :]
     chosen = jnp.where(place_ref[0] == 0, pack_ref[0], pack_ref[1])
@@ -226,7 +241,7 @@
         cost_estimate=pl.CostEstimate(
             flops=10 * NP * NJ, bytes_accessed=3 * 2**20, transcendentals=2 * NP * NJ
         ),
-    )(place, own, other, first, cols, partner.reshape(1, ROWS), most, most_other)
+    )(place, own, other, first, cols, partner, most, most_other)
 
 
 def merged(lses):
@@ -398,7 +413,8 @@
     give = jnp.where(xl == 0, view_two[HALF:], view_two[:HALF])
     side = swap(give, "xl")
     lines = spread(view_one, 0)
-    lines, side = lax.optimization_barrier((lines, side))
+    partner = numbers(partner)
+    lines, side, partner = lax.optimization_barrier((lines, side, partner))
     here = jnp.where(xl == 0, jnp.stack([keep, side]), jnp.stack([side, keep]))
     up2, down2 = to_plane(here, -2), to_plane(here, 2)
     v1_all = spread(lines, 1).reshape(16, ROWS, WIDTH)

time: 111 us -> 109 us (0.982)
  starting transfers between devices: 39.1 us -> 42.8 us
  blocking collectives: 14.4 us -> 10.8 us
  waiting for transfers between devices: 37.4 us -> 34.9 us
    all_to_all x2, waiting for transfers between devices: 2.08 us -> 7.96 us  [spread(): lax.all_to_all(jnp.broadcast_to(x[None], (4,) + x.shape), EVERY, 0, 0, ax...]
    ppermute x6, waiting for transfers between devices: 6.78 us -> 2.76 us  [swap(): return lax.ppermute(x, axis, [(0, 1), (1, 0)])]
    ppermute x12, waiting for transfers between devices: 26.1 us -> 22.3 us  [to_plane(): return lax.ppermute(x, 'z', [(z, (z + dz) % NZ) for z in range(NZ)])]
    all_to_all x1, blocking collectives: 14.4 us -> 10.8 us  [on_device(): lax.all_to_all(pack, EVERY, 0, 0, axis_index_groups=stat_groups(), tiled=...]
    ppermute x6, starting transfers between devices: 3.65 us -> 6.85 us  [swap(): return lax.ppermute(x, axis, [(0, 1), (1, 0)])]
  transfers between devices with their start and end apart: 21 -> 21, of which waited for: 14 -> 14; matrix products, arithmetic and copies ran while one was open for 3% -> 5% of each run, Pallas kernels for 2% -> 3%
where the time goes in v11:
time: 109 us; the launch traced here: 108 us
  starting transfers between devices  42.8 us (39%)
  waiting for transfers between devices  34.9 us (32%)
  blocking collectives  10.8 us (10%)
  Pallas kernels  7.19 us (7%)
  local copies, waits for them, and re-layouts  4.21 us (4%)
  matrix products  4.09 us (4%)
  other arithmetic  3.63 us (3%)
    ppermute x12, waiting for transfers between devices, to_plane(): return lax.ppermute(x, 'z', [(z, (z + dz) % NZ) for z in range(NZ)])  22.3 us
    ppermute x12, starting transfers between devices, to_plane(): return lax.ppermute(x, 'z', [(z, (z + dz) % NZ) for z in range(NZ)])  21.2 us
    all_to_all x1, blocking collectives, on_device(): lax.all_to_all(pack, EVERY, 0, 0, axis_index_groups=stat_groups(), tiled=...  10.8 us
    all_to_all x2, starting transfers between devices, spread(): lax.all_to_all(jnp.broadcast_to(x[None], (4,) + x.shape), EVERY, 0, 0, ax...  9.26 us
    all_to_all x2, waiting for transfers between devices, spread(): lax.all_to_all(jnp.broadcast_to(x[None], (4,) + x.shape), EVERY, 0, 0, ax...  7.96 us
    ppermute x6, starting transfers between devices, swap(): return lax.ppermute(x, axis, [(0, 1), (1, 0)])  6.85 us
    all_to_all x1, starting transfers between devices, on_device(): lax.all_to_all(part_one.reshape(16, ROWS, WIDTH), PLANE, 0, 0, tiled=True)  5.45 us
    broadcast_in_dim x2, local copies, waits for them, and re-layouts, spread(): jnp.broadcast_to(x[None], (4,) + x.shape)  3.32 us
  transfers between devices with their start and end apart: 21, of which 14 were waited for; matrix products, arithmetic and copies ran while one was open for 5% of the time, Pallas kernels for 3%

profile of v11, /device:TPU:4, one launch (start us, length us, event | category | flops | bytes accessed | tf_op | source)
XLA Modules:
  0.0 108.5 jit_solution(5763670225862852127)
XLA Ops:
  0.6 0.9 select_bitcast_fusion.2
  1.5 1.3 %collective-permute-start = (bf16[64,512]{1,0:T(8,128)(2,1)S(1)}, bf16[64,512]{1,0:T(8,128)(2,1)S(1)}, u32[]{:S(2)}, u32[]{:S(2)}) collective-permute-start(bf16[64,512]{1,0:T(8,128)(2,1)S(1)} %get-tuple-element.61), channel_id=1, source_target_pairs={{0,2},{2,0},{1,3},{3,1},{4,6},{6,4},{5,7},{7,5},{8,10},{10,8},{9,1... | collective-permute-start | bytes 196616 | tf_op jit(solution)/shard_map/ppermute | solution.py:351
  2.8 1.8 %broadcast_in_dim.6 = bf16[4,128,512]{2,1,0:T(8,128)(2,1)} broadcast(bf16[128,512]{1,0:T(8,128)(2,1)} %param.3), dimensions={1,2} | broadcast | bytes 655360 | tf_op jit(solution)/shard_map/broadcast_in_dim | solution.py:375
  4.6 4.5 %all-to-all-start = ((bf16[4,128,512]{2,1,0:T(8,128)(2,1)}), bf16[4,128,512]{2,1,0:T(8,128)(2,1)S(1)}, u32[]{:S(2)}, u32[]{:S(2)}) async-start(bf16[4,128,512]{2,1,0:T(8,128)(2,1)} %broadcast_in_dim.6), calls=%async_computation | async-start | bytes 1048576 | tf_op jit(solution)/shard_map/all_to_all | solution.py:374
  9.0 0.7 copy-done
  9.7 0.0 collective-permute-done
  9.7 7.4 %all-to-all-done = bf16[4,128,512]{2,1,0:T(8,128)(2,1)S(1)} async-done(((bf16[4,128,512]{2,1,0:T(8,128)(2,1)}), bf16[4,128,512]{2,1,0:T(8,128)(2,1)S(1)}, u32[]{:S(2)}, u32[]{:S(2)}) %all-to-all-start) | async-done | bytes 524320 | tf_op jit(solution)/shard_map/all_to_all | solution.py:374
  17.1 3.3 %collective-permute-start.3 = (bf16[2,64,512]{2,1,0:T(8,128)(2,1)S(1)}, bf16[2,64,512]{2,1,0:T(8,128)(2,1)S(1)}, u32[]{:S(2)}, u32[]{:S(2)}) collective-permute-start(bf16[2,64,512]{2,1,0:T(8,128)(2,1)S(1)} %maximum_select_fusion.1.own), channel_id=1, source_target_pairs={{0,64},{32,96},{64,128},{96,160},{128,192},{160,224},{192,0},{224,... | collective-permute-start | bytes 393224 | tf_op jit(solution)/shard_map/ppermute | solution.py:398
  20.5 3.1 %collective-permute-start.1 = (bf16[2,64,512]{2,1,0:T(8,128)(2,1)S(1)}, bf16[2,64,512]{2,1,0:T(8,128)(2,1)S(1)}, u32[]{:S(2)}, u32[]{:S(2)}) collective-permute-start(bf16[2,64,512]{2,1,0:T(8,128)(2,1)S(1)} %maximum_select_fusion.1.own), channel_id=1, source_target_pairs={{0,192},{32,224},{64,0},{96,32},{128,64},{160,96},{192,128},{224,1... | collective-permute-start | bytes 393224 | tf_op jit(solution)/shard_map/ppermute | solution.py:398
  23.6 1.6 %broadcast_in_dim.7 = bf16[4,4,128,512]{3,2,1,0:T(8,128)(2,1)} broadcast(bf16[4,128,512]{2,1,0:T(8,128)(2,1)S(1)} %all-to-all-done), dimensions={1,2,3} | broadcast | bytes 2621440 | tf_op jit(solution)/shard_map/broadcast_in_dim | solution.py:375
  25.2 4.8 %all-to-all-start.1 = ((bf16[4,4,128,512]{3,2,1,0:T(8,128)(2,1)}), bf16[4,4,128,512]{3,2,1,0:T(8,128)(2,1)S(1)}, u32[]{:S(2)}, u32[]{:S(2)}) async-start(bf16[4,4,128,512]{3,2,1,0:T(8,128)(2,1)} %broadcast_in_dim.7), calls=%async_computation.1 | async-start | bytes 4194304 | tf_op jit(solution)/shard_map/all_to_all | solution.py:374
  30.0 1.4 %collective-permute-start.4 = (bf16[64,512]{1,0:T(8,128)(2,1)S(1)}, bf16[64,512]{1,0:T(8,128)(2,1)S(1)}, u32[]{:S(2)}, u32[]{:S(2)}) collective-permute-start(bf16[64,512]{1,0:T(8,128)(2,1)S(1)} %slice_bitcast_fusion.12), channel_id=1, source_target_pairs={{0,64},{32,96},{64,128},{96,160},{128,192},{160,224},{192,0},{224,... | collective-permute-start | bytes 196616 | tf_op jit(solution)/shard_map/ppermute | solution.py:398
  31.4 0.0 collective-permute-done.1.up2
  31.5 1.1 %collective-permute-start.6 = (bf16[2,128,512]{2,1,0:T(8,128)(2,1)S(1)}, bf16[2,128,512]{2,1,0:T(8,128)(2,1)S(1)}, u32[]{:S(2)}, u32[]{:S(2)}) collective-permute-start(bf16[2,128,512]{2,1,0:T(8,128)(2,1)S(1)} %get-tuple-element.58), channel_id=1, source_target_pairs={{0,32},{32,64},{64,96},{96,128},{128,160},{160,192},{192,224},{224... | collective-permute-start | bytes 786440 | tf_op jit(solution)/shard_map/ppermute | solution.py:398
  32.6 2.2 %collective-permute-start.5 = (bf16[2,128,512]{2,1,0:T(8,128)(2,1)S(1)}, bf16[2,128,512]{2,1,0:T(8,128)(2,1)S(1)}, u32[]{:S(2)}, u32[]{:S(2)}) collective-permute-start(bf16[2,128,512]{2,1,0:T(8,128)(2,1)S(1)} %get-tuple-element.59), channel_id=1, source_target_pairs={{0,224},{32,0},{64,32},{96,64},{128,96},{160,128},{192,160},{224,1... | collective-permute-start | bytes 786440 | tf_op jit(solution)/shard_map/ppermute | solution.py:398
  34.8 1.6 %collective-permute-start.2 = (bf16[64,512]{1,0:T(8,128)(2,1)S(1)}, bf16[64,512]{1,0:T(8,128)(2,1)S(1)}, u32[]{:S(2)}, u32[]{:S(2)}) collective-permute-start(bf16[64,512]{1,0:T(8,128)(2,1)S(1)} %slice_bitcast_fusion.13), channel_id=1, source_target_pairs={{0,192},{32,224},{64,0},{96,32},{128,64},{160,96},{192,128},{224,1... | collective-permute-start | bytes 196616 | tf_op jit(solution)/shard_map/ppermute | solution.py:398
  36.4 0.1 pad_add_fusion.place_ref
  36.4 0.1 collective-permute-done.4.four1
  36.5 6.9 %collective-permute-done.2.four0 = bf16[64,512]{1,0:T(8,128)(2,1)S(1)} collective-permute-done((bf16[64,512]{1,0:T(8,128)(2,1)S(1)}, bf16[64,512]{1,0:T(8,128)(2,1)S(1)}, u32[]{:S(2)}, u32[]{:S(2)}) %collective-permute-start.2) | collective-permute-done | bytes 65568 | tf_op jit(solution)/shard_map/ppermute | solution.py:398
  43.5 0.0 collective-permute-done.6.down
  43.5 0.2 shard_map.51
  43.6 0.5 all-to-all-done.1
  44.2 1.3 %shard_map.52.own_ref = f32[512,512]{1,0:T(8,128)S(1)} custom-call(s32[4]{0:T(128)S(1)} %pad_add_fusion.place_ref, bf16[16,128,512]{2,1,0:T(8,128)(2,1)S(1)} %bitcast.64, bf16[2,512,512]{2,1,0:T(8,128)(2,1)S(1)} %get-tuple-element.25.v2_ref), custom_call_target="tpu_custom_call" | custom-call | flops 536870912 | bytes 3145728 | tf_op jit(solution)/shard_map/pallas_call | solution.py:111
  45.5 0.1 collective-permute-start.7
  45.6 1.3 %shard_map.54.own_ref = f32[512,512]{1,0:T(8,128)S(1)} custom-call(s32[4]{0:T(128)S(1)} %pad_add_fusion.place_ref, bf16[16,128,512]{2,1,0:T(8,128)(2,1)S(1)} %bitcast.65, bf16[2,512,512]{2,1,0:T(8,128)(2,1)S(1)} %get-tuple-element.25.v2_ref), custom_call_target="tpu_custom_call" | custom-call | flops 536870912 | bytes 3145728 | tf_op jit(solution)/shard_map/pallas_call | solution.py:111
  46.8 0.6 collective-permute-start.8
  47.4 0.2 abs_reduce_fusion
  47.7 0.1 collective-permute-start.9
  47.8 0.4 collective-permute-done.7.other_ref
  48.2 0.6 shard_map.53
  48.8 0.9 collective-permute-done.9.most_other_ref
  49.7 1.2 %shard_map.55 = (f32[512,512]{1,0:T(8,128)S(1)}, f32[16,16,128]{2,1,0:T(8,128)S(1)}) custom-call(s32[4]{0:T(128)S(1)} %pad_add_fusion.place_ref, f32[512,512]{1,0:T(8,128)S(1)} %shard_map.54.own_ref, f32[512,512]{1,0:T(8,128)S(1)} %collective-permute-done.8.other_ref, f32[4,128]{1,0:T(4,128)S(1)} %get-tuple-element.27.first_ref, ...), custom_call_target="tpu_custom_call" | custom-call | flops 2621440 | bytes 3145728 | tf_op jit(solution)/shard_map/pallas_call | solution.py:231
  50.9 10.8 %all_to_all.20.seen_ref = f32[16,16,128]{2,1,0:T(8,128)S(1)} all-to-all(f32[16,16,128]{2,1,0:T(8,128)S(1)} %get-tuple-element.32), channel_id=1, replica_groups={{0,8,16,24,4,12,20,28,2,10,18,26,6,14,22,30},{32,40,48,56,36,44,52,60,3..., dimensions={0} | all-to-all | bytes 262144 | tf_op jit(solution)/shard_map/all_to_all | solution.py:436
  61.7 0.6 shard_map.56.known_ref
  62.3 3.5 %collective-permute-start.10 = (f32[24,128]{1,0:T(8,128)S(1)}, f32[24,128]{1,0:T(8,128)S(1)}, u32[]{:S(2)}, u32[]{:S(2)}) collective-permute-start(f32[24,128]{1,0:T(8,128)S(1)} %shard_map.56.known_ref), channel_id=1, source_target_pairs={{0,1},{1,0},{2,3},{3,2},{4,5},{5,4},{6,7},{7,6},{8,9},{9,8},{10,11... | collective-permute-start | bytes 36872 | tf_op jit(solution)/shard_map/ppermute | solution.py:351
  65.8 0.7 shard_map.58
  66.5 0.2 collective-permute-done.10.told_ref
  66.6 1.4 %shard_map.57 = (bf16[1024,512]{1,0:T(8,128)(2,1)S(1)}, f32[1,512]{1,0:T(1,128)S(1)}, f32[1,512]{1,0:T(1,128)S(1)}, f32[1,512]{1,0:T(1,128)S(1)}, f32[1,512]{1,0:T(1,128)S(1)}) custom-call(s32[4]{0:T(128)S(1)} %pad_add_fusion.place_ref, f32[512,512]{1,0:T(8,128)S(1)} %get-tuple-element.26.s0_ref, f32[512,512]{1,0:T(8,128)S(1)} %get-tuple-element.31.s1_ref, ...), custom_call_target="tpu_custom_call" | custom-call | flops 4194304 | bytes 3145728 | tf_op jit(solution)/shard_map/pallas_call | solution.py:335
  68.0 2.6 %multiply_convert_fusion = f16[2,1024,512]{2,1,0:T(8,128)(2,1)} fusion(bf16[2,512,512]{2,1,0:T(8,128)(2,1)S(1)} %get-tuple-element.25.v2_ref, f32[512]{0:T(512)S(1)} %bitcast.71, bf16[1024,512]{1,0:T(8,128)(2,1)S(1)} %get-tuple-element.35), kind=kOutput, calls=%fused_computation.1 | convolution fusion | flops 1075838976 | bytes 4196352 | tf_op jit(solution)/shard_map/dot_general | solution.py:446
  70.6 0.7 fusion.1
  71.4 0.7 fusion
  72.1 5.4 %all-to-all-start.3 = ((f16[16,128,512]{2,1,0:T(8,128)(2,1)}), f16[16,128,512]{2,1,0:T(8,128)(2,1)S(1)}, u32[]{:S(2)}, u32[]{:S(2)}) async-start(f16[16,128,512]{2,1,0:T(8,128)(2,1)} %bitcast.73), calls=%async_computation.3 | async-start | bytes 4194304 | tf_op jit(solution)/shard_map/all_to_all | solution.py:455
  77.6 0.1 slice_bitcast_fusion.4
  77.7 0.1 pad_maximum_fusion.3
  77.8 1.5 %collective-permute-start.12 = (f16[2,128,512]{2,1,0:T(8,128)(2,1)S(1)}, f16[2,128,512]{2,1,0:T(8,128)(2,1)S(1)}, u32[]{:S(2)}, u32[]{:S(2)}) collective-permute-start(f16[2,128,512]{2,1,0:T(8,128)(2,1)S(1)} %pad_maximum_fusion.3), channel_id=1, source_target_pairs={{0,224},{32,0},{64,32},{96,64},{128,96},{160,128},{192,160},{224,1... | collective-permute-start | bytes 786440 | tf_op jit(solution)/shard_map/ppermute | solution.py:398
  79.4 1.6 %collective-permute-start.15 = (f16[64,512]{1,0:T(8,128)(2,1)S(1)}, f16[64,512]{1,0:T(8,128)(2,1)S(1)}, u32[]{:S(2)}, u32[]{:S(2)}) collective-permute-start(f16[64,512]{1,0:T(8,128)(2,1)S(1)} %get-tuple-element.49), channel_id=1, source_target_pairs={{0,192},{32,224},{64,0},{96,32},{128,64},{160,96},{192,128},{224,1... | collective-permute-start | bytes 196616 | tf_op jit(solution)/shard_map/ppermute | solution.py:398
  81.0 1.4 %collective-permute-start.13 = (f16[64,512]{1,0:T(8,128)(2,1)S(1)}, f16[64,512]{1,0:T(8,128)(2,1)S(1)}, u32[]{:S(2)}, u32[]{:S(2)}) collective-permute-start(f16[64,512]{1,0:T(8,128)(2,1)S(1)} %get-tuple-element.46), channel_id=1, source_target_pairs={{0,64},{32,96},{64,128},{96,160},{128,192},{160,224},{192,0},{224,... | collective-permute-start | bytes 196616 | tf_op jit(solution)/shard_map/ppermute | solution.py:398
  82.4 0.1 pad_maximum_fusion.2
  82.4 0.7 collective-permute-start.11
  83.1 4.0 %collective-permute-done.12 = f16[2,128,512]{2,1,0:T(8,128)(2,1)S(1)} collective-permute-done((f16[2,128,512]{2,1,0:T(8,128)(2,1)S(1)}, f16[2,128,512]{2,1,0:T(8,128)(2,1)S(1)}, u32[]{:S(2)}, u32[]{:S(2)}) %collective-permute-start.12) | collective-permute-done | bytes 262176 | tf_op jit(solution)/shard_map/ppermute | solution.py:398
  87.1 0.1 convert_element_type.65
  87.2 2.4 %collective-permute-done.15 = f16[64,512]{1,0:T(8,128)(2,1)S(1)} collective-permute-done((f16[64,512]{1,0:T(8,128)(2,1)S(1)}, f16[64,512]{1,0:T(8,128)(2,1)S(1)}, u32[]{:S(2)}, u32[]{:S(2)}) %collective-permute-start.15) | collective-permute-done | bytes 65568 | tf_op jit(solution)/shard_map/ppermute | solution.py:398
  89.6 2.9 %collective-permute-start.16 = (f16[2,64,512]{2,1,0:T(8,128)(2,1)S(1)}, f16[2,64,512]{2,1,0:T(8,128)(2,1)S(1)}, u32[]{:S(2)}, u32[]{:S(2)}) collective-permute-start(f16[2,64,512]{2,1,0:T(8,128)(2,1)S(1)} %fusion.6), channel_id=1, source_target_pairs={{0,192},{32,224},{64,0},{96,32},{128,64},{160,96},{192,128},{224,1... | collective-permute-start | bytes 393224 | tf_op jit(solution)/shard_map/ppermute | solution.py:398
  92.5 0.3 collective-permute-done.11
  92.8 0.1 convert_element_type.64
  93.0 0.3 collective-permute-start.14
  93.3 3.5 %collective-permute-done.16 = f16[2,64,512]{2,1,0:T(8,128)(2,1)S(1)} collective-permute-done((f16[2,64,512]{2,1,0:T(8,128)(2,1)S(1)}, f16[2,64,512]{2,1,0:T(8,128)(2,1)S(1)}, u32[]{:S(2)}, u32[]{:S(2)}) %collective-permute-start.16) | collective-permute-done | bytes 131104 | tf_op jit(solution)/shard_map/ppermute | solution.py:398
  96.8 5.1 %collective-permute-done.14 = f16[2,64,512]{2,1,0:T(8,128)(2,1)S(1)} collective-permute-done((f16[2,64,512]{2,1,0:T(8,128)(2,1)S(1)}, f16[2,64,512]{2,1,0:T(8,128)(2,1)S(1)}, u32[]{:S(2)}, u32[]{:S(2)}) %collective-permute-start.14) | collective-permute-done | bytes 131104 | tf_op jit(solution)/shard_map/ppermute | solution.py:398
  102.0 0.1 fusion.4
  102.1 1.3 %collective-permute-start.17 = (f32[64,512]{1,0:T(8,128)S(1)}, f32[64,512]{1,0:T(8,128)S(1)}, u32[]{:S(2)}, u32[]{:S(2)}) collective-permute-start(f32[64,512]{1,0:T(8,128)S(1)} %get-tuple-element.57), channel_id=1, source_target_pairs={{0,2},{2,0},{1,3},{3,1},{4,6},{6,4},{5,7},{7,5},{8,10},{10,8},{9,1... | collective-permute-start | bytes 393224 | tf_op jit(solution)/shard_map/ppermute | solution.py:351
  103.4 1.9 %all-to-all-done.3 = f16[16,128,512]{2,1,0:T(8,128)(2,1)S(1)} async-done(((f16[16,128,512]{2,1,0:T(8,128)(2,1)}), f16[16,128,512]{2,1,0:T(8,128)(2,1)S(1)}, u32[]{:S(2)}, u32[]{:S(2)}) %all-to-all-start.3) | async-done | bytes 2097184 | tf_op jit(solution)/shard_map/all_to_all | solution.py:455
  105.3 1.1 %multiply_reduce_fusion = f32[128,512]{1,0:T(8,128)} fusion(f16[16,128,512]{2,1,0:T(8,128)(2,1)S(1)} %all-to-all-done.3, f32[512]{0:T(512)S(1)} %bitcast.68), kind=kLoop, calls=%fused_computation | loop fusion | flops 3080192 | bytes 2361344 | tf_op jit(solution)/shard_map/reduce_sum | solution.py:484
  106.5 1.3 %collective-permute-done.17 = f32[64,512]{1,0:T(8,128)S(1)} collective-permute-done((f32[64,512]{1,0:T(8,128)S(1)}, f32[64,512]{1,0:T(8,128)S(1)}, u32[]{:S(2)}, u32[]{:S(2)}) %collective-permute-start.17) | collective-permute-done | bytes 131104 | tf_op jit(solution)/shard_map/ppermute | solution.py:351
  107.8 0.7 maximum_select_fusion
  (23 shorter events, 0.4 us)
Async XLA Ops:
  1.5 8.2 %collective-permute-start = (bf16[64,512]{1,0:T(8,128)(2,1)S(1)}, bf16[64,512]{1,0:T(8,128)(2,1)S(1)}, u32[]{:S(2)}, u32[]{:S(2)}) collective-permute-start(bf16[64,512]{1,0:T(8,128)(2,1)S(1)} %get-tuple-element.61), channel_id=1, source_target_pairs={{0,2},{2,0},{1,3},{3,1},{4,6},{6,4},{5,7},{7,5},{8,10},{10,8},{9,1... | collective-permute-start | bytes 196616 | tf_op jit(solution)/shard_map/ppermute | solution.py:351
  4.6 12.5 %all-to-all-start = ((bf16[4,128,512]{2,1,0:T(8,128)(2,1)}), bf16[4,128,512]{2,1,0:T(8,128)(2,1)S(1)}, u32[]{:S(2)}, u32[]{:S(2)}) async-start(bf16[4,128,512]{2,1,0:T(8,128)(2,1)} %broadcast_in_dim.6), calls=%async_computation | async-start | bytes 1048576 | tf_op jit(solution)/shard_map/all_to_all | solution.py:374
  9.0 0.7 copy-start
  17.1 12.8 %collective-permute-start.3 = (bf16[2,64,512]{2,1,0:T(8,128)(2,1)S(1)}, bf16[2,64,512]{2,1,0:T(8,128)(2,1)S(1)}, u32[]{:S(2)}, u32[]{:S(2)}) collective-permute-start(bf16[2,64,512]{2,1,0:T(8,128)(2,1)S(1)} %maximum_select_fusion.1.own), channel_id=1, source_target_pairs={{0,64},{32,96},{64,128},{96,160},{128,192},{160,224},{192,0},{224,... | collective-permute-start | bytes 393224 | tf_op jit(solution)/shard_map/ppermute | solution.py:398
  20.5 10.9 %collective-permute-start.1 = (bf16[2,64,512]{2,1,0:T(8,128)(2,1)S(1)}, bf16[2,64,512]{2,1,0:T(8,128)(2,1)S(1)}, u32[]{:S(2)}, u32[]{:S(2)}) collective-permute-start(bf16[2,64,512]{2,1,0:T(8,128)(2,1)S(1)} %maximum_select_fusion.1.own), channel_id=1, source_target_pairs={{0,192},{32,224},{64,0},{96,32},{128,64},{160,96},{192,128},{224,1... | collective-permute-start | bytes 393224 | tf_op jit(solution)/shard_map/ppermute | solution.py:398
  25.2 19.0 %all-to-all-start.1 = ((bf16[4,4,128,512]{3,2,1,0:T(8,128)(2,1)}), bf16[4,4,128,512]{3,2,1,0:T(8,128)(2,1)S(1)}, u32[]{:S(2)}, u32[]{:S(2)}) async-start(bf16[4,4,128,512]{3,2,1,0:T(8,128)(2,1)} %broadcast_in_dim.7), calls=%async_computation.1 | async-start | bytes 4194304 | tf_op jit(solution)/shard_map/all_to_all | solution.py:374
  30.0 6.6 %collective-permute-start.4 = (bf16[64,512]{1,0:T(8,128)(2,1)S(1)}, bf16[64,512]{1,0:T(8,128)(2,1)S(1)}, u32[]{:S(2)}, u32[]{:S(2)}) collective-permute-start(bf16[64,512]{1,0:T(8,128)(2,1)S(1)} %slice_bitcast_fusion.12), channel_id=1, source_target_pairs={{0,64},{32,96},{64,128},{96,160},{128,192},{160,224},{192,0},{224,... | collective-permute-start | bytes 196616 | tf_op jit(solution)/shard_map/ppermute | solution.py:398
  31.5 12.0 %collective-permute-start.6 = (bf16[2,128,512]{2,1,0:T(8,128)(2,1)S(1)}, bf16[2,128,512]{2,1,0:T(8,128)(2,1)S(1)}, u32[]{:S(2)}, u32[]{:S(2)}) collective-permute-start(bf16[2,128,512]{2,1,0:T(8,128)(2,1)S(1)} %get-tuple-element.58), channel_id=1, source_target_pairs={{0,32},{32,64},{64,96},{96,128},{128,160},{160,192},{192,224},{224... | collective-permute-start | bytes 786440 | tf_op jit(solution)/shard_map/ppermute | solution.py:398
  32.6 10.9 %collective-permute-start.5 = (bf16[2,128,512]{2,1,0:T(8,128)(2,1)S(1)}, bf16[2,128,512]{2,1,0:T(8,128)(2,1)S(1)}, u32[]{:S(2)}, u32[]{:S(2)}) collective-permute-start(bf16[2,128,512]{2,1,0:T(8,128)(2,1)S(1)} %get-tuple-element.59), channel_id=1, source_target_pairs={{0,224},{32,0},{64,32},{96,64},{128,96},{160,128},{192,160},{224,1... | collective-permute-start | bytes 786440 | tf_op jit(solution)/shard_map/ppermute | solution.py:398
  34.8 8.7 %collective-permute-start.2 = (bf16[64,512]{1,0:T(8,128)(2,1)S(1)}, bf16[64,512]{1,0:T(8,128)(2,1)S(1)}, u32[]{:S(2)}, u32[]{:S(2)}) collective-permute-start(bf16[64,512]{1,0:T(8,128)(2,1)S(1)} %slice_bitcast_fusion.13), channel_id=1, source_target_pairs={{0,192},{32,224},{64,0},{96,32},{128,64},{160,96},{192,128},{224,1... | collective-permute-start | bytes 196616 | tf_op jit(solution)/shard_map/ppermute | solution.py:398
  45.5 2.7 %collective-permute-start.7 = (f32[512,512]{1,0:T(8,128)S(1)}, f32[512,512]{1,0:T(8,128)S(1)}, u32[]{:S(2)}, u32[]{:S(2)}) collective-permute-start(f32[512,512]{1,0:T(8,128)S(1)} %shard_map.52.own_ref), channel_id=1, source_target_pairs={{0,1},{1,0},{2,3},{3,2},{4,5},{5,4},{6,7},{7,6},{8,9},{9,8},{10,11... | collective-permute-start | bytes 3145736 | tf_op jit(solution)/shard_map/ppermute | solution.py:351
  46.8 2.9 %collective-permute-start.8 = (f32[512,512]{1,0:T(8,128)S(1)}, f32[512,512]{1,0:T(8,128)S(1)}, u32[]{:S(2)}, u32[]{:S(2)}) collective-permute-start(f32[512,512]{1,0:T(8,128)S(1)} %shard_map.54.own_ref), channel_id=1, source_target_pairs={{0,1},{1,0},{2,3},{3,2},{4,5},{5,4},{6,7},{7,6},{8,9},{9,8},{10,11... | collective-permute-start | bytes 3145736 | tf_op jit(solution)/shard_map/ppermute | solution.py:351
  47.7 2.0 %collective-permute-start.9 = (f32[2,512]{1,0:T(2,128)S(1)}, f32[2,512]{1,0:T(2,128)S(1)}, u32[]{:S(2)}, u32[]{:S(2)}) collective-permute-start(f32[2,512]{1,0:T(2,128)S(1)} %pad_maximum_fusion.4.most_ref), channel_id=1, source_target_pairs={{0,1},{1,0},{2,3},{3,2},{4,5},{5,4},{6,7},{7,6},{8,9},{9,8},{10,11... | collective-permute-start | bytes 12296 | tf_op jit(solution)/shard_map/ppermute | solution.py:351
  62.3 4.3 %collective-permute-start.10 = (f32[24,128]{1,0:T(8,128)S(1)}, f32[24,128]{1,0:T(8,128)S(1)}, u32[]{:S(2)}, u32[]{:S(2)}) collective-permute-start(f32[24,128]{1,0:T(8,128)S(1)} %shard_map.56.known_ref), channel_id=1, source_target_pairs={{0,1},{1,0},{2,3},{3,2},{4,5},{5,4},{6,7},{7,6},{8,9},{9,8},{10,11... | collective-permute-start | bytes 36872 | tf_op jit(solution)/shard_map/ppermute | solution.py:351
  72.1 33.2 %all-to-all-start.3 = ((f16[16,128,512]{2,1,0:T(8,128)(2,1)}), f16[16,128,512]{2,1,0:T(8,128)(2,1)S(1)}, u32[]{:S(2)}, u32[]{:S(2)}) async-start(f16[16,128,512]{2,1,0:T(8,128)(2,1)} %bitcast.73), calls=%async_computation.3 | async-start | bytes 4194304 | tf_op jit(solution)/shard_map/all_to_all | solution.py:455
  77.8 9.3 %collective-permute-start.12 = (f16[2,128,512]{2,1,0:T(8,128)(2,1)S(1)}, f16[2,128,512]{2,1,0:T(8,128)(2,1)S(1)}, u32[]{:S(2)}, u32[]{:S(2)}) collective-permute-start(f16[2,128,512]{2,1,0:T(8,128)(2,1)S(1)} %pad_maximum_fusion.3), channel_id=1, source_target_pairs={{0,224},{32,0},{64,32},{96,64},{128,96},{160,128},{192,160},{224,1... | collective-permute-start | bytes 786440 | tf_op jit(solution)/shard_map/ppermute | solution.py:398
  79.4 10.2 %collective-permute-start.15 = (f16[64,512]{1,0:T(8,128)(2,1)S(1)}, f16[64,512]{1,0:T(8,128)(2,1)S(1)}, u32[]{:S(2)}, u32[]{:S(2)}) collective-permute-start(f16[64,512]{1,0:T(8,128)(2,1)S(1)} %get-tuple-element.49), channel_id=1, source_target_pairs={{0,192},{32,224},{64,0},{96,32},{128,64},{160,96},{192,128},{224,1... | collective-permute-start | bytes 196616 | tf_op jit(solution)/shard_map/ppermute | solution.py:398
  81.0 12.0 %collective-permute-start.13 = (f16[64,512]{1,0:T(8,128)(2,1)S(1)}, f16[64,512]{1,0:T(8,128)(2,1)S(1)}, u32[]{:S(2)}, u32[]{:S(2)}) collective-permute-start(f16[64,512]{1,0:T(8,128)(2,1)S(1)} %get-tuple-element.46), channel_id=1, source_target_pairs={{0,64},{32,96},{64,128},{96,160},{128,192},{160,224},{192,0},{224,... | collective-permute-start | bytes 196616 | tf_op jit(solution)/shard_map/ppermute | solution.py:398
  82.4 10.4 %collective-permute-start.11 = (f16[2,128,512]{2,1,0:T(8,128)(2,1)S(1)}, f16[2,128,512]{2,1,0:T(8,128)(2,1)S(1)}, u32[]{:S(2)}, u32[]{:S(2)}) collective-permute-start(f16[2,128,512]{2,1,0:T(8,128)(2,1)S(1)} %pad_maximum_fusion.2), channel_id=1, source_target_pairs={{0,32},{32,64},{64,96},{96,128},{128,160},{160,192},{192,224},{224... | collective-permute-start | bytes 786440 | tf_op jit(solution)/shard_map/ppermute | solution.py:398
  89.6 7.2 %collective-permute-start.16 = (f16[2,64,512]{2,1,0:T(8,128)(2,1)S(1)}, f16[2,64,512]{2,1,0:T(8,128)(2,1)S(1)}, u32[]{:S(2)}, u32[]{:S(2)}) collective-permute-start(f16[2,64,512]{2,1,0:T(8,128)(2,1)S(1)} %fusion.6), channel_id=1, source_target_pairs={{0,192},{32,224},{64,0},{96,32},{128,64},{160,96},{192,128},{224,1... | collective-permute-start | bytes 393224 | tf_op jit(solution)/shard_map/ppermute | solution.py:398
  93.0 9.0 %collective-permute-start.14 = (f16[2,64,512]{2,1,0:T(8,128)(2,1)S(1)}, f16[2,64,512]{2,1,0:T(8,128)(2,1)S(1)}, u32[]{:S(2)}, u32[]{:S(2)}) collective-permute-start(f16[2,64,512]{2,1,0:T(8,128)(2,1)S(1)} %fusion.5), channel_id=1, source_target_pairs={{0,64},{32,96},{64,128},{96,160},{128,192},{160,224},{192,0},{224,... | collective-permute-start | bytes 393224 | tf_op jit(solution)/shard_map/ppermute | solution.py:398
  102.1 5.7 %collective-permute-start.17 = (f32[64,512]{1,0:T(8,128)S(1)}, f32[64,512]{1,0:T(8,128)S(1)}, u32[]{:S(2)}, u32[]{:S(2)}) collective-permute-start(f32[64,512]{1,0:T(8,128)S(1)} %get-tuple-element.57), channel_id=1, source_target_pairs={{0,2},{2,0},{1,3},{3,1},{4,6},{6,4},{5,7},{7,5},{8,10},{10,8},{9,1... | collective-permute-start | bytes 393224 | tf_op jit(solution)/shard_map/ppermute | solution.py:351

commit v12 on v11

--- a/solution.py
+++ b/solution.py
@@ -89,7 +89,7 @@
         in_specs=[VMEM] * 7,
         out_specs=(VMEM, VMEM),
         compiler_params=limit(4),
-        cost_estimate=pl.CostEstimate(flops=12 * 2**30, bytes_accessed=2**21, transcendentals=0),
+        cost_estimate=pl.CostEstimate(flops=10 * 2**30, bytes_accessed=2**21, transcendentals=0),
     )(*parts)
 
 
@@ -414,7 +414,8 @@
     side = swap(give, "xl")
     lines = spread(view_one, 0)
     partner = numbers(partner)
-    lines, side, partner = lax.optimization_barrier((lines, side, partner))
+    side, partner = lax.optimization_barrier((side, partner))
+    lines, _ = lax.optimization_barrier((lines, side))
     here = jnp.where(xl == 0, jnp.stack([keep, side]), jnp.stack([side, keep]))
     up2, down2 = to_plane(here, -2), to_plane(here, 2)
     v1_all = spread(lines, 1).reshape(16, ROWS, WIDTH)

time: 109 us -> 105 us (0.963)
  waiting for transfers between devices: 34.9 us -> 26.9 us
  starting transfers between devices: 42.8 us -> 45.3 us
  blocking collectives: 10.8 us -> 12.1 us
    all_to_all x2, waiting for transfers between devices: 7.96 us -> 0.93 us  [spread(): lax.all_to_all(jnp.broadcast_to(x[None], (4,) + x.shape), EVERY, 0, 0, ax...]
    ppermute x12, starting transfers between devices: 21.2 us -> 23.8 us  [to_plane(): return lax.ppermute(x, 'z', [(z, (z + dz) % NZ) for z in range(NZ)])]
    all_to_all x1, blocking collectives: 10.8 us -> 12.1 us  [on_device(): lax.all_to_all(pack, EVERY, 0, 0, axis_index_groups=stat_groups(), tiled=...]
  transfers between devices with their start and end apart: 21 -> 21, of which waited for: 14 -> 12; matrix products, arithmetic and copies ran while one was open for 5% -> 5% of each run, Pallas kernels for 3% -> 3%
where the time goes in v12:
time: 105 us; the launch traced here: 104 us
  starting transfers between devices  45.3 us (43%)
  waiting for transfers between devices  26.9 us (26%)
  blocking collectives  12.1 us (12%)
  Pallas kernels  7.2 us (7%)
  local copies, waits for them, and re-layouts  4.21 us (4%)
  matrix products  4.09 us (4%)
  other arithmetic  3.63 us (3%)
    ppermute x12, starting transfers between devices, to_plane(): return lax.ppermute(x, 'z', [(z, (z + dz) % NZ) for z in range(NZ)])  23.8 us
    ppermute x12, waiting for transfers between devices, to_plane(): return lax.ppermute(x, 'z', [(z, (z + dz) % NZ) for z in range(NZ)])  21.2 us
    all_to_all x1, blocking collectives, on_device(): lax.all_to_all(pack, EVERY, 0, 0, axis_index_groups=stat_groups(), tiled=...  12.1 us
    all_to_all x2, starting transfers between devices, spread(): lax.all_to_all(jnp.broadcast_to(x[None], (4,) + x.shape), EVERY, 0, 0, ax...  9.26 us
    ppermute x6, starting transfers between devices, swap(): return lax.ppermute(x, axis, [(0, 1), (1, 0)])  6.79 us
    all_to_all x1, starting transfers between devices, on_device(): lax.all_to_all(part_one.reshape(16, ROWS, WIDTH), PLANE, 0, 0, tiled=True)  5.44 us
    broadcast_in_dim x2, local copies, waits for them, and re-layouts, spread(): jnp.broadcast_to(x[None], (4,) + x.shape)  3.33 us
    ppermute x6, waiting for transfers between devices, swap(): return lax.ppermute(x, axis, [(0, 1), (1, 0)])  2.77 us
  transfers between devices with their start and end apart: 21, of which 12 were waited for; matrix products, arithmetic and copies ran while one was open for 5% of the time, Pallas kernels for 3%

profile of v12, /device:TPU:4, one launch (start us, length us, event | category | flops | bytes accessed | tf_op | source)
XLA Modules:
  0.0 104.3 jit_solution(2403648044649629888)
XLA Ops:
  0.6 0.9 select_bitcast_fusion.2
  1.5 1.3 %collective-permute-start = (bf16[64,512]{1,0:T(8,128)(2,1)S(1)}, bf16[64,512]{1,0:T(8,128)(2,1)S(1)}, u32[]{:S(2)}, u32[]{:S(2)}) collective-permute-start(bf16[64,512]{1,0:T(8,128)(2,1)S(1)} %get-tuple-element.61), channel_id=1, source_target_pairs={{0,2},{2,0},{1,3},{3,1},{4,6},{6,4},{5,7},{7,5},{8,10},{10,8},{9,1... | collective-permute-start | bytes 196616 | tf_op jit(solution)/shard_map/ppermute | solution.py:351
  2.8 1.8 %broadcast_in_dim.6 = bf16[4,128,512]{2,1,0:T(8,128)(2,1)} broadcast(bf16[128,512]{1,0:T(8,128)(2,1)} %param.3), dimensions={1,2} | broadcast | bytes 655360 | tf_op jit(solution)/shard_map/broadcast_in_dim | solution.py:375
  4.6 4.5 %all-to-all-start = ((bf16[4,128,512]{2,1,0:T(8,128)(2,1)}), bf16[4,128,512]{2,1,0:T(8,128)(2,1)S(1)}, u32[]{:S(2)}, u32[]{:S(2)}) async-start(bf16[4,128,512]{2,1,0:T(8,128)(2,1)} %broadcast_in_dim.6), calls=%async_computation | async-start | bytes 1048576 | tf_op jit(solution)/shard_map/all_to_all | solution.py:374
  9.0 0.7 copy-done
  9.7 0.0 collective-permute-done
  9.7 3.3 %collective-permute-start.3 = (bf16[2,64,512]{2,1,0:T(8,128)(2,1)S(1)}, bf16[2,64,512]{2,1,0:T(8,128)(2,1)S(1)}, u32[]{:S(2)}, u32[]{:S(2)}) collective-permute-start(bf16[2,64,512]{2,1,0:T(8,128)(2,1)S(1)} %maximum_select_fusion.1.own), channel_id=1, source_target_pairs={{0,64},{32,96},{64,128},{96,160},{128,192},{160,224},{192,0},{224,... | collective-permute-start | bytes 393224 | tf_op jit(solution)/shard_map/ppermute | solution.py:398
  13.1 3.1 %collective-permute-start.1 = (bf16[2,64,512]{2,1,0:T(8,128)(2,1)S(1)}, bf16[2,64,512]{2,1,0:T(8,128)(2,1)S(1)}, u32[]{:S(2)}, u32[]{:S(2)}) collective-permute-start(bf16[2,64,512]{2,1,0:T(8,128)(2,1)S(1)} %maximum_select_fusion.1.own), channel_id=1, source_target_pairs={{0,192},{32,224},{64,0},{96,32},{128,64},{160,96},{192,128},{224,1... | collective-permute-start | bytes 393224 | tf_op jit(solution)/shard_map/ppermute | solution.py:398
  16.2 0.9 all-to-all-done
  17.1 1.6 %broadcast_in_dim.7 = bf16[4,4,128,512]{3,2,1,0:T(8,128)(2,1)} broadcast(bf16[4,128,512]{2,1,0:T(8,128)(2,1)S(1)} %all-to-all-done), dimensions={1,2,3} | broadcast | bytes 2621440 | tf_op jit(solution)/shard_map/broadcast_in_dim | solution.py:375
  18.7 4.8 %all-to-all-start.1 = ((bf16[4,4,128,512]{3,2,1,0:T(8,128)(2,1)}), bf16[4,4,128,512]{3,2,1,0:T(8,128)(2,1)S(1)}, u32[]{:S(2)}, u32[]{:S(2)}) async-start(bf16[4,4,128,512]{3,2,1,0:T(8,128)(2,1)} %broadcast_in_dim.7), calls=%async_computation.1 | async-start | bytes 4194304 | tf_op jit(solution)/shard_map/all_to_all | solution.py:374
  23.5 0.0 collective-permute-done.3.down2
  23.5 3.3 %collective-permute-start.4 = (bf16[64,512]{1,0:T(8,128)(2,1)S(1)}, bf16[64,512]{1,0:T(8,128)(2,1)S(1)}, u32[]{:S(2)}, u32[]{:S(2)}) collective-permute-start(bf16[64,512]{1,0:T(8,128)(2,1)S(1)} %slice_bitcast_fusion.12), channel_id=1, source_target_pairs={{0,64},{32,96},{64,128},{96,160},{128,192},{160,224},{192,0},{224,... | collective-permute-start | bytes 196616 | tf_op jit(solution)/shard_map/ppermute | solution.py:398
  26.9 2.0 %collective-permute-start.6 = (bf16[2,128,512]{2,1,0:T(8,128)(2,1)S(1)}, bf16[2,128,512]{2,1,0:T(8,128)(2,1)S(1)}, u32[]{:S(2)}, u32[]{:S(2)}) collective-permute-start(bf16[2,128,512]{2,1,0:T(8,128)(2,1)S(1)} %get-tuple-element.58), channel_id=1, source_target_pairs={{0,32},{32,64},{64,96},{96,128},{128,160},{160,192},{192,224},{224... | collective-permute-start | bytes 786440 | tf_op jit(solution)/shard_map/ppermute | solution.py:398
  28.9 1.3 %collective-permute-start.5 = (bf16[2,128,512]{2,1,0:T(8,128)(2,1)S(1)}, bf16[2,128,512]{2,1,0:T(8,128)(2,1)S(1)}, u32[]{:S(2)}, u32[]{:S(2)}) collective-permute-start(bf16[2,128,512]{2,1,0:T(8,128)(2,1)S(1)} %get-tuple-element.59), channel_id=1, source_target_pairs={{0,224},{32,0},{64,32},{96,64},{128,96},{160,128},{192,160},{224,1... | collective-permute-start | bytes 786440 | tf_op jit(solution)/shard_map/ppermute | solution.py:398
  30.2 2.4 %collective-permute-start.2 = (bf16[64,512]{1,0:T(8,128)(2,1)S(1)}, bf16[64,512]{1,0:T(8,128)(2,1)S(1)}, u32[]{:S(2)}, u32[]{:S(2)}) collective-permute-start(bf16[64,512]{1,0:T(8,128)(2,1)S(1)} %slice_bitcast_fusion.13), channel_id=1, source_target_pairs={{0,192},{32,224},{64,0},{96,32},{128,64},{160,96},{192,128},{224,1... | collective-permute-start | bytes 196616 | tf_op jit(solution)/shard_map/ppermute | solution.py:398
  32.6 0.1 pad_add_fusion.place_ref
  32.7 5.9 %collective-permute-done.2.four0 = bf16[64,512]{1,0:T(8,128)(2,1)S(1)} collective-permute-done((bf16[64,512]{1,0:T(8,128)(2,1)S(1)}, bf16[64,512]{1,0:T(8,128)(2,1)S(1)}, u32[]{:S(2)}, u32[]{:S(2)}) %collective-permute-start.2) | collective-permute-done | bytes 65568 | tf_op jit(solution)/shard_map/ppermute | solution.py:398
  38.5 0.2 shard_map.51
  38.7 0.0 all-to-all-done.1
  38.7 1.3 %shard_map.52.own_ref = f32[512,512]{1,0:T(8,128)S(1)} custom-call(s32[4]{0:T(128)S(1)} %pad_add_fusion.place_ref, bf16[16,128,512]{2,1,0:T(8,128)(2,1)S(1)} %bitcast.64, bf16[2,512,512]{2,1,0:T(8,128)(2,1)S(1)} %get-tuple-element.25.v2_ref), custom_call_target="tpu_custom_call" | custom-call | flops 536870912 | bytes 3145728 | tf_op jit(solution)/shard_map/pallas_call | solution.py:111
  40.0 0.1 collective-permute-start.7
  40.1 1.3 %shard_map.54.own_ref = f32[512,512]{1,0:T(8,128)S(1)} custom-call(s32[4]{0:T(128)S(1)} %pad_add_fusion.place_ref, bf16[16,128,512]{2,1,0:T(8,128)(2,1)S(1)} %bitcast.65, bf16[2,512,512]{2,1,0:T(8,128)(2,1)S(1)} %get-tuple-element.25.v2_ref), custom_call_target="tpu_custom_call" | custom-call | flops 536870912 | bytes 3145728 | tf_op jit(solution)/shard_map/pallas_call | solution.py:111
  41.4 0.6 collective-permute-start.8
  42.0 0.2 abs_reduce_fusion
  42.2 0.1 collective-permute-start.9
  42.3 0.4 collective-permute-done.7.other_ref
  42.7 0.6 shard_map.53
  43.4 0.9 collective-permute-done.9.most_other_ref
  44.3 0.0 collective-permute-done.8.other_ref
  44.3 1.2 %shard_map.55 = (f32[512,512]{1,0:T(8,128)S(1)}, f32[16,16,128]{2,1,0:T(8,128)S(1)}) custom-call(s32[4]{0:T(128)S(1)} %pad_add_fusion.place_ref, f32[512,512]{1,0:T(8,128)S(1)} %shard_map.54.own_ref, f32[512,512]{1,0:T(8,128)S(1)} %collective-permute-done.8.other_ref, f32[4,128]{1,0:T(4,128)S(1)} %get-tuple-element.27.first_ref, ...), custom_call_target="tpu_custom_call" | custom-call | flops 2621440 | bytes 3145728 | tf_op jit(solution)/shard_map/pallas_call | solution.py:231
  45.4 12.1 %all_to_all.20.seen_ref = f32[16,16,128]{2,1,0:T(8,128)S(1)} all-to-all(f32[16,16,128]{2,1,0:T(8,128)S(1)} %get-tuple-element.32), channel_id=1, replica_groups={{0,8,16,24,4,12,20,28,2,10,18,26,6,14,22,30},{32,40,48,56,36,44,52,60,3..., dimensions={0} | all-to-all | bytes 262144 | tf_op jit(solution)/shard_map/all_to_all | solution.py:437
  57.5 0.6 shard_map.56.known_ref
  58.1 3.4 %collective-permute-start.10 = (f32[24,128]{1,0:T(8,128)S(1)}, f32[24,128]{1,0:T(8,128)S(1)}, u32[]{:S(2)}, u32[]{:S(2)}) collective-permute-start(f32[24,128]{1,0:T(8,128)S(1)} %shard_map.56.known_ref), channel_id=1, source_target_pairs={{0,1},{1,0},{2,3},{3,2},{4,5},{5,4},{6,7},{7,6},{8,9},{9,8},{10,11... | collective-permute-start | bytes 36872 | tf_op jit(solution)/shard_map/ppermute | solution.py:351
  61.5 0.7 shard_map.58
  62.2 0.2 collective-permute-done.10.told_ref
  62.4 1.4 %shard_map.57 = (bf16[1024,512]{1,0:T(8,128)(2,1)S(1)}, f32[1,512]{1,0:T(1,128)S(1)}, f32[1,512]{1,0:T(1,128)S(1)}, f32[1,512]{1,0:T(1,128)S(1)}, f32[1,512]{1,0:T(1,128)S(1)}) custom-call(s32[4]{0:T(128)S(1)} %pad_add_fusion.place_ref, f32[512,512]{1,0:T(8,128)S(1)} %get-tuple-element.26.s0_ref, f32[512,512]{1,0:T(8,128)S(1)} %get-tuple-element.31.s1_ref, ...), custom_call_target="tpu_custom_call" | custom-call | flops 4194304 | bytes 3145728 | tf_op jit(solution)/shard_map/pallas_call | solution.py:335
  63.8 2.6 %multiply_convert_fusion = f16[2,1024,512]{2,1,0:T(8,128)(2,1)} fusion(bf16[2,512,512]{2,1,0:T(8,128)(2,1)S(1)} %get-tuple-element.25.v2_ref, f32[512]{0:T(512)S(1)} %bitcast.71, bf16[1024,512]{1,0:T(8,128)(2,1)S(1)} %get-tuple-element.35), kind=kOutput, calls=%fused_computation.1 | convolution fusion | flops 1075838976 | bytes 4196352 | tf_op jit(solution)/shard_map/dot_general | solution.py:447
  66.4 0.7 fusion.1
  67.1 0.7 fusion
  67.9 5.4 %all-to-all-start.3 = ((f16[16,128,512]{2,1,0:T(8,128)(2,1)}), f16[16,128,512]{2,1,0:T(8,128)(2,1)S(1)}, u32[]{:S(2)}, u32[]{:S(2)}) async-start(f16[16,128,512]{2,1,0:T(8,128)(2,1)} %bitcast.73), calls=%async_computation.3 | async-start | bytes 4194304 | tf_op jit(solution)/shard_map/all_to_all | solution.py:456
  73.4 0.1 slice_bitcast_fusion.4
  73.5 0.1 pad_maximum_fusion.3
  73.6 1.5 %collective-permute-start.12 = (f16[2,128,512]{2,1,0:T(8,128)(2,1)S(1)}, f16[2,128,512]{2,1,0:T(8,128)(2,1)S(1)}, u32[]{:S(2)}, u32[]{:S(2)}) collective-permute-start(f16[2,128,512]{2,1,0:T(8,128)(2,1)S(1)} %pad_maximum_fusion.3), channel_id=1, source_target_pairs={{0,224},{32,0},{64,32},{96,64},{128,96},{160,128},{192,160},{224,1... | collective-permute-start | bytes 786440 | tf_op jit(solution)/shard_map/ppermute | solution.py:398
  75.1 1.6 %collective-permute-start.15 = (f16[64,512]{1,0:T(8,128)(2,1)S(1)}, f16[64,512]{1,0:T(8,128)(2,1)S(1)}, u32[]{:S(2)}, u32[]{:S(2)}) collective-permute-start(f16[64,512]{1,0:T(8,128)(2,1)S(1)} %get-tuple-element.49), channel_id=1, source_target_pairs={{0,192},{32,224},{64,0},{96,32},{128,64},{160,96},{192,128},{224,1... | collective-permute-start | bytes 196616 | tf_op jit(solution)/shard_map/ppermute | solution.py:398
  76.7 1.4 %collective-permute-start.13 = (f16[64,512]{1,0:T(8,128)(2,1)S(1)}, f16[64,512]{1,0:T(8,128)(2,1)S(1)}, u32[]{:S(2)}, u32[]{:S(2)}) collective-permute-start(f16[64,512]{1,0:T(8,128)(2,1)S(1)} %get-tuple-element.46), channel_id=1, source_target_pairs={{0,64},{32,96},{64,128},{96,160},{128,192},{160,224},{192,0},{224,... | collective-permute-start | bytes 196616 | tf_op jit(solution)/shard_map/ppermute | solution.py:398
  78.1 0.1 pad_maximum_fusion.2
  78.2 0.7 collective-permute-start.11
  78.9 4.0 %collective-permute-done.12 = f16[2,128,512]{2,1,0:T(8,128)(2,1)S(1)} collective-permute-done((f16[2,128,512]{2,1,0:T(8,128)(2,1)S(1)}, f16[2,128,512]{2,1,0:T(8,128)(2,1)S(1)}, u32[]{:S(2)}, u32[]{:S(2)}) %collective-permute-start.12) | collective-permute-done | bytes 262176 | tf_op jit(solution)/shard_map/ppermute | solution.py:398
  82.9 0.1 convert_element_type.65
  83.0 2.4 %collective-permute-done.15 = f16[64,512]{1,0:T(8,128)(2,1)S(1)} collective-permute-done((f16[64,512]{1,0:T(8,128)(2,1)S(1)}, f16[64,512]{1,0:T(8,128)(2,1)S(1)}, u32[]{:S(2)}, u32[]{:S(2)}) %collective-permute-start.15) | collective-permute-done | bytes 65568 | tf_op jit(solution)/shard_map/ppermute | solution.py:398
  85.4 2.9 %collective-permute-start.16 = (f16[2,64,512]{2,1,0:T(8,128)(2,1)S(1)}, f16[2,64,512]{2,1,0:T(8,128)(2,1)S(1)}, u32[]{:S(2)}, u32[]{:S(2)}) collective-permute-start(f16[2,64,512]{2,1,0:T(8,128)(2,1)S(1)} %fusion.6), channel_id=1, source_target_pairs={{0,192},{32,224},{64,0},{96,32},{128,64},{160,96},{192,128},{224,1... | collective-permute-start | bytes 393224 | tf_op jit(solution)/shard_map/ppermute | solution.py:398
  88.3 0.4 collective-permute-done.11
  88.7 0.1 convert_element_type.64
  88.8 0.0 collective-permute-done.13
  88.9 0.2 collective-permute-start.14
  89.1 3.5 %collective-permute-done.16 = f16[2,64,512]{2,1,0:T(8,128)(2,1)S(1)} collective-permute-done((f16[2,64,512]{2,1,0:T(8,128)(2,1)S(1)}, f16[2,64,512]{2,1,0:T(8,128)(2,1)S(1)}, u32[]{:S(2)}, u32[]{:S(2)}) %collective-permute-start.16) | collective-permute-done | bytes 131104 | tf_op jit(solution)/shard_map/ppermute | solution.py:398
  92.6 5.0 %collective-permute-done.14 = f16[2,64,512]{2,1,0:T(8,128)(2,1)S(1)} collective-permute-done((f16[2,64,512]{2,1,0:T(8,128)(2,1)S(1)}, f16[2,64,512]{2,1,0:T(8,128)(2,1)S(1)}, u32[]{:S(2)}, u32[]{:S(2)}) %collective-permute-start.14) | collective-permute-done | bytes 131104 | tf_op jit(solution)/shard_map/ppermute | solution.py:398
  97.7 0.1 fusion.4
  97.8 1.3 %collective-permute-start.17 = (f32[64,512]{1,0:T(8,128)S(1)}, f32[64,512]{1,0:T(8,128)S(1)}, u32[]{:S(2)}, u32[]{:S(2)}) collective-permute-start(f32[64,512]{1,0:T(8,128)S(1)} %get-tuple-element.57), channel_id=1, source_target_pairs={{0,2},{2,0},{1,3},{3,1},{4,6},{6,4},{5,7},{7,5},{8,10},{10,8},{9,1... | collective-permute-start | bytes 393224 | tf_op jit(solution)/shard_map/ppermute | solution.py:351
  99.1 2.0 %all-to-all-done.3 = f16[16,128,512]{2,1,0:T(8,128)(2,1)S(1)} async-done(((f16[16,128,512]{2,1,0:T(8,128)(2,1)}), f16[16,128,512]{2,1,0:T(8,128)(2,1)S(1)}, u32[]{:S(2)}, u32[]{:S(2)}) %all-to-all-start.3) | async-done | bytes 2097184 | tf_op jit(solution)/shard_map/all_to_all | solution.py:456
  101.1 1.1 %multiply_reduce_fusion = f32[128,512]{1,0:T(8,128)} fusion(f16[16,128,512]{2,1,0:T(8,128)(2,1)S(1)} %all-to-all-done.3, f32[512]{0:T(512)S(1)} %bitcast.68), kind=kLoop, calls=%fused_computation | loop fusion | flops 3080192 | bytes 2361344 | tf_op jit(solution)/shard_map/reduce_sum | solution.py:485
  102.2 1.3 %collective-permute-done.17 = f32[64,512]{1,0:T(8,128)S(1)} collective-permute-done((f32[64,512]{1,0:T(8,128)S(1)}, f32[64,512]{1,0:T(8,128)S(1)}, u32[]{:S(2)}, u32[]{:S(2)}) %collective-permute-start.17) | collective-permute-done | bytes 131104 | tf_op jit(solution)/shard_map/ppermute | solution.py:351
  103.5 0.7 maximum_select_fusion
  (23 shorter events, 0.4 us)
Async XLA Ops:
  1.5 8.2 %collective-permute-start = (bf16[64,512]{1,0:T(8,128)(2,1)S(1)}, bf16[64,512]{1,0:T(8,128)(2,1)S(1)}, u32[]{:S(2)}, u32[]{:S(2)}) collective-permute-start(bf16[64,512]{1,0:T(8,128)(2,1)S(1)} %get-tuple-element.61), channel_id=1, source_target_pairs={{0,2},{2,0},{1,3},{3,1},{4,6},{6,4},{5,7},{7,5},{8,10},{10,8},{9,1... | collective-permute-start | bytes 196616 | tf_op jit(solution)/shard_map/ppermute | solution.py:351
  4.6 12.5 %all-to-all-start = ((bf16[4,128,512]{2,1,0:T(8,128)(2,1)}), bf16[4,128,512]{2,1,0:T(8,128)(2,1)S(1)}, u32[]{:S(2)}, u32[]{:S(2)}) async-start(bf16[4,128,512]{2,1,0:T(8,128)(2,1)} %broadcast_in_dim.6), calls=%async_computation | async-start | bytes 1048576 | tf_op jit(solution)/shard_map/all_to_all | solution.py:374
  9.0 0.7 copy-start
  9.7 13.8 %collective-permute-start.3 = (bf16[2,64,512]{2,1,0:T(8,128)(2,1)S(1)}, bf16[2,64,512]{2,1,0:T(8,128)(2,1)S(1)}, u32[]{:S(2)}, u32[]{:S(2)}) collective-permute-start(bf16[2,64,512]{2,1,0:T(8,128)(2,1)S(1)} %maximum_select_fusion.1.own), channel_id=1, source_target_pairs={{0,64},{32,96},{64,128},{96,160},{128,192},{160,224},{192,0},{224,... | collective-permute-start | bytes 393224 | tf_op jit(solution)/shard_map/ppermute | solution.py:398
  13.1 13.8 %collective-permute-start.1 = (bf16[2,64,512]{2,1,0:T(8,128)(2,1)S(1)}, bf16[2,64,512]{2,1,0:T(8,128)(2,1)S(1)}, u32[]{:S(2)}, u32[]{:S(2)}) collective-permute-start(bf16[2,64,512]{2,1,0:T(8,128)(2,1)S(1)} %maximum_select_fusion.1.own), channel_id=1, source_target_pairs={{0,192},{32,224},{64,0},{96,32},{128,64},{160,96},{192,128},{224,1... | collective-permute-start | bytes 393224 | tf_op jit(solution)/shard_map/ppermute | solution.py:398
  18.7 20.0 %all-to-all-start.1 = ((bf16[4,4,128,512]{3,2,1,0:T(8,128)(2,1)}), bf16[4,4,128,512]{3,2,1,0:T(8,128)(2,1)S(1)}, u32[]{:S(2)}, u32[]{:S(2)}) async-start(bf16[4,4,128,512]{3,2,1,0:T(8,128)(2,1)} %broadcast_in_dim.7), calls=%async_computation.1 | async-start | bytes 4194304 | tf_op jit(solution)/shard_map/all_to_all | solution.py:374
  23.5 9.2 %collective-permute-start.4 = (bf16[64,512]{1,0:T(8,128)(2,1)S(1)}, bf16[64,512]{1,0:T(8,128)(2,1)S(1)}, u32[]{:S(2)}, u32[]{:S(2)}) collective-permute-start(bf16[64,512]{1,0:T(8,128)(2,1)S(1)} %slice_bitcast_fusion.12), channel_id=1, source_target_pairs={{0,64},{32,96},{64,128},{96,160},{128,192},{160,224},{192,0},{224,... | collective-permute-start | bytes 196616 | tf_op jit(solution)/shard_map/ppermute | solution.py:398
  26.9 11.6 %collective-permute-start.6 = (bf16[2,128,512]{2,1,0:T(8,128)(2,1)S(1)}, bf16[2,128,512]{2,1,0:T(8,128)(2,1)S(1)}, u32[]{:S(2)}, u32[]{:S(2)}) collective-permute-start(bf16[2,128,512]{2,1,0:T(8,128)(2,1)S(1)} %get-tuple-element.58), channel_id=1, source_target_pairs={{0,32},{32,64},{64,96},{96,128},{128,160},{160,192},{192,224},{224... | collective-permute-start | bytes 786440 | tf_op jit(solution)/shard_map/ppermute | solution.py:398
  28.9 9.7 %collective-permute-start.5 = (bf16[2,128,512]{2,1,0:T(8,128)(2,1)S(1)}, bf16[2,128,512]{2,1,0:T(8,128)(2,1)S(1)}, u32[]{:S(2)}, u32[]{:S(2)}) collective-permute-start(bf16[2,128,512]{2,1,0:T(8,128)(2,1)S(1)} %get-tuple-element.59), channel_id=1, source_target_pairs={{0,224},{32,0},{64,32},{96,64},{128,96},{160,128},{192,160},{224,1... | collective-permute-start | bytes 786440 | tf_op jit(solution)/shard_map/ppermute | solution.py:398
  30.2 8.3 %collective-permute-start.2 = (bf16[64,512]{1,0:T(8,128)(2,1)S(1)}, bf16[64,512]{1,0:T(8,128)(2,1)S(1)}, u32[]{:S(2)}, u32[]{:S(2)}) collective-permute-start(bf16[64,512]{1,0:T(8,128)(2,1)S(1)} %slice_bitcast_fusion.13), channel_id=1, source_target_pairs={{0,192},{32,224},{64,0},{96,32},{128,64},{160,96},{192,128},{224,1... | collective-permute-start | bytes 196616 | tf_op jit(solution)/shard_map/ppermute | solution.py:398
  40.0 2.7 %collective-permute-start.7 = (f32[512,512]{1,0:T(8,128)S(1)}, f32[512,512]{1,0:T(8,128)S(1)}, u32[]{:S(2)}, u32[]{:S(2)}) collective-permute-start(f32[512,512]{1,0:T(8,128)S(1)} %shard_map.52.own_ref), channel_id=1, source_target_pairs={{0,1},{1,0},{2,3},{3,2},{4,5},{5,4},{6,7},{7,6},{8,9},{9,8},{10,11... | collective-permute-start | bytes 3145736 | tf_op jit(solution)/shard_map/ppermute | solution.py:351
  41.4 2.9 %collective-permute-start.8 = (f32[512,512]{1,0:T(8,128)S(1)}, f32[512,512]{1,0:T(8,128)S(1)}, u32[]{:S(2)}, u32[]{:S(2)}) collective-permute-start(f32[512,512]{1,0:T(8,128)S(1)} %shard_map.54.own_ref), channel_id=1, source_target_pairs={{0,1},{1,0},{2,3},{3,2},{4,5},{5,4},{6,7},{7,6},{8,9},{9,8},{10,11... | collective-permute-start | bytes 3145736 | tf_op jit(solution)/shard_map/ppermute | solution.py:351
  42.2 2.0 %collective-permute-start.9 = (f32[2,512]{1,0:T(2,128)S(1)}, f32[2,512]{1,0:T(2,128)S(1)}, u32[]{:S(2)}, u32[]{:S(2)}) collective-permute-start(f32[2,512]{1,0:T(2,128)S(1)} %pad_maximum_fusion.4.most_ref), channel_id=1, source_target_pairs={{0,1},{1,0},{2,3},{3,2},{4,5},{5,4},{6,7},{7,6},{8,9},{9,8},{10,11... | collective-permute-start | bytes 12296 | tf_op jit(solution)/shard_map/ppermute | solution.py:351
  58.1 4.2 %collective-permute-start.10 = (f32[24,128]{1,0:T(8,128)S(1)}, f32[24,128]{1,0:T(8,128)S(1)}, u32[]{:S(2)}, u32[]{:S(2)}) collective-permute-start(f32[24,128]{1,0:T(8,128)S(1)} %shard_map.56.known_ref), channel_id=1, source_target_pairs={{0,1},{1,0},{2,3},{3,2},{4,5},{5,4},{6,7},{7,6},{8,9},{9,8},{10,11... | collective-permute-start | bytes 36872 | tf_op jit(solution)/shard_map/ppermute | solution.py:351
  67.9 33.2 %all-to-all-start.3 = ((f16[16,128,512]{2,1,0:T(8,128)(2,1)}), f16[16,128,512]{2,1,0:T(8,128)(2,1)S(1)}, u32[]{:S(2)}, u32[]{:S(2)}) async-start(f16[16,128,512]{2,1,0:T(8,128)(2,1)} %bitcast.73), calls=%async_computation.3 | async-start | bytes 4194304 | tf_op jit(solution)/shard_map/all_to_all | solution.py:456
  73.6 9.3 %collective-permute-start.12 = (f16[2,128,512]{2,1,0:T(8,128)(2,1)S(1)}, f16[2,128,512]{2,1,0:T(8,128)(2,1)S(1)}, u32[]{:S(2)}, u32[]{:S(2)}) collective-permute-start(f16[2,128,512]{2,1,0:T(8,128)(2,1)S(1)} %pad_maximum_fusion.3), channel_id=1, source_target_pairs={{0,224},{32,0},{64,32},{96,64},{128,96},{160,128},{192,160},{224,1... | collective-permute-start | bytes 786440 | tf_op jit(solution)/shard_map/ppermute | solution.py:398
  75.1 10.2 %collective-permute-start.15 = (f16[64,512]{1,0:T(8,128)(2,1)S(1)}, f16[64,512]{1,0:T(8,128)(2,1)S(1)}, u32[]{:S(2)}, u32[]{:S(2)}) collective-permute-start(f16[64,512]{1,0:T(8,128)(2,1)S(1)} %get-tuple-element.49), channel_id=1, source_target_pairs={{0,192},{32,224},{64,0},{96,32},{128,64},{160,96},{192,128},{224,1... | collective-permute-start | bytes 196616 | tf_op jit(solution)/shard_map/ppermute | solution.py:398
  76.7 12.1 %collective-permute-start.13 = (f16[64,512]{1,0:T(8,128)(2,1)S(1)}, f16[64,512]{1,0:T(8,128)(2,1)S(1)}, u32[]{:S(2)}, u32[]{:S(2)}) collective-permute-start(f16[64,512]{1,0:T(8,128)(2,1)S(1)} %get-tuple-element.46), channel_id=1, source_target_pairs={{0,64},{32,96},{64,128},{96,160},{128,192},{160,224},{192,0},{224,... | collective-permute-start | bytes 196616 | tf_op jit(solution)/shard_map/ppermute | solution.py:398
  78.2 10.5 %collective-permute-start.11 = (f16[2,128,512]{2,1,0:T(8,128)(2,1)S(1)}, f16[2,128,512]{2,1,0:T(8,128)(2,1)S(1)}, u32[]{:S(2)}, u32[]{:S(2)}) collective-permute-start(f16[2,128,512]{2,1,0:T(8,128)(2,1)S(1)} %pad_maximum_fusion.2), channel_id=1, source_target_pairs={{0,32},{32,64},{64,96},{96,128},{128,160},{160,192},{192,224},{224... | collective-permute-start | bytes 786440 | tf_op jit(solution)/shard_map/ppermute | solution.py:398
  85.4 7.2 %collective-permute-start.16 = (f16[2,64,512]{2,1,0:T(8,128)(2,1)S(1)}, f16[2,64,512]{2,1,0:T(8,128)(2,1)S(1)}, u32[]{:S(2)}, u32[]{:S(2)}) collective-permute-start(f16[2,64,512]{2,1,0:T(8,128)(2,1)S(1)} %fusion.6), channel_id=1, source_target_pairs={{0,192},{32,224},{64,0},{96,32},{128,64},{160,96},{192,128},{224,1... | collective-permute-start | bytes 393224 | tf_op jit(solution)/shard_map/ppermute | solution.py:398
  88.9 8.8 %collective-permute-start.14 = (f16[2,64,512]{2,1,0:T(8,128)(2,1)S(1)}, f16[2,64,512]{2,1,0:T(8,128)(2,1)S(1)}, u32[]{:S(2)}, u32[]{:S(2)}) collective-permute-start(f16[2,64,512]{2,1,0:T(8,128)(2,1)S(1)} %fusion.5), channel_id=1, source_target_pairs={{0,64},{32,96},{64,128},{96,160},{128,192},{160,224},{192,0},{224,... | collective-permute-start | bytes 393224 | tf_op jit(solution)/shard_map/ppermute | solution.py:398
  97.8 5.7 %collective-permute-start.17 = (f32[64,512]{1,0:T(8,128)S(1)}, f32[64,512]{1,0:T(8,128)S(1)}, u32[]{:S(2)}, u32[]{:S(2)}) collective-permute-start(f32[64,512]{1,0:T(8,128)S(1)} %get-tuple-element.57), channel_id=1, source_target_pairs={{0,2},{2,0},{1,3},{3,1},{4,6},{6,4},{5,7},{7,5},{8,10},{10,8},{9,1... | collective-permute-start | bytes 393224 | tf_op jit(solution)/shard_map/ppermute | solution.py:351

commit v13 on v12

--- a/solution.py
+++ b/solution.py
@@ -409,14 +409,16 @@
     core = lax.axis_index("core")
     place = jnp.stack([core, xl, z, uhigh]).astype(jnp.int32)
 
-    keep = jnp.where(xl == 0, view_two[:HALF], view_two[HALF:])
-    give = jnp.where(xl == 0, view_two[HALF:], view_two[:HALF])
-    side = swap(give, "xl")
+    side = swap(view_two, "xl")
     lines = spread(view_one, 0)
     partner = numbers(partner)
     side, partner = lax.optimization_barrier((side, partner))
     lines, _ = lax.optimization_barrier((lines, side))
-    here = jnp.where(xl == 0, jnp.stack([keep, side]), jnp.stack([side, keep]))
+    here = jnp.where(
+        xl == 0,
+        jnp.stack([view_two[:HALF], side[:HALF]]),
+        jnp.stack([side[HALF:], view_two[HALF:]]),
+    )
     up2, down2 = to_plane(here, -2), to_plane(here, 2)
     v1_all = spread(lines, 1).reshape(16, ROWS, WIDTH)
     up = to_plane(jnp.concatenate([here, up2], axis=1), -1)

time: 105 us -> 103 us (0.981)
  waiting for transfers between devices: 26.9 us -> 25.5 us
  transfers between devices with their start and end apart: 21 -> 21, of which waited for: 12 -> 11; matrix products, arithmetic and copies ran while one was open for 5% -> 5% of each run, Pallas kernels for 3% -> 3%
where the time goes in v13:
time: 103 us
  starting transfers between devices  45.4 us (44%)
  waiting for transfers between devices  25.5 us (25%)
  blocking collectives  12.2 us (12%)
  Pallas kernels  7.2 us (7%)
  local copies, waits for them, and re-layouts  5.12 us (5%)
  matrix products  4.1 us (4%)
  other arithmetic  2.76 us (3%)
    ppermute x12, starting transfers between devices, to_plane(): return lax.ppermute(x, 'z', [(z, (z + dz) % NZ) for z in range(NZ)])  23.8 us
    ppermute x12, waiting for transfers between devices, to_plane(): return lax.ppermute(x, 'z', [(z, (z + dz) % NZ) for z in range(NZ)])  21.1 us
    all_to_all x1, blocking collectives, on_device(): lax.all_to_all(pack, EVERY, 0, 0, axis_index_groups=stat_groups(), tiled=...  12.2 us
    all_to_all x2, starting transfers between devices, spread(): lax.all_to_all(jnp.broadcast_to(x[None], (4,) + x.shape), EVERY, 0, 0, ax...  9.26 us
    ppermute x6, starting transfers between devices, swap(): return lax.ppermute(x, axis, [(0, 1), (1, 0)])  6.71 us
    all_to_all x1, starting transfers between devices, on_device(): lax.all_to_all(part_one.reshape(16, ROWS, WIDTH), PLANE, 0, 0, tiled=True)  5.56 us
    broadcast_in_dim x2, local copies, waits for them, and re-layouts, spread(): jnp.broadcast_to(x[None], (4,) + x.shape)  3.32 us
    ppermute x6, waiting for transfers between devices, swap(): return lax.ppermute(x, axis, [(0, 1), (1, 0)])  2.62 us
  transfers between devices with their start and end apart: 21, of which 11 were waited for; matrix products, arithmetic and copies ran while one was open for 5% of the time, Pallas kernels for 3%

profile of v13, /device:TPU:4, one launch (start us, length us, event | category | flops | bytes accessed | tf_op | source)
XLA Modules:
  0.0 103.1 jit_solution(1861410012556641242)
XLA Ops:
  0.6 1.3 %collective-permute-start = (bf16[128,512]{1,0:T(8,128)(2,1)}, bf16[128,512]{1,0:T(8,128)(2,1)S(1)}, u32[]{:S(2)}, u32[]{:S(2)}) collective-permute-start(bf16[128,512]{1,0:T(8,128)(2,1)} %param.4), channel_id=1, source_target_pairs={{0,2},{2,0},{1,3},{3,1},{4,6},{6,4},{5,7},{7,5},{8,10},{10,8},{9,1... | collective-permute-start | bytes 393224 | tf_op jit(solution)/shard_map/ppermute | solution.py:351
  1.9 1.8 %broadcast_in_dim.6 = bf16[4,128,512]{2,1,0:T(8,128)(2,1)} broadcast(bf16[128,512]{1,0:T(8,128)(2,1)} %param.3), dimensions={1,2} | broadcast | bytes 655360 | tf_op jit(solution)/shard_map/broadcast_in_dim | solution.py:375
  3.7 4.5 %all-to-all-start = ((bf16[4,128,512]{2,1,0:T(8,128)(2,1)}), bf16[4,128,512]{2,1,0:T(8,128)(2,1)S(1)}, u32[]{:S(2)}, u32[]{:S(2)}) async-start(bf16[4,128,512]{2,1,0:T(8,128)(2,1)} %broadcast_in_dim.6), calls=%async_computation | async-start | bytes 1048576 | tf_op jit(solution)/shard_map/all_to_all | solution.py:374
  8.1 0.7 copy-done
  8.8 0.9 copy-done.1
  9.7 0.0 collective-permute-done
  9.8 3.3 %collective-permute-start.3 = (bf16[2,64,512]{2,1,0:T(8,128)(2,1)S(1)}, bf16[2,64,512]{2,1,0:T(8,128)(2,1)S(1)}, u32[]{:S(2)}, u32[]{:S(2)}) collective-permute-start(bf16[2,64,512]{2,1,0:T(8,128)(2,1)S(1)} %maximum_select_fusion.1.own), channel_id=1, source_target_pairs={{0,64},{32,96},{64,128},{96,160},{128,192},{160,224},{192,0},{224,... | collective-permute-start | bytes 393224 | tf_op jit(solution)/shard_map/ppermute | solution.py:398
  13.1 3.1 %collective-permute-start.1 = (bf16[2,64,512]{2,1,0:T(8,128)(2,1)S(1)}, bf16[2,64,512]{2,1,0:T(8,128)(2,1)S(1)}, u32[]{:S(2)}, u32[]{:S(2)}) collective-permute-start(bf16[2,64,512]{2,1,0:T(8,128)(2,1)S(1)} %maximum_select_fusion.1.own), channel_id=1, source_target_pairs={{0,192},{32,224},{64,0},{96,32},{128,64},{160,96},{192,128},{224,1... | collective-permute-start | bytes 393224 | tf_op jit(solution)/shard_map/ppermute | solution.py:398
  16.2 0.0 all-to-all-done
  16.2 1.6 %broadcast_in_dim.7 = bf16[4,4,128,512]{3,2,1,0:T(8,128)(2,1)} broadcast(bf16[4,128,512]{2,1,0:T(8,128)(2,1)S(1)} %all-to-all-done), dimensions={1,2,3} | broadcast | bytes 2621440 | tf_op jit(solution)/shard_map/broadcast_in_dim | solution.py:375
  17.8 4.8 %all-to-all-start.1 = ((bf16[4,4,128,512]{3,2,1,0:T(8,128)(2,1)}), bf16[4,4,128,512]{3,2,1,0:T(8,128)(2,1)S(1)}, u32[]{:S(2)}, u32[]{:S(2)}) async-start(bf16[4,4,128,512]{3,2,1,0:T(8,128)(2,1)} %broadcast_in_dim.7), calls=%async_computation.1 | async-start | bytes 4194304 | tf_op jit(solution)/shard_map/all_to_all | solution.py:374
  22.6 0.0 collective-permute-done.3.down2
  22.6 3.3 %collective-permute-start.4 = (bf16[64,512]{1,0:T(8,128)(2,1)S(1)}, bf16[64,512]{1,0:T(8,128)(2,1)S(1)}, u32[]{:S(2)}, u32[]{:S(2)}) collective-permute-start(bf16[64,512]{1,0:T(8,128)(2,1)S(1)} %slice_bitcast_fusion.12), channel_id=1, source_target_pairs={{0,64},{32,96},{64,128},{96,160},{128,192},{160,224},{192,0},{224,... | collective-permute-start | bytes 196616 | tf_op jit(solution)/shard_map/ppermute | solution.py:398
  26.0 2.0 %collective-permute-start.6 = (bf16[2,128,512]{2,1,0:T(8,128)(2,1)S(1)}, bf16[2,128,512]{2,1,0:T(8,128)(2,1)S(1)}, u32[]{:S(2)}, u32[]{:S(2)}) collective-permute-start(bf16[2,128,512]{2,1,0:T(8,128)(2,1)S(1)} %get-tuple-element.58), channel_id=1, source_target_pairs={{0,32},{32,64},{64,96},{96,128},{128,160},{160,192},{192,224},{224... | collective-permute-start | bytes 786440 | tf_op jit(solution)/shard_map/ppermute | solution.py:398
  28.0 1.3 %collective-permute-start.5 = (bf16[2,128,512]{2,1,0:T(8,128)(2,1)S(1)}, bf16[2,128,512]{2,1,0:T(8,128)(2,1)S(1)}, u32[]{:S(2)}, u32[]{:S(2)}) collective-permute-start(bf16[2,128,512]{2,1,0:T(8,128)(2,1)S(1)} %get-tuple-element.59), channel_id=1, source_target_pairs={{0,224},{32,0},{64,32},{96,64},{128,96},{160,128},{192,160},{224,1... | collective-permute-start | bytes 786440 | tf_op jit(solution)/shard_map/ppermute | solution.py:398
  29.3 2.4 %collective-permute-start.2 = (bf16[64,512]{1,0:T(8,128)(2,1)S(1)}, bf16[64,512]{1,0:T(8,128)(2,1)S(1)}, u32[]{:S(2)}, u32[]{:S(2)}) collective-permute-start(bf16[64,512]{1,0:T(8,128)(2,1)S(1)} %slice_bitcast_fusion.13), channel_id=1, source_target_pairs={{0,192},{32,224},{64,0},{96,32},{128,64},{160,96},{192,128},{224,1... | collective-permute-start | bytes 196616 | tf_op jit(solution)/shard_map/ppermute | solution.py:398
  31.7 0.1 pad_add_fusion.place_ref
  31.7 0.0 collective-permute-done.4.four1
  31.8 5.9 %collective-permute-done.2.four0 = bf16[64,512]{1,0:T(8,128)(2,1)S(1)} collective-permute-done((bf16[64,512]{1,0:T(8,128)(2,1)S(1)}, bf16[64,512]{1,0:T(8,128)(2,1)S(1)}, u32[]{:S(2)}, u32[]{:S(2)}) %collective-permute-start.2) | collective-permute-done | bytes 65568 | tf_op jit(solution)/shard_map/ppermute | solution.py:398
  37.6 0.2 shard_map.51
  37.8 1.3 %shard_map.52.own_ref = f32[512,512]{1,0:T(8,128)S(1)} custom-call(s32[4]{0:T(128)S(1)} %pad_add_fusion.place_ref, bf16[16,128,512]{2,1,0:T(8,128)(2,1)S(1)} %bitcast.69, bf16[2,512,512]{2,1,0:T(8,128)(2,1)S(1)} %get-tuple-element.25.v2_ref), custom_call_target="tpu_custom_call" | custom-call | flops 536870912 | bytes 3145728 | tf_op jit(solution)/shard_map/pallas_call | solution.py:111
  39.1 0.1 collective-permute-start.7
  39.2 1.3 %shard_map.54.own_ref = f32[512,512]{1,0:T(8,128)S(1)} custom-call(s32[4]{0:T(128)S(1)} %pad_add_fusion.place_ref, bf16[16,128,512]{2,1,0:T(8,128)(2,1)S(1)} %bitcast.70, bf16[2,512,512]{2,1,0:T(8,128)(2,1)S(1)} %get-tuple-element.25.v2_ref), custom_call_target="tpu_custom_call" | custom-call | flops 536870912 | bytes 3145728 | tf_op jit(solution)/shard_map/pallas_call | solution.py:111
  40.5 0.6 collective-permute-start.8
  41.1 0.2 abs_reduce_fusion
  41.3 0.1 collective-permute-start.9
  41.4 0.4 collective-permute-done.7.other_ref
  41.8 0.6 shard_map.53
  42.5 0.9 collective-permute-done.9.most_other_ref
  43.4 0.0 collective-permute-done.8.other_ref
  43.4 1.2 %shard_map.55 = (f32[512,512]{1,0:T(8,128)S(1)}, f32[16,16,128]{2,1,0:T(8,128)S(1)}) custom-call(s32[4]{0:T(128)S(1)} %pad_add_fusion.place_ref, f32[512,512]{1,0:T(8,128)S(1)} %shard_map.54.own_ref, f32[512,512]{1,0:T(8,128)S(1)} %collective-permute-done.8.other_ref, f32[4,128]{1,0:T(4,128)S(1)} %get-tuple-element.27.first_ref, ...), custom_call_target="tpu_custom_call" | custom-call | flops 2621440 | bytes 3145728 | tf_op jit(solution)/shard_map/pallas_call | solution.py:231
  44.5 12.2 %all_to_all.20.seen_ref = f32[16,16,128]{2,1,0:T(8,128)S(1)} all-to-all(f32[16,16,128]{2,1,0:T(8,128)S(1)} %get-tuple-element.32), channel_id=1, replica_groups={{0,8,16,24,4,12,20,28,2,10,18,26,6,14,22,30},{32,40,48,56,36,44,52,60,3..., dimensions={0} | all-to-all | bytes 262144 | tf_op jit(solution)/shard_map/all_to_all | solution.py:439
  56.7 0.6 shard_map.56.known_ref
  57.3 3.3 %collective-permute-start.10 = (f32[24,128]{1,0:T(8,128)S(1)}, f32[24,128]{1,0:T(8,128)S(1)}, u32[]{:S(2)}, u32[]{:S(2)}) collective-permute-start(f32[24,128]{1,0:T(8,128)S(1)} %shard_map.56.known_ref), channel_id=1, source_target_pairs={{0,1},{1,0},{2,3},{3,2},{4,5},{5,4},{6,7},{7,6},{8,9},{9,8},{10,11... | collective-permute-start | bytes 36872 | tf_op jit(solution)/shard_map/ppermute | solution.py:351
  60.6 0.7 shard_map.58
  61.3 0.2 collective-permute-done.10.told_ref
  61.5 1.4 %shard_map.57 = (bf16[1024,512]{1,0:T(8,128)(2,1)S(1)}, f32[1,512]{1,0:T(1,128)S(1)}, f32[1,512]{1,0:T(1,128)S(1)}, f32[1,512]{1,0:T(1,128)S(1)}, f32[1,512]{1,0:T(1,128)S(1)}) custom-call(s32[4]{0:T(128)S(1)} %pad_add_fusion.place_ref, f32[512,512]{1,0:T(8,128)S(1)} %get-tuple-element.26.s0_ref, f32[512,512]{1,0:T(8,128)S(1)} %get-tuple-element.31.s1_ref, ...), custom_call_target="tpu_custom_call" | custom-call | flops 4194304 | bytes 3145728 | tf_op jit(solution)/shard_map/pallas_call | solution.py:335
  62.9 2.6 %multiply_convert_fusion = f16[2,1024,512]{2,1,0:T(8,128)(2,1)} fusion(bf16[2,512,512]{2,1,0:T(8,128)(2,1)S(1)} %get-tuple-element.25.v2_ref, f32[512]{0:T(512)S(1)} %bitcast.76, bf16[1024,512]{1,0:T(8,128)(2,1)S(1)} %get-tuple-element.35), kind=kOutput, calls=%fused_computation.1 | convolution fusion | flops 1075838976 | bytes 4196352 | tf_op jit(solution)/shard_map/dot_general | solution.py:449
  65.5 0.7 fusion.1
  66.3 0.7 fusion
  67.0 5.6 %all-to-all-start.3 = ((f16[16,128,512]{2,1,0:T(8,128)(2,1)}), f16[16,128,512]{2,1,0:T(8,128)(2,1)S(1)}, u32[]{:S(2)}, u32[]{:S(2)}) async-start(f16[16,128,512]{2,1,0:T(8,128)(2,1)} %bitcast.78), calls=%async_computation.3 | async-start | bytes 4194304 | tf_op jit(solution)/shard_map/all_to_all | solution.py:458
  72.6 0.1 slice_bitcast_fusion.4
  72.7 0.1 pad_maximum_fusion.3
  72.8 1.5 %collective-permute-start.12 = (f16[2,128,512]{2,1,0:T(8,128)(2,1)S(1)}, f16[2,128,512]{2,1,0:T(8,128)(2,1)S(1)}, u32[]{:S(2)}, u32[]{:S(2)}) collective-permute-start(f16[2,128,512]{2,1,0:T(8,128)(2,1)S(1)} %pad_maximum_fusion.3), channel_id=1, source_target_pairs={{0,224},{32,0},{64,32},{96,64},{128,96},{160,128},{192,160},{224,1... | collective-permute-start | bytes 786440 | tf_op jit(solution)/shard_map/ppermute | solution.py:398
  74.4 1.6 %collective-permute-start.15 = (f16[64,512]{1,0:T(8,128)(2,1)S(1)}, f16[64,512]{1,0:T(8,128)(2,1)S(1)}, u32[]{:S(2)}, u32[]{:S(2)}) collective-permute-start(f16[64,512]{1,0:T(8,128)(2,1)S(1)} %get-tuple-element.49), channel_id=1, source_target_pairs={{0,192},{32,224},{64,0},{96,32},{128,64},{160,96},{192,128},{224,1... | collective-permute-start | bytes 196616 | tf_op jit(solution)/shard_map/ppermute | solution.py:398
  76.0 1.4 %collective-permute-start.13 = (f16[64,512]{1,0:T(8,128)(2,1)S(1)}, f16[64,512]{1,0:T(8,128)(2,1)S(1)}, u32[]{:S(2)}, u32[]{:S(2)}) collective-permute-start(f16[64,512]{1,0:T(8,128)(2,1)S(1)} %get-tuple-element.46), channel_id=1, source_target_pairs={{0,64},{32,96},{64,128},{96,160},{128,192},{160,224},{192,0},{224,... | collective-permute-start | bytes 196616 | tf_op jit(solution)/shard_map/ppermute | solution.py:398
  77.4 0.1 pad_maximum_fusion.2
  77.4 0.7 collective-permute-start.11
  78.1 4.0 %collective-permute-done.12 = f16[2,128,512]{2,1,0:T(8,128)(2,1)S(1)} collective-permute-done((f16[2,128,512]{2,1,0:T(8,128)(2,1)S(1)}, f16[2,128,512]{2,1,0:T(8,128)(2,1)S(1)}, u32[]{:S(2)}, u32[]{:S(2)}) %collective-permute-start.12) | collective-permute-done | bytes 262176 | tf_op jit(solution)/shard_map/ppermute | solution.py:398
  82.1 0.1 convert_element_type.65
  82.2 2.3 %collective-permute-done.15 = f16[64,512]{1,0:T(8,128)(2,1)S(1)} collective-permute-done((f16[64,512]{1,0:T(8,128)(2,1)S(1)}, f16[64,512]{1,0:T(8,128)(2,1)S(1)}, u32[]{:S(2)}, u32[]{:S(2)}) %collective-permute-start.15) | collective-permute-done | bytes 65568 | tf_op jit(solution)/shard_map/ppermute | solution.py:398
  84.5 2.9 %collective-permute-start.16 = (f16[2,64,512]{2,1,0:T(8,128)(2,1)S(1)}, f16[2,64,512]{2,1,0:T(8,128)(2,1)S(1)}, u32[]{:S(2)}, u32[]{:S(2)}) collective-permute-start(f16[2,64,512]{2,1,0:T(8,128)(2,1)S(1)} %fusion.6), channel_id=1, source_target_pairs={{0,192},{32,224},{64,0},{96,32},{128,64},{160,96},{192,128},{224,1... | collective-permute-start | bytes 393224 | tf_op jit(solution)/shard_map/ppermute | solution.py:398
  87.4 0.3 collective-permute-done.11
  87.7 0.1 convert_element_type.64
  87.9 0.0 collective-permute-done.13
  87.9 0.3 collective-permute-start.14
  88.3 3.4 %collective-permute-done.16 = f16[2,64,512]{2,1,0:T(8,128)(2,1)S(1)} collective-permute-done((f16[2,64,512]{2,1,0:T(8,128)(2,1)S(1)}, f16[2,64,512]{2,1,0:T(8,128)(2,1)S(1)}, u32[]{:S(2)}, u32[]{:S(2)}) %collective-permute-start.16) | collective-permute-done | bytes 131104 | tf_op jit(solution)/shard_map/ppermute | solution.py:398
  91.7 5.1 %collective-permute-done.14 = f16[2,64,512]{2,1,0:T(8,128)(2,1)S(1)} collective-permute-done((f16[2,64,512]{2,1,0:T(8,128)(2,1)S(1)}, f16[2,64,512]{2,1,0:T(8,128)(2,1)S(1)}, u32[]{:S(2)}, u32[]{:S(2)}) %collective-permute-start.14) | collective-permute-done | bytes 131104 | tf_op jit(solution)/shard_map/ppermute | solution.py:398
  96.8 0.1 fusion.4
  97.0 1.3 %collective-permute-start.17 = (f32[64,512]{1,0:T(8,128)S(1)}, f32[64,512]{1,0:T(8,128)S(1)}, u32[]{:S(2)}, u32[]{:S(2)}) collective-permute-start(f32[64,512]{1,0:T(8,128)S(1)} %get-tuple-element.57), channel_id=1, source_target_pairs={{0,2},{2,0},{1,3},{3,1},{4,6},{6,4},{5,7},{7,5},{8,10},{10,8},{9,1... | collective-permute-start | bytes 393224 | tf_op jit(solution)/shard_map/ppermute | solution.py:351
  98.3 1.8 %all-to-all-done.3 = f16[16,128,512]{2,1,0:T(8,128)(2,1)S(1)} async-done(((f16[16,128,512]{2,1,0:T(8,128)(2,1)}), f16[16,128,512]{2,1,0:T(8,128)(2,1)S(1)}, u32[]{:S(2)}, u32[]{:S(2)}) %all-to-all-start.3) | async-done | bytes 2097184 | tf_op jit(solution)/shard_map/all_to_all | solution.py:458
  100.1 1.1 %multiply_reduce_fusion = f32[128,512]{1,0:T(8,128)} fusion(f16[16,128,512]{2,1,0:T(8,128)(2,1)S(1)} %all-to-all-done.3, f32[512]{0:T(512)S(1)} %bitcast.73), kind=kLoop, calls=%fused_computation | loop fusion | flops 3080192 | bytes 2361344 | tf_op jit(solution)/shard_map/reduce_sum | solution.py:487
  101.2 1.1 %collective-permute-done.17 = f32[64,512]{1,0:T(8,128)S(1)} collective-permute-done((f32[64,512]{1,0:T(8,128)S(1)}, f32[64,512]{1,0:T(8,128)S(1)}, u32[]{:S(2)}, u32[]{:S(2)}) %collective-permute-start.17) | collective-permute-done | bytes 131104 | tf_op jit(solution)/shard_map/ppermute | solution.py:351
  102.4 0.7 maximum_select_fusion
  (26 shorter events, 0.4 us)
Async XLA Ops:
  0.6 9.1 %collective-permute-start = (bf16[128,512]{1,0:T(8,128)(2,1)}, bf16[128,512]{1,0:T(8,128)(2,1)S(1)}, u32[]{:S(2)}, u32[]{:S(2)}) collective-permute-start(bf16[128,512]{1,0:T(8,128)(2,1)} %param.4), channel_id=1, source_target_pairs={{0,2},{2,0},{1,3},{3,1},{4,6},{6,4},{5,7},{7,5},{8,10},{10,8},{9,1... | collective-permute-start | bytes 393224 | tf_op jit(solution)/shard_map/ppermute | solution.py:351
  3.7 12.6 %all-to-all-start = ((bf16[4,128,512]{2,1,0:T(8,128)(2,1)}), bf16[4,128,512]{2,1,0:T(8,128)(2,1)S(1)}, u32[]{:S(2)}, u32[]{:S(2)}) async-start(bf16[4,128,512]{2,1,0:T(8,128)(2,1)} %broadcast_in_dim.6), calls=%async_computation | async-start | bytes 1048576 | tf_op jit(solution)/shard_map/all_to_all | solution.py:374
  8.1 0.7 copy-start
  8.8 0.9 copy-start.1
  9.8 12.8 %collective-permute-start.3 = (bf16[2,64,512]{2,1,0:T(8,128)(2,1)S(1)}, bf16[2,64,512]{2,1,0:T(8,128)(2,1)S(1)}, u32[]{:S(2)}, u32[]{:S(2)}) collective-permute-start(bf16[2,64,512]{2,1,0:T(8,128)(2,1)S(1)} %maximum_select_fusion.1.own), channel_id=1, source_target_pairs={{0,64},{32,96},{64,128},{96,160},{128,192},{160,224},{192,0},{224,... | collective-permute-start | bytes 393224 | tf_op jit(solution)/shard_map/ppermute | solution.py:398
  13.1 12.8 %collective-permute-start.1 = (bf16[2,64,512]{2,1,0:T(8,128)(2,1)S(1)}, bf16[2,64,512]{2,1,0:T(8,128)(2,1)S(1)}, u32[]{:S(2)}, u32[]{:S(2)}) collective-permute-start(bf16[2,64,512]{2,1,0:T(8,128)(2,1)S(1)} %maximum_select_fusion.1.own), channel_id=1, source_target_pairs={{0,192},{32,224},{64,0},{96,32},{128,64},{160,96},{192,128},{224,1... | collective-permute-start | bytes 393224 | tf_op jit(solution)/shard_map/ppermute | solution.py:398
  17.8 20.0 %all-to-all-start.1 = ((bf16[4,4,128,512]{3,2,1,0:T(8,128)(2,1)}), bf16[4,4,128,512]{3,2,1,0:T(8,128)(2,1)S(1)}, u32[]{:S(2)}, u32[]{:S(2)}) async-start(bf16[4,4,128,512]{3,2,1,0:T(8,128)(2,1)} %broadcast_in_dim.7), calls=%async_computation.1 | async-start | bytes 4194304 | tf_op jit(solution)/shard_map/all_to_all | solution.py:374
  22.6 9.1 %collective-permute-start.4 = (bf16[64,512]{1,0:T(8,128)(2,1)S(1)}, bf16[64,512]{1,0:T(8,128)(2,1)S(1)}, u32[]{:S(2)}, u32[]{:S(2)}) collective-permute-start(bf16[64,512]{1,0:T(8,128)(2,1)S(1)} %slice_bitcast_fusion.12), channel_id=1, source_target_pairs={{0,64},{32,96},{64,128},{96,160},{128,192},{160,224},{192,0},{224,... | collective-permute-start | bytes 196616 | tf_op jit(solution)/shard_map/ppermute | solution.py:398
  26.0 11.6 %collective-permute-start.6 = (bf16[2,128,512]{2,1,0:T(8,128)(2,1)S(1)}, bf16[2,128,512]{2,1,0:T(8,128)(2,1)S(1)}, u32[]{:S(2)}, u32[]{:S(2)}) collective-permute-start(bf16[2,128,512]{2,1,0:T(8,128)(2,1)S(1)} %get-tuple-element.58), channel_id=1, source_target_pairs={{0,32},{32,64},{64,96},{96,128},{128,160},{160,192},{192,224},{224... | collective-permute-start | bytes 786440 | tf_op jit(solution)/shard_map/ppermute | solution.py:398
  28.0 9.7 %collective-permute-start.5 = (bf16[2,128,512]{2,1,0:T(8,128)(2,1)S(1)}, bf16[2,128,512]{2,1,0:T(8,128)(2,1)S(1)}, u32[]{:S(2)}, u32[]{:S(2)}) collective-permute-start(bf16[2,128,512]{2,1,0:T(8,128)(2,1)S(1)} %get-tuple-element.59), channel_id=1, source_target_pairs={{0,224},{32,0},{64,32},{96,64},{128,96},{160,128},{192,160},{224,1... | collective-permute-start | bytes 786440 | tf_op jit(solution)/shard_map/ppermute | solution.py:398
  29.3 8.3 %collective-permute-start.2 = (bf16[64,512]{1,0:T(8,128)(2,1)S(1)}, bf16[64,512]{1,0:T(8,128)(2,1)S(1)}, u32[]{:S(2)}, u32[]{:S(2)}) collective-permute-start(bf16[64,512]{1,0:T(8,128)(2,1)S(1)} %slice_bitcast_fusion.13), channel_id=1, source_target_pairs={{0,192},{32,224},{64,0},{96,32},{128,64},{160,96},{192,128},{224,1... | collective-permute-start | bytes 196616 | tf_op jit(solution)/shard_map/ppermute | solution.py:398
  39.1 2.7 %collective-permute-start.7 = (f32[512,512]{1,0:T(8,128)S(1)}, f32[512,512]{1,0:T(8,128)S(1)}, u32[]{:S(2)}, u32[]{:S(2)}) collective-permute-start(f32[512,512]{1,0:T(8,128)S(1)} %shard_map.52.own_ref), channel_id=1, source_target_pairs={{0,1},{1,0},{2,3},{3,2},{4,5},{5,4},{6,7},{7,6},{8,9},{9,8},{10,11... | collective-permute-start | bytes 3145736 | tf_op jit(solution)/shard_map/ppermute | solution.py:351
  40.5 2.9 %collective-permute-start.8 = (f32[512,512]{1,0:T(8,128)S(1)}, f32[512,512]{1,0:T(8,128)S(1)}, u32[]{:S(2)}, u32[]{:S(2)}) collective-permute-start(f32[512,512]{1,0:T(8,128)S(1)} %shard_map.54.own_ref), channel_id=1, source_target_pairs={{0,1},{1,0},{2,3},{3,2},{4,5},{5,4},{6,7},{7,6},{8,9},{9,8},{10,11... | collective-permute-start | bytes 3145736 | tf_op jit(solution)/shard_map/ppermute | solution.py:351
  41.3 2.0 %collective-permute-start.9 = (f32[2,512]{1,0:T(2,128)S(1)}, f32[2,512]{1,0:T(2,128)S(1)}, u32[]{:S(2)}, u32[]{:S(2)}) collective-permute-start(f32[2,512]{1,0:T(2,128)S(1)} %pad_maximum_fusion.4.most_ref), channel_id=1, source_target_pairs={{0,1},{1,0},{2,3},{3,2},{4,5},{5,4},{6,7},{7,6},{8,9},{9,8},{10,11... | collective-permute-start | bytes 12296 | tf_op jit(solution)/shard_map/ppermute | solution.py:351
  57.3 4.2 %collective-permute-start.10 = (f32[24,128]{1,0:T(8,128)S(1)}, f32[24,128]{1,0:T(8,128)S(1)}, u32[]{:S(2)}, u32[]{:S(2)}) collective-permute-start(f32[24,128]{1,0:T(8,128)S(1)} %shard_map.56.known_ref), channel_id=1, source_target_pairs={{0,1},{1,0},{2,3},{3,2},{4,5},{5,4},{6,7},{7,6},{8,9},{9,8},{10,11... | collective-permute-start | bytes 36872 | tf_op jit(solution)/shard_map/ppermute | solution.py:351
  67.0 33.1 %all-to-all-start.3 = ((f16[16,128,512]{2,1,0:T(8,128)(2,1)}), f16[16,128,512]{2,1,0:T(8,128)(2,1)S(1)}, u32[]{:S(2)}, u32[]{:S(2)}) async-start(f16[16,128,512]{2,1,0:T(8,128)(2,1)} %bitcast.78), calls=%async_computation.3 | async-start | bytes 4194304 | tf_op jit(solution)/shard_map/all_to_all | solution.py:458
  72.8 9.3 %collective-permute-start.12 = (f16[2,128,512]{2,1,0:T(8,128)(2,1)S(1)}, f16[2,128,512]{2,1,0:T(8,128)(2,1)S(1)}, u32[]{:S(2)}, u32[]{:S(2)}) collective-permute-start(f16[2,128,512]{2,1,0:T(8,128)(2,1)S(1)} %pad_maximum_fusion.3), channel_id=1, source_target_pairs={{0,224},{32,0},{64,32},{96,64},{128,96},{160,128},{192,160},{224,1... | collective-permute-start | bytes 786440 | tf_op jit(solution)/shard_map/ppermute | solution.py:398
  74.4 10.1 %collective-permute-start.15 = (f16[64,512]{1,0:T(8,128)(2,1)S(1)}, f16[64,512]{1,0:T(8,128)(2,1)S(1)}, u32[]{:S(2)}, u32[]{:S(2)}) collective-permute-start(f16[64,512]{1,0:T(8,128)(2,1)S(1)} %get-tuple-element.49), channel_id=1, source_target_pairs={{0,192},{32,224},{64,0},{96,32},{128,64},{160,96},{192,128},{224,1... | collective-permute-start | bytes 196616 | tf_op jit(solution)/shard_map/ppermute | solution.py:398
  76.0 11.9 %collective-permute-start.13 = (f16[64,512]{1,0:T(8,128)(2,1)S(1)}, f16[64,512]{1,0:T(8,128)(2,1)S(1)}, u32[]{:S(2)}, u32[]{:S(2)}) collective-permute-start(f16[64,512]{1,0:T(8,128)(2,1)S(1)} %get-tuple-element.46), channel_id=1, source_target_pairs={{0,64},{32,96},{64,128},{96,160},{128,192},{160,224},{192,0},{224,... | collective-permute-start | bytes 196616 | tf_op jit(solution)/shard_map/ppermute | solution.py:398
  77.4 10.3 %collective-permute-start.11 = (f16[2,128,512]{2,1,0:T(8,128)(2,1)S(1)}, f16[2,128,512]{2,1,0:T(8,128)(2,1)S(1)}, u32[]{:S(2)}, u32[]{:S(2)}) collective-permute-start(f16[2,128,512]{2,1,0:T(8,128)(2,1)S(1)} %pad_maximum_fusion.2), channel_id=1, source_target_pairs={{0,32},{32,64},{64,96},{96,128},{128,160},{160,192},{192,224},{224... | collective-permute-start | bytes 786440 | tf_op jit(solution)/shard_map/ppermute | solution.py:398
  84.5 7.2 %collective-permute-start.16 = (f16[2,64,512]{2,1,0:T(8,128)(2,1)S(1)}, f16[2,64,512]{2,1,0:T(8,128)(2,1)S(1)}, u32[]{:S(2)}, u32[]{:S(2)}) collective-permute-start(f16[2,64,512]{2,1,0:T(8,128)(2,1)S(1)} %fusion.6), channel_id=1, source_target_pairs={{0,192},{32,224},{64,0},{96,32},{128,64},{160,96},{192,128},{224,1... | collective-permute-start | bytes 393224 | tf_op jit(solution)/shard_map/ppermute | solution.py:398
  87.9 8.9 %collective-permute-start.14 = (f16[2,64,512]{2,1,0:T(8,128)(2,1)S(1)}, f16[2,64,512]{2,1,0:T(8,128)(2,1)S(1)}, u32[]{:S(2)}, u32[]{:S(2)}) collective-permute-start(f16[2,64,512]{2,1,0:T(8,128)(2,1)S(1)} %fusion.5), channel_id=1, source_target_pairs={{0,64},{32,96},{64,128},{96,160},{128,192},{160,224},{192,0},{224,... | collective-permute-start | bytes 393224 | tf_op jit(solution)/shard_map/ppermute | solution.py:398
  97.0 5.4 %collective-permute-start.17 = (f32[64,512]{1,0:T(8,128)S(1)}, f32[64,512]{1,0:T(8,128)S(1)}, u32[]{:S(2)}, u32[]{:S(2)}) collective-permute-start(f32[64,512]{1,0:T(8,128)S(1)} %get-tuple-element.57), channel_id=1, source_target_pairs={{0,2},{2,0},{1,3},{3,1},{4,6},{6,4},{5,7},{7,5},{8,10},{10,8},{9,1... | collective-permute-start | bytes 393224 | tf_op jit(solution)/shard_map/ppermute | solution.py:351

commit v14 on v13

--- a/solution.py
+++ b/solution.py
@@ -65,6 +65,22 @@
         compiler_params=limit(1),
         cost_estimate=pl.CostEstimate(flops=8 * 2**30, bytes_accessed=2**10, transcendentals=0),
     )(partner.reshape(1, ROWS))
+
+
+def four_kernel(x_ref, o_ref):
+    for p in range(4):
+        o_ref[p] = x_ref[...]
+
+
+def four_copies(x):
+    return pl.pallas_call(
+        four_kernel,
+        out_shape=jax.ShapeDtypeStruct((4,) + x.shape, x.dtype),
+        in_specs=[VMEM],
+        out_specs=VMEM,
+        compiler_params=limit(2),
+        cost_estimate=pl.CostEstimate(flops=0, bytes_accessed=2**19, transcendentals=0),
+    )(x)
 
 
 def join_kernel(own, four0, four1, up2, down2, up, down, v2_ref, most_ref):
@@ -370,9 +386,9 @@
     return alongs_y + alongs_x
 
 
-def spread(x, turn):
+def spread(copies, turn):
     return lax.all_to_all(
-        jnp.broadcast_to(x[None], (4,) + x.shape),
+        copies,
         EVERY,
         0,
         0,
@@ -410,7 +426,7 @@
     place = jnp.stack([core, xl, z, uhigh]).astype(jnp.int32)
 
     side = swap(view_two, "xl")
-    lines = spread(view_one, 0)
+    lines = spread(four_copies(view_one), 0)
     partner = numbers(partner)
     side, partner = lax.optimization_barrier((side, partner))
     lines, _ = lax.optimization_barrier((lines, side))
@@ -420,7 +436,7 @@
         jnp.stack([side[HALF:], view_two[HALF:]]),
     )
     up2, down2 = to_plane(here, -2), to_plane(here, 2)
-    v1_all = spread(lines, 1).reshape(16, ROWS, WIDTH)
+    v1_all = spread(jnp.broadcast_to(lines[None], (4,) + lines.shape), 1).reshape(16, ROWS, WIDTH)
     up = to_plane(jnp.concatenate([here, up2], axis=1), -1)
     down = to_plane(jnp.concatenate([here, down2], axis=1), 1)
     v2_all, most_v2 = join(

time: 103 us -> 103 us (level)
    broadcast_in_dim x2 -> x1, local copies, waits for them, and re-layouts: 3.32 us -> 1.56 us  [on_device(): jnp.broadcast_to(lines[None], (4,) + lines.shape)]
    unnamed x4 -> x6, local copies, waits for them, and re-layouts: 1.56 us -> 2.46 us
  transfers between devices with their start and end apart: 21 -> 21, of which waited for: 11 -> 11; matrix products, arithmetic and copies ran while one was open for 5% -> 4% of each run, Pallas kernels for 3% -> 3%
where the time goes in v14:
time: 103 us
  starting transfers between devices  45.4 us (44%)
  waiting for transfers between devices  25.5 us (25%)
  blocking collectives  12.2 us (12%)
  Pallas kernels  8.02 us (8%)
  local copies, waits for them, and re-layouts  4.27 us (4%)
  matrix products  4.1 us (4%)
  other arithmetic  2.76 us (3%)
    ppermute x12, starting transfers between devices, to_plane(): return lax.ppermute(x, 'z', [(z, (z + dz) % NZ) for z in range(NZ)])  23.8 us
    ppermute x12, waiting for transfers between devices, to_plane(): return lax.ppermute(x, 'z', [(z, (z + dz) % NZ) for z in range(NZ)])  21.1 us
    all_to_all x1, blocking collectives, on_device(): lax.all_to_all(pack, EVERY, 0, 0, axis_index_groups=stat_groups(), tiled=...  12.2 us
    all_to_all x2, starting transfers between devices, spread(): lax.all_to_all(copies, EVERY, 0, 0, axis_index_groups=line_groups(turn),...  9.26 us
    ppermute x6, starting transfers between devices, swap(): return lax.ppermute(x, axis, [(0, 1), (1, 0)])  6.7 us
    all_to_all x1, starting transfers between devices, on_device(): lax.all_to_all(part_one.reshape(16, ROWS, WIDTH), PLANE, 0, 0, tiled=True)  5.57 us
    ppermute x6, waiting for transfers between devices, swap(): return lax.ppermute(x, axis, [(0, 1), (1, 0)])  2.65 us
    dot_general x1, matrix products, on_device(): lax.dot_general(jnp.broadcast_to(coupling[None], (NXL, NI, NJ)), v2_all,...  2.61 us
  transfers between devices with their start and end apart: 21, of which 11 were waited for; matrix products, arithmetic and copies ran while one was open for 4% of the time, Pallas kernels for 3%

profile of v14, /device:TPU:4, one launch (start us, length us, event | category | flops | bytes accessed | tf_op | source)
XLA Modules:
  0.0 103.1 jit_solution(3634596631265631600)
XLA Ops:
  0.6 1.3 %collective-permute-start = (bf16[128,512]{1,0:T(8,128)(2,1)}, bf16[128,512]{1,0:T(8,128)(2,1)S(1)}, u32[]{:S(2)}, u32[]{:S(2)}) collective-permute-start(bf16[128,512]{1,0:T(8,128)(2,1)} %param.4), channel_id=1, source_target_pairs={{0,2},{2,0},{1,3},{3,1},{4,6},{6,4},{5,7},{7,5},{8,10},{10,8},{9,1... | collective-permute-start | bytes 393224 | tf_op jit(solution)/shard_map/ppermute | solution.py:367
  1.9 0.9 copy-done
  2.8 0.8 shard_map.50
  3.6 4.5 %all-to-all-start = ((bf16[4,128,512]{2,1,0:T(8,128)(2,1)}), bf16[4,128,512]{2,1,0:T(8,128)(2,1)S(1)}, u32[]{:S(2)}, u32[]{:S(2)}) async-start(bf16[4,128,512]{2,1,0:T(8,128)(2,1)} %shard_map.50), calls=%async_computation | async-start | bytes 1048576 | tf_op jit(solution)/shard_map/all_to_all | solution.py:390
  8.1 0.7 copy-done.1
  8.8 0.9 copy-done.2
  9.7 3.3 %collective-permute-start.3 = (bf16[2,64,512]{2,1,0:T(8,128)(2,1)S(1)}, bf16[2,64,512]{2,1,0:T(8,128)(2,1)S(1)}, u32[]{:S(2)}, u32[]{:S(2)}) collective-permute-start(bf16[2,64,512]{2,1,0:T(8,128)(2,1)S(1)} %maximum_select_fusion.1.own), channel_id=1, source_target_pairs={{0,64},{32,96},{64,128},{96,160},{128,192},{160,224},{192,0},{224,... | collective-permute-start | bytes 393224 | tf_op jit(solution)/shard_map/ppermute | solution.py:414
  13.1 3.1 %collective-permute-start.1 = (bf16[2,64,512]{2,1,0:T(8,128)(2,1)S(1)}, bf16[2,64,512]{2,1,0:T(8,128)(2,1)S(1)}, u32[]{:S(2)}, u32[]{:S(2)}) collective-permute-start(bf16[2,64,512]{2,1,0:T(8,128)(2,1)S(1)} %maximum_select_fusion.1.own), channel_id=1, source_target_pairs={{0,192},{32,224},{64,0},{96,32},{128,64},{160,96},{192,128},{224,1... | collective-permute-start | bytes 393224 | tf_op jit(solution)/shard_map/ppermute | solution.py:414
  16.2 1.6 %broadcast_in_dim.4 = bf16[4,4,128,512]{3,2,1,0:T(8,128)(2,1)} broadcast(bf16[4,128,512]{2,1,0:T(8,128)(2,1)S(1)} %all-to-all-done), dimensions={1,2,3} | broadcast | bytes 2621440 | tf_op jit(solution)/shard_map/broadcast_in_dim | solution.py:439
  17.8 4.8 %all-to-all-start.1 = ((bf16[4,4,128,512]{3,2,1,0:T(8,128)(2,1)}), bf16[4,4,128,512]{3,2,1,0:T(8,128)(2,1)S(1)}, u32[]{:S(2)}, u32[]{:S(2)}) async-start(bf16[4,4,128,512]{3,2,1,0:T(8,128)(2,1)} %broadcast_in_dim.4), calls=%async_computation.1 | async-start | bytes 4194304 | tf_op jit(solution)/shard_map/all_to_all | solution.py:390
  22.6 0.0 collective-permute-done.3.down2
  22.6 3.3 %collective-permute-start.4 = (bf16[64,512]{1,0:T(8,128)(2,1)S(1)}, bf16[64,512]{1,0:T(8,128)(2,1)S(1)}, u32[]{:S(2)}, u32[]{:S(2)}) collective-permute-start(bf16[64,512]{1,0:T(8,128)(2,1)S(1)} %slice_bitcast_fusion.12), channel_id=1, source_target_pairs={{0,64},{32,96},{64,128},{96,160},{128,192},{160,224},{192,0},{224,... | collective-permute-start | bytes 196616 | tf_op jit(solution)/shard_map/ppermute | solution.py:414
  25.9 0.0 collective-permute-done.1.up2
  26.0 2.0 %collective-permute-start.6 = (bf16[2,128,512]{2,1,0:T(8,128)(2,1)S(1)}, bf16[2,128,512]{2,1,0:T(8,128)(2,1)S(1)}, u32[]{:S(2)}, u32[]{:S(2)}) collective-permute-start(bf16[2,128,512]{2,1,0:T(8,128)(2,1)S(1)} %get-tuple-element.58), channel_id=1, source_target_pairs={{0,32},{32,64},{64,96},{96,128},{128,160},{160,192},{192,224},{224... | collective-permute-start | bytes 786440 | tf_op jit(solution)/shard_map/ppermute | solution.py:414
  28.0 1.3 %collective-permute-start.5 = (bf16[2,128,512]{2,1,0:T(8,128)(2,1)S(1)}, bf16[2,128,512]{2,1,0:T(8,128)(2,1)S(1)}, u32[]{:S(2)}, u32[]{:S(2)}) collective-permute-start(bf16[2,128,512]{2,1,0:T(8,128)(2,1)S(1)} %get-tuple-element.59), channel_id=1, source_target_pairs={{0,224},{32,0},{64,32},{96,64},{128,96},{160,128},{192,160},{224,1... | collective-permute-start | bytes 786440 | tf_op jit(solution)/shard_map/ppermute | solution.py:414
  29.3 2.4 %collective-permute-start.2 = (bf16[64,512]{1,0:T(8,128)(2,1)S(1)}, bf16[64,512]{1,0:T(8,128)(2,1)S(1)}, u32[]{:S(2)}, u32[]{:S(2)}) collective-permute-start(bf16[64,512]{1,0:T(8,128)(2,1)S(1)} %slice_bitcast_fusion.13), channel_id=1, source_target_pairs={{0,192},{32,224},{64,0},{96,32},{128,64},{160,96},{192,128},{224,1... | collective-permute-start | bytes 196616 | tf_op jit(solution)/shard_map/ppermute | solution.py:414
  31.6 0.1 pad_add_fusion.place_ref
  31.7 0.0 collective-permute-done.4.four1
  31.7 5.9 %collective-permute-done.2.four0 = bf16[64,512]{1,0:T(8,128)(2,1)S(1)} collective-permute-done((bf16[64,512]{1,0:T(8,128)(2,1)S(1)}, bf16[64,512]{1,0:T(8,128)(2,1)S(1)}, u32[]{:S(2)}, u32[]{:S(2)}) %collective-permute-start.2) | collective-permute-done | bytes 65568 | tf_op jit(solution)/shard_map/ppermute | solution.py:414
  37.6 0.0 collective-permute-done.6.down
  37.6 0.0 collective-permute-done.5.up
  37.6 0.2 shard_map.52
  37.8 1.3 %shard_map.53.own_ref = f32[512,512]{1,0:T(8,128)S(1)} custom-call(s32[4]{0:T(128)S(1)} %pad_add_fusion.place_ref, bf16[16,128,512]{2,1,0:T(8,128)(2,1)S(1)} %bitcast.69, bf16[2,512,512]{2,1,0:T(8,128)(2,1)S(1)} %get-tuple-element.25.v2_ref), custom_call_target="tpu_custom_call" | custom-call | flops 536870912 | bytes 3145728 | tf_op jit(solution)/shard_map/pallas_call | solution.py:127
  39.1 0.1 collective-permute-start.7
  39.2 1.3 %shard_map.55.own_ref = f32[512,512]{1,0:T(8,128)S(1)} custom-call(s32[4]{0:T(128)S(1)} %pad_add_fusion.place_ref, bf16[16,128,512]{2,1,0:T(8,128)(2,1)S(1)} %bitcast.70, bf16[2,512,512]{2,1,0:T(8,128)(2,1)S(1)} %get-tuple-element.25.v2_ref), custom_call_target="tpu_custom_call" | custom-call | flops 536870912 | bytes 3145728 | tf_op jit(solution)/shard_map/pallas_call | solution.py:127
  40.4 0.6 collective-permute-start.8
  41.0 0.2 abs_reduce_fusion
  41.3 0.1 collective-permute-start.9
  41.4 0.4 collective-permute-done.7.other_ref
  41.8 0.6 shard_map.54
  42.4 0.9 collective-permute-done.9.most_other_ref
  43.3 1.2 %shard_map.56 = (f32[512,512]{1,0:T(8,128)S(1)}, f32[16,16,128]{2,1,0:T(8,128)S(1)}) custom-call(s32[4]{0:T(128)S(1)} %pad_add_fusion.place_ref, f32[512,512]{1,0:T(8,128)S(1)} %shard_map.55.own_ref, f32[512,512]{1,0:T(8,128)S(1)} %collective-permute-done.8.other_ref, f32[4,128]{1,0:T(4,128)S(1)} %get-tuple-element.27.first_ref, ...), custom_call_target="tpu_custom_call" | custom-call | flops 2621440 | bytes 3145728 | tf_op jit(solution)/shard_map/pallas_call | solution.py:247
  44.5 12.2 %all_to_all.20.seen_ref = f32[16,16,128]{2,1,0:T(8,128)S(1)} all-to-all(f32[16,16,128]{2,1,0:T(8,128)S(1)} %get-tuple-element.32), channel_id=1, replica_groups={{0,8,16,24,4,12,20,28,2,10,18,26,6,14,22,30},{32,40,48,56,36,44,52,60,3..., dimensions={0} | all-to-all | bytes 262144 | tf_op jit(solution)/shard_map/all_to_all | solution.py:455
  56.7 0.6 shard_map.57.known_ref
  57.3 3.3 %collective-permute-start.10 = (f32[24,128]{1,0:T(8,128)S(1)}, f32[24,128]{1,0:T(8,128)S(1)}, u32[]{:S(2)}, u32[]{:S(2)}) collective-permute-start(f32[24,128]{1,0:T(8,128)S(1)} %shard_map.57.known_ref), channel_id=1, source_target_pairs={{0,1},{1,0},{2,3},{3,2},{4,5},{5,4},{6,7},{7,6},{8,9},{9,8},{10,11... | collective-permute-start | bytes 36872 | tf_op jit(solution)/shard_map/ppermute | solution.py:367
  60.6 0.7 shard_map.59
  61.3 0.2 collective-permute-done.10.told_ref
  61.4 1.4 %shard_map.58 = (bf16[1024,512]{1,0:T(8,128)(2,1)S(1)}, f32[1,512]{1,0:T(1,128)S(1)}, f32[1,512]{1,0:T(1,128)S(1)}, f32[1,512]{1,0:T(1,128)S(1)}, f32[1,512]{1,0:T(1,128)S(1)}) custom-call(s32[4]{0:T(128)S(1)} %pad_add_fusion.place_ref, f32[512,512]{1,0:T(8,128)S(1)} %get-tuple-element.26.s0_ref, f32[512,512]{1,0:T(8,128)S(1)} %get-tuple-element.31.s1_ref, ...), custom_call_target="tpu_custom_call" | custom-call | flops 4194304 | bytes 3145728 | tf_op jit(solution)/shard_map/pallas_call | solution.py:351
  62.9 2.6 %multiply_convert_fusion = f16[2,1024,512]{2,1,0:T(8,128)(2,1)} fusion(bf16[2,512,512]{2,1,0:T(8,128)(2,1)S(1)} %get-tuple-element.25.v2_ref, f32[512]{0:T(512)S(1)} %bitcast.76, bf16[1024,512]{1,0:T(8,128)(2,1)S(1)} %get-tuple-element.35), kind=kOutput, calls=%fused_computation.1 | convolution fusion | flops 1075838976 | bytes 4196352 | tf_op jit(solution)/shard_map/dot_general | solution.py:465
  65.5 0.7 fusion.1
  66.2 0.7 fusion
  67.0 5.6 %all-to-all-start.3 = ((f16[16,128,512]{2,1,0:T(8,128)(2,1)}), f16[16,128,512]{2,1,0:T(8,128)(2,1)S(1)}, u32[]{:S(2)}, u32[]{:S(2)}) async-start(f16[16,128,512]{2,1,0:T(8,128)(2,1)} %bitcast.78), calls=%async_computation.3 | async-start | bytes 4194304 | tf_op jit(solution)/shard_map/all_to_all | solution.py:474
  72.6 0.1 slice_bitcast_fusion.4
  72.7 0.1 pad_maximum_fusion.3
  72.8 1.5 %collective-permute-start.12 = (f16[2,128,512]{2,1,0:T(8,128)(2,1)S(1)}, f16[2,128,512]{2,1,0:T(8,128)(2,1)S(1)}, u32[]{:S(2)}, u32[]{:S(2)}) collective-permute-start(f16[2,128,512]{2,1,0:T(8,128)(2,1)S(1)} %pad_maximum_fusion.3), channel_id=1, source_target_pairs={{0,224},{32,0},{64,32},{96,64},{128,96},{160,128},{192,160},{224,1... | collective-permute-start | bytes 786440 | tf_op jit(solution)/shard_map/ppermute | solution.py:414
  74.3 1.6 %collective-permute-start.15 = (f16[64,512]{1,0:T(8,128)(2,1)S(1)}, f16[64,512]{1,0:T(8,128)(2,1)S(1)}, u32[]{:S(2)}, u32[]{:S(2)}) collective-permute-start(f16[64,512]{1,0:T(8,128)(2,1)S(1)} %get-tuple-element.49), channel_id=1, source_target_pairs={{0,192},{32,224},{64,0},{96,32},{128,64},{160,96},{192,128},{224,1... | collective-permute-start | bytes 196616 | tf_op jit(solution)/shard_map/ppermute | solution.py:414
  75.9 1.4 %collective-permute-start.13 = (f16[64,512]{1,0:T(8,128)(2,1)S(1)}, f16[64,512]{1,0:T(8,128)(2,1)S(1)}, u32[]{:S(2)}, u32[]{:S(2)}) collective-permute-start(f16[64,512]{1,0:T(8,128)(2,1)S(1)} %get-tuple-element.46), channel_id=1, source_target_pairs={{0,64},{32,96},{64,128},{96,160},{128,192},{160,224},{192,0},{224,... | collective-permute-start | bytes 196616 | tf_op jit(solution)/shard_map/ppermute | solution.py:414
  77.3 0.1 pad_maximum_fusion.2
  77.4 0.7 collective-permute-start.11
  78.1 3.9 %collective-permute-done.12 = f16[2,128,512]{2,1,0:T(8,128)(2,1)S(1)} collective-permute-done((f16[2,128,512]{2,1,0:T(8,128)(2,1)S(1)}, f16[2,128,512]{2,1,0:T(8,128)(2,1)S(1)}, u32[]{:S(2)}, u32[]{:S(2)}) %collective-permute-start.12) | collective-permute-done | bytes 262176 | tf_op jit(solution)/shard_map/ppermute | solution.py:414
  82.0 0.1 convert_element_type.65
  82.1 2.3 %collective-permute-done.15 = f16[64,512]{1,0:T(8,128)(2,1)S(1)} collective-permute-done((f16[64,512]{1,0:T(8,128)(2,1)S(1)}, f16[64,512]{1,0:T(8,128)(2,1)S(1)}, u32[]{:S(2)}, u32[]{:S(2)}) %collective-permute-start.15) | collective-permute-done | bytes 65568 | tf_op jit(solution)/shard_map/ppermute | solution.py:414
  84.5 2.9 %collective-permute-start.16 = (f16[2,64,512]{2,1,0:T(8,128)(2,1)S(1)}, f16[2,64,512]{2,1,0:T(8,128)(2,1)S(1)}, u32[]{:S(2)}, u32[]{:S(2)}) collective-permute-start(f16[2,64,512]{2,1,0:T(8,128)(2,1)S(1)} %fusion.6), channel_id=1, source_target_pairs={{0,192},{32,224},{64,0},{96,32},{128,64},{160,96},{192,128},{224,1... | collective-permute-start | bytes 393224 | tf_op jit(solution)/shard_map/ppermute | solution.py:414
  87.4 0.3 collective-permute-done.11
  87.7 0.1 convert_element_type.64
  87.9 0.3 collective-permute-start.14
  88.2 3.4 %collective-permute-done.16 = f16[2,64,512]{2,1,0:T(8,128)(2,1)S(1)} collective-permute-done((f16[2,64,512]{2,1,0:T(8,128)(2,1)S(1)}, f16[2,64,512]{2,1,0:T(8,128)(2,1)S(1)}, u32[]{:S(2)}, u32[]{:S(2)}) %collective-permute-start.16) | collective-permute-done | bytes 131104 | tf_op jit(solution)/shard_map/ppermute | solution.py:414
  91.6 5.2 %collective-permute-done.14 = f16[2,64,512]{2,1,0:T(8,128)(2,1)S(1)} collective-permute-done((f16[2,64,512]{2,1,0:T(8,128)(2,1)S(1)}, f16[2,64,512]{2,1,0:T(8,128)(2,1)S(1)}, u32[]{:S(2)}, u32[]{:S(2)}) %collective-permute-start.14) | collective-permute-done | bytes 131104 | tf_op jit(solution)/shard_map/ppermute | solution.py:414
  96.9 0.1 fusion.4
  97.0 1.3 %collective-permute-start.17 = (f32[64,512]{1,0:T(8,128)S(1)}, f32[64,512]{1,0:T(8,128)S(1)}, u32[]{:S(2)}, u32[]{:S(2)}) collective-permute-start(f32[64,512]{1,0:T(8,128)S(1)} %get-tuple-element.57), channel_id=1, source_target_pairs={{0,2},{2,0},{1,3},{3,1},{4,6},{6,4},{5,7},{7,5},{8,10},{10,8},{9,1... | collective-permute-start | bytes 393224 | tf_op jit(solution)/shard_map/ppermute | solution.py:367
  98.3 1.8 %all-to-all-done.3 = f16[16,128,512]{2,1,0:T(8,128)(2,1)S(1)} async-done(((f16[16,128,512]{2,1,0:T(8,128)(2,1)}), f16[16,128,512]{2,1,0:T(8,128)(2,1)S(1)}, u32[]{:S(2)}, u32[]{:S(2)}) %all-to-all-start.3) | async-done | bytes 2097184 | tf_op jit(solution)/shard_map/all_to_all | solution.py:474
  100.1 1.1 %multiply_reduce_fusion = f32[128,512]{1,0:T(8,128)} fusion(f16[16,128,512]{2,1,0:T(8,128)(2,1)S(1)} %all-to-all-done.3, f32[512]{0:T(512)S(1)} %bitcast.73), kind=kLoop, calls=%fused_computation | loop fusion | flops 3080192 | bytes 2361344 | tf_op jit(solution)/shard_map/reduce_sum | solution.py:503
  101.2 1.2 %collective-permute-done.17 = f32[64,512]{1,0:T(8,128)S(1)} collective-permute-done((f32[64,512]{1,0:T(8,128)S(1)}, f32[64,512]{1,0:T(8,128)S(1)}, u32[]{:S(2)}, u32[]{:S(2)}) %collective-permute-start.17) | collective-permute-done | bytes 131104 | tf_op jit(solution)/shard_map/ppermute | solution.py:367
  102.4 0.7 maximum_select_fusion
  (28 shorter events, 0.4 us)
Async XLA Ops:
  0.6 9.1 %collective-permute-start = (bf16[128,512]{1,0:T(8,128)(2,1)}, bf16[128,512]{1,0:T(8,128)(2,1)S(1)}, u32[]{:S(2)}, u32[]{:S(2)}) collective-permute-start(bf16[128,512]{1,0:T(8,128)(2,1)} %param.4), channel_id=1, source_target_pairs={{0,2},{2,0},{1,3},{3,1},{4,6},{6,4},{5,7},{7,5},{8,10},{10,8},{9,1... | collective-permute-start | bytes 393224 | tf_op jit(solution)/shard_map/ppermute | solution.py:367
  1.9 0.9 copy-start
  3.6 12.6 %all-to-all-start = ((bf16[4,128,512]{2,1,0:T(8,128)(2,1)}), bf16[4,128,512]{2,1,0:T(8,128)(2,1)S(1)}, u32[]{:S(2)}, u32[]{:S(2)}) async-start(bf16[4,128,512]{2,1,0:T(8,128)(2,1)} %shard_map.50), calls=%async_computation | async-start | bytes 1048576 | tf_op jit(solution)/shard_map/all_to_all | solution.py:390
  8.1 0.7 copy-start.1
  8.8 0.9 copy-start.2
  9.7 12.8 %collective-permute-start.3 = (bf16[2,64,512]{2,1,0:T(8,128)(2,1)S(1)}, bf16[2,64,512]{2,1,0:T(8,128)(2,1)S(1)}, u32[]{:S(2)}, u32[]{:S(2)}) collective-permute-start(bf16[2,64,512]{2,1,0:T(8,128)(2,1)S(1)} %maximum_select_fusion.1.own), channel_id=1, source_target_pairs={{0,64},{32,96},{64,128},{96,160},{128,192},{160,224},{192,0},{224,... | collective-permute-start | bytes 393224 | tf_op jit(solution)/shard_map/ppermute | solution.py:414
  13.1 12.8 %collective-permute-start.1 = (bf16[2,64,512]{2,1,0:T(8,128)(2,1)S(1)}, bf16[2,64,512]{2,1,0:T(8,128)(2,1)S(1)}, u32[]{:S(2)}, u32[]{:S(2)}) collective-permute-start(bf16[2,64,512]{2,1,0:T(8,128)(2,1)S(1)} %maximum_select_fusion.1.own), channel_id=1, source_target_pairs={{0,192},{32,224},{64,0},{96,32},{128,64},{160,96},{192,128},{224,1... | collective-permute-start | bytes 393224 | tf_op jit(solution)/shard_map/ppermute | solution.py:414
  17.8 20.0 %all-to-all-start.1 = ((bf16[4,4,128,512]{3,2,1,0:T(8,128)(2,1)}), bf16[4,4,128,512]{3,2,1,0:T(8,128)(2,1)S(1)}, u32[]{:S(2)}, u32[]{:S(2)}) async-start(bf16[4,4,128,512]{3,2,1,0:T(8,128)(2,1)} %broadcast_in_dim.4), calls=%async_computation.1 | async-start | bytes 4194304 | tf_op jit(solution)/shard_map/all_to_all | solution.py:390
  22.6 9.1 %collective-permute-start.4 = (bf16[64,512]{1,0:T(8,128)(2,1)S(1)}, bf16[64,512]{1,0:T(8,128)(2,1)S(1)}, u32[]{:S(2)}, u32[]{:S(2)}) collective-permute-start(bf16[64,512]{1,0:T(8,128)(2,1)S(1)} %slice_bitcast_fusion.12), channel_id=1, source_target_pairs={{0,64},{32,96},{64,128},{96,160},{128,192},{160,224},{192,0},{224,... | collective-permute-start | bytes 196616 | tf_op jit(solution)/shard_map/ppermute | solution.py:414
  26.0 11.6 %collective-permute-start.6 = (bf16[2,128,512]{2,1,0:T(8,128)(2,1)S(1)}, bf16[2,128,512]{2,1,0:T(8,128)(2,1)S(1)}, u32[]{:S(2)}, u32[]{:S(2)}) collective-permute-start(bf16[2,128,512]{2,1,0:T(8,128)(2,1)S(1)} %get-tuple-element.58), channel_id=1, source_target_pairs={{0,32},{32,64},{64,96},{96,128},{128,160},{160,192},{192,224},{224... | collective-permute-start | bytes 786440 | tf_op jit(solution)/shard_map/ppermute | solution.py:414
  28.0 9.7 %collective-permute-start.5 = (bf16[2,128,512]{2,1,0:T(8,128)(2,1)S(1)}, bf16[2,128,512]{2,1,0:T(8,128)(2,1)S(1)}, u32[]{:S(2)}, u32[]{:S(2)}) collective-permute-start(bf16[2,128,512]{2,1,0:T(8,128)(2,1)S(1)} %get-tuple-element.59), channel_id=1, source_target_pairs={{0,224},{32,0},{64,32},{96,64},{128,96},{160,128},{192,160},{224,1... | collective-permute-start | bytes 786440 | tf_op jit(solution)/shard_map/ppermute | solution.py:414
  29.3 8.3 %collective-permute-start.2 = (bf16[64,512]{1,0:T(8,128)(2,1)S(1)}, bf16[64,512]{1,0:T(8,128)(2,1)S(1)}, u32[]{:S(2)}, u32[]{:S(2)}) collective-permute-start(bf16[64,512]{1,0:T(8,128)(2,1)S(1)} %slice_bitcast_fusion.13), channel_id=1, source_target_pairs={{0,192},{32,224},{64,0},{96,32},{128,64},{160,96},{192,128},{224,1... | collective-permute-start | bytes 196616 | tf_op jit(solution)/shard_map/ppermute | solution.py:414
  39.1 2.7 %collective-permute-start.7 = (f32[512,512]{1,0:T(8,128)S(1)}, f32[512,512]{1,0:T(8,128)S(1)}, u32[]{:S(2)}, u32[]{:S(2)}) collective-permute-start(f32[512,512]{1,0:T(8,128)S(1)} %shard_map.53.own_ref), channel_id=1, source_target_pairs={{0,1},{1,0},{2,3},{3,2},{4,5},{5,4},{6,7},{7,6},{8,9},{9,8},{10,11... | collective-permute-start | bytes 3145736 | tf_op jit(solution)/shard_map/ppermute | solution.py:367
  40.4 2.9 %collective-permute-start.8 = (f32[512,512]{1,0:T(8,128)S(1)}, f32[512,512]{1,0:T(8,128)S(1)}, u32[]{:S(2)}, u32[]{:S(2)}) collective-permute-start(f32[512,512]{1,0:T(8,128)S(1)} %shard_map.55.own_ref), channel_id=1, source_target_pairs={{0,1},{1,0},{2,3},{3,2},{4,5},{5,4},{6,7},{7,6},{8,9},{9,8},{10,11... | collective-permute-start | bytes 3145736 | tf_op jit(solution)/shard_map/ppermute | solution.py:367
  41.3 2.0 %collective-permute-start.9 = (f32[2,512]{1,0:T(2,128)S(1)}, f32[2,512]{1,0:T(2,128)S(1)}, u32[]{:S(2)}, u32[]{:S(2)}) collective-permute-start(f32[2,512]{1,0:T(2,128)S(1)} %pad_maximum_fusion.4.most_ref), channel_id=1, source_target_pairs={{0,1},{1,0},{2,3},{3,2},{4,5},{5,4},{6,7},{7,6},{8,9},{9,8},{10,11... | collective-permute-start | bytes 12296 | tf_op jit(solution)/shard_map/ppermute | solution.py:367
  57.3 4.1 %collective-permute-start.10 = (f32[24,128]{1,0:T(8,128)S(1)}, f32[24,128]{1,0:T(8,128)S(1)}, u32[]{:S(2)}, u32[]{:S(2)}) collective-permute-start(f32[24,128]{1,0:T(8,128)S(1)} %shard_map.57.known_ref), channel_id=1, source_target_pairs={{0,1},{1,0},{2,3},{3,2},{4,5},{5,4},{6,7},{7,6},{8,9},{9,8},{10,11... | collective-permute-start | bytes 36872 | tf_op jit(solution)/shard_map/ppermute | solution.py:367
  67.0 33.1 %all-to-all-start.3 = ((f16[16,128,512]{2,1,0:T(8,128)(2,1)}), f16[16,128,512]{2,1,0:T(8,128)(2,1)S(1)}, u32[]{:S(2)}, u32[]{:S(2)}) async-start(f16[16,128,512]{2,1,0:T(8,128)(2,1)} %bitcast.78), calls=%async_computation.3 | async-start | bytes 4194304 | tf_op jit(solution)/shard_map/all_to_all | solution.py:474
  72.8 9.2 %collective-permute-start.12 = (f16[2,128,512]{2,1,0:T(8,128)(2,1)S(1)}, f16[2,128,512]{2,1,0:T(8,128)(2,1)S(1)}, u32[]{:S(2)}, u32[]{:S(2)}) collective-permute-start(f16[2,128,512]{2,1,0:T(8,128)(2,1)S(1)} %pad_maximum_fusion.3), channel_id=1, source_target_pairs={{0,224},{32,0},{64,32},{96,64},{128,96},{160,128},{192,160},{224,1... | collective-permute-start | bytes 786440 | tf_op jit(solution)/shard_map/ppermute | solution.py:414
  74.3 10.1 %collective-permute-start.15 = (f16[64,512]{1,0:T(8,128)(2,1)S(1)}, f16[64,512]{1,0:T(8,128)(2,1)S(1)}, u32[]{:S(2)}, u32[]{:S(2)}) collective-permute-start(f16[64,512]{1,0:T(8,128)(2,1)S(1)} %get-tuple-element.49), channel_id=1, source_target_pairs={{0,192},{32,224},{64,0},{96,32},{128,64},{160,96},{192,128},{224,1... | collective-permute-start | bytes 196616 | tf_op jit(solution)/shard_map/ppermute | solution.py:414
  75.9 11.9 %collective-permute-start.13 = (f16[64,512]{1,0:T(8,128)(2,1)S(1)}, f16[64,512]{1,0:T(8,128)(2,1)S(1)}, u32[]{:S(2)}, u32[]{:S(2)}) collective-permute-start(f16[64,512]{1,0:T(8,128)(2,1)S(1)} %get-tuple-element.46), channel_id=1, source_target_pairs={{0,64},{32,96},{64,128},{96,160},{128,192},{160,224},{192,0},{224,... | collective-permute-start | bytes 196616 | tf_op jit(solution)/shard_map/ppermute | solution.py:414
  77.4 10.3 %collective-permute-start.11 = (f16[2,128,512]{2,1,0:T(8,128)(2,1)S(1)}, f16[2,128,512]{2,1,0:T(8,128)(2,1)S(1)}, u32[]{:S(2)}, u32[]{:S(2)}) collective-permute-start(f16[2,128,512]{2,1,0:T(8,128)(2,1)S(1)} %pad_maximum_fusion.2), channel_id=1, source_target_pairs={{0,32},{32,64},{64,96},{96,128},{128,160},{160,192},{192,224},{224... | collective-permute-start | bytes 786440 | tf_op jit(solution)/shard_map/ppermute | solution.py:414
  84.5 7.1 %collective-permute-start.16 = (f16[2,64,512]{2,1,0:T(8,128)(2,1)S(1)}, f16[2,64,512]{2,1,0:T(8,128)(2,1)S(1)}, u32[]{:S(2)}, u32[]{:S(2)}) collective-permute-start(f16[2,64,512]{2,1,0:T(8,128)(2,1)S(1)} %fusion.6), channel_id=1, source_target_pairs={{0,192},{32,224},{64,0},{96,32},{128,64},{160,96},{192,128},{224,1... | collective-permute-start | bytes 393224 | tf_op jit(solution)/shard_map/ppermute | solution.py:414
  87.9 8.9 %collective-permute-start.14 = (f16[2,64,512]{2,1,0:T(8,128)(2,1)S(1)}, f16[2,64,512]{2,1,0:T(8,128)(2,1)S(1)}, u32[]{:S(2)}, u32[]{:S(2)}) collective-permute-start(f16[2,64,512]{2,1,0:T(8,128)(2,1)S(1)} %fusion.5), channel_id=1, source_target_pairs={{0,64},{32,96},{64,128},{96,160},{128,192},{160,224},{192,0},{224,... | collective-permute-start | bytes 393224 | tf_op jit(solution)/shard_map/ppermute | solution.py:414
  97.0 5.4 %collective-permute-start.17 = (f32[64,512]{1,0:T(8,128)S(1)}, f32[64,512]{1,0:T(8,128)S(1)}, u32[]{:S(2)}, u32[]{:S(2)}) collective-permute-start(f32[64,512]{1,0:T(8,128)S(1)} %get-tuple-element.57), channel_id=1, source_target_pairs={{0,2},{2,0},{1,3},{3,1},{4,6},{6,4},{5,7},{7,5},{8,10},{10,8},{9,1... | collective-permute-start | bytes 393224 | tf_op jit(solution)/shard_map/ppermute | solution.py:367

commit v15 on v13

--- a/solution.py
+++ b/solution.py
@@ -454,7 +454,6 @@
         )
         * give_one
     ).astype(jnp.float16)
-    coupling, part_one = lax.optimization_barrier((coupling, part_one))
     one_parts = lax.all_to_all(part_one.reshape(16, ROWS, WIDTH), PLANE, 0, 0, tiled=True)
     part_two = [
         (

time: 103 us -> 105 us (1.019)
  matrix products: 4.1 us -> 5.68 us
    dot_general x2, matrix products: 1.49 us -> 3.07 us  [on_device(): lax.dot_general(coupling, v1_rows[x], (((0,), (0,)), ((), ())), preferred...]
where the time goes in v15:
time: 105 us
  starting transfers between devices  45.5 us (43%)
  waiting for transfers between devices  25.5 us (24%)
  blocking collectives  12.2 us (12%)
  Pallas kernels  7.21 us (7%)
  matrix products  5.68 us (5%)
  local copies, waits for them, and re-layouts  5.11 us (5%)
  other arithmetic  2.76 us (3%)
    ppermute x12, starting transfers between devices, to_plane(): return lax.ppermute(x, 'z', [(z, (z + dz) % NZ) for z in range(NZ)])  23.8 us
    ppermute x12, waiting for transfers between devices, to_plane(): return lax.ppermute(x, 'z', [(z, (z + dz) % NZ) for z in range(NZ)])  21.1 us
    all_to_all x1, blocking collectives, on_device(): lax.all_to_all(pack, EVERY, 0, 0, axis_index_groups=stat_groups(), tiled=...  12.2 us
    all_to_all x2, starting transfers between devices, spread(): lax.all_to_all(jnp.broadcast_to(x[None], (4,) + x.shape), EVERY, 0, 0, ax...  9.26 us
    ppermute x6, starting transfers between devices, swap(): return lax.ppermute(x, axis, [(0, 1), (1, 0)])  6.71 us
    all_to_all x1, starting transfers between devices, on_device(): lax.all_to_all(part_one.reshape(16, ROWS, WIDTH), PLANE, 0, 0, tiled=True)  5.68 us
    broadcast_in_dim x2, local copies, waits for them, and re-layouts, spread(): jnp.broadcast_to(x[None], (4,) + x.shape)  3.29 us
    dot_general x2, matrix products, on_device(): lax.dot_general(coupling, v1_rows[x], (((0,), (0,)), ((), ())), preferred...  3.07 us
  transfers between devices with their start and end apart: 21, of which 11 were waited for; matrix products, arithmetic and copies ran while one was open for 5% of the time, Pallas kernels for 3%

profile of v15, /device:TPU:4, one launch (start us, length us, event | category | flops | bytes accessed | tf_op | source)
XLA Modules:
  0.0 104.8 jit_solution(3092412829027179100)
XLA Ops:
  0.6 1.3 %collective-permute-start = (bf16[128,512]{1,0:T(8,128)(2,1)}, bf16[128,512]{1,0:T(8,128)(2,1)S(1)}, u32[]{:S(2)}, u32[]{:S(2)}) collective-permute-start(bf16[128,512]{1,0:T(8,128)(2,1)} %param.4), channel_id=1, source_target_pairs={{0,2},{2,0},{1,3},{3,1},{4,6},{6,4},{5,7},{7,5},{8,10},{10,8},{9,1... | collective-permute-start | bytes 393224 | tf_op jit(solution)/shard_map/ppermute | solution.py:351
  1.9 1.7 %broadcast_in_dim.6 = bf16[4,128,512]{2,1,0:T(8,128)(2,1)} broadcast(bf16[128,512]{1,0:T(8,128)(2,1)} %param.3), dimensions={1,2} | broadcast | bytes 655360 | tf_op jit(solution)/shard_map/broadcast_in_dim | solution.py:375
  3.7 4.5 %all-to-all-start = ((bf16[4,128,512]{2,1,0:T(8,128)(2,1)}), bf16[4,128,512]{2,1,0:T(8,128)(2,1)S(1)}, u32[]{:S(2)}, u32[]{:S(2)}) async-start(bf16[4,128,512]{2,1,0:T(8,128)(2,1)} %broadcast_in_dim.6), calls=%async_computation | async-start | bytes 1048576 | tf_op jit(solution)/shard_map/all_to_all | solution.py:374
  8.1 0.7 copy-done
  8.8 0.9 copy-done.3
  9.7 0.0 collective-permute-done
  9.8 3.3 %collective-permute-start.3 = (bf16[2,64,512]{2,1,0:T(8,128)(2,1)S(1)}, bf16[2,64,512]{2,1,0:T(8,128)(2,1)S(1)}, u32[]{:S(2)}, u32[]{:S(2)}) collective-permute-start(bf16[2,64,512]{2,1,0:T(8,128)(2,1)S(1)} %maximum_select_fusion.1.own), channel_id=1, source_target_pairs={{0,64},{32,96},{64,128},{96,160},{128,192},{160,224},{192,0},{224,... | collective-permute-start | bytes 393224 | tf_op jit(solution)/shard_map/ppermute | solution.py:398
  13.1 3.1 %collective-permute-start.1 = (bf16[2,64,512]{2,1,0:T(8,128)(2,1)S(1)}, bf16[2,64,512]{2,1,0:T(8,128)(2,1)S(1)}, u32[]{:S(2)}, u32[]{:S(2)}) collective-permute-start(bf16[2,64,512]{2,1,0:T(8,128)(2,1)S(1)} %maximum_select_fusion.1.own), channel_id=1, source_target_pairs={{0,192},{32,224},{64,0},{96,32},{128,64},{160,96},{192,128},{224,1... | collective-permute-start | bytes 393224 | tf_op jit(solution)/shard_map/ppermute | solution.py:398
  16.2 0.0 all-to-all-done
  16.2 1.6 %broadcast_in_dim.7 = bf16[4,4,128,512]{3,2,1,0:T(8,128)(2,1)} broadcast(bf16[4,128,512]{2,1,0:T(8,128)(2,1)S(1)} %all-to-all-done), dimensions={1,2,3} | broadcast | bytes 2621440 | tf_op jit(solution)/shard_map/broadcast_in_dim | solution.py:375
  17.8 4.8 %all-to-all-start.1 = ((bf16[4,4,128,512]{3,2,1,0:T(8,128)(2,1)}), bf16[4,4,128,512]{3,2,1,0:T(8,128)(2,1)S(1)}, u32[]{:S(2)}, u32[]{:S(2)}) async-start(bf16[4,4,128,512]{3,2,1,0:T(8,128)(2,1)} %broadcast_in_dim.7), calls=%async_computation.1 | async-start | bytes 4194304 | tf_op jit(solution)/shard_map/all_to_all | solution.py:374
  22.6 3.3 %collective-permute-start.4 = (bf16[64,512]{1,0:T(8,128)(2,1)S(1)}, bf16[64,512]{1,0:T(8,128)(2,1)S(1)}, u32[]{:S(2)}, u32[]{:S(2)}) collective-permute-start(bf16[64,512]{1,0:T(8,128)(2,1)S(1)} %slice_bitcast_fusion.12), channel_id=1, source_target_pairs={{0,64},{32,96},{64,128},{96,160},{128,192},{160,224},{192,0},{224,... | collective-permute-start | bytes 196616 | tf_op jit(solution)/shard_map/ppermute | solution.py:398
  26.0 2.0 %collective-permute-start.6 = (bf16[2,128,512]{2,1,0:T(8,128)(2,1)S(1)}, bf16[2,128,512]{2,1,0:T(8,128)(2,1)S(1)}, u32[]{:S(2)}, u32[]{:S(2)}) collective-permute-start(bf16[2,128,512]{2,1,0:T(8,128)(2,1)S(1)} %get-tuple-element.54), channel_id=1, source_target_pairs={{0,32},{32,64},{64,96},{96,128},{128,160},{160,192},{192,224},{224... | collective-permute-start | bytes 786440 | tf_op jit(solution)/shard_map/ppermute | solution.py:398
  28.0 1.3 %collective-permute-start.5 = (bf16[2,128,512]{2,1,0:T(8,128)(2,1)S(1)}, bf16[2,128,512]{2,1,0:T(8,128)(2,1)S(1)}, u32[]{:S(2)}, u32[]{:S(2)}) collective-permute-start(bf16[2,128,512]{2,1,0:T(8,128)(2,1)S(1)} %get-tuple-element.55), channel_id=1, source_target_pairs={{0,224},{32,0},{64,32},{96,64},{128,96},{160,128},{192,160},{224,1... | collective-permute-start | bytes 786440 | tf_op jit(solution)/shard_map/ppermute | solution.py:398
  29.3 2.4 %collective-permute-start.2 = (bf16[64,512]{1,0:T(8,128)(2,1)S(1)}, bf16[64,512]{1,0:T(8,128)(2,1)S(1)}, u32[]{:S(2)}, u32[]{:S(2)}) collective-permute-start(bf16[64,512]{1,0:T(8,128)(2,1)S(1)} %slice_bitcast_fusion.13), channel_id=1, source_target_pairs={{0,192},{32,224},{64,0},{96,32},{128,64},{160,96},{192,128},{224,1... | collective-permute-start | bytes 196616 | tf_op jit(solution)/shard_map/ppermute | solution.py:398
  31.6 0.1 pad_add_fusion.place_ref
  31.7 0.0 collective-permute-done.4.four1
  31.7 5.9 %collective-permute-done.2.four0 = bf16[64,512]{1,0:T(8,128)(2,1)S(1)} collective-permute-done((bf16[64,512]{1,0:T(8,128)(2,1)S(1)}, bf16[64,512]{1,0:T(8,128)(2,1)S(1)}, u32[]{:S(2)}, u32[]{:S(2)}) %collective-permute-start.2) | collective-permute-done | bytes 65568 | tf_op jit(solution)/shard_map/ppermute | solution.py:398
  37.6 0.0 collective-permute-done.6.down
  37.6 0.0 collective-permute-done.5.up
  37.6 0.2 shard_map.51
  37.8 1.3 %shard_map.52.own_ref = f32[512,512]{1,0:T(8,128)S(1)} custom-call(s32[4]{0:T(128)S(1)} %pad_add_fusion.place_ref, bf16[16,128,512]{2,1,0:T(8,128)(2,1)S(1)} %bitcast.69, bf16[2,512,512]{2,1,0:T(8,128)(2,1)S(1)} %get-tuple-element.23.v2_ref), custom_call_target="tpu_custom_call" | custom-call | flops 536870912 | bytes 3145728 | tf_op jit(solution)/shard_map/pallas_call | solution.py:111
  39.1 0.1 collective-permute-start.7
  39.2 1.3 %shard_map.54.own_ref = f32[512,512]{1,0:T(8,128)S(1)} custom-call(s32[4]{0:T(128)S(1)} %pad_add_fusion.place_ref, bf16[16,128,512]{2,1,0:T(8,128)(2,1)S(1)} %bitcast.70, bf16[2,512,512]{2,1,0:T(8,128)(2,1)S(1)} %get-tuple-element.23.v2_ref), custom_call_target="tpu_custom_call" | custom-call | flops 536870912 | bytes 3145728 | tf_op jit(solution)/shard_map/pallas_call | solution.py:111
  40.4 0.6 collective-permute-start.8
  41.0 0.2 abs_reduce_fusion
  41.3 0.1 collective-permute-start.9
  41.4 0.4 collective-permute-done.7.other_ref
  41.8 0.6 shard_map.53
  42.4 0.9 collective-permute-done.9.most_other_ref
  43.3 0.0 collective-permute-done.8.other_ref
  43.3 1.2 %shard_map.55 = (f32[512,512]{1,0:T(8,128)S(1)}, f32[16,16,128]{2,1,0:T(8,128)S(1)}) custom-call(s32[4]{0:T(128)S(1)} %pad_add_fusion.place_ref, f32[512,512]{1,0:T(8,128)S(1)} %shard_map.54.own_ref, f32[512,512]{1,0:T(8,128)S(1)} %collective-permute-done.8.other_ref, f32[4,128]{1,0:T(4,128)S(1)} %get-tuple-element.25.first_ref, ...), custom_call_target="tpu_custom_call" | custom-call | flops 2621440 | bytes 3145728 | tf_op jit(solution)/shard_map/pallas_call | solution.py:231
  44.5 12.2 %all_to_all.20.seen_ref = f32[16,16,128]{2,1,0:T(8,128)S(1)} all-to-all(f32[16,16,128]{2,1,0:T(8,128)S(1)} %get-tuple-element.30), channel_id=1, replica_groups={{0,8,16,24,4,12,20,28,2,10,18,26,6,14,22,30},{32,40,48,56,36,44,52,60,3..., dimensions={0} | all-to-all | bytes 262144 | tf_op jit(solution)/shard_map/all_to_all | solution.py:439
  56.7 0.6 shard_map.56.known_ref
  57.3 3.3 %collective-permute-start.10 = (f32[24,128]{1,0:T(8,128)S(1)}, f32[24,128]{1,0:T(8,128)S(1)}, u32[]{:S(2)}, u32[]{:S(2)}) collective-permute-start(f32[24,128]{1,0:T(8,128)S(1)} %shard_map.56.known_ref), channel_id=1, source_target_pairs={{0,1},{1,0},{2,3},{3,2},{4,5},{5,4},{6,7},{7,6},{8,9},{9,8},{10,11... | collective-permute-start | bytes 36872 | tf_op jit(solution)/shard_map/ppermute | solution.py:351
  60.6 0.7 shard_map.58
  61.3 0.2 collective-permute-done.10.told_ref
  61.5 1.4 %shard_map.57 = (bf16[1024,512]{1,0:T(8,128)(2,1)S(1)}, f32[1,512]{1,0:T(1,128)S(1)}, f32[1,512]{1,0:T(1,128)S(1)}, f32[1,512]{1,0:T(1,128)S(1)}, f32[1,512]{1,0:T(1,128)S(1)}) custom-call(s32[4]{0:T(128)S(1)} %pad_add_fusion.place_ref, f32[512,512]{1,0:T(8,128)S(1)} %get-tuple-element.24.s0_ref, f32[512,512]{1,0:T(8,128)S(1)} %get-tuple-element.29.s1_ref, ...), custom_call_target="tpu_custom_call" | custom-call | flops 4194304 | bytes 3145728 | tf_op jit(solution)/shard_map/pallas_call | solution.py:335
  62.9 1.5 %fusion.1 = f16[512,512]{1,0:T(8,128)(2,1)} fusion(bf16[1024,512]{1,0:T(8,128)(2,1)S(1)} %get-tuple-element.31, bf16[1024,512]{1,0:T(8,128)(2,1)S(1)} %get-tuple-element.34, f32[512]{0:T(512)S(1)} %bitcast.75), kind=kOutput, calls=%fused_computation.6 | convolution fusion | flops 537395200 | bytes 2623488 | tf_op jit(solution)/shard_map/dot_general | solution.py:460
  64.4 1.5 %fusion = f16[512,512]{1,0:T(8,128)(2,1)} fusion(bf16[1024,512]{1,0:T(8,128)(2,1)S(1)} %get-tuple-element.31, bf16[1024,512]{1,0:T(8,128)(2,1)S(1)} %get-tuple-element.32, f32[512]{0:T(512)S(1)} %bitcast.76), kind=kOutput, calls=%fused_computation.5 | convolution fusion | flops 537395200 | bytes 2623488 | tf_op jit(solution)/shard_map/dot_general | solution.py:460
  66.0 2.6 %multiply_convert_fusion = f16[2,1024,512]{2,1,0:T(8,128)(2,1)} fusion(bf16[2,512,512]{2,1,0:T(8,128)(2,1)S(1)} %get-tuple-element.23.v2_ref, f32[512]{0:T(512)S(1)} %bitcast.74, bf16[1024,512]{1,0:T(8,128)(2,1)S(1)} %get-tuple-element.31), kind=kOutput, calls=%fused_computation.1 | convolution fusion | flops 1075838976 | bytes 4196352 | tf_op jit(solution)/shard_map/dot_general | solution.py:449
  68.6 5.7 %all-to-all-start.3 = ((f16[16,128,512]{2,1,0:T(8,128)(2,1)}), f16[16,128,512]{2,1,0:T(8,128)(2,1)S(1)}, u32[]{:S(2)}, u32[]{:S(2)}) async-start(f16[16,128,512]{2,1,0:T(8,128)(2,1)} %bitcast.78), calls=%async_computation.3 | async-start | bytes 4194304 | tf_op jit(solution)/shard_map/all_to_all | solution.py:457
  74.3 0.1 slice_bitcast_fusion.4
  74.4 0.1 pad_maximum_fusion.3
  74.5 1.5 %collective-permute-start.12 = (f16[2,128,512]{2,1,0:T(8,128)(2,1)S(1)}, f16[2,128,512]{2,1,0:T(8,128)(2,1)S(1)}, u32[]{:S(2)}, u32[]{:S(2)}) collective-permute-start(f16[2,128,512]{2,1,0:T(8,128)(2,1)S(1)} %pad_maximum_fusion.3), channel_id=1, source_target_pairs={{0,224},{32,0},{64,32},{96,64},{128,96},{160,128},{192,160},{224,1... | collective-permute-start | bytes 786440 | tf_op jit(solution)/shard_map/ppermute | solution.py:398
  76.1 1.6 %collective-permute-start.15 = (f16[64,512]{1,0:T(8,128)(2,1)S(1)}, f16[64,512]{1,0:T(8,128)(2,1)S(1)}, u32[]{:S(2)}, u32[]{:S(2)}) collective-permute-start(f16[64,512]{1,0:T(8,128)(2,1)S(1)} %get-tuple-element.45), channel_id=1, source_target_pairs={{0,192},{32,224},{64,0},{96,32},{128,64},{160,96},{192,128},{224,1... | collective-permute-start | bytes 196616 | tf_op jit(solution)/shard_map/ppermute | solution.py:398
  77.7 1.4 %collective-permute-start.13 = (f16[64,512]{1,0:T(8,128)(2,1)S(1)}, f16[64,512]{1,0:T(8,128)(2,1)S(1)}, u32[]{:S(2)}, u32[]{:S(2)}) collective-permute-start(f16[64,512]{1,0:T(8,128)(2,1)S(1)} %get-tuple-element.42), channel_id=1, source_target_pairs={{0,64},{32,96},{64,128},{96,160},{128,192},{160,224},{192,0},{224,... | collective-permute-start | bytes 196616 | tf_op jit(solution)/shard_map/ppermute | solution.py:398
  79.1 0.1 pad_maximum_fusion.2
  79.1 0.7 collective-permute-start.11
  79.8 3.9 %collective-permute-done.12 = f16[2,128,512]{2,1,0:T(8,128)(2,1)S(1)} collective-permute-done((f16[2,128,512]{2,1,0:T(8,128)(2,1)S(1)}, f16[2,128,512]{2,1,0:T(8,128)(2,1)S(1)}, u32[]{:S(2)}, u32[]{:S(2)}) %collective-permute-start.12) | collective-permute-done | bytes 262176 | tf_op jit(solution)/shard_map/ppermute | solution.py:398
  83.7 0.1 convert_element_type.64
  83.9 2.3 %collective-permute-done.15 = f16[64,512]{1,0:T(8,128)(2,1)S(1)} collective-permute-done((f16[64,512]{1,0:T(8,128)(2,1)S(1)}, f16[64,512]{1,0:T(8,128)(2,1)S(1)}, u32[]{:S(2)}, u32[]{:S(2)}) %collective-permute-start.15) | collective-permute-done | bytes 65568 | tf_op jit(solution)/shard_map/ppermute | solution.py:398
  86.2 2.9 %collective-permute-start.16 = (f16[2,64,512]{2,1,0:T(8,128)(2,1)S(1)}, f16[2,64,512]{2,1,0:T(8,128)(2,1)S(1)}, u32[]{:S(2)}, u32[]{:S(2)}) collective-permute-start(f16[2,64,512]{2,1,0:T(8,128)(2,1)S(1)} %fusion.6), channel_id=1, source_target_pairs={{0,192},{32,224},{64,0},{96,32},{128,64},{160,96},{192,128},{224,1... | collective-permute-start | bytes 393224 | tf_op jit(solution)/shard_map/ppermute | solution.py:398
  89.1 0.3 collective-permute-done.11
  89.4 0.1 convert_element_type.63
  89.6 0.3 collective-permute-start.14
  90.0 3.4 %collective-permute-done.16 = f16[2,64,512]{2,1,0:T(8,128)(2,1)S(1)} collective-permute-done((f16[2,64,512]{2,1,0:T(8,128)(2,1)S(1)}, f16[2,64,512]{2,1,0:T(8,128)(2,1)S(1)}, u32[]{:S(2)}, u32[]{:S(2)}) %collective-permute-start.16) | collective-permute-done | bytes 131104 | tf_op jit(solution)/shard_map/ppermute | solution.py:398
  93.4 5.2 %collective-permute-done.14 = f16[2,64,512]{2,1,0:T(8,128)(2,1)S(1)} collective-permute-done((f16[2,64,512]{2,1,0:T(8,128)(2,1)S(1)}, f16[2,64,512]{2,1,0:T(8,128)(2,1)S(1)}, u32[]{:S(2)}, u32[]{:S(2)}) %collective-permute-start.14) | collective-permute-done | bytes 131104 | tf_op jit(solution)/shard_map/ppermute | solution.py:398
  98.6 0.1 fusion.4
  98.7 1.3 %collective-permute-start.17 = (f32[64,512]{1,0:T(8,128)S(1)}, f32[64,512]{1,0:T(8,128)S(1)}, u32[]{:S(2)}, u32[]{:S(2)}) collective-permute-start(f32[64,512]{1,0:T(8,128)S(1)} %get-tuple-element.53), channel_id=1, source_target_pairs={{0,2},{2,0},{1,3},{3,1},{4,6},{6,4},{5,7},{7,5},{8,10},{10,8},{9,1... | collective-permute-start | bytes 393224 | tf_op jit(solution)/shard_map/ppermute | solution.py:351
  100.0 1.8 %all-to-all-done.3 = f16[16,128,512]{2,1,0:T(8,128)(2,1)S(1)} async-done(((f16[16,128,512]{2,1,0:T(8,128)(2,1)}), f16[16,128,512]{2,1,0:T(8,128)(2,1)S(1)}, u32[]{:S(2)}, u32[]{:S(2)}) %all-to-all-start.3) | async-done | bytes 2097184 | tf_op jit(solution)/shard_map/all_to_all | solution.py:457
  101.8 1.1 %multiply_reduce_fusion = f32[128,512]{1,0:T(8,128)} fusion(f16[16,128,512]{2,1,0:T(8,128)(2,1)S(1)} %all-to-all-done.3, f32[512]{0:T(512)S(1)} %bitcast.73), kind=kLoop, calls=%fused_computation | loop fusion | flops 3080192 | bytes 2361344 | tf_op jit(solution)/shard_map/reduce_sum | solution.py:486
  102.9 1.2 %collective-permute-done.17 = f32[64,512]{1,0:T(8,128)S(1)} collective-permute-done((f32[64,512]{1,0:T(8,128)S(1)}, f32[64,512]{1,0:T(8,128)S(1)}, u32[]{:S(2)}, u32[]{:S(2)}) %collective-permute-start.17) | collective-permute-done | bytes 131104 | tf_op jit(solution)/shard_map/ppermute | solution.py:351
  104.1 0.7 maximum_select_fusion
  (30 shorter events, 0.4 us)
Async XLA Ops:
  0.6 9.1 %collective-permute-start = (bf16[128,512]{1,0:T(8,128)(2,1)}, bf16[128,512]{1,0:T(8,128)(2,1)S(1)}, u32[]{:S(2)}, u32[]{:S(2)}) collective-permute-start(bf16[128,512]{1,0:T(8,128)(2,1)} %param.4), channel_id=1, source_target_pairs={{0,2},{2,0},{1,3},{3,1},{4,6},{6,4},{5,7},{7,5},{8,10},{10,8},{9,1... | collective-permute-start | bytes 393224 | tf_op jit(solution)/shard_map/ppermute | solution.py:351
  3.7 12.6 %all-to-all-start = ((bf16[4,128,512]{2,1,0:T(8,128)(2,1)}), bf16[4,128,512]{2,1,0:T(8,128)(2,1)S(1)}, u32[]{:S(2)}, u32[]{:S(2)}) async-start(bf16[4,128,512]{2,1,0:T(8,128)(2,1)} %broadcast_in_dim.6), calls=%async_computation | async-start | bytes 1048576 | tf_op jit(solution)/shard_map/all_to_all | solution.py:374
  8.1 0.7 copy-start
  8.8 0.9 copy-start.3
  9.8 12.8 %collective-permute-start.3 = (bf16[2,64,512]{2,1,0:T(8,128)(2,1)S(1)}, bf16[2,64,512]{2,1,0:T(8,128)(2,1)S(1)}, u32[]{:S(2)}, u32[]{:S(2)}) collective-permute-start(bf16[2,64,512]{2,1,0:T(8,128)(2,1)S(1)} %maximum_select_fusion.1.own), channel_id=1, source_target_pairs={{0,64},{32,96},{64,128},{96,160},{128,192},{160,224},{192,0},{224,... | collective-permute-start | bytes 393224 | tf_op jit(solution)/shard_map/ppermute | solution.py:398
  13.1 12.8 %collective-permute-start.1 = (bf16[2,64,512]{2,1,0:T(8,128)(2,1)S(1)}, bf16[2,64,512]{2,1,0:T(8,128)(2,1)S(1)}, u32[]{:S(2)}, u32[]{:S(2)}) collective-permute-start(bf16[2,64,512]{2,1,0:T(8,128)(2,1)S(1)} %maximum_select_fusion.1.own), channel_id=1, source_target_pairs={{0,192},{32,224},{64,0},{96,32},{128,64},{160,96},{192,128},{224,1... | collective-permute-start | bytes 393224 | tf_op jit(solution)/shard_map/ppermute | solution.py:398
  17.8 20.0 %all-to-all-start.1 = ((bf16[4,4,128,512]{3,2,1,0:T(8,128)(2,1)}), bf16[4,4,128,512]{3,2,1,0:T(8,128)(2,1)S(1)}, u32[]{:S(2)}, u32[]{:S(2)}) async-start(bf16[4,4,128,512]{3,2,1,0:T(8,128)(2,1)} %broadcast_in_dim.7), calls=%async_computation.1 | async-start | bytes 4194304 | tf_op jit(solution)/shard_map/all_to_all | solution.py:374
  22.6 9.1 %collective-permute-start.4 = (bf16[64,512]{1,0:T(8,128)(2,1)S(1)}, bf16[64,512]{1,0:T(8,128)(2,1)S(1)}, u32[]{:S(2)}, u32[]{:S(2)}) collective-permute-start(bf16[64,512]{1,0:T(8,128)(2,1)S(1)} %slice_bitcast_fusion.12), channel_id=1, source_target_pairs={{0,64},{32,96},{64,128},{96,160},{128,192},{160,224},{192,0},{224,... | collective-permute-start | bytes 196616 | tf_op jit(solution)/shard_map/ppermute | solution.py:398
  26.0 11.6 %collective-permute-start.6 = (bf16[2,128,512]{2,1,0:T(8,128)(2,1)S(1)}, bf16[2,128,512]{2,1,0:T(8,128)(2,1)S(1)}, u32[]{:S(2)}, u32[]{:S(2)}) collective-permute-start(bf16[2,128,512]{2,1,0:T(8,128)(2,1)S(1)} %get-tuple-element.54), channel_id=1, source_target_pairs={{0,32},{32,64},{64,96},{96,128},{128,160},{160,192},{192,224},{224... | collective-permute-start | bytes 786440 | tf_op jit(solution)/shard_map/ppermute | solution.py:398
  28.0 9.7 %collective-permute-start.5 = (bf16[2,128,512]{2,1,0:T(8,128)(2,1)S(1)}, bf16[2,128,512]{2,1,0:T(8,128)(2,1)S(1)}, u32[]{:S(2)}, u32[]{:S(2)}) collective-permute-start(bf16[2,128,512]{2,1,0:T(8,128)(2,1)S(1)} %get-tuple-element.55), channel_id=1, source_target_pairs={{0,224},{32,0},{64,32},{96,64},{128,96},{160,128},{192,160},{224,1... | collective-permute-start | bytes 786440 | tf_op jit(solution)/shard_map/ppermute | solution.py:398
  29.3 8.3 %collective-permute-start.2 = (bf16[64,512]{1,0:T(8,128)(2,1)S(1)}, bf16[64,512]{1,0:T(8,128)(2,1)S(1)}, u32[]{:S(2)}, u32[]{:S(2)}) collective-permute-start(bf16[64,512]{1,0:T(8,128)(2,1)S(1)} %slice_bitcast_fusion.13), channel_id=1, source_target_pairs={{0,192},{32,224},{64,0},{96,32},{128,64},{160,96},{192,128},{224,1... | collective-permute-start | bytes 196616 | tf_op jit(solution)/shard_map/ppermute | solution.py:398
  39.1 2.7 %collective-permute-start.7 = (f32[512,512]{1,0:T(8,128)S(1)}, f32[512,512]{1,0:T(8,128)S(1)}, u32[]{:S(2)}, u32[]{:S(2)}) collective-permute-start(f32[512,512]{1,0:T(8,128)S(1)} %shard_map.52.own_ref), channel_id=1, source_target_pairs={{0,1},{1,0},{2,3},{3,2},{4,5},{5,4},{6,7},{7,6},{8,9},{9,8},{10,11... | collective-permute-start | bytes 3145736 | tf_op jit(solution)/shard_map/ppermute | solution.py:351
  40.4 2.9 %collective-permute-start.8 = (f32[512,512]{1,0:T(8,128)S(1)}, f32[512,512]{1,0:T(8,128)S(1)}, u32[]{:S(2)}, u32[]{:S(2)}) collective-permute-start(f32[512,512]{1,0:T(8,128)S(1)} %shard_map.54.own_ref), channel_id=1, source_target_pairs={{0,1},{1,0},{2,3},{3,2},{4,5},{5,4},{6,7},{7,6},{8,9},{9,8},{10,11... | collective-permute-start | bytes 3145736 | tf_op jit(solution)/shard_map/ppermute | solution.py:351
  41.3 2.0 %collective-permute-start.9 = (f32[2,512]{1,0:T(2,128)S(1)}, f32[2,512]{1,0:T(2,128)S(1)}, u32[]{:S(2)}, u32[]{:S(2)}) collective-permute-start(f32[2,512]{1,0:T(2,128)S(1)} %pad_maximum_fusion.4.most_ref), channel_id=1, source_target_pairs={{0,1},{1,0},{2,3},{3,2},{4,5},{5,4},{6,7},{7,6},{8,9},{9,8},{10,11... | collective-permute-start | bytes 12296 | tf_op jit(solution)/shard_map/ppermute | solution.py:351
  57.3 4.2 %collective-permute-start.10 = (f32[24,128]{1,0:T(8,128)S(1)}, f32[24,128]{1,0:T(8,128)S(1)}, u32[]{:S(2)}, u32[]{:S(2)}) collective-permute-start(f32[24,128]{1,0:T(8,128)S(1)} %shard_map.56.known_ref), channel_id=1, source_target_pairs={{0,1},{1,0},{2,3},{3,2},{4,5},{5,4},{6,7},{7,6},{8,9},{9,8},{10,11... | collective-permute-start | bytes 36872 | tf_op jit(solution)/shard_map/ppermute | solution.py:351
  68.6 5.7 %copy-start.2 = (f16[512,512]{1,0:T(8,128)(2,1)S(1)}, f16[512,512]{1,0:T(8,128)(2,1)}, u32[]{:S(2)}) copy-start(f16[512,512]{1,0:T(8,128)(2,1)} %fusion) | copy-start | bytes 1572868
  68.6 5.7 %copy-start.1 = (f16[512,512]{1,0:T(8,128)(2,1)S(1)}, f16[512,512]{1,0:T(8,128)(2,1)}, u32[]{:S(2)}) copy-start(f16[512,512]{1,0:T(8,128)(2,1)} %fusion.1) | copy-start | bytes 1572868
  68.6 33.2 %all-to-all-start.3 = ((f16[16,128,512]{2,1,0:T(8,128)(2,1)}), f16[16,128,512]{2,1,0:T(8,128)(2,1)S(1)}, u32[]{:S(2)}, u32[]{:S(2)}) async-start(f16[16,128,512]{2,1,0:T(8,128)(2,1)} %bitcast.78), calls=%async_computation.3 | async-start | bytes 4194304 | tf_op jit(solution)/shard_map/all_to_all | solution.py:457
  74.5 9.2 %collective-permute-start.12 = (f16[2,128,512]{2,1,0:T(8,128)(2,1)S(1)}, f16[2,128,512]{2,1,0:T(8,128)(2,1)S(1)}, u32[]{:S(2)}, u32[]{:S(2)}) collective-permute-start(f16[2,128,512]{2,1,0:T(8,128)(2,1)S(1)} %pad_maximum_fusion.3), channel_id=1, source_target_pairs={{0,224},{32,0},{64,32},{96,64},{128,96},{160,128},{192,160},{224,1... | collective-permute-start | bytes 786440 | tf_op jit(solution)/shard_map/ppermute | solution.py:398
  76.1 10.1 %collective-permute-start.15 = (f16[64,512]{1,0:T(8,128)(2,1)S(1)}, f16[64,512]{1,0:T(8,128)(2,1)S(1)}, u32[]{:S(2)}, u32[]{:S(2)}) collective-permute-start(f16[64,512]{1,0:T(8,128)(2,1)S(1)} %get-tuple-element.45), channel_id=1, source_target_pairs={{0,192},{32,224},{64,0},{96,32},{128,64},{160,96},{192,128},{224,1... | collective-permute-start | bytes 196616 | tf_op jit(solution)/shard_map/ppermute | solution.py:398
  77.7 11.9 %collective-permute-start.13 = (f16[64,512]{1,0:T(8,128)(2,1)S(1)}, f16[64,512]{1,0:T(8,128)(2,1)S(1)}, u32[]{:S(2)}, u32[]{:S(2)}) collective-permute-start(f16[64,512]{1,0:T(8,128)(2,1)S(1)} %get-tuple-element.42), channel_id=1, source_target_pairs={{0,64},{32,96},{64,128},{96,160},{128,192},{160,224},{192,0},{224,... | collective-permute-start | bytes 196616 | tf_op jit(solution)/shard_map/ppermute | solution.py:398
  79.1 10.3 %collective-permute-start.11 = (f16[2,128,512]{2,1,0:T(8,128)(2,1)S(1)}, f16[2,128,512]{2,1,0:T(8,128)(2,1)S(1)}, u32[]{:S(2)}, u32[]{:S(2)}) collective-permute-start(f16[2,128,512]{2,1,0:T(8,128)(2,1)S(1)} %pad_maximum_fusion.2), channel_id=1, source_target_pairs={{0,32},{32,64},{64,96},{96,128},{128,160},{160,192},{192,224},{224... | collective-permute-start | bytes 786440 | tf_op jit(solution)/shard_map/ppermute | solution.py:398
  86.2 7.1 %collective-permute-start.16 = (f16[2,64,512]{2,1,0:T(8,128)(2,1)S(1)}, f16[2,64,512]{2,1,0:T(8,128)(2,1)S(1)}, u32[]{:S(2)}, u32[]{:S(2)}) collective-permute-start(f16[2,64,512]{2,1,0:T(8,128)(2,1)S(1)} %fusion.6), channel_id=1, source_target_pairs={{0,192},{32,224},{64,0},{96,32},{128,64},{160,96},{192,128},{224,1... | collective-permute-start | bytes 393224 | tf_op jit(solution)/shard_map/ppermute | solution.py:398
  89.6 8.9 %collective-permute-start.14 = (f16[2,64,512]{2,1,0:T(8,128)(2,1)S(1)}, f16[2,64,512]{2,1,0:T(8,128)(2,1)S(1)}, u32[]{:S(2)}, u32[]{:S(2)}) collective-permute-start(f16[2,64,512]{2,1,0:T(8,128)(2,1)S(1)} %fusion.5), channel_id=1, source_target_pairs={{0,64},{32,96},{64,128},{96,160},{128,192},{160,224},{192,0},{224,... | collective-permute-start | bytes 393224 | tf_op jit(solution)/shard_map/ppermute | solution.py:398
  98.7 5.4 %collective-permute-start.17 = (f32[64,512]{1,0:T(8,128)S(1)}, f32[64,512]{1,0:T(8,128)S(1)}, u32[]{:S(2)}, u32[]{:S(2)}) collective-permute-start(f32[64,512]{1,0:T(8,128)S(1)} %get-tuple-element.53), channel_id=1, source_target_pairs={{0,2},{2,0},{1,3},{3,1},{4,6},{6,4},{5,7},{7,5},{8,10},{10,8},{9,1... | collective-permute-start | bytes 393224 | tf_op jit(solution)/shard_map/ppermute | solution.py:351
